TPU v7x, 32 devices: a whole 2x2x4 slice. The times are simulated.
32 devices in a mesh: groups: 2 (over x), paths: 16 (over z, y, core).
Axes of the slice: x: 2, y: 2, z: 4, core: 2. Of those that a mesh axis runs over, the one named last changes fastest.
Arguments:
- path_basis: bfloat16 [4096, 512], P(('groups', 'paths')), parts along dimension 0, may hold values from -6 to 6
- proxy_weight: bfloat16 [4096, 512], P(('groups', 'paths')), parts along dimension 0, may hold values from -0.25 to 0.25
- notional: bfloat16 [4096], P(('groups', 'paths')), parts along dimension 0, may hold values from -4 to 4
- set_of: int32 [4096], P('groups'), parts along dimension 0, may hold values from 0 to 511
- threshold_index: int32 [1024], P('groups'), parts along dimension 0, may hold values from 0 to 15
- threshold_levels: float32 [32], P('groups'), parts along dimension 0, may hold values from 0.5 to 20
- loss_rate: float32 [1024], P('groups'), parts along dimension 0, may hold values from 0.4 to 1
Outputs:
- expected_loss: float32 [2], P('groups'), parts along dimension 0
- basis_adjoint: float32 [4096, 512], P(('groups', 'paths')), parts along dimension 0
- weight_adjoint: float32 [4096, 512], P(('groups', 'paths')), parts along dimension 0
There are 2 independent parts, one for each index of `groups`. A program takes and returns all parts, laid end to end along the dimension named above; each array names one. Nothing has to cross between parts.
Inputs may be any that keep to these rules, and one draw needn't show every extreme that they name: `set_of`: netting set of each trade; set sizes are uneven.
All inputs are finite; a program needn't handle non-finite values.
Results may differ from a plain program's by a relative error of at most 0.0041.
Values may be sent and summed in bfloat16 or wider, within the bound.
No kernel may reach another device: no remote copies, remote signals or barrier semaphores. Data moves between devices by JAX's collectives and lax.ppermute only.
A program may use at most 64 MiB of HBM per device.

v0:
```python
import math
from functools import partial

import jax
import jax.numpy as jnp
from jax import lax
from jax.experimental import pallas as pl
from jax.experimental.pallas import tpu as pltpu
from jax.sharding import PartitionSpec as P

REGRESSORS = 32
RIDGE_SCALE = 0.01
PRECISE = lax.Precision.HIGHEST
F32 = jnp.float32
BF16 = jnp.bfloat16
LANES = 128
CHUNK = 256
VMEM_BYTES = 48 * 1024 * 1024
LOG2_E = math.log2(math.e)
CONSTANT = REGRESSORS - 1


def split_bits(size):
    count = size.bit_length() - 1
    half = count // 2
    return list(range(1, half + 1)), list(range(count - 1, half, -1)) + [0]


def dot(a, b, ca=1, cb=0, precision=None):
    return lax.dot_general(
        a, b, (((ca,), (cb,)), ((), ())), precision=precision, preferred_element_type=F32
    )


def three(x, axis):
    high = x.astype(BF16)
    rest = x - high.astype(F32)
    middle = rest.astype(BF16)
    low = (rest - middle.astype(F32)).astype(BF16)
    return jnp.concatenate([high, middle, low], axis=axis)


def three_rows(x):
    blank = jnp.zeros((LANES - 3 * REGRESSORS, x.shape[1]), BF16)
    return jnp.concatenate([three(x, 0), blank], axis=0)


def lanes(shape):
    return lax.broadcasted_iota(jnp.int32, shape, len(shape) - 1)


def rows(shape):
    return lax.broadcasted_iota(jnp.int32, shape, len(shape) - 2)


def softplus(x):
    return jnp.maximum(x, 0.0) + jnp.log1p(jnp.exp(-jnp.abs(x)))


def sigmoid(x):
    small = jnp.exp(-jnp.abs(x))
    return jnp.where(x >= 0.0, 1.0, small) / (1.0 + small)


def each_chunk(size, step):
    count = size // CHUNK

    def body(i, carry):
        step(pl.ds(pl.multiple_of(i * CHUNK, CHUNK), CHUNK))
        return carry

    lax.fori_loop(0, count, body, 0, unroll=count <= 8)


def invert(matrix):
    size = matrix.shape[0]
    work = jnp.concatenate([matrix, jnp.eye(size, dtype=F32)], axis=1)
    row = rows(work.shape)
    for k in range(0, size, 2):
        left, right = work[:, k : k + 1], work[:, k + 1 : k + 2]
        upper, lower = work[k : k + 1], work[k + 1 : k + 2]
        a, b, c, d = left[k : k + 1], right[k : k + 1], left[k + 1 : k + 2], right[k + 1 : k + 2]
        scale = 1.0 / (a * d - b * c)
        upper, lower = (d * upper - b * lower) * scale, (a * lower - c * upper) * scale
        work = work - left * upper - right * lower
        work = jnp.where(row == k, upper, jnp.where(row == k + 1, lower, work))
    return work[:, size:]


def lead_kernel(*refs):
    x_refs, lead_ref = refs[:-1], refs[-1]
    start = 0
    for x in x_refs:
        turned = x[:, :LANES].astype(F32).T[:REGRESSORS]
        turned = jnp.where(rows(turned.shape) == CONSTANT, 1.0, turned)
        lead_ref[:, start : start + x.shape[0]] = turned.astype(BF16)
        start += x.shape[0]


def tables_kernel(
    trade_masks, inner, me_ref, level_ref, set_ref, index_ref, rate_ref,
    member_ref, thresh_out_ref, rate_out_ref,
):
    me = me_ref[0]
    place = (me >> 1) & (inner - 1)
    size = member_ref.shape[0] // inner
    trades = set_ref.shape[-1]
    for m in range(inner):
        here = slice(m * size, (m + 1) * size)
        label = (place ^ m) * size + rows((size, 1))
        for j, mask in enumerate(trade_masks):
            member_ref[here, j * trades : (j + 1) * trades] = jnp.where(
                set_ref[me ^ mask] == label, 1.0, 0.0
            ).astype(BF16)
        index = index_ref[place ^ m]
        thresh = jnp.zeros(index.shape, F32)
        for k in range(level_ref.shape[0]):
            thresh = jnp.where(index == k, level_ref[k], thresh)
        thresh_out_ref[:, here] = thresh
        rate_out_ref[:, here] = rate_ref[place ^ m]


def design_kernel(*refs):
    lead_refs, (design_ref, rows_ref) = refs[:-2], refs[-2:]
    size = lead_refs[0].shape[1]
    for d, lead_ref in enumerate(lead_refs):
        here = slice(d * size, (d + 1) * size)
        design_ref[:, here] = lead_ref[...]
        turned = lead_ref[...].astype(F32).T
        blank = jnp.zeros((size, LANES - 3 * REGRESSORS), F32)
        rows_ref[here] = jnp.concatenate([turned] * 3 + [blank], axis=1).astype(BF16)


def inverse_kernel(ridge, *refs):
    square = (REGRESSORS, REGRESSORS)
    gram = jnp.where(rows(square) == lanes(square), ridge, 0.0)
    for lead_ref in refs[:-1]:
        gram = gram + dot(lead_ref[...], lead_ref[...], 1, 1)
    refs[-1][...] = invert(gram)


def joined_weights(refs):
    return jnp.concatenate([ref[...] for ref in refs], axis=0)


def joined_notionals(refs):
    return jnp.concatenate([ref[...].astype(F32) for ref in refs], axis=1)


def forward_kernel(paths, trades, *refs):
    x_refs, refs = refs[:paths], refs[paths:]
    weights, notional = joined_weights(refs[:trades]), joined_notionals(refs[trades : 2 * trades])
    lead_ref, member_ref, value_ref, *moment_refs = refs[2 * trades :]
    start = 0
    for x in x_refs:
        pre_act = dot(x[...], weights, 1, 1)
        value_ref[start : start + x.shape[0]] = (notional * softplus(pre_act)).astype(BF16)
        start += x.shape[0]
    trade_moment = dot(lead_ref[...], value_ref[...])
    parts = dot(three(trade_moment, 0), member_ref[...], 1, 1)
    moment = parts[:REGRESSORS] + parts[REGRESSORS : 2 * REGRESSORS] + parts[2 * REGRESSORS :]
    size = moment.shape[1] // len(moment_refs)
    for m, moment_ref in enumerate(moment_refs):
        moment_ref[...] = moment[:, m * size : (m + 1) * size]


def slope_kernel(paths, trades, *refs):
    x_refs, refs, slope_ref = refs[:paths], refs[paths:], refs[-1]
    weights, notional = joined_weights(refs[:trades]), joined_notionals(refs[trades : 2 * trades])
    start = 0
    for x in x_refs:
        slope_ref[start : start + x.shape[0]] = notional * sigmoid(dot(x[...], weights, 1, 1))
        start += x.shape[0]


def solve_kernel(
    terms, inverse_ref, design_ref, rows_ref, thresh_ref, rate_ref, *refs
):
    solved_ref, turn_ref, total_ref = refs[terms:]
    moment = refs[0][...]
    for ref in refs[1:terms]:
        moment = moment + ref[...]
    size = moment.shape[1]
    inverse = inverse_ref[...]
    coeffs = dot(inverse, moment, precision=PRECISE)
    solved_ref[REGRESSORS:] = coeffs
    is_constant = rows(coeffs.shape) == CONSTANT
    shifted = coeffs - jnp.where(is_constant, thresh_ref[:, :size], 0.0)
    turn_ref[...] = three_rows(-LOG2_E * shifted)
    total_ref[...] = jnp.zeros(total_ref.shape, F32)

    def seeds(here):
        power = jnp.exp2(jnp.minimum(dot(rows_ref[here], turn_ref[...]), 126.0))
        seed = (1.0 / (1.0 + power)).astype(BF16)
        total_ref[...] += dot(design_ref[:, here], seed)

    each_chunk(rows_ref.shape[0], seeds)
    solved_ref[:REGRESSORS] = dot(inverse, total_ref[...] * rate_ref[:, :size], precision=PRECISE)


def joined(refs, part):
    here = slice(part * REGRESSORS, (part + 1) * REGRESSORS)
    return jnp.concatenate([ref[here] for ref in refs], axis=1)


def backward_kernel(scale, paths, trades, member_ref, rows_ref, slope_ref, value_ref, *refs):
    solved_refs, refs = refs[:paths], refs[paths:]
    x_refs, refs = refs[:paths], refs[paths:]
    w_refs, refs = refs[:trades], refs[trades:]
    weight_refs, basis_refs, slopes_ref = refs[:trades], refs[trades:-1], refs[-1]
    traded = dot(three_rows(joined(solved_refs, 0)), member_ref[...]).astype(BF16)
    group = slopes_ref.shape[0]
    spread = dot(rows_ref[:group], traded).astype(BF16).astype(F32)
    slopes_ref[...] = (slope_ref[...] * spread).astype(BF16)
    basis = jnp.concatenate([x[...] for x in x_refs], axis=0)
    weight = (dot(slopes_ref[...], basis, 0, 0) * scale).astype(BF16)
    start = 0
    for part in weight_refs:
        part[...] = weight[start : start + part.shape[0]]
        start += part.shape[0]
    weights = joined_weights(w_refs)
    start = 0
    for part in basis_refs:
        here = slice(start, start + part.shape[0])
        total = dot(slopes_ref[here], weights)
        wide = dot(value_ref[here], traded, 1, 1)
        design = wide
        for k in range(1, 3):
            design = design + pltpu.roll(wide, LANES - k * REGRESSORS, 1)
        design = jnp.where(lanes(design.shape) < CONSTANT, design, 0.0)
        part[:, :LANES] = (total[:, :LANES] + design).astype(BF16)
        part[:, LANES:] = total[:, LANES:].astype(BF16)
        start += part.shape[0]


def loss_kernel(rows_ref, thresh_ref, rate_ref, *refs):
    solved_refs, (loss_ref, own_ref, split_ref, total_ref) = refs[:-4], refs[-4:]
    adjoint = joined(solved_refs, 0)
    coeffs = joined(solved_refs, 1)
    thresh = thresh_ref[...]
    rate = rate_ref[...]
    split_ref[...] = three_rows(coeffs)
    total_ref[...] = jnp.zeros(total_ref.shape, F32)

    def losses(here):
        loss = softplus(dot(rows_ref[here], split_ref[...]) - thresh)
        total_ref[...] += jnp.sum(loss.reshape(-1, *total_ref.shape), axis=0)

    each_chunk(rows_ref.shape[0], losses)
    summed = jnp.sum(jnp.sum(total_ref[...] * rate, axis=0, keepdims=True), axis=1, keepdims=True)
    loss_ref[...] = jnp.broadcast_to(
        summed / (rows_ref.shape[0] * coeffs.shape[1]), loss_ref.shape
    )
    own = rows_ref[: own_ref.shape[0]]
    fitted = dot(own, split_ref[...])
    seed = rate * sigmoid(fitted - thresh)
    rest = seed - dot(own, three_rows(adjoint))
    design = dot(rest, coeffs, 1, 1, PRECISE) - dot(fitted, adjoint, 1, 1, PRECISE)
    blank = jnp.zeros((design.shape[0], LANES - REGRESSORS), F32)
    design = jnp.concatenate([design, blank], axis=1)
    own_ref[...] = jnp.where(lanes(design.shape) < CONSTANT, design, 0.0)


def total(refs):
    out = refs[0][...].astype(F32)
    for ref in refs[1:]:
        out = out + ref[...].astype(F32)
    return out


def sum_kernel(first, own_ref, *refs):
    basis_ref, weight_ref = refs[-2:]
    basis = total(refs[:first])
    basis_ref[:, :LANES] = basis[:, :LANES] + own_ref[...]
    basis_ref[:, LANES:] = basis[:, LANES:]
    weight_ref[...] = total(refs[first:-2])


def call(kernel, outs, *args, name, flops=0, scratch=(), scalars=0):
    size = sum(a.size * a.dtype.itemsize for a in args) + sum(
        math.prod(s) * jnp.dtype(d).itemsize for s, d in outs
    )
    return pl.pallas_call(
        kernel,
        out_shape=[jax.ShapeDtypeStruct(s, d) for s, d in outs],
        in_specs=[pl.BlockSpec(memory_space=pltpu.SMEM)] * scalars
        + [pl.BlockSpec(memory_space=pltpu.VMEM)] * (len(args) - scalars),
        out_specs=[pl.BlockSpec(memory_space=pltpu.VMEM)] * len(outs),
        scratch_shapes=scratch,
        compiler_params=pltpu.CompilerParams(vmem_limit_bytes=VMEM_BYTES),
        cost_estimate=pl.CostEstimate(flops=int(flops), bytes_accessed=int(size), transcendentals=0),
        name=name,
    )(*args)


def shards(
    path_basis, proxy_weight, notional, set_of, threshold_index, threshold_levels, loss_rate
):
    n = lax.axis_size("paths")
    me = lax.axis_index("paths")
    inner_bits, outer_bits = split_bits(n)
    inner, outer = 1 << len(inner_bits), 1 << len(outer_bits)
    path_rows, features = path_basis.shape
    trade_rows = proxy_weight.shape[0]
    paths_all = path_rows * n
    sets = loss_rate.shape[0]
    quarter = sets // inner
    group_paths, group_trades = inner * path_rows, outer * trade_rows

    def swap(x, mask):
        return lax.ppermute(x, "paths", [(d, d ^ mask) for d in range(n)])

    def masks(bits):
        return [
            sum(((m >> j) & 1) << bit for j, bit in enumerate(bits)) for m in range(1 << len(bits))
        ]

    def after(x, *others):
        return lax.optimization_barrier((x, *others))[0]

    def direct(slots, bits):
        sent = [swap(x, mask) for x, mask in zip(slots[:0:-1], masks(bits)[:0:-1])]
        return sent[::-1]

    first_bit = outer_bits[0]
    weights = [proxy_weight, swap(proxy_weight, 1 << first_bit)]
    basis = [path_basis] + direct([path_basis] * inner, inner_bits)
    notionals = [notional, swap(notional, 1 << first_bit)]

    member, thresh, rate = call(
        partial(tables_kernel, masks(outer_bits), inner),
        [((sets, group_trades), BF16), ((1, sets), F32), ((1, sets), F32)],
        me.astype(jnp.int32).reshape(1),
        threshold_levels,
        set_of.reshape(n, 1, trade_rows),
        threshold_index.reshape(inner, 1, quarter),
        loss_rate.reshape(inner, 1, quarter),
        name="tables",
        scalars=2,
    )
    for bit in outer_bits[1:]:
        weights = weights + [
            swap(w if k else after(w, member), 1 << bit) for k, w in enumerate(weights)
        ]
        notionals = notionals + [swap(x, 1 << bit) for x in notionals]
    notionals = [x[None, :] for x in notionals]
    (lead,) = call(lead_kernel, [((REGRESSORS, group_paths), BF16)], *basis, name="lead")
    leads = [lead] + direct([lead] * outer, outer_bits)
    value, *moments = call(
        partial(forward_kernel, inner, outer),
        [((group_paths, group_trades), BF16)] + [((REGRESSORS, quarter), F32)] * inner,
        *basis, *weights, *notionals, lead, member,
        name="forward",
    )
    moment = sum(direct(moments, inner_bits), moments[0])
    for bit in outer_bits[:0:-1]:
        moment = moment + swap(moment, 1 << bit)
    moments = [moment, swap(moment, 1 << first_bit)]
    (inverse,) = call(
        partial(inverse_kernel, RIDGE_SCALE * paths_all),
        [((REGRESSORS, REGRESSORS), F32)],
        *leads,
        name="inverse",
    )
    design_all, design_rows = call(
        design_kernel,
        [((REGRESSORS, paths_all), BF16), ((paths_all, LANES), BF16)],
        *leads,
        name="design",
    )
    (solved,) = call(
        partial(solve_kernel, len(moments)),
        [((2 * REGRESSORS, quarter), F32)],
        inverse, design_all, design_rows, thresh, rate, *moments,
        name="solve",
        scratch=[pltpu.VMEM((LANES, quarter), BF16), pltpu.VMEM((REGRESSORS, quarter), F32)],
    )
    solved = [solved] + direct([solved] * inner, inner_bits)
    (slope,) = call(
        partial(slope_kernel, inner, outer),
        [((group_paths, group_trades), F32)],
        *basis, *weights, *notionals,
        name="slope",
    )
    parts = call(
        partial(backward_kernel, 1.0 / math.sqrt(paths_all), inner, outer),
        [((trade_rows, features), BF16)] * outer + [((path_rows, features), BF16)] * inner,
        member, design_rows, slope, value, *solved, *basis, *weights,
        name="backward",
        scratch=[pltpu.VMEM((group_paths, group_trades), BF16)],
    )
    terms = [[part] for part in parts[:outer]]
    for bit in reversed(outer_bits):
        count = len(terms) // 2
        arrived = None
        for k in reversed(range(count)):
            gone = terms[count + k]
            gone = gone[0] if len(gone) == 1 else sum(g.astype(F32) for g in gone).astype(BF16)
            if arrived is not None:
                gone = after(gone, arrived)
            arrived = swap(gone, 1 << bit)
            terms[k].append(arrived)
            if bit == outer_bits[-1] and k == count - 1:
                basis_parts = list(parts[outer:])
                basis_parts[1] = after(basis_parts[1], arrived)
        terms = terms[:count]
    weight_terms = terms[0]
    basis_terms = [basis_parts[0]] + direct(basis_parts, inner_bits)
    loss, own_adjoint = call(
        loss_kernel,
        [((8, LANES), F32), ((path_rows, LANES), F32)],
        design_rows, thresh, rate, *solved,
        name="loss",
        scratch=[pltpu.VMEM((LANES, sets), BF16), pltpu.VMEM((8, sets), F32)],
    )
    basis_adjoint, weight_adjoint = call(
        partial(sum_kernel, len(basis_terms)),
        [((path_rows, features), F32), ((trade_rows, features), F32)],
        own_adjoint, *basis_terms, *weight_terms,
        name="sums",
    )
    return (loss[0, :1], basis_adjoint, weight_adjoint)


def solution(mesh):
    placed = (
        P(("groups", "paths"), None),
        P(("groups", "paths"), None),
        P(("groups", "paths")),
        P("groups"),
        P("groups"),
        P("groups"),
        P("groups"),
    )
    return jax.shard_map(
        shards,
        mesh=mesh,
        in_specs=placed,
        out_specs=(P("groups"), P(("groups", "paths"), None), P(("groups", "paths"), None)),
        check_vma=False,
    )
```

profile of v0, /device:TPU:0, one launch (start us, length us, event | category | flops | bytes accessed | tf_op | source)
XLA Modules:
  0.0 57.1 jit_solution(2659818939588442802)
XLA Ops:
  0.6 4.1 %collective-permute-start.6 = (bf16[128,512]{1,0:T(8,128)(2,1)}, bf16[128,512]{1,0:T(8,128)(2,1)S(1)}, u32[]{:S(2)}, u32[]{:S(2)}) collective-permute-start(bf16[128,512]{1,0:T(8,128)(2,1)} %refs_8_.1), channel_id=1, source_target_pairs={{0,8},{1,9},{2,10},{3,11},{4,12},{5,13},{6,14},{7,15},{8,0},{9,1},... | collective-permute-start | bytes 393224 | tf_op jit(solution)/shard_map/ppermute | solution.py:311
  4.7 1.5 %collective-permute-start = (bf16[128,512]{1,0:T(8,128)(2,1)}, bf16[128,512]{1,0:T(8,128)(2,1)S(1)}, u32[]{:S(2)}, u32[]{:S(2)}) collective-permute-start(bf16[128,512]{1,0:T(8,128)(2,1)} %refs_4_.5), channel_id=1, source_target_pairs={{0,2},{1,3},{2,0},{3,1},{4,6},{5,7},{6,4},{7,5},{8,10},{9,11},{10,... | collective-permute-start | bytes 393224 | tf_op jit(solution)/shard_map/ppermute | solution.py:311
  6.3 1.6 %collective-permute-start.1 = (bf16[128,512]{1,0:T(8,128)(2,1)}, bf16[128,512]{1,0:T(8,128)(2,1)S(1)}, u32[]{:S(2)}, u32[]{:S(2)}) collective-permute-start(bf16[128,512]{1,0:T(8,128)(2,1)} %refs_4_.5), channel_id=1, source_target_pairs={{0,4},{1,5},{2,6},{3,7},{4,0},{5,1},{6,2},{7,3},{8,12},{9,13},{10,... | collective-permute-start | bytes 393224 | tf_op jit(solution)/shard_map/ppermute | solution.py:311
  9.7 3.8 %collective-permute-done.9 = bf16[128]{0:T(256)(128)(2,1)S(1)} collective-permute-done((bf16[128]{0:T(256)(128)(2,1)}, bf16[128]{0:T(256)(128)(2,1)S(1)}, u32[]{:S(2)}, u32[]{:S(2)}) %collective-permute-start.9) | collective-permute-done | bytes 288 | tf_op jit(solution)/shard_map/ppermute | solution.py:311
  14.5 1.2 %collective-permute-done.2.refs_3_.refs_7_ = bf16[128,512]{1,0:T(8,128)(2,1)S(1)} collective-permute-done((bf16[128,512]{1,0:T(8,128)(2,1)}, bf16[128,512]{1,0:T(8,128)(2,1)S(1)}, u32[]{:S(2)}, u32[]{:S(2)}) %collective-permute-start.2) | collective-permute-done | bytes 131104 | tf_op jit(solution)/shard_map/ppermute | solution.py:311
  17.5 1.3 %forward.1 = (bf16[512,512]{1,0:T(8,128)(2,1)S(1)}, f32[32,128]{1,0:T(8,128)S(1)}, f32[32,128]{1,0:T(8,128)S(1)}, f32[32,128]{1,0:T(8,128)S(1)}, f32[32,128]{1,0:T(8,128)S(1)}) custom-call(bf16[128,512]{1,0:T(8,128)(2,1)S(1)} %copy-done, bf16[128,512]{1,0:T(8,128)(2,1)S(1)} %collective-permute-done.refs_1_.refs_5_, ...), custom_call_target="tpu_custom_call" | custom-call | bytes 2196480 | tf_op jit(solution)/shard_map/forward/pallas_call | solution.py:283
  18.8 1.5 %collective-permute-start.12 = (f32[32,128]{1,0:T(8,128)S(1)}, f32[32,128]{1,0:T(8,128)S(1)}, u32[]{:S(2)}, u32[]{:S(2)}) collective-permute-start(f32[32,128]{1,0:T(8,128)S(1)} %get-tuple-element.35), channel_id=1, source_target_pairs={{0,2},{1,3},{2,0},{3,1},{4,6},{5,7},{6,4},{7,5},{8,10},{9,11},{10,... | collective-permute-start | bytes 49160 | tf_op jit(solution)/shard_map/ppermute | solution.py:311
  20.2 1.2 %collective-permute-start.13 = (f32[32,128]{1,0:T(8,128)S(1)}, f32[32,128]{1,0:T(8,128)S(1)}, u32[]{:S(2)}, u32[]{:S(2)}) collective-permute-start(f32[32,128]{1,0:T(8,128)S(1)} %get-tuple-element.36), channel_id=1, source_target_pairs={{0,4},{1,5},{2,6},{3,7},{4,0},{5,1},{6,2},{7,3},{8,12},{9,13},{10,... | collective-permute-start | bytes 49160 | tf_op jit(solution)/shard_map/ppermute | solution.py:311
  22.3 2.1 %collective-permute-start.3 = (bf16[32,512]{1,0:T(8,128)(2,1)S(1)}, bf16[32,512]{1,0:T(8,128)(2,1)S(1)}, u32[]{:S(2)}, u32[]{:S(2)}) collective-permute-start(bf16[32,512]{1,0:T(8,128)(2,1)S(1)} %lead.1.refs_0_.refs_12_), channel_id=1, source_target_pairs={{0,8},{1,9},{2,10},{3,11},{4,12},{5,13},{6,14},{7,15},{8,0},{9,1},... | collective-permute-start | bytes 98312 | tf_op jit(solution)/shard_map/ppermute | solution.py:311
  24.4 0.9 %collective-permute-start.5 = (bf16[32,512]{1,0:T(8,128)(2,1)S(1)}, bf16[32,512]{1,0:T(8,128)(2,1)S(1)}, u32[]{:S(2)}, u32[]{:S(2)}) collective-permute-start(bf16[32,512]{1,0:T(8,128)(2,1)S(1)} %lead.1.refs_0_.refs_12_), channel_id=1, source_target_pairs={{0,9},{1,8},{2,11},{3,10},{4,13},{5,12},{6,15},{7,14},{8,1},{9,0},... | collective-permute-start | bytes 98312 | tf_op jit(solution)/shard_map/ppermute | solution.py:311
  26.1 1.2 %collective-permute-done.15 = f32[32,128]{1,0:T(8,128)S(1)} collective-permute-done((f32[32,128]{1,0:T(8,128)S(1)}, f32[32,128]{1,0:T(8,128)S(1)}, u32[]{:S(2)}, u32[]{:S(2)}) %collective-permute-start.15) | collective-permute-done | bytes 16416 | tf_op jit(solution)/shard_map/ppermute | solution.py:311
  27.2 1.9 %collective-permute-start.16 = (f32[32,128]{1,0:T(8,128)S(1)}, f32[32,128]{1,0:T(8,128)S(1)}, u32[]{:S(2)}, u32[]{:S(2)}) collective-permute-start(f32[32,128]{1,0:T(8,128)S(1)} %add.18.refs_0_), channel_id=1, source_target_pairs={{0,8},{1,9},{2,10},{3,11},{4,12},{5,13},{6,14},{7,15},{8,0},{9,1},... | collective-permute-start | bytes 49160 | tf_op jit(solution)/shard_map/ppermute | solution.py:311
  29.6 3.7 %inverse.1.inverse_ref = f32[32,32]{1,0:T(8,128)S(1)} custom-call(bf16[32,512]{1,0:T(8,128)(2,1)S(1)} %lead.1.refs_0_.refs_12_, bf16[32,512]{1,0:T(8,128)(2,1)S(1)} %collective-permute-done.3.refs_1_, bf16[32,512]{1,0:T(8,128)(2,1)S(1)} %collective-permute-done.4.refs_2_, bf16[32,512]{1,0:T(8,128)(2,1)S(1)} %collective-permute-done.5.refs_3_), custom_call_target="tpu_custom_call" | custom-call | bytes 135168 | tf_op jit(solution)/shard_map/inverse/pallas_call | solution.py:283
  33.4 1.8 %solve.1.refs_0_ = f32[64,128]{1,0:T(8,128)S(1)} custom-call(f32[32,32]{1,0:T(8,128)S(1)} %inverse.1.inverse_ref, bf16[32,2048]{1,0:T(8,128)(2,1)S(1)} %get-tuple-element.31.design_ref, bf16[2048,128]{1,0:T(8,128)(2,1)S(1)} %get-tuple-element.28.rows_ref, f32[1,512]{1,0:T(1,128)S(1)} %get-tuple-element.29.thresh_ref, ...), custom_call_target="tpu_custom_call" | custom-call | bytes 729088 | tf_op jit(solution)/shard_map/solve/pallas_call | solution.py:283
  35.1 1.1 %collective-permute-start.17 = (f32[64,128]{1,0:T(8,128)S(1)}, f32[64,128]{1,0:T(8,128)S(1)}, u32[]{:S(2)}, u32[]{:S(2)}) collective-permute-start(f32[64,128]{1,0:T(8,128)S(1)} %solve.1.refs_0_), channel_id=1, source_target_pairs={{0,2},{1,3},{2,0},{3,1},{4,6},{5,7},{6,4},{7,5},{8,10},{9,11},{10,... | collective-permute-start | bytes 98312 | tf_op jit(solution)/shard_map/ppermute | solution.py:311
  37.1 1.5 %collective-permute-start.19 = (f32[64,128]{1,0:T(8,128)S(1)}, f32[64,128]{1,0:T(8,128)S(1)}, u32[]{:S(2)}, u32[]{:S(2)}) collective-permute-start(f32[64,128]{1,0:T(8,128)S(1)} %solve.1.refs_0_), channel_id=1, source_target_pairs={{0,6},{1,7},{2,4},{3,5},{4,2},{5,3},{6,0},{7,1},{8,14},{9,15},{10,... | collective-permute-start | bytes 98312 | tf_op jit(solution)/shard_map/ppermute | solution.py:311
  40.4 1.5 %collective-permute-done.19.refs_3_ = f32[64,128]{1,0:T(8,128)S(1)} collective-permute-done((f32[64,128]{1,0:T(8,128)S(1)}, f32[64,128]{1,0:T(8,128)S(1)}, u32[]{:S(2)}, u32[]{:S(2)}) %collective-permute-start.19) | collective-permute-done | bytes 32800 | tf_op jit(solution)/shard_map/ppermute | solution.py:311
  41.9 1.4 %backward.1 = (bf16[128,512]{1,0:T(8,128)(2,1)S(1)}, bf16[128,512]{1,0:T(8,128)(2,1)S(1)}, bf16[128,512]{1,0:T(8,128)(2,1)S(1)}, bf16[128,512]{1,0:T(8,128)(2,1)...) custom-call(bf16[512,512]{1,0:T(8,128)(2,1)S(1)} %get-tuple-element., ...), custom_call_target="tpu_custom_call" | custom-call | bytes 4849664 | tf_op jit(solution)/shard_map/backward/pallas_call | solution.py:283
  43.4 1.2 %collective-permute-start.22 = (bf16[128,512]{1,0:T(8,128)(2,1)S(1)}, bf16[128,512]{1,0:T(8,128)(2,1)S(1)}, u32[]{:S(2)}, u32[]{:S(2)}) collective-permute-start(bf16[128,512]{1,0:T(8,128)(2,1)S(1)} %get-tuple-element.45), channel_id=1, source_target_pairs={{0,4},{1,5},{2,6},{3,7},{4,0},{5,1},{6,2},{7,3},{8,12},{9,13},{10,... | collective-permute-start | bytes 393224 | tf_op jit(solution)/shard_map/ppermute | solution.py:311
  44.6 1.5 %collective-permute-start.23 = (bf16[128,512]{1,0:T(8,128)(2,1)S(1)}, bf16[128,512]{1,0:T(8,128)(2,1)S(1)}, u32[]{:S(2)}, u32[]{:S(2)}) collective-permute-start(bf16[128,512]{1,0:T(8,128)(2,1)S(1)} %get-tuple-element.46), channel_id=1, source_target_pairs={{0,6},{1,7},{2,4},{3,5},{4,2},{5,3},{6,0},{7,1},{8,14},{9,15},{10,... | collective-permute-start | bytes 393224 | tf_op jit(solution)/shard_map/ppermute | solution.py:311
  46.2 1.6 %collective-permute-start.25 = (bf16[128,512]{1,0:T(8,128)(2,1)S(1)}, bf16[128,512]{1,0:T(8,128)(2,1)S(1)}, u32[]{:S(2)}, u32[]{:S(2)}) collective-permute-start(bf16[128,512]{1,0:T(8,128)(2,1)S(1)} %add_convert_fusion), channel_id=1, source_target_pairs={{0,8},{1,9},{2,10},{3,11},{4,12},{5,13},{6,14},{7,15},{8,0},{9,1},... | collective-permute-start | bytes 393224 | tf_op jit(solution)/shard_map/ppermute | solution.py:311
  47.7 1.5 %collective-permute-start.21 = (bf16[128,512]{1,0:T(8,128)(2,1)S(1)}, bf16[128,512]{1,0:T(8,128)(2,1)S(1)}, u32[]{:S(2)}, u32[]{:S(2)}) collective-permute-start(bf16[128,512]{1,0:T(8,128)(2,1)S(1)} %get-tuple-element.44), channel_id=1, source_target_pairs={{0,2},{1,3},{2,0},{3,1},{4,6},{5,7},{6,4},{7,5},{8,10},{9,11},{10,... | collective-permute-start | bytes 393224 | tf_op jit(solution)/shard_map/ppermute | solution.py:311
  49.3 3.2 %loss.1 = (f32[8,128]{1,0:T(8,128)S(1)}, f32[128,128]{1,0:T(8,128)S(1)}) custom-call(bf16[2048,128]{1,0:T(8,128)(2,1)S(1)} %get-tuple-element.28.rows_ref, f32[1,512]{1,0:T(1,128)S(1)} %get-tuple-element.29.thresh_ref, f32[1,512]{1,0:T(1,128)S(1)} %get-tuple-element.30.rate_ref, f32[64,128]{1,0:T(8,128)S(1)} %solve.1.refs_0_, ...), custom_call_target="tpu_custom_call" | custom-call | bytes 729088 | tf_op jit(solution)/shard_map/loss/pallas_call | solution.py:283
  53.0 2.7 %collective-permute-done.23.refs_3_ = bf16[128,512]{1,0:T(8,128)(2,1)S(1)} collective-permute-done((bf16[128,512]{1,0:T(8,128)(2,1)S(1)}, bf16[128,512]{1,0:T(8,128)(2,1)S(1)}, u32[]{:S(2)}, u32[]{:S(2)}) %collective-permute-start.23) | collective-permute-done | bytes 131104 | tf_op jit(solution)/shard_map/ppermute | solution.py:311
  (58 shorter events, 11.4 us)
Async XLA Ops:
  0.6 12.8 %collective-permute-start.6 = (bf16[128,512]{1,0:T(8,128)(2,1)}, bf16[128,512]{1,0:T(8,128)(2,1)S(1)}, u32[]{:S(2)}, u32[]{:S(2)}) collective-permute-start(bf16[128,512]{1,0:T(8,128)(2,1)} %refs_8_.1), channel_id=1, source_target_pairs={{0,8},{1,9},{2,10},{3,11},{4,12},{5,13},{6,14},{7,15},{8,0},{9,1},... | collective-permute-start | bytes 393224 | tf_op jit(solution)/shard_map/ppermute | solution.py:311
  4.7 9.3 %collective-permute-start = (bf16[128,512]{1,0:T(8,128)(2,1)}, bf16[128,512]{1,0:T(8,128)(2,1)S(1)}, u32[]{:S(2)}, u32[]{:S(2)}) collective-permute-start(bf16[128,512]{1,0:T(8,128)(2,1)} %refs_4_.5), channel_id=1, source_target_pairs={{0,2},{1,3},{2,0},{3,1},{4,6},{5,7},{6,4},{7,5},{8,10},{9,11},{10,... | collective-permute-start | bytes 393224 | tf_op jit(solution)/shard_map/ppermute | solution.py:311
  6.3 7.8 %collective-permute-start.1 = (bf16[128,512]{1,0:T(8,128)(2,1)}, bf16[128,512]{1,0:T(8,128)(2,1)S(1)}, u32[]{:S(2)}, u32[]{:S(2)}) collective-permute-start(bf16[128,512]{1,0:T(8,128)(2,1)} %refs_4_.5), channel_id=1, source_target_pairs={{0,4},{1,5},{2,6},{3,7},{4,0},{5,1},{6,2},{7,3},{8,12},{9,13},{10,... | collective-permute-start | bytes 393224 | tf_op jit(solution)/shard_map/ppermute | solution.py:311
  7.8 7.8 %collective-permute-start.2 = (bf16[128,512]{1,0:T(8,128)(2,1)}, bf16[128,512]{1,0:T(8,128)(2,1)S(1)}, u32[]{:S(2)}, u32[]{:S(2)}) collective-permute-start(bf16[128,512]{1,0:T(8,128)(2,1)} %refs_4_.5), channel_id=1, source_target_pairs={{0,6},{1,7},{2,4},{3,5},{4,2},{5,3},{6,0},{7,1},{8,14},{9,15},{10,... | collective-permute-start | bytes 393224 | tf_op jit(solution)/shard_map/ppermute | solution.py:311
  8.2 5.2 %collective-permute-start.9 = (bf16[128]{0:T(256)(128)(2,1)}, bf16[128]{0:T(256)(128)(2,1)S(1)}, u32[]{:S(2)}, u32[]{:S(2)}) collective-permute-start(bf16[128]{0:T(256)(128)(2,1)} %param.9), channel_id=1, source_target_pairs={{0,8},{1,9},{2,10},{3,11},{4,12},{5,13},{6,14},{7,15},{8,0},{9,1},... | collective-permute-start | bytes 776 | tf_op jit(solution)/shard_map/ppermute | solution.py:311
  13.5 3.2 %collective-permute-start.7 = (bf16[128,512]{1,0:T(8,128)(2,1)}, bf16[128,512]{1,0:T(8,128)(2,1)S(1)}, u32[]{:S(2)}, u32[]{:S(2)}) collective-permute-start(bf16[128,512]{1,0:T(8,128)(2,1)} %refs_8_.1), channel_id=1, source_target_pairs={{0,1},{1,0},{2,3},{3,2},{4,5},{5,4},{6,7},{7,6},{8,9},{9,8},{10,11... | collective-permute-start | bytes 393224 | tf_op jit(solution)/shard_map/ppermute | solution.py:311
  13.5 3.2 %collective-permute-start.8 = (bf16[128,512]{1,0:T(8,128)(2,1)S(1)}, bf16[128,512]{1,0:T(8,128)(2,1)S(1)}, u32[]{:S(2)}, u32[]{:S(2)}) collective-permute-start(bf16[128,512]{1,0:T(8,128)(2,1)S(1)} %collective-permute-done.6.refs_5_.refs_9_), channel_id=1, source_target_pairs={{0,1},{1,0},{2,3},{3,2},{4,5},{5,4},{6,7},{7,6},{8,9},{9,8},{10,11... | collective-permute-start | bytes 393224 | tf_op jit(solution)/shard_map/ppermute | solution.py:311
  14.0 2.7 %collective-permute-start.10 = (bf16[128]{0:T(256)(128)(2,1)S(1)}, bf16[128]{0:T(256)(128)(2,1)S(1)}, u32[]{:S(2)}, u32[]{:S(2)}) collective-permute-start(bf16[128]{0:T(256)(128)(2,1)S(1)} %copy-done.4), channel_id=1, source_target_pairs={{0,1},{1,0},{2,3},{3,2},{4,5},{5,4},{6,7},{7,6},{8,9},{9,8},{10,11... | collective-permute-start | bytes 776 | tf_op jit(solution)/shard_map/ppermute | solution.py:311
  18.8 5.6 %collective-permute-start.12 = (f32[32,128]{1,0:T(8,128)S(1)}, f32[32,128]{1,0:T(8,128)S(1)}, u32[]{:S(2)}, u32[]{:S(2)}) collective-permute-start(f32[32,128]{1,0:T(8,128)S(1)} %get-tuple-element.35), channel_id=1, source_target_pairs={{0,2},{1,3},{2,0},{3,1},{4,6},{5,7},{6,4},{7,5},{8,10},{9,11},{10,... | collective-permute-start | bytes 49160 | tf_op jit(solution)/shard_map/ppermute | solution.py:311
  20.2 5.1 %collective-permute-start.13 = (f32[32,128]{1,0:T(8,128)S(1)}, f32[32,128]{1,0:T(8,128)S(1)}, u32[]{:S(2)}, u32[]{:S(2)}) collective-permute-start(f32[32,128]{1,0:T(8,128)S(1)} %get-tuple-element.36), channel_id=1, source_target_pairs={{0,4},{1,5},{2,6},{3,7},{4,0},{5,1},{6,2},{7,3},{8,12},{9,13},{10,... | collective-permute-start | bytes 49160 | tf_op jit(solution)/shard_map/ppermute | solution.py:311
  21.4 4.6 %collective-permute-start.14 = (f32[32,128]{1,0:T(8,128)S(1)}, f32[32,128]{1,0:T(8,128)S(1)}, u32[]{:S(2)}, u32[]{:S(2)}) collective-permute-start(f32[32,128]{1,0:T(8,128)S(1)} %get-tuple-element.37), channel_id=1, source_target_pairs={{0,6},{1,7},{2,4},{3,5},{4,2},{5,3},{6,0},{7,1},{8,14},{9,15},{10,... | collective-permute-start | bytes 49160 | tf_op jit(solution)/shard_map/ppermute | solution.py:311
  22.3 6.8 %collective-permute-start.3 = (bf16[32,512]{1,0:T(8,128)(2,1)S(1)}, bf16[32,512]{1,0:T(8,128)(2,1)S(1)}, u32[]{:S(2)}, u32[]{:S(2)}) collective-permute-start(bf16[32,512]{1,0:T(8,128)(2,1)S(1)} %lead.1.refs_0_.refs_12_), channel_id=1, source_target_pairs={{0,8},{1,9},{2,10},{3,11},{4,12},{5,13},{6,14},{7,15},{8,0},{9,1},... | collective-permute-start | bytes 98312 | tf_op jit(solution)/shard_map/ppermute | solution.py:311
  24.4 4.7 %collective-permute-start.4 = (bf16[32,512]{1,0:T(8,128)(2,1)S(1)}, bf16[32,512]{1,0:T(8,128)(2,1)S(1)}, u32[]{:S(2)}, u32[]{:S(2)}) collective-permute-start(bf16[32,512]{1,0:T(8,128)(2,1)S(1)} %lead.1.refs_0_.refs_12_), channel_id=1, source_target_pairs={{0,1},{1,0},{2,3},{3,2},{4,5},{5,4},{6,7},{7,6},{8,9},{9,8},{10,11... | collective-permute-start | bytes 98312 | tf_op jit(solution)/shard_map/ppermute | solution.py:311
  24.4 4.7 %collective-permute-start.5 = (bf16[32,512]{1,0:T(8,128)(2,1)S(1)}, bf16[32,512]{1,0:T(8,128)(2,1)S(1)}, u32[]{:S(2)}, u32[]{:S(2)}) collective-permute-start(bf16[32,512]{1,0:T(8,128)(2,1)S(1)} %lead.1.refs_0_.refs_12_), channel_id=1, source_target_pairs={{0,9},{1,8},{2,11},{3,10},{4,13},{5,12},{6,15},{7,14},{8,1},{9,0},... | collective-permute-start | bytes 98312 | tf_op jit(solution)/shard_map/ppermute | solution.py:311
  27.2 6.1 %collective-permute-start.16 = (f32[32,128]{1,0:T(8,128)S(1)}, f32[32,128]{1,0:T(8,128)S(1)}, u32[]{:S(2)}, u32[]{:S(2)}) collective-permute-start(f32[32,128]{1,0:T(8,128)S(1)} %add.18.refs_0_), channel_id=1, source_target_pairs={{0,8},{1,9},{2,10},{3,11},{4,12},{5,13},{6,14},{7,15},{8,0},{9,1},... | collective-permute-start | bytes 49160 | tf_op jit(solution)/shard_map/ppermute | solution.py:311
  35.1 4.4 %collective-permute-start.17 = (f32[64,128]{1,0:T(8,128)S(1)}, f32[64,128]{1,0:T(8,128)S(1)}, u32[]{:S(2)}, u32[]{:S(2)}) collective-permute-start(f32[64,128]{1,0:T(8,128)S(1)} %solve.1.refs_0_), channel_id=1, source_target_pairs={{0,2},{1,3},{2,0},{3,1},{4,6},{5,7},{6,4},{7,5},{8,10},{9,11},{10,... | collective-permute-start | bytes 98312 | tf_op jit(solution)/shard_map/ppermute | solution.py:311
  36.2 4.2 %collective-permute-start.18 = (f32[64,128]{1,0:T(8,128)S(1)}, f32[64,128]{1,0:T(8,128)S(1)}, u32[]{:S(2)}, u32[]{:S(2)}) collective-permute-start(f32[64,128]{1,0:T(8,128)S(1)} %solve.1.refs_0_), channel_id=1, source_target_pairs={{0,4},{1,5},{2,6},{3,7},{4,0},{5,1},{6,2},{7,3},{8,12},{9,13},{10,... | collective-permute-start | bytes 98312 | tf_op jit(solution)/shard_map/ppermute | solution.py:311
  37.1 4.8 %collective-permute-start.19 = (f32[64,128]{1,0:T(8,128)S(1)}, f32[64,128]{1,0:T(8,128)S(1)}, u32[]{:S(2)}, u32[]{:S(2)}) collective-permute-start(f32[64,128]{1,0:T(8,128)S(1)} %solve.1.refs_0_), channel_id=1, source_target_pairs={{0,6},{1,7},{2,4},{3,5},{4,2},{5,3},{6,0},{7,1},{8,14},{9,15},{10,... | collective-permute-start | bytes 98312 | tf_op jit(solution)/shard_map/ppermute | solution.py:311
  43.3 2.8 %collective-permute-start.20 = (bf16[128,512]{1,0:T(8,128)(2,1)S(1)}, bf16[128,512]{1,0:T(8,128)(2,1)S(1)}, u32[]{:S(2)}, u32[]{:S(2)}) collective-permute-start(bf16[128,512]{1,0:T(8,128)(2,1)S(1)} %get-tuple-element.43), channel_id=1, source_target_pairs={{0,1},{1,0},{2,3},{3,2},{4,5},{5,4},{6,7},{7,6},{8,9},{9,8},{10,11... | collective-permute-start | bytes 393224 | tf_op jit(solution)/shard_map/ppermute | solution.py:311
  43.4 9.5 %collective-permute-start.22 = (bf16[128,512]{1,0:T(8,128)(2,1)S(1)}, bf16[128,512]{1,0:T(8,128)(2,1)S(1)}, u32[]{:S(2)}, u32[]{:S(2)}) collective-permute-start(bf16[128,512]{1,0:T(8,128)(2,1)S(1)} %get-tuple-element.45), channel_id=1, source_target_pairs={{0,4},{1,5},{2,6},{3,7},{4,0},{5,1},{6,2},{7,3},{8,12},{9,13},{10,... | collective-permute-start | bytes 393224 | tf_op jit(solution)/shard_map/ppermute | solution.py:311
  44.6 11.1 %collective-permute-start.23 = (bf16[128,512]{1,0:T(8,128)(2,1)S(1)}, bf16[128,512]{1,0:T(8,128)(2,1)S(1)}, u32[]{:S(2)}, u32[]{:S(2)}) collective-permute-start(bf16[128,512]{1,0:T(8,128)(2,1)S(1)} %get-tuple-element.46), channel_id=1, source_target_pairs={{0,6},{1,7},{2,4},{3,5},{4,2},{5,3},{6,0},{7,1},{8,14},{9,15},{10,... | collective-permute-start | bytes 393224 | tf_op jit(solution)/shard_map/ppermute | solution.py:311
  46.2 9.5 %collective-permute-start.25 = (bf16[128,512]{1,0:T(8,128)(2,1)S(1)}, bf16[128,512]{1,0:T(8,128)(2,1)S(1)}, u32[]{:S(2)}, u32[]{:S(2)}) collective-permute-start(bf16[128,512]{1,0:T(8,128)(2,1)S(1)} %add_convert_fusion), channel_id=1, source_target_pairs={{0,8},{1,9},{2,10},{3,11},{4,12},{5,13},{6,14},{7,15},{8,0},{9,1},... | collective-permute-start | bytes 393224 | tf_op jit(solution)/shard_map/ppermute | solution.py:311
  47.7 7.9 %collective-permute-start.24 = (bf16[128,512]{1,0:T(8,128)(2,1)S(1)}, bf16[128,512]{1,0:T(8,128)(2,1)S(1)}, u32[]{:S(2)}, u32[]{:S(2)}) collective-permute-start(bf16[128,512]{1,0:T(8,128)(2,1)S(1)} %get-tuple-element.49), channel_id=1, source_target_pairs={{0,1},{1,0},{2,3},{3,2},{4,5},{5,4},{6,7},{7,6},{8,9},{9,8},{10,11... | collective-permute-start | bytes 393224 | tf_op jit(solution)/shard_map/ppermute | solution.py:311
  47.7 8.5 %collective-permute-start.21 = (bf16[128,512]{1,0:T(8,128)(2,1)S(1)}, bf16[128,512]{1,0:T(8,128)(2,1)S(1)}, u32[]{:S(2)}, u32[]{:S(2)}) collective-permute-start(bf16[128,512]{1,0:T(8,128)(2,1)S(1)} %get-tuple-element.44), channel_id=1, source_target_pairs={{0,2},{1,3},{2,0},{3,1},{4,6},{5,7},{6,4},{7,5},{8,10},{9,11},{10,... | collective-permute-start | bytes 393224 | tf_op jit(solution)/shard_map/ppermute | solution.py:311
  (10 other events, 25.0 us)
where the time goes:
time: 57.3 us; the launch traced here: 57.1 us
  starting transfers between devices  26.6 us (46%)
  Pallas kernels  14.3 us (25%)
  waiting for transfers between devices  12.5 us (22%)
  local copies, waits for them, and re-layouts  2.9 us (5%)
  between operations  0.79 us (1%)
    ppermute x26, starting transfers between devices, swap(): return lax.ppermute(x, 'paths', [(d, d ^ mask) for d in range(n)])  26.6 us
    pallas_call x10, Pallas kernels, call(): pl.pallas_call(kernel, out_shape=[jax.ShapeDtypeStruct(s, d) for s, d in...  14.3 us
    ppermute x26, waiting for transfers between devices, swap(): return lax.ppermute(x, 'paths', [(d, d ^ mask) for d in range(n)])  12.5 us
    unnamed x16, local copies, waits for them, and re-layouts  2.39 us
  transfers between devices with their start and end apart: 26, of which 8 were waited for; matrix products, arithmetic and copies ran while one was open for 1% of the time, Pallas kernels for 16%

commit v1 on v0

--- a/solution.py
+++ b/solution.py
@@ -14,9 +14,11 @@
 F32 = jnp.float32
 BF16 = jnp.bfloat16
 LANES = 128
+SUBLANES = 8
 CHUNK = 256
 VMEM_BYTES = 48 * 1024 * 1024
 LOG2_E = math.log2(math.e)
+SHARES = 2
 CONSTANT = REGRESSORS - 1
 
 
@@ -75,16 +77,26 @@
 def invert(matrix):
     size = matrix.shape[0]
     work = jnp.concatenate([matrix, jnp.eye(size, dtype=F32)], axis=1)
-    row = rows(work.shape)
+    shape = (SUBLANES, 2 * size)
+    blocks = [work[i : i + SUBLANES] for i in range(0, size, SUBLANES)]
+    row = rows(shape)
+
+    def one_row(block, k):
+        return jnp.broadcast_to(block[k : k + 1], shape)
+
     for k in range(0, size, 2):
-        left, right = work[:, k : k + 1], work[:, k + 1 : k + 2]
-        upper, lower = work[k : k + 1], work[k + 1 : k + 2]
-        a, b, c, d = left[k : k + 1], right[k : k + 1], left[k + 1 : k + 2], right[k + 1 : k + 2]
+        left = [jnp.broadcast_to(block[:, k : k + 1], shape) for block in blocks]
+        right = [jnp.broadcast_to(block[:, k + 1 : k + 2], shape) for block in blocks]
+        at, here = k // SUBLANES, k % SUBLANES
+        a, b = one_row(left[at], here), one_row(right[at], here)
+        c, d = one_row(left[at], here + 1), one_row(right[at], here + 1)
+        upper, lower = one_row(blocks[at], here), one_row(blocks[at], here + 1)
         scale = 1.0 / (a * d - b * c)
         upper, lower = (d * upper - b * lower) * scale, (a * lower - c * upper) * scale
-        work = work - left * upper - right * lower
-        work = jnp.where(row == k, upper, jnp.where(row == k + 1, lower, work))
-    return work[:, size:]
+        blocks = [w - x * upper - y * lower for w, x, y in zip(blocks, left, right)]
+        kept = jnp.where(row == here + 1, lower, blocks[at])
+        blocks[at] = jnp.where(row == here, upper, kept)
+    return jnp.concatenate(blocks, axis=0)[:, size:]
 
 
 def lead_kernel(*refs):
@@ -98,14 +110,17 @@
 
 
 def tables_kernel(
-    trade_masks, inner, me_ref, level_ref, set_ref, index_ref, rate_ref,
-    member_ref, thresh_out_ref, rate_out_ref,
+    trade_masks, me_ref, level_ref, set_ref, index_ref, rate_ref, x_ref, w_ref,
+    member_ref, thresh_out_ref, rate_out_ref, x_out_ref, w_out_ref,
 ):
+    x_out_ref[...] = x_ref[...]
+    w_out_ref[...] = w_ref[...]
     me = me_ref[0]
-    place = (me >> 1) & (inner - 1)
-    size = member_ref.shape[0] // inner
+    shares = index_ref.shape[0]
+    place = me & (shares - 1)
+    size = member_ref.shape[0] // shares
     trades = set_ref.shape[-1]
-    for m in range(inner):
+    for m in range(shares):
         here = slice(m * size, (m + 1) * size)
         label = (place ^ m) * size + rows((size, 1))
         for j, mask in enumerate(trade_masks):
@@ -203,8 +218,8 @@
     return jnp.concatenate([ref[here] for ref in refs], axis=1)
 
 
-def backward_kernel(scale, paths, trades, member_ref, rows_ref, slope_ref, value_ref, *refs):
-    solved_refs, refs = refs[:paths], refs[paths:]
+def backward_kernel(scale, shares, paths, trades, member_ref, rows_ref, slope_ref, value_ref, *refs):
+    solved_refs, refs = refs[:shares], refs[shares:]
     x_refs, refs = refs[:paths], refs[paths:]
     w_refs, refs = refs[:trades], refs[trades:]
     weight_refs, basis_refs, slopes_ref = refs[:trades], refs[trades:-1], refs[-1]
@@ -304,7 +319,7 @@
     trade_rows = proxy_weight.shape[0]
     paths_all = path_rows * n
     sets = loss_rate.shape[0]
-    quarter = sets // inner
+    share = sets // SHARES
     group_paths, group_trades = inner * path_rows, outer * trade_rows
 
     def swap(x, mask):
@@ -319,22 +334,29 @@
         return lax.optimization_barrier((x, *others))[0]
 
     def direct(slots, bits):
-        sent = [swap(x, mask) for x, mask in zip(slots[:0:-1], masks(bits)[:0:-1])]
-        return sent[::-1]
+        return [swap(x, mask) for x, mask in zip(slots[1:], masks(bits)[1:])]
 
     first_bit = outer_bits[0]
     weights = [proxy_weight, swap(proxy_weight, 1 << first_bit)]
     basis = [path_basis] + direct([path_basis] * inner, inner_bits)
     notionals = [notional, swap(notional, 1 << first_bit)]
 
-    member, thresh, rate = call(
-        partial(tables_kernel, masks(outer_bits), inner),
-        [((sets, group_trades), BF16), ((1, sets), F32), ((1, sets), F32)],
+    member, thresh, rate, basis[0], own_weight = call(
+        partial(tables_kernel, masks(outer_bits)),
+        [
+            ((sets, group_trades), BF16),
+            ((1, sets), F32),
+            ((1, sets), F32),
+            (path_basis.shape, BF16),
+            (proxy_weight.shape, BF16),
+        ],
         me.astype(jnp.int32).reshape(1),
         threshold_levels,
         set_of.reshape(n, 1, trade_rows),
-        threshold_index.reshape(inner, 1, quarter),
-        loss_rate.reshape(inner, 1, quarter),
+        threshold_index.reshape(SHARES, 1, share),
+        loss_rate.reshape(SHARES, 1, share),
+        path_basis,
+        proxy_weight,
         name="tables",
         scalars=2,
     )
@@ -343,17 +365,18 @@
             swap(w if k else after(w, member), 1 << bit) for k, w in enumerate(weights)
         ]
         notionals = notionals + [swap(x, 1 << bit) for x in notionals]
+    weights[0] = own_weight
     notionals = [x[None, :] for x in notionals]
     (lead,) = call(lead_kernel, [((REGRESSORS, group_paths), BF16)], *basis, name="lead")
     leads = [lead] + direct([lead] * outer, outer_bits)
     value, *moments = call(
         partial(forward_kernel, inner, outer),
-        [((group_paths, group_trades), BF16)] + [((REGRESSORS, quarter), F32)] * inner,
+        [((group_paths, group_trades), BF16)] + [((REGRESSORS, share), F32)] * SHARES,
         *basis, *weights, *notionals, lead, member,
         name="forward",
     )
-    moment = sum(direct(moments, inner_bits), moments[0])
-    for bit in outer_bits[:0:-1]:
+    moment = moments[0] + swap(moments[1], SHARES - 1)
+    for bit in inner_bits + outer_bits[-2:0:-1]:
         moment = moment + swap(moment, 1 << bit)
     moments = [moment, swap(moment, 1 << first_bit)]
     (inverse,) = call(
@@ -370,12 +393,12 @@
     )
     (solved,) = call(
         partial(solve_kernel, len(moments)),
-        [((2 * REGRESSORS, quarter), F32)],
+        [((2 * REGRESSORS, share), F32)],
         inverse, design_all, design_rows, thresh, rate, *moments,
         name="solve",
-        scratch=[pltpu.VMEM((LANES, quarter), BF16), pltpu.VMEM((REGRESSORS, quarter), F32)],
-    )
-    solved = [solved] + direct([solved] * inner, inner_bits)
+        scratch=[pltpu.VMEM((LANES, share), BF16), pltpu.VMEM((REGRESSORS, share), F32)],
+    )
+    solved = [solved, swap(solved, SHARES - 1)]
     (slope,) = call(
         partial(slope_kernel, inner, outer),
         [((group_paths, group_trades), F32)],
@@ -383,7 +406,7 @@
         name="slope",
     )
     parts = call(
-        partial(backward_kernel, 1.0 / math.sqrt(paths_all), inner, outer),
+        partial(backward_kernel, 1.0 / math.sqrt(paths_all), SHARES, inner, outer),
         [((trade_rows, features), BF16)] * outer + [((path_rows, features), BF16)] * inner,
         member, design_rows, slope, value, *solved, *basis, *weights,
         name="backward",

time: 57.3 us -> 51.7 us (0.902)
  starting transfers between devices: 26.6 us -> 23.1 us
  Pallas kernels: 14.3 us -> 12.7 us
  waiting for transfers between devices: 12.5 us -> 11.8 us
    ppermute x26 -> x23, starting transfers between devices: 26.6 us -> 23.1 us  [swap(): return lax.ppermute(x, 'paths', [(d, d ^ mask) for d in range(n)])]
    pallas_call x10, Pallas kernels: 14.3 us -> 12.7 us  [call(): pl.pallas_call(kernel, out_shape=[jax.ShapeDtypeStruct(s, d) for s, d in...]
    ppermute x26 -> x23, waiting for transfers between devices: 12.5 us -> 11.8 us  [swap(): return lax.ppermute(x, 'paths', [(d, d ^ mask) for d in range(n)])]
    unnamed x16 -> x14, local copies, waits for them, and re-layouts: 2.39 us -> 2.51 us
  transfers between devices with their start and end apart: 26 -> 23, of which waited for: 8 -> 8; matrix products, arithmetic and copies ran while one was open for 1% -> 1% of each run, Pallas kernels for 16% -> 15%
where the time goes in v1:
time: 51.7 us; the launch traced here: 51.5 us
  starting transfers between devices  23.1 us (45%)
  Pallas kernels  12.7 us (25%)
  waiting for transfers between devices  11.8 us (23%)
  local copies, waits for them, and re-layouts  3.02 us (6%)
  between operations  0.76 us (1%)
    ppermute x23, starting transfers between devices, swap(): return lax.ppermute(x, 'paths', [(d, d ^ mask) for d in range(n)])  23.1 us
    pallas_call x10, Pallas kernels, call(): pl.pallas_call(kernel, out_shape=[jax.ShapeDtypeStruct(s, d) for s, d in...  12.7 us
    ppermute x23, waiting for transfers between devices, swap(): return lax.ppermute(x, 'paths', [(d, d ^ mask) for d in range(n)])  11.8 us
    unnamed x14, local copies, waits for them, and re-layouts  2.51 us
  transfers between devices with their start and end apart: 23, of which 8 were waited for; matrix products, arithmetic and copies ran while one was open for 1% of the time, Pallas kernels for 15%

profile of v1, /device:TPU:0, one launch (start us, length us, event | category | flops | bytes accessed | tf_op | source)
XLA Modules:
  0.0 51.5 jit_solution(495420889627337236)
XLA Ops:
  0.6 4.1 %collective-permute-start.6 = (bf16[128,512]{1,0:T(8,128)(2,1)}, bf16[128,512]{1,0:T(8,128)(2,1)S(1)}, u32[]{:S(2)}, u32[]{:S(2)}) collective-permute-start(bf16[128,512]{1,0:T(8,128)(2,1)} %w_ref.1), channel_id=1, source_target_pairs={{0,8},{1,9},{2,10},{3,11},{4,12},{5,13},{6,14},{7,15},{8,0},{9,1},... | collective-permute-start | bytes 393224 | tf_op jit(solution)/shard_map/ppermute | solution.py:326
  4.7 1.5 %collective-permute-start = (bf16[128,512]{1,0:T(8,128)(2,1)}, bf16[128,512]{1,0:T(8,128)(2,1)S(1)}, u32[]{:S(2)}, u32[]{:S(2)}) collective-permute-start(bf16[128,512]{1,0:T(8,128)(2,1)} %x_ref.1), channel_id=1, source_target_pairs={{0,2},{1,3},{2,0},{3,1},{4,6},{5,7},{6,4},{7,5},{8,10},{9,11},{10,... | collective-permute-start | bytes 393224 | tf_op jit(solution)/shard_map/ppermute | solution.py:326
  6.3 1.6 %collective-permute-start.1 = (bf16[128,512]{1,0:T(8,128)(2,1)}, bf16[128,512]{1,0:T(8,128)(2,1)S(1)}, u32[]{:S(2)}, u32[]{:S(2)}) collective-permute-start(bf16[128,512]{1,0:T(8,128)(2,1)} %x_ref.1), channel_id=1, source_target_pairs={{0,4},{1,5},{2,6},{3,7},{4,0},{5,1},{6,2},{7,3},{8,12},{9,13},{10,... | collective-permute-start | bytes 393224 | tf_op jit(solution)/shard_map/ppermute | solution.py:326
  9.0 0.9 %copy-done = bf16[128,512]{1,0:T(8,128)(2,1)S(1)} copy-done((bf16[128,512]{1,0:T(8,128)(2,1)S(1)}, bf16[128,512]{1,0:T(8,128)(2,1)}, u32[]{:S(2)}) %copy-start) | copy-done | bytes 131096
  9.9 0.9 %copy-done.1 = bf16[128,512]{1,0:T(8,128)(2,1)S(1)} copy-done((bf16[128,512]{1,0:T(8,128)(2,1)S(1)}, bf16[128,512]{1,0:T(8,128)(2,1)}, u32[]{:S(2)}) %copy-start.1) | copy-done | bytes 131096
  11.5 2.0 %collective-permute-done.9 = bf16[128]{0:T(256)(128)(2,1)S(1)} collective-permute-done((bf16[128]{0:T(256)(128)(2,1)}, bf16[128]{0:T(256)(128)(2,1)S(1)}, u32[]{:S(2)}, u32[]{:S(2)}) %collective-permute-start.9) | collective-permute-done | bytes 288 | tf_op jit(solution)/shard_map/ppermute | solution.py:326
  14.5 1.2 %collective-permute-done.2.refs_3_.refs_5_ = bf16[128,512]{1,0:T(8,128)(2,1)S(1)} collective-permute-done((bf16[128,512]{1,0:T(8,128)(2,1)}, bf16[128,512]{1,0:T(8,128)(2,1)S(1)}, u32[]{:S(2)}, u32[]{:S(2)}) %collective-permute-start.2) | collective-permute-done | bytes 131104 | tf_op jit(solution)/shard_map/ppermute | solution.py:326
  15.8 1.3 %forward.1 = (bf16[512,512]{1,0:T(8,128)(2,1)S(1)}, f32[32,256]{1,0:T(8,128)S(1)}, f32[32,256]{1,0:T(8,128)S(1)}) custom-call(bf16[128,512]{1,0:T(8,128)(2,1)S(1)} %get-tuple-element.28.refs_0_.refs_2_, bf16[128,512]{1,0:T(8,128)(2,1)S(1)} %collective-permute-done.refs_1_.refs_3_, bf16[128,512]{1,0:T(8,128)(2,1)S(1)} %collective-permute-done.1.refs_2_.refs_4_, ...), custom_call_target="tpu_custom_call" | custom-call | bytes 2196480 | tf_op jit(solution)/shard_map/forward/pallas_call | solution.py:298
  17.1 1.2 %collective-permute-done.12 = f32[32,256]{1,0:T(8,128)S(1)} collective-permute-done((f32[32,256]{1,0:T(8,128)S(1)}, f32[32,256]{1,0:T(8,128)S(1)}, u32[]{:S(2)}, u32[]{:S(2)}) %collective-permute-start.12) | collective-permute-done | bytes 32800 | tf_op jit(solution)/shard_map/ppermute | solution.py:326
  18.3 1.4 %collective-permute-start.13 = (f32[32,256]{1,0:T(8,128)S(1)}, f32[32,256]{1,0:T(8,128)S(1)}, u32[]{:S(2)}, u32[]{:S(2)}) collective-permute-start(f32[32,256]{1,0:T(8,128)S(1)} %add.12), channel_id=1, source_target_pairs={{0,2},{1,3},{2,0},{3,1},{4,6},{5,7},{6,4},{7,5},{8,10},{9,11},{10,... | collective-permute-start | bytes 98312 | tf_op jit(solution)/shard_map/ppermute | solution.py:326
  19.7 2.5 %collective-permute-done.13 = f32[32,256]{1,0:T(8,128)S(1)} collective-permute-done((f32[32,256]{1,0:T(8,128)S(1)}, f32[32,256]{1,0:T(8,128)S(1)}, u32[]{:S(2)}, u32[]{:S(2)}) %collective-permute-start.13) | collective-permute-done | bytes 32800 | tf_op jit(solution)/shard_map/ppermute | solution.py:326
  22.2 1.8 %collective-permute-start.14 = (f32[32,256]{1,0:T(8,128)S(1)}, f32[32,256]{1,0:T(8,128)S(1)}, u32[]{:S(2)}, u32[]{:S(2)}) collective-permute-start(f32[32,256]{1,0:T(8,128)S(1)} %add.13), channel_id=1, source_target_pairs={{0,4},{1,5},{2,6},{3,7},{4,0},{5,1},{6,2},{7,3},{8,12},{9,13},{10,... | collective-permute-start | bytes 98312 | tf_op jit(solution)/shard_map/ppermute | solution.py:326
  24.0 1.2 %collective-permute-start.3 = (bf16[32,512]{1,0:T(8,128)(2,1)S(1)}, bf16[32,512]{1,0:T(8,128)(2,1)S(1)}, u32[]{:S(2)}, u32[]{:S(2)}) collective-permute-start(bf16[32,512]{1,0:T(8,128)(2,1)S(1)} %lead.1.refs_0_.refs_12_), channel_id=1, source_target_pairs={{0,8},{1,9},{2,10},{3,11},{4,12},{5,13},{6,14},{7,15},{8,0},{9,1},... | collective-permute-start | bytes 98312 | tf_op jit(solution)/shard_map/ppermute | solution.py:326
  25.2 1.8 %collective-permute-start.5 = (bf16[32,512]{1,0:T(8,128)(2,1)S(1)}, bf16[32,512]{1,0:T(8,128)(2,1)S(1)}, u32[]{:S(2)}, u32[]{:S(2)}) collective-permute-start(bf16[32,512]{1,0:T(8,128)(2,1)S(1)} %lead.1.refs_0_.refs_12_), channel_id=1, source_target_pairs={{0,9},{1,8},{2,11},{3,10},{4,13},{5,12},{6,15},{7,14},{8,1},{9,0},... | collective-permute-start | bytes 98312 | tf_op jit(solution)/shard_map/ppermute | solution.py:326
  27.1 1.9 %collective-permute-start.15 = (f32[32,256]{1,0:T(8,128)S(1)}, f32[32,256]{1,0:T(8,128)S(1)}, u32[]{:S(2)}, u32[]{:S(2)}) collective-permute-start(f32[32,256]{1,0:T(8,128)S(1)} %add.14.refs_0_), channel_id=1, source_target_pairs={{0,8},{1,9},{2,10},{3,11},{4,12},{5,13},{6,14},{7,15},{8,0},{9,1},... | collective-permute-start | bytes 98312 | tf_op jit(solution)/shard_map/ppermute | solution.py:326
  30.0 2.5 %inverse.1.inverse_ref = f32[32,32]{1,0:T(8,128)S(1)} custom-call(bf16[32,512]{1,0:T(8,128)(2,1)S(1)} %lead.1.refs_0_.refs_12_, bf16[32,512]{1,0:T(8,128)(2,1)S(1)} %collective-permute-done.3.refs_1_, bf16[32,512]{1,0:T(8,128)(2,1)S(1)} %collective-permute-done.4.refs_2_, bf16[32,512]{1,0:T(8,128)(2,1)S(1)} %collective-permute-done.5.refs_3_), custom_call_target="tpu_custom_call" | custom-call | bytes 135168 | tf_op jit(solution)/shard_map/inverse/pallas_call | solution.py:298
  32.5 1.4 %solve.1.refs_0_ = f32[64,256]{1,0:T(8,128)S(1)} custom-call(f32[32,32]{1,0:T(8,128)S(1)} %inverse.1.inverse_ref, bf16[32,2048]{1,0:T(8,128)(2,1)S(1)} %get-tuple-element.32.design_ref, bf16[2048,128]{1,0:T(8,128)(2,1)S(1)} %get-tuple-element.29.rows_ref, f32[1,512]{1,0:T(1,128)S(1)} %get-tuple-element.30.thresh_ref, ...), custom_call_target="tpu_custom_call" | custom-call | bytes 794624 | tf_op jit(solution)/shard_map/solve/pallas_call | solution.py:298
  35.4 1.4 %backward.1 = (bf16[128,512]{1,0:T(8,128)(2,1)S(1)}, bf16[128,512]{1,0:T(8,128)(2,1)S(1)}, bf16[128,512]{1,0:T(8,128)(2,1)S(1)}, bf16[128,512]{1,0:T(8,128)(2,1)...) custom-call(bf16[512,512]{1,0:T(8,128)(2,1)S(1)} %get-tuple-element., ...), custom_call_target="tpu_custom_call" | custom-call | bytes 4849664 | tf_op jit(solution)/shard_map/backward/pallas_call | solution.py:298
  37.2 1.9 %collective-permute-start.19 = (bf16[128,512]{1,0:T(8,128)(2,1)S(1)}, bf16[128,512]{1,0:T(8,128)(2,1)S(1)}, u32[]{:S(2)}, u32[]{:S(2)}) collective-permute-start(bf16[128,512]{1,0:T(8,128)(2,1)S(1)} %get-tuple-element.45), channel_id=1, source_target_pairs={{0,4},{1,5},{2,6},{3,7},{4,0},{5,1},{6,2},{7,3},{8,12},{9,13},{10,... | collective-permute-start | bytes 393224 | tf_op jit(solution)/shard_map/ppermute | solution.py:326
  39.2 1.0 %collective-permute-start.20 = (bf16[128,512]{1,0:T(8,128)(2,1)S(1)}, bf16[128,512]{1,0:T(8,128)(2,1)S(1)}, u32[]{:S(2)}, u32[]{:S(2)}) collective-permute-start(bf16[128,512]{1,0:T(8,128)(2,1)S(1)} %get-tuple-element.46), channel_id=1, source_target_pairs={{0,6},{1,7},{2,4},{3,5},{4,2},{5,3},{6,0},{7,1},{8,14},{9,15},{10,... | collective-permute-start | bytes 393224 | tf_op jit(solution)/shard_map/ppermute | solution.py:326
  40.2 1.9 %collective-permute-start.22 = (bf16[128,512]{1,0:T(8,128)(2,1)S(1)}, bf16[128,512]{1,0:T(8,128)(2,1)S(1)}, u32[]{:S(2)}, u32[]{:S(2)}) collective-permute-start(bf16[128,512]{1,0:T(8,128)(2,1)S(1)} %add_convert_fusion), channel_id=1, source_target_pairs={{0,8},{1,9},{2,10},{3,11},{4,12},{5,13},{6,14},{7,15},{8,0},{9,1},... | collective-permute-start | bytes 393224 | tf_op jit(solution)/shard_map/ppermute | solution.py:326
  42.6 3.2 %loss.1 = (f32[8,128]{1,0:T(8,128)S(1)}, f32[128,128]{1,0:T(8,128)S(1)}) custom-call(bf16[2048,128]{1,0:T(8,128)(2,1)S(1)} %get-tuple-element.29.rows_ref, f32[1,512]{1,0:T(1,128)S(1)} %get-tuple-element.30.thresh_ref, f32[1,512]{1,0:T(1,128)S(1)} %get-tuple-element.31.rate_ref, f32[64,256]{1,0:T(8,128)S(1)} %solve.1.refs_0_, ...), custom_call_target="tpu_custom_call" | custom-call | bytes 729088 | tf_op jit(solution)/shard_map/loss/pallas_call | solution.py:298
  46.3 3.3 %collective-permute-done.20.refs_3_ = bf16[128,512]{1,0:T(8,128)(2,1)S(1)} collective-permute-done((bf16[128,512]{1,0:T(8,128)(2,1)S(1)}, bf16[128,512]{1,0:T(8,128)(2,1)S(1)}, u32[]{:S(2)}, u32[]{:S(2)}) %collective-permute-start.20) | collective-permute-done | bytes 131104 | tf_op jit(solution)/shard_map/ppermute | solution.py:326
  49.6 1.0 %collective-permute-done.18.refs_1_ = bf16[128,512]{1,0:T(8,128)(2,1)S(1)} collective-permute-done((bf16[128,512]{1,0:T(8,128)(2,1)S(1)}, bf16[128,512]{1,0:T(8,128)(2,1)S(1)}, u32[]{:S(2)}, u32[]{:S(2)}) %collective-permute-start.18) | collective-permute-done | bytes 131104 | tf_op jit(solution)/shard_map/ppermute | solution.py:326
  (51 shorter events, 7.8 us)
Async XLA Ops:
  0.6 7.7 %copy-start.2 = (s32[2048]{0:T(1024)S(1)}, s32[2048]{0:T(1024)}, u32[]{:S(2)}) copy-start(s32[2048]{0:T(1024)} %param.10) | copy-start | bytes 24580
  0.6 12.8 %collective-permute-start.6 = (bf16[128,512]{1,0:T(8,128)(2,1)}, bf16[128,512]{1,0:T(8,128)(2,1)S(1)}, u32[]{:S(2)}, u32[]{:S(2)}) collective-permute-start(bf16[128,512]{1,0:T(8,128)(2,1)} %w_ref.1), channel_id=1, source_target_pairs={{0,8},{1,9},{2,10},{3,11},{4,12},{5,13},{6,14},{7,15},{8,0},{9,1},... | collective-permute-start | bytes 393224 | tf_op jit(solution)/shard_map/ppermute | solution.py:326
  4.7 9.3 %collective-permute-start = (bf16[128,512]{1,0:T(8,128)(2,1)}, bf16[128,512]{1,0:T(8,128)(2,1)S(1)}, u32[]{:S(2)}, u32[]{:S(2)}) collective-permute-start(bf16[128,512]{1,0:T(8,128)(2,1)} %x_ref.1), channel_id=1, source_target_pairs={{0,2},{1,3},{2,0},{3,1},{4,6},{5,7},{6,4},{7,5},{8,10},{9,11},{10,... | collective-permute-start | bytes 393224 | tf_op jit(solution)/shard_map/ppermute | solution.py:326
  6.3 7.8 %collective-permute-start.1 = (bf16[128,512]{1,0:T(8,128)(2,1)}, bf16[128,512]{1,0:T(8,128)(2,1)S(1)}, u32[]{:S(2)}, u32[]{:S(2)}) collective-permute-start(bf16[128,512]{1,0:T(8,128)(2,1)} %x_ref.1), channel_id=1, source_target_pairs={{0,4},{1,5},{2,6},{3,7},{4,0},{5,1},{6,2},{7,3},{8,12},{9,13},{10,... | collective-permute-start | bytes 393224 | tf_op jit(solution)/shard_map/ppermute | solution.py:326
  7.8 7.8 %collective-permute-start.2 = (bf16[128,512]{1,0:T(8,128)(2,1)}, bf16[128,512]{1,0:T(8,128)(2,1)S(1)}, u32[]{:S(2)}, u32[]{:S(2)}) collective-permute-start(bf16[128,512]{1,0:T(8,128)(2,1)} %x_ref.1), channel_id=1, source_target_pairs={{0,6},{1,7},{2,4},{3,5},{4,2},{5,3},{6,0},{7,1},{8,14},{9,15},{10,... | collective-permute-start | bytes 393224 | tf_op jit(solution)/shard_map/ppermute | solution.py:326
  8.2 5.2 %collective-permute-start.9 = (bf16[128]{0:T(256)(128)(2,1)}, bf16[128]{0:T(256)(128)(2,1)S(1)}, u32[]{:S(2)}, u32[]{:S(2)}) collective-permute-start(bf16[128]{0:T(256)(128)(2,1)} %param.9), channel_id=1, source_target_pairs={{0,8},{1,9},{2,10},{3,11},{4,12},{5,13},{6,14},{7,15},{8,0},{9,1},... | collective-permute-start | bytes 776 | tf_op jit(solution)/shard_map/ppermute | solution.py:326
  13.5 2.3 %collective-permute-start.7 = (bf16[128,512]{1,0:T(8,128)(2,1)S(1)}, bf16[128,512]{1,0:T(8,128)(2,1)S(1)}, u32[]{:S(2)}, u32[]{:S(2)}) collective-permute-start(bf16[128,512]{1,0:T(8,128)(2,1)S(1)} %copy-done.1), channel_id=1, source_target_pairs={{0,1},{1,0},{2,3},{3,2},{4,5},{5,4},{6,7},{7,6},{8,9},{9,8},{10,11... | collective-permute-start | bytes 393224 | tf_op jit(solution)/shard_map/ppermute | solution.py:326
  13.5 2.3 %collective-permute-start.8 = (bf16[128,512]{1,0:T(8,128)(2,1)S(1)}, bf16[128,512]{1,0:T(8,128)(2,1)S(1)}, u32[]{:S(2)}, u32[]{:S(2)}) collective-permute-start(bf16[128,512]{1,0:T(8,128)(2,1)S(1)} %collective-permute-done.6.refs_5_.refs_7_), channel_id=1, source_target_pairs={{0,1},{1,0},{2,3},{3,2},{4,5},{5,4},{6,7},{7,6},{8,9},{9,8},{10,11... | collective-permute-start | bytes 393224 | tf_op jit(solution)/shard_map/ppermute | solution.py:326
  14.0 1.8 %collective-permute-start.10 = (bf16[128]{0:T(256)(128)(2,1)S(1)}, bf16[128]{0:T(256)(128)(2,1)S(1)}, u32[]{:S(2)}, u32[]{:S(2)}) collective-permute-start(bf16[128]{0:T(256)(128)(2,1)S(1)} %copy-done.5), channel_id=1, source_target_pairs={{0,1},{1,0},{2,3},{3,2},{4,5},{5,4},{6,7},{7,6},{8,9},{9,8},{10,11... | collective-permute-start | bytes 776 | tf_op jit(solution)/shard_map/ppermute | solution.py:326
  14.1 1.7 %collective-permute-start.11 = (bf16[128]{0:T(256)(128)(2,1)S(1)}, bf16[128]{0:T(256)(128)(2,1)S(1)}, u32[]{:S(2)}, u32[]{:S(2)}) collective-permute-start(bf16[128]{0:T(256)(128)(2,1)S(1)} %collective-permute-done.9), channel_id=1, source_target_pairs={{0,1},{1,0},{2,3},{3,2},{4,5},{5,4},{6,7},{7,6},{8,9},{9,8},{10,11... | collective-permute-start | bytes 776 | tf_op jit(solution)/shard_map/ppermute | solution.py:326
  17.1 1.3 %collective-permute-start.12 = (f32[32,256]{1,0:T(8,128)S(1)}, f32[32,256]{1,0:T(8,128)S(1)}, u32[]{:S(2)}, u32[]{:S(2)}) collective-permute-start(f32[32,256]{1,0:T(8,128)S(1)} %get-tuple-element.37), channel_id=1, source_target_pairs={{0,1},{1,0},{2,3},{3,2},{4,5},{5,4},{6,7},{7,6},{8,9},{9,8},{10,11... | collective-permute-start | bytes 98312 | tf_op jit(solution)/shard_map/ppermute | solution.py:326
  18.3 3.9 %collective-permute-start.13 = (f32[32,256]{1,0:T(8,128)S(1)}, f32[32,256]{1,0:T(8,128)S(1)}, u32[]{:S(2)}, u32[]{:S(2)}) collective-permute-start(f32[32,256]{1,0:T(8,128)S(1)} %add.12), channel_id=1, source_target_pairs={{0,2},{1,3},{2,0},{3,1},{4,6},{5,7},{6,4},{7,5},{8,10},{9,11},{10,... | collective-permute-start | bytes 98312 | tf_op jit(solution)/shard_map/ppermute | solution.py:326
  22.2 4.8 %collective-permute-start.14 = (f32[32,256]{1,0:T(8,128)S(1)}, f32[32,256]{1,0:T(8,128)S(1)}, u32[]{:S(2)}, u32[]{:S(2)}) collective-permute-start(f32[32,256]{1,0:T(8,128)S(1)} %add.13), channel_id=1, source_target_pairs={{0,4},{1,5},{2,6},{3,7},{4,0},{5,1},{6,2},{7,3},{8,12},{9,13},{10,... | collective-permute-start | bytes 98312 | tf_op jit(solution)/shard_map/ppermute | solution.py:326
  24.0 5.1 %collective-permute-start.3 = (bf16[32,512]{1,0:T(8,128)(2,1)S(1)}, bf16[32,512]{1,0:T(8,128)(2,1)S(1)}, u32[]{:S(2)}, u32[]{:S(2)}) collective-permute-start(bf16[32,512]{1,0:T(8,128)(2,1)S(1)} %lead.1.refs_0_.refs_12_), channel_id=1, source_target_pairs={{0,8},{1,9},{2,10},{3,11},{4,12},{5,13},{6,14},{7,15},{8,0},{9,1},... | collective-permute-start | bytes 98312 | tf_op jit(solution)/shard_map/ppermute | solution.py:326
  25.2 3.9 %collective-permute-start.4 = (bf16[32,512]{1,0:T(8,128)(2,1)S(1)}, bf16[32,512]{1,0:T(8,128)(2,1)S(1)}, u32[]{:S(2)}, u32[]{:S(2)}) collective-permute-start(bf16[32,512]{1,0:T(8,128)(2,1)S(1)} %lead.1.refs_0_.refs_12_), channel_id=1, source_target_pairs={{0,1},{1,0},{2,3},{3,2},{4,5},{5,4},{6,7},{7,6},{8,9},{9,8},{10,11... | collective-permute-start | bytes 98312 | tf_op jit(solution)/shard_map/ppermute | solution.py:326
  25.2 4.2 %collective-permute-start.5 = (bf16[32,512]{1,0:T(8,128)(2,1)S(1)}, bf16[32,512]{1,0:T(8,128)(2,1)S(1)}, u32[]{:S(2)}, u32[]{:S(2)}) collective-permute-start(bf16[32,512]{1,0:T(8,128)(2,1)S(1)} %lead.1.refs_0_.refs_12_), channel_id=1, source_target_pairs={{0,9},{1,8},{2,11},{3,10},{4,13},{5,12},{6,15},{7,14},{8,1},{9,0},... | collective-permute-start | bytes 98312 | tf_op jit(solution)/shard_map/ppermute | solution.py:326
  27.1 5.4 %collective-permute-start.15 = (f32[32,256]{1,0:T(8,128)S(1)}, f32[32,256]{1,0:T(8,128)S(1)}, u32[]{:S(2)}, u32[]{:S(2)}) collective-permute-start(f32[32,256]{1,0:T(8,128)S(1)} %add.14.refs_0_), channel_id=1, source_target_pairs={{0,8},{1,9},{2,10},{3,11},{4,12},{5,13},{6,14},{7,15},{8,0},{9,1},... | collective-permute-start | bytes 98312 | tf_op jit(solution)/shard_map/ppermute | solution.py:326
  33.9 1.5 %collective-permute-start.16 = (f32[64,256]{1,0:T(8,128)S(1)}, f32[64,256]{1,0:T(8,128)S(1)}, u32[]{:S(2)}, u32[]{:S(2)}) collective-permute-start(f32[64,256]{1,0:T(8,128)S(1)} %solve.1.refs_0_), channel_id=1, source_target_pairs={{0,1},{1,0},{2,3},{3,2},{4,5},{5,4},{6,7},{7,6},{8,9},{9,8},{10,11... | collective-permute-start | bytes 196616 | tf_op jit(solution)/shard_map/ppermute | solution.py:326
  36.8 3.4 %collective-permute-start.17 = (bf16[128,512]{1,0:T(8,128)(2,1)S(1)}, bf16[128,512]{1,0:T(8,128)(2,1)S(1)}, u32[]{:S(2)}, u32[]{:S(2)}) collective-permute-start(bf16[128,512]{1,0:T(8,128)(2,1)S(1)} %get-tuple-element.43), channel_id=1, source_target_pairs={{0,1},{1,0},{2,3},{3,2},{4,5},{5,4},{6,7},{7,6},{8,9},{9,8},{10,11... | collective-permute-start | bytes 393224 | tf_op jit(solution)/shard_map/ppermute | solution.py:326
  37.2 9.1 %collective-permute-start.19 = (bf16[128,512]{1,0:T(8,128)(2,1)S(1)}, bf16[128,512]{1,0:T(8,128)(2,1)S(1)}, u32[]{:S(2)}, u32[]{:S(2)}) collective-permute-start(bf16[128,512]{1,0:T(8,128)(2,1)S(1)} %get-tuple-element.45), channel_id=1, source_target_pairs={{0,4},{1,5},{2,6},{3,7},{4,0},{5,1},{6,2},{7,3},{8,12},{9,13},{10,... | collective-permute-start | bytes 393224 | tf_op jit(solution)/shard_map/ppermute | solution.py:326
  39.2 10.5 %collective-permute-start.20 = (bf16[128,512]{1,0:T(8,128)(2,1)S(1)}, bf16[128,512]{1,0:T(8,128)(2,1)S(1)}, u32[]{:S(2)}, u32[]{:S(2)}) collective-permute-start(bf16[128,512]{1,0:T(8,128)(2,1)S(1)} %get-tuple-element.46), channel_id=1, source_target_pairs={{0,6},{1,7},{2,4},{3,5},{4,2},{5,3},{6,0},{7,1},{8,14},{9,15},{10,... | collective-permute-start | bytes 393224 | tf_op jit(solution)/shard_map/ppermute | solution.py:326
  40.2 9.4 %collective-permute-start.22 = (bf16[128,512]{1,0:T(8,128)(2,1)S(1)}, bf16[128,512]{1,0:T(8,128)(2,1)S(1)}, u32[]{:S(2)}, u32[]{:S(2)}) collective-permute-start(bf16[128,512]{1,0:T(8,128)(2,1)S(1)} %add_convert_fusion), channel_id=1, source_target_pairs={{0,8},{1,9},{2,10},{3,11},{4,12},{5,13},{6,14},{7,15},{8,0},{9,1},... | collective-permute-start | bytes 393224 | tf_op jit(solution)/shard_map/ppermute | solution.py:326
  42.1 7.5 %collective-permute-start.21 = (bf16[128,512]{1,0:T(8,128)(2,1)S(1)}, bf16[128,512]{1,0:T(8,128)(2,1)S(1)}, u32[]{:S(2)}, u32[]{:S(2)}) collective-permute-start(bf16[128,512]{1,0:T(8,128)(2,1)S(1)} %get-tuple-element.49), channel_id=1, source_target_pairs={{0,1},{1,0},{2,3},{3,2},{4,5},{5,4},{6,7},{7,6},{8,9},{9,8},{10,11... | collective-permute-start | bytes 393224 | tf_op jit(solution)/shard_map/ppermute | solution.py:326
  42.1 8.6 %collective-permute-start.18 = (bf16[128,512]{1,0:T(8,128)(2,1)S(1)}, bf16[128,512]{1,0:T(8,128)(2,1)S(1)}, u32[]{:S(2)}, u32[]{:S(2)}) collective-permute-start(bf16[128,512]{1,0:T(8,128)(2,1)S(1)} %get-tuple-element.44), channel_id=1, source_target_pairs={{0,2},{1,3},{2,0},{3,1},{4,6},{5,7},{6,4},{7,5},{8,10},{9,11},{10,... | collective-permute-start | bytes 393224 | tf_op jit(solution)/shard_map/ppermute | solution.py:326
  (6 other events, 6.4 us)

commit v2 on v1

--- a/solution.py
+++ b/solution.py
@@ -16,6 +16,7 @@
 LANES = 128
 SUBLANES = 8
 CHUNK = 256
+CHUNKS = 2
 VMEM_BYTES = 48 * 1024 * 1024
 LOG2_E = math.log2(math.e)
 SHARES = 2
@@ -135,23 +136,22 @@
         rate_out_ref[:, here] = rate_ref[place ^ m]
 
 
-def design_kernel(*refs):
-    lead_refs, (design_ref, rows_ref) = refs[:-2], refs[-2:]
-    size = lead_refs[0].shape[1]
-    for d, lead_ref in enumerate(lead_refs):
+def design_kernel(small_ref, design_ref, rows_ref):
+    size = small_ref.shape[2]
+    for d in range(small_ref.shape[0]):
         here = slice(d * size, (d + 1) * size)
-        design_ref[:, here] = lead_ref[...]
-        turned = lead_ref[...].astype(F32).T
+        design_ref[:, here] = small_ref[d]
+        turned = small_ref[d].astype(F32).T
         blank = jnp.zeros((size, LANES - 3 * REGRESSORS), F32)
         rows_ref[here] = jnp.concatenate([turned] * 3 + [blank], axis=1).astype(BF16)
 
 
-def inverse_kernel(ridge, *refs):
+def inverse_kernel(ridge, small_ref, inverse_ref):
     square = (REGRESSORS, REGRESSORS)
     gram = jnp.where(rows(square) == lanes(square), ridge, 0.0)
-    for lead_ref in refs[:-1]:
-        gram = gram + dot(lead_ref[...], lead_ref[...], 1, 1)
-    refs[-1][...] = invert(gram)
+    for d in range(small_ref.shape[0]):
+        gram = gram + dot(small_ref[d], small_ref[d], 1, 1)
+    inverse_ref[...] = invert(gram)
 
 
 def joined_weights(refs):
@@ -218,7 +218,9 @@
     return jnp.concatenate([ref[here] for ref in refs], axis=1)
 
 
-def backward_kernel(scale, shares, paths, trades, member_ref, rows_ref, slope_ref, value_ref, *refs):
+def backward_kernel(
+    scale, shares, paths, trades, member_ref, rows_ref, slope_ref, value_ref, *refs
+):
     solved_refs, refs = refs[:shares], refs[shares:]
     x_refs, refs = refs[:paths], refs[paths:]
     w_refs, refs = refs[:trades], refs[trades:]
@@ -283,12 +285,17 @@
     return out
 
 
-def sum_kernel(first, own_ref, *refs):
+def sum_kernel(whole, pieces, own_ref, *refs):
     basis_ref, weight_ref = refs[-2:]
-    basis = total(refs[:first])
-    basis_ref[:, :LANES] = basis[:, :LANES] + own_ref[...]
-    basis_ref[:, LANES:] = basis[:, LANES:]
-    weight_ref[...] = total(refs[first:-2])
+    chunks, last = refs[whole : whole + pieces * CHUNKS], refs[whole + pieces * CHUNKS : -2]
+    basis = total(refs[:whole])
+    size = basis.shape[0] // CHUNKS
+    for k in range(CHUNKS):
+        here = slice(k * size, (k + 1) * size)
+        part = basis[here] + total(chunks[k * pieces : (k + 1) * pieces])
+        basis_ref[here, :LANES] = part[:, :LANES] + own_ref[here]
+        basis_ref[here, LANES:] = part[:, LANES:]
+    weight_ref[...] = total(last)
 
 
 def call(kernel, outs, *args, name, flops=0, scratch=(), scalars=0):
@@ -368,13 +375,15 @@
     weights[0] = own_weight
     notionals = [x[None, :] for x in notionals]
     (lead,) = call(lead_kernel, [((REGRESSORS, group_paths), BF16)], *basis, name="lead")
-    leads = [lead] + direct([lead] * outer, outer_bits)
     value, *moments = call(
         partial(forward_kernel, inner, outer),
         [((group_paths, group_trades), BF16)] + [((REGRESSORS, share), F32)] * SHARES,
         *basis, *weights, *notionals, lead, member,
         name="forward",
     )
+    small = lead[None]
+    for bit in outer_bits:
+        small = jnp.concatenate([small, swap(small, 1 << bit)], axis=0)
     moment = moments[0] + swap(moments[1], SHARES - 1)
     for bit in inner_bits + outer_bits[-2:0:-1]:
         moment = moment + swap(moment, 1 << bit)
@@ -382,13 +391,13 @@
     (inverse,) = call(
         partial(inverse_kernel, RIDGE_SCALE * paths_all),
         [((REGRESSORS, REGRESSORS), F32)],
-        *leads,
+        small,
         name="inverse",
     )
     design_all, design_rows = call(
         design_kernel,
         [((REGRESSORS, paths_all), BF16), ((paths_all, LANES), BF16)],
-        *leads,
+        small,
         name="design",
     )
     (solved,) = call(
@@ -405,30 +414,49 @@
         *basis, *weights, *notionals,
         name="slope",
     )
+    heights = [path_rows] * 2 + [path_rows // CHUNKS] * (CHUNKS * (inner - 2))
     parts = call(
         partial(backward_kernel, 1.0 / math.sqrt(paths_all), SHARES, inner, outer),
-        [((trade_rows, features), BF16)] * outer + [((path_rows, features), BF16)] * inner,
+        [((trade_rows, features), BF16)] * outer + [((h, features), BF16) for h in heights],
         member, design_rows, slope, value, *solved, *basis, *weights,
         name="backward",
         scratch=[pltpu.VMEM((group_paths, group_trades), BF16)],
     )
+
+    def rounded_sum(terms):
+        return terms[0] if len(terms) == 1 else sum(t.astype(F32) for t in terms).astype(BF16)
+
     terms = [[part] for part in parts[:outer]]
+    core_step = None
     for bit in reversed(outer_bits):
         count = len(terms) // 2
         arrived = None
         for k in reversed(range(count)):
-            gone = terms[count + k]
-            gone = gone[0] if len(gone) == 1 else sum(g.astype(F32) for g in gone).astype(BF16)
+            gone = rounded_sum(terms[count + k])
             if arrived is not None:
                 gone = after(gone, arrived)
             arrived = swap(gone, 1 << bit)
             terms[k].append(arrived)
-            if bit == outer_bits[-1] and k == count - 1:
-                basis_parts = list(parts[outer:])
-                basis_parts[1] = after(basis_parts[1], arrived)
+            core_step = arrived if core_step is None else core_step
         terms = terms[:count]
     weight_terms = terms[0]
-    basis_terms = [basis_parts[0]] + direct(basis_parts, inner_bits)
+    own, first, *rest = parts[outer:]
+    pieces = [[[piece] for piece in rest[m * CHUNKS : (m + 1) * CHUNKS]] for m in range(inner - 2)]
+    pieces = [None, None] + pieces
+    whole_terms, piece_terms = [own], [[] for _ in range(CHUNKS)]
+    for j, bit in enumerate(inner_bits):
+        for m in reversed(range(2, inner)):
+            if (m >> j) & 1 and m % (1 << j) == 0:
+                for k in range(CHUNKS):
+                    gone = rounded_sum(pieces[m][k])
+                    if j == 0:
+                        gone = after(gone, core_step)
+                    arrived = swap(gone, 1 << bit)
+                    target = piece_terms[k] if m == 1 << j else pieces[m - (1 << j)][k]
+                    target.append(arrived)
+        if j == 0:
+            whole_terms.append(swap(after(first, core_step), 1 << bit))
+    piece_terms = [t for terms in piece_terms for t in terms]
     loss, own_adjoint = call(
         loss_kernel,
         [((8, LANES), F32), ((path_rows, LANES), F32)],
@@ -437,9 +465,9 @@
         scratch=[pltpu.VMEM((LANES, sets), BF16), pltpu.VMEM((8, sets), F32)],
     )
     basis_adjoint, weight_adjoint = call(
-        partial(sum_kernel, len(basis_terms)),
+        partial(sum_kernel, len(whole_terms), len(piece_terms) // CHUNKS),
         [((path_rows, features), F32), ((trade_rows, features), F32)],
-        own_adjoint, *basis_terms, *weight_terms,
+        own_adjoint, *whole_terms, *piece_terms, *weight_terms,
         name="sums",
     )
     return (loss[0, :1], basis_adjoint, weight_adjoint)

time: 51.7 us -> 52.8 us (1.021)
  waiting for transfers between devices: 11.8 us -> 14.5 us
  starting transfers between devices: 23.1 us -> 21.1 us
    ppermute x23 -> x24, waiting for transfers between devices: 11.8 us -> 14.5 us  [swap(): return lax.ppermute(x, 'paths', [(d, d ^ mask) for d in range(n)])]
    ppermute x23 -> x24, starting transfers between devices: 23.1 us -> 21.1 us  [swap(): return lax.ppermute(x, 'paths', [(d, d ^ mask) for d in range(n)])]
  transfers between devices with their start and end apart: 23 -> 24, of which waited for: 8 -> 10; matrix products, arithmetic and copies ran while one was open for 1% -> 1% of each run, Pallas kernels for 15% -> 15%
where the time goes in v2:
time: 52.8 us; the launch traced here: 52.6 us
  starting transfers between devices  21.1 us (40%)
  waiting for transfers between devices  14.5 us (27%)
  Pallas kernels  13 us (25%)
  local copies, waits for them, and re-layouts  3.02 us (6%)
  between operations  0.8 us (2%)
    ppermute x24, starting transfers between devices, swap(): return lax.ppermute(x, 'paths', [(d, d ^ mask) for d in range(n)])  21.1 us
    ppermute x24, waiting for transfers between devices, swap(): return lax.ppermute(x, 'paths', [(d, d ^ mask) for d in range(n)])  14.5 us
    pallas_call x10, Pallas kernels, call(): pl.pallas_call(kernel, out_shape=[jax.ShapeDtypeStruct(s, d) for s, d in...  13 us
    unnamed x14, local copies, waits for them, and re-layouts  2.51 us
  transfers between devices with their start and end apart: 24, of which 10 were waited for; matrix products, arithmetic and copies ran while one was open for 1% of the time, Pallas kernels for 15%

profile of v2, /device:TPU:0, one launch (start us, length us, event | category | flops | bytes accessed | tf_op | source)
XLA Modules:
  0.0 52.6 jit_solution(7793894437464495224)
XLA Ops:
  0.6 4.1 %collective-permute-start.5 = (bf16[128,512]{1,0:T(8,128)(2,1)}, bf16[128,512]{1,0:T(8,128)(2,1)S(1)}, u32[]{:S(2)}, u32[]{:S(2)}) collective-permute-start(bf16[128,512]{1,0:T(8,128)(2,1)} %w_ref.1), channel_id=1, source_target_pairs={{0,8},{1,9},{2,10},{3,11},{4,12},{5,13},{6,14},{7,15},{8,0},{9,1},... | collective-permute-start | bytes 393224 | tf_op jit(solution)/shard_map/ppermute | solution.py:333
  4.7 1.5 %collective-permute-start = (bf16[128,512]{1,0:T(8,128)(2,1)}, bf16[128,512]{1,0:T(8,128)(2,1)S(1)}, u32[]{:S(2)}, u32[]{:S(2)}) collective-permute-start(bf16[128,512]{1,0:T(8,128)(2,1)} %x_ref.1), channel_id=1, source_target_pairs={{0,2},{1,3},{2,0},{3,1},{4,6},{5,7},{6,4},{7,5},{8,10},{9,11},{10,... | collective-permute-start | bytes 393224 | tf_op jit(solution)/shard_map/ppermute | solution.py:333
  6.3 1.6 %collective-permute-start.1 = (bf16[128,512]{1,0:T(8,128)(2,1)}, bf16[128,512]{1,0:T(8,128)(2,1)S(1)}, u32[]{:S(2)}, u32[]{:S(2)}) collective-permute-start(bf16[128,512]{1,0:T(8,128)(2,1)} %x_ref.1), channel_id=1, source_target_pairs={{0,4},{1,5},{2,6},{3,7},{4,0},{5,1},{6,2},{7,3},{8,12},{9,13},{10,... | collective-permute-start | bytes 393224 | tf_op jit(solution)/shard_map/ppermute | solution.py:333
  9.0 0.9 %copy-done = bf16[128,512]{1,0:T(8,128)(2,1)S(1)} copy-done((bf16[128,512]{1,0:T(8,128)(2,1)S(1)}, bf16[128,512]{1,0:T(8,128)(2,1)}, u32[]{:S(2)}) %copy-start) | copy-done | bytes 131096
  9.9 0.9 %copy-done.1 = bf16[128,512]{1,0:T(8,128)(2,1)S(1)} copy-done((bf16[128,512]{1,0:T(8,128)(2,1)S(1)}, bf16[128,512]{1,0:T(8,128)(2,1)}, u32[]{:S(2)}) %copy-start.1) | copy-done | bytes 131096
  11.5 2.0 %collective-permute-done.8 = bf16[128]{0:T(256)(128)(2,1)S(1)} collective-permute-done((bf16[128]{0:T(256)(128)(2,1)}, bf16[128]{0:T(256)(128)(2,1)S(1)}, u32[]{:S(2)}, u32[]{:S(2)}) %collective-permute-start.8) | collective-permute-done | bytes 288 | tf_op jit(solution)/shard_map/ppermute | solution.py:333
  14.5 1.2 %collective-permute-done.2.refs_3_.refs_5_ = bf16[128,512]{1,0:T(8,128)(2,1)S(1)} collective-permute-done((bf16[128,512]{1,0:T(8,128)(2,1)}, bf16[128,512]{1,0:T(8,128)(2,1)S(1)}, u32[]{:S(2)}, u32[]{:S(2)}) %collective-permute-start.2) | collective-permute-done | bytes 131104 | tf_op jit(solution)/shard_map/ppermute | solution.py:333
  15.8 1.3 %forward.1 = (bf16[512,512]{1,0:T(8,128)(2,1)S(1)}, f32[32,256]{1,0:T(8,128)S(1)}, f32[32,256]{1,0:T(8,128)S(1)}) custom-call(bf16[128,512]{1,0:T(8,128)(2,1)S(1)} %get-tuple-element.32.refs_0_.refs_2_, bf16[128,512]{1,0:T(8,128)(2,1)S(1)} %collective-permute-done.refs_1_.refs_3_, bf16[128,512]{1,0:T(8,128)(2,1)S(1)} %collective-permute-done.1.refs_2_.refs_4_, ...), custom_call_target="tpu_custom_call" | custom-call | bytes 2196480 | tf_op jit(solution)/shard_map/forward/pallas_call | solution.py:305
  17.1 3.1 %collective-permute-start.3 = (bf16[1,32,512]{2,1,0:T(8,128)(2,1)S(1)}, bf16[1,32,512]{2,1,0:T(8,128)(2,1)S(1)}, u32[]{:S(2)}, u32[]{:S(2)}) collective-permute-start(bf16[1,32,512]{2,1,0:T(8,128)(2,1)S(1)} %bitcast.10), channel_id=1, source_target_pairs={{0,8},{1,9},{2,10},{3,11},{4,12},{5,13},{6,14},{7,15},{8,0},{9,1},... | collective-permute-start | bytes 98312 | tf_op jit(solution)/shard_map/ppermute | solution.py:333
  20.2 1.6 %collective-permute-start.12 = (f32[32,256]{1,0:T(8,128)S(1)}, f32[32,256]{1,0:T(8,128)S(1)}, u32[]{:S(2)}, u32[]{:S(2)}) collective-permute-start(f32[32,256]{1,0:T(8,128)S(1)} %add.18), channel_id=1, source_target_pairs={{0,2},{1,3},{2,0},{3,1},{4,6},{5,7},{6,4},{7,5},{8,10},{9,11},{10,... | collective-permute-start | bytes 98312 | tf_op jit(solution)/shard_map/ppermute | solution.py:333
  22.2 2.0 %collective-permute-done.12 = f32[32,256]{1,0:T(8,128)S(1)} collective-permute-done((f32[32,256]{1,0:T(8,128)S(1)}, f32[32,256]{1,0:T(8,128)S(1)}, u32[]{:S(2)}, u32[]{:S(2)}) %collective-permute-start.12) | collective-permute-done | bytes 32800 | tf_op jit(solution)/shard_map/ppermute | solution.py:333
  24.2 3.9 %collective-permute-done.13 = f32[32,256]{1,0:T(8,128)S(1)} collective-permute-done((f32[32,256]{1,0:T(8,128)S(1)}, f32[32,256]{1,0:T(8,128)S(1)}, u32[]{:S(2)}, u32[]{:S(2)}) %collective-permute-start.13) | collective-permute-done | bytes 32800 | tf_op jit(solution)/shard_map/ppermute | solution.py:333
  28.1 1.0 %collective-permute-start.14 = (f32[32,256]{1,0:T(8,128)S(1)}, f32[32,256]{1,0:T(8,128)S(1)}, u32[]{:S(2)}, u32[]{:S(2)}) collective-permute-start(f32[32,256]{1,0:T(8,128)S(1)} %add.20.refs_0_), channel_id=1, source_target_pairs={{0,8},{1,9},{2,10},{3,11},{4,12},{5,13},{6,14},{7,15},{8,0},{9,1},... | collective-permute-start | bytes 98312 | tf_op jit(solution)/shard_map/ppermute | solution.py:333
  29.7 2.5 %inverse.1.inverse_ref = f32[32,32]{1,0:T(8,128)S(1)} custom-call(bf16[4,32,512]{2,1,0:T(8,128)(2,1)S(1)} %pad_maximum_fusion.small_ref), custom_call_target="tpu_custom_call" | custom-call | bytes 135168 | tf_op jit(solution)/shard_map/inverse/pallas_call | solution.py:305
  32.9 1.4 %solve.1.refs_0_ = f32[64,256]{1,0:T(8,128)S(1)} custom-call(f32[32,32]{1,0:T(8,128)S(1)} %inverse.1.inverse_ref, bf16[32,2048]{1,0:T(8,128)(2,1)S(1)} %get-tuple-element.36.design_ref, bf16[2048,128]{1,0:T(8,128)(2,1)S(1)} %get-tuple-element.33.rows_ref, f32[1,512]{1,0:T(1,128)S(1)} %get-tuple-element.34.thresh_ref, ...), custom_call_target="tpu_custom_call" | custom-call | bytes 794624 | tf_op jit(solution)/shard_map/solve/pallas_call | solution.py:305
  34.4 0.9 %slope.1.slope_ref = f32[512,512]{1,0:T(8,128)S(1)} custom-call(bf16[128,512]{1,0:T(8,128)(2,1)S(1)} %get-tuple-element.32.refs_0_.refs_2_, bf16[128,512]{1,0:T(8,128)(2,1)S(1)} %collective-permute-done.refs_1_.refs_3_, bf16[128,512]{1,0:T(8,128)(2,1)S(1)} %collective-permute-done.1.refs_2_.refs_4_, ...), custom_call_target="tpu_custom_call" | custom-call | bytes 2098176 | tf_op jit(solution)/shard_map/slope/pallas_call | solution.py:305
  35.6 1.7 %backward.1 = (bf16[128,512]{1,0:T(8,128)(2,1)S(1)}, bf16[128,512]{1,0:T(8,128)(2,1)S(1)}, bf16[128,512]{1,0:T(8,128)(2,1)S(1)}, bf16[128,512]{1,0:T(8,128)(2,1)...) custom-call(bf16[512,512]{1,0:T(8,128)(2,1)S(1)} %get-tuple-element., ...), custom_call_target="tpu_custom_call" | custom-call | bytes 4849664 | tf_op jit(solution)/shard_map/backward/pallas_call | solution.py:305
  37.6 1.2 %collective-permute-done.16 = bf16[128,512]{1,0:T(8,128)(2,1)S(1)} collective-permute-done((bf16[128,512]{1,0:T(8,128)(2,1)S(1)}, bf16[128,512]{1,0:T(8,128)(2,1)S(1)}, u32[]{:S(2)}, u32[]{:S(2)}) %collective-permute-start.16) | collective-permute-done | bytes 131104 | tf_op jit(solution)/shard_map/ppermute | solution.py:333
  38.8 1.5 %collective-permute-start.20 = (bf16[64,512]{1,0:T(8,128)(2,1)S(1)}, bf16[64,512]{1,0:T(8,128)(2,1)S(1)}, u32[]{:S(2)}, u32[]{:S(2)}) collective-permute-start(bf16[64,512]{1,0:T(8,128)(2,1)S(1)} %get-tuple-element.54), channel_id=1, source_target_pairs={{0,2},{1,3},{2,0},{3,1},{4,6},{5,7},{6,4},{7,5},{8,10},{9,11},{10,... | collective-permute-start | bytes 196616 | tf_op jit(solution)/shard_map/ppermute | solution.py:333
  40.3 1.3 %collective-permute-start.23 = (bf16[128,512]{1,0:T(8,128)(2,1)S(1)}, bf16[128,512]{1,0:T(8,128)(2,1)S(1)}, u32[]{:S(2)}, u32[]{:S(2)}) collective-permute-start(bf16[128,512]{1,0:T(8,128)(2,1)S(1)} %add_convert_fusion), channel_id=1, source_target_pairs={{0,8},{1,9},{2,10},{3,11},{4,12},{5,13},{6,14},{7,15},{8,0},{9,1},... | collective-permute-start | bytes 393224 | tf_op jit(solution)/shard_map/ppermute | solution.py:333
  42.1 1.5 %collective-permute-start.17 = (bf16[128,512]{1,0:T(8,128)(2,1)S(1)}, bf16[128,512]{1,0:T(8,128)(2,1)S(1)}, u32[]{:S(2)}, u32[]{:S(2)}) collective-permute-start(bf16[128,512]{1,0:T(8,128)(2,1)S(1)} %get-tuple-element.48), channel_id=1, source_target_pairs={{0,2},{1,3},{2,0},{3,1},{4,6},{5,7},{6,4},{7,5},{8,10},{9,11},{10,... | collective-permute-start | bytes 393224 | tf_op jit(solution)/shard_map/ppermute | solution.py:333
  44.4 2.0 %collective-permute-done.18 = bf16[64,512]{1,0:T(8,128)(2,1)S(1)} collective-permute-done((bf16[64,512]{1,0:T(8,128)(2,1)S(1)}, bf16[64,512]{1,0:T(8,128)(2,1)S(1)}, u32[]{:S(2)}, u32[]{:S(2)}) %collective-permute-start.18) | collective-permute-done | bytes 65568 | tf_op jit(solution)/shard_map/ppermute | solution.py:333
  47.3 3.2 %loss.1 = (f32[8,128]{1,0:T(8,128)S(1)}, f32[128,128]{1,0:T(8,128)S(1)}) custom-call(bf16[2048,128]{1,0:T(8,128)(2,1)S(1)} %get-tuple-element.33.rows_ref, f32[1,512]{1,0:T(1,128)S(1)} %get-tuple-element.34.thresh_ref, f32[1,512]{1,0:T(1,128)S(1)} %get-tuple-element.35.rate_ref, f32[64,256]{1,0:T(8,128)S(1)} %solve.1.refs_0_, ...), custom_call_target="tpu_custom_call" | custom-call | bytes 729088 | tf_op jit(solution)/shard_map/loss/pallas_call | solution.py:305
  51.7 0.8 %sums.1 = (f32[128,512]{1,0:T(8,128)}, f32[128,512]{1,0:T(8,128)}) custom-call(f32[128,128]{1,0:T(8,128)S(1)} %get-tuple-element.43.own_ref, bf16[128,512]{1,0:T(8,128)(2,1)S(1)} %get-tuple-element.45.refs_0_, bf16[128,512]{1,0:T(8,128)(2,1)S(1)} %collective-permute-done.17.refs_1_, bf16[64,512]{1,0:T(8,128)(2,1)S(1)} %collective-permute-done.19.refs_2_, ...), custom_call_target="tpu_custom_call" | custom-call | bytes 1376256 | tf_op jit(solution)/shard_map/sums/pallas_call | solution.py:305
  (57 shorter events, 8.9 us)
Async XLA Ops:
  0.6 12.8 %collective-permute-start.5 = (bf16[128,512]{1,0:T(8,128)(2,1)}, bf16[128,512]{1,0:T(8,128)(2,1)S(1)}, u32[]{:S(2)}, u32[]{:S(2)}) collective-permute-start(bf16[128,512]{1,0:T(8,128)(2,1)} %w_ref.1), channel_id=1, source_target_pairs={{0,8},{1,9},{2,10},{3,11},{4,12},{5,13},{6,14},{7,15},{8,0},{9,1},... | collective-permute-start | bytes 393224 | tf_op jit(solution)/shard_map/ppermute | solution.py:333
  4.7 9.3 %collective-permute-start = (bf16[128,512]{1,0:T(8,128)(2,1)}, bf16[128,512]{1,0:T(8,128)(2,1)S(1)}, u32[]{:S(2)}, u32[]{:S(2)}) collective-permute-start(bf16[128,512]{1,0:T(8,128)(2,1)} %x_ref.1), channel_id=1, source_target_pairs={{0,2},{1,3},{2,0},{3,1},{4,6},{5,7},{6,4},{7,5},{8,10},{9,11},{10,... | collective-permute-start | bytes 393224 | tf_op jit(solution)/shard_map/ppermute | solution.py:333
  6.3 7.8 %collective-permute-start.1 = (bf16[128,512]{1,0:T(8,128)(2,1)}, bf16[128,512]{1,0:T(8,128)(2,1)S(1)}, u32[]{:S(2)}, u32[]{:S(2)}) collective-permute-start(bf16[128,512]{1,0:T(8,128)(2,1)} %x_ref.1), channel_id=1, source_target_pairs={{0,4},{1,5},{2,6},{3,7},{4,0},{5,1},{6,2},{7,3},{8,12},{9,13},{10,... | collective-permute-start | bytes 393224 | tf_op jit(solution)/shard_map/ppermute | solution.py:333
  7.8 7.8 %collective-permute-start.2 = (bf16[128,512]{1,0:T(8,128)(2,1)}, bf16[128,512]{1,0:T(8,128)(2,1)S(1)}, u32[]{:S(2)}, u32[]{:S(2)}) collective-permute-start(bf16[128,512]{1,0:T(8,128)(2,1)} %x_ref.1), channel_id=1, source_target_pairs={{0,6},{1,7},{2,4},{3,5},{4,2},{5,3},{6,0},{7,1},{8,14},{9,15},{10,... | collective-permute-start | bytes 393224 | tf_op jit(solution)/shard_map/ppermute | solution.py:333
  8.2 5.2 %collective-permute-start.8 = (bf16[128]{0:T(256)(128)(2,1)}, bf16[128]{0:T(256)(128)(2,1)S(1)}, u32[]{:S(2)}, u32[]{:S(2)}) collective-permute-start(bf16[128]{0:T(256)(128)(2,1)} %param.9), channel_id=1, source_target_pairs={{0,8},{1,9},{2,10},{3,11},{4,12},{5,13},{6,14},{7,15},{8,0},{9,1},... | collective-permute-start | bytes 776 | tf_op jit(solution)/shard_map/ppermute | solution.py:333
  13.5 2.3 %collective-permute-start.6 = (bf16[128,512]{1,0:T(8,128)(2,1)S(1)}, bf16[128,512]{1,0:T(8,128)(2,1)S(1)}, u32[]{:S(2)}, u32[]{:S(2)}) collective-permute-start(bf16[128,512]{1,0:T(8,128)(2,1)S(1)} %copy-done.1), channel_id=1, source_target_pairs={{0,1},{1,0},{2,3},{3,2},{4,5},{5,4},{6,7},{7,6},{8,9},{9,8},{10,11... | collective-permute-start | bytes 393224 | tf_op jit(solution)/shard_map/ppermute | solution.py:333
  13.5 2.3 %collective-permute-start.7 = (bf16[128,512]{1,0:T(8,128)(2,1)S(1)}, bf16[128,512]{1,0:T(8,128)(2,1)S(1)}, u32[]{:S(2)}, u32[]{:S(2)}) collective-permute-start(bf16[128,512]{1,0:T(8,128)(2,1)S(1)} %collective-permute-done.5.refs_5_.refs_7_), channel_id=1, source_target_pairs={{0,1},{1,0},{2,3},{3,2},{4,5},{5,4},{6,7},{7,6},{8,9},{9,8},{10,11... | collective-permute-start | bytes 393224 | tf_op jit(solution)/shard_map/ppermute | solution.py:333
  14.0 1.8 %collective-permute-start.9 = (bf16[128]{0:T(256)(128)(2,1)S(1)}, bf16[128]{0:T(256)(128)(2,1)S(1)}, u32[]{:S(2)}, u32[]{:S(2)}) collective-permute-start(bf16[128]{0:T(256)(128)(2,1)S(1)} %copy-done.5), channel_id=1, source_target_pairs={{0,1},{1,0},{2,3},{3,2},{4,5},{5,4},{6,7},{7,6},{8,9},{9,8},{10,11... | collective-permute-start | bytes 776 | tf_op jit(solution)/shard_map/ppermute | solution.py:333
  14.1 1.7 %collective-permute-start.10 = (bf16[128]{0:T(256)(128)(2,1)S(1)}, bf16[128]{0:T(256)(128)(2,1)S(1)}, u32[]{:S(2)}, u32[]{:S(2)}) collective-permute-start(bf16[128]{0:T(256)(128)(2,1)S(1)} %collective-permute-done.8), channel_id=1, source_target_pairs={{0,1},{1,0},{2,3},{3,2},{4,5},{5,4},{6,7},{7,6},{8,9},{9,8},{10,11... | collective-permute-start | bytes 776 | tf_op jit(solution)/shard_map/ppermute | solution.py:333
  17.1 3.1 %collective-permute-start.11 = (f32[32,256]{1,0:T(8,128)S(1)}, f32[32,256]{1,0:T(8,128)S(1)}, u32[]{:S(2)}, u32[]{:S(2)}) collective-permute-start(f32[32,256]{1,0:T(8,128)S(1)} %get-tuple-element.41), channel_id=1, source_target_pairs={{0,1},{1,0},{2,3},{3,2},{4,5},{5,4},{6,7},{7,6},{8,9},{9,8},{10,11... | collective-permute-start | bytes 98312 | tf_op jit(solution)/shard_map/ppermute | solution.py:333
  17.1 5.0 %collective-permute-start.3 = (bf16[1,32,512]{2,1,0:T(8,128)(2,1)S(1)}, bf16[1,32,512]{2,1,0:T(8,128)(2,1)S(1)}, u32[]{:S(2)}, u32[]{:S(2)}) collective-permute-start(bf16[1,32,512]{2,1,0:T(8,128)(2,1)S(1)} %bitcast.10), channel_id=1, source_target_pairs={{0,8},{1,9},{2,10},{3,11},{4,12},{5,13},{6,14},{7,15},{8,0},{9,1},... | collective-permute-start | bytes 98312 | tf_op jit(solution)/shard_map/ppermute | solution.py:333
  20.2 4.0 %collective-permute-start.12 = (f32[32,256]{1,0:T(8,128)S(1)}, f32[32,256]{1,0:T(8,128)S(1)}, u32[]{:S(2)}, u32[]{:S(2)}) collective-permute-start(f32[32,256]{1,0:T(8,128)S(1)} %add.18), channel_id=1, source_target_pairs={{0,2},{1,3},{2,0},{3,1},{4,6},{5,7},{6,4},{7,5},{8,10},{9,11},{10,... | collective-permute-start | bytes 98312 | tf_op jit(solution)/shard_map/ppermute | solution.py:333
  22.1 7.0 %collective-permute-start.4 = (bf16[2,32,512]{2,1,0:T(8,128)(2,1)S(1)}, bf16[2,32,512]{2,1,0:T(8,128)(2,1)S(1)}, u32[]{:S(2)}, u32[]{:S(2)}) collective-permute-start(bf16[2,32,512]{2,1,0:T(8,128)(2,1)S(1)} %pad_maximum_fusion.1), channel_id=1, source_target_pairs={{0,1},{1,0},{2,3},{3,2},{4,5},{5,4},{6,7},{7,6},{8,9},{9,8},{10,11... | collective-permute-start | bytes 196616 | tf_op jit(solution)/shard_map/ppermute | solution.py:333
  24.2 3.9 %collective-permute-start.13 = (f32[32,256]{1,0:T(8,128)S(1)}, f32[32,256]{1,0:T(8,128)S(1)}, u32[]{:S(2)}, u32[]{:S(2)}) collective-permute-start(f32[32,256]{1,0:T(8,128)S(1)} %add.19), channel_id=1, source_target_pairs={{0,4},{1,5},{2,6},{3,7},{4,0},{5,1},{6,2},{7,3},{8,12},{9,13},{10,... | collective-permute-start | bytes 98312 | tf_op jit(solution)/shard_map/ppermute | solution.py:333
  28.1 4.8 %collective-permute-start.14 = (f32[32,256]{1,0:T(8,128)S(1)}, f32[32,256]{1,0:T(8,128)S(1)}, u32[]{:S(2)}, u32[]{:S(2)}) collective-permute-start(f32[32,256]{1,0:T(8,128)S(1)} %add.20.refs_0_), channel_id=1, source_target_pairs={{0,8},{1,9},{2,10},{3,11},{4,12},{5,13},{6,14},{7,15},{8,0},{9,1},... | collective-permute-start | bytes 98312 | tf_op jit(solution)/shard_map/ppermute | solution.py:333
  34.3 1.3 %collective-permute-start.15 = (f32[64,256]{1,0:T(8,128)S(1)}, f32[64,256]{1,0:T(8,128)S(1)}, u32[]{:S(2)}, u32[]{:S(2)}) collective-permute-start(f32[64,256]{1,0:T(8,128)S(1)} %solve.1.refs_0_), channel_id=1, source_target_pairs={{0,1},{1,0},{2,3},{3,2},{4,5},{5,4},{6,7},{7,6},{8,9},{9,8},{10,11... | collective-permute-start | bytes 196616 | tf_op jit(solution)/shard_map/ppermute | solution.py:333
  37.3 1.4 %collective-permute-start.16 = (bf16[128,512]{1,0:T(8,128)(2,1)S(1)}, bf16[128,512]{1,0:T(8,128)(2,1)S(1)}, u32[]{:S(2)}, u32[]{:S(2)}) collective-permute-start(bf16[128,512]{1,0:T(8,128)(2,1)S(1)} %get-tuple-element.47), channel_id=1, source_target_pairs={{0,1},{1,0},{2,3},{3,2},{4,5},{5,4},{6,7},{7,6},{8,9},{9,8},{10,11... | collective-permute-start | bytes 393224 | tf_op jit(solution)/shard_map/ppermute | solution.py:333
  38.8 4.8 %collective-permute-start.20 = (bf16[64,512]{1,0:T(8,128)(2,1)S(1)}, bf16[64,512]{1,0:T(8,128)(2,1)S(1)}, u32[]{:S(2)}, u32[]{:S(2)}) collective-permute-start(bf16[64,512]{1,0:T(8,128)(2,1)S(1)} %get-tuple-element.54), channel_id=1, source_target_pairs={{0,2},{1,3},{2,0},{3,1},{4,6},{5,7},{6,4},{7,5},{8,10},{9,11},{10,... | collective-permute-start | bytes 196616 | tf_op jit(solution)/shard_map/ppermute | solution.py:333
  40.3 11.5 %collective-permute-start.23 = (bf16[128,512]{1,0:T(8,128)(2,1)S(1)}, bf16[128,512]{1,0:T(8,128)(2,1)S(1)}, u32[]{:S(2)}, u32[]{:S(2)}) collective-permute-start(bf16[128,512]{1,0:T(8,128)(2,1)S(1)} %add_convert_fusion), channel_id=1, source_target_pairs={{0,8},{1,9},{2,10},{3,11},{4,12},{5,13},{6,14},{7,15},{8,0},{9,1},... | collective-permute-start | bytes 393224 | tf_op jit(solution)/shard_map/ppermute | solution.py:333
  41.6 10.2 %collective-permute-start.22 = (bf16[128,512]{1,0:T(8,128)(2,1)S(1)}, bf16[128,512]{1,0:T(8,128)(2,1)S(1)}, u32[]{:S(2)}, u32[]{:S(2)}) collective-permute-start(bf16[128,512]{1,0:T(8,128)(2,1)S(1)} %get-tuple-element.57), channel_id=1, source_target_pairs={{0,1},{1,0},{2,3},{3,2},{4,5},{5,4},{6,7},{7,6},{8,9},{9,8},{10,11... | collective-permute-start | bytes 393224 | tf_op jit(solution)/shard_map/ppermute | solution.py:333
  41.6 4.9 %collective-permute-start.18 = (bf16[64,512]{1,0:T(8,128)(2,1)S(1)}, bf16[64,512]{1,0:T(8,128)(2,1)S(1)}, u32[]{:S(2)}, u32[]{:S(2)}) collective-permute-start(bf16[64,512]{1,0:T(8,128)(2,1)S(1)} %get-tuple-element.51), channel_id=1, source_target_pairs={{0,2},{1,3},{2,0},{3,1},{4,6},{5,7},{6,4},{7,5},{8,10},{9,11},{10,... | collective-permute-start | bytes 196616 | tf_op jit(solution)/shard_map/ppermute | solution.py:333
  42.1 9.6 %collective-permute-start.17 = (bf16[128,512]{1,0:T(8,128)(2,1)S(1)}, bf16[128,512]{1,0:T(8,128)(2,1)S(1)}, u32[]{:S(2)}, u32[]{:S(2)}) collective-permute-start(bf16[128,512]{1,0:T(8,128)(2,1)S(1)} %get-tuple-element.48), channel_id=1, source_target_pairs={{0,2},{1,3},{2,0},{3,1},{4,6},{5,7},{6,4},{7,5},{8,10},{9,11},{10,... | collective-permute-start | bytes 393224 | tf_op jit(solution)/shard_map/ppermute | solution.py:333
  43.6 7.4 %collective-permute-start.21 = (bf16[64,512]{1,0:T(8,128)(2,1)S(1)}, bf16[64,512]{1,0:T(8,128)(2,1)S(1)}, u32[]{:S(2)}, u32[]{:S(2)}) collective-permute-start(bf16[64,512]{1,0:T(8,128)(2,1)S(1)} %add_convert_fusion.1), channel_id=1, source_target_pairs={{0,4},{1,5},{2,6},{3,7},{4,0},{5,1},{6,2},{7,3},{8,12},{9,13},{10,... | collective-permute-start | bytes 196616 | tf_op jit(solution)/shard_map/ppermute | solution.py:333
  46.5 5.3 %collective-permute-start.19 = (bf16[64,512]{1,0:T(8,128)(2,1)S(1)}, bf16[64,512]{1,0:T(8,128)(2,1)S(1)}, u32[]{:S(2)}, u32[]{:S(2)}) collective-permute-start(bf16[64,512]{1,0:T(8,128)(2,1)S(1)} %add_convert_fusion.2), channel_id=1, source_target_pairs={{0,4},{1,5},{2,6},{3,7},{4,0},{5,1},{6,2},{7,3},{8,12},{9,13},{10,... | collective-permute-start | bytes 196616 | tf_op jit(solution)/shard_map/ppermute | solution.py:333
  (7 other events, 14.1 us)

commit v3 on v1

--- a/solution.py
+++ b/solution.py
@@ -135,23 +135,22 @@
         rate_out_ref[:, here] = rate_ref[place ^ m]
 
 
-def design_kernel(*refs):
-    lead_refs, (design_ref, rows_ref) = refs[:-2], refs[-2:]
-    size = lead_refs[0].shape[1]
-    for d, lead_ref in enumerate(lead_refs):
+def design_kernel(small_ref, design_ref, rows_ref):
+    size = small_ref.shape[2]
+    for d in range(small_ref.shape[0]):
         here = slice(d * size, (d + 1) * size)
-        design_ref[:, here] = lead_ref[...]
-        turned = lead_ref[...].astype(F32).T
+        design_ref[:, here] = small_ref[d]
+        turned = small_ref[d].astype(F32).T
         blank = jnp.zeros((size, LANES - 3 * REGRESSORS), F32)
         rows_ref[here] = jnp.concatenate([turned] * 3 + [blank], axis=1).astype(BF16)
 
 
-def inverse_kernel(ridge, *refs):
+def inverse_kernel(ridge, small_ref, inverse_ref):
     square = (REGRESSORS, REGRESSORS)
     gram = jnp.where(rows(square) == lanes(square), ridge, 0.0)
-    for lead_ref in refs[:-1]:
-        gram = gram + dot(lead_ref[...], lead_ref[...], 1, 1)
-    refs[-1][...] = invert(gram)
+    for d in range(small_ref.shape[0]):
+        gram = gram + dot(small_ref[d], small_ref[d], 1, 1)
+    inverse_ref[...] = invert(gram)
 
 
 def joined_weights(refs):
@@ -368,7 +367,6 @@
     weights[0] = own_weight
     notionals = [x[None, :] for x in notionals]
     (lead,) = call(lead_kernel, [((REGRESSORS, group_paths), BF16)], *basis, name="lead")
-    leads = [lead] + direct([lead] * outer, outer_bits)
     value, *moments = call(
         partial(forward_kernel, inner, outer),
         [((group_paths, group_trades), BF16)] + [((REGRESSORS, share), F32)] * SHARES,
@@ -376,19 +374,26 @@
         name="forward",
     )
     moment = moments[0] + swap(moments[1], SHARES - 1)
-    for bit in inner_bits + outer_bits[-2:0:-1]:
-        moment = moment + swap(moment, 1 << bit)
+    small = after(lead, moment)[None]
+    steps = inner_bits + outer_bits[-2:0:-1]
+    for k in range(max(len(steps), outer_bits.index(0) + 1)):
+        if k < len(outer_bits):
+            if k > 0:
+                small = after(small, moment)
+            small = jnp.concatenate([small, swap(small, 1 << outer_bits[k])], axis=0)
+        if k < len(steps):
+            moment = moment + swap(moment, 1 << steps[k])
     moments = [moment, swap(moment, 1 << first_bit)]
     (inverse,) = call(
         partial(inverse_kernel, RIDGE_SCALE * paths_all),
         [((REGRESSORS, REGRESSORS), F32)],
-        *leads,
+        small,
         name="inverse",
     )
     design_all, design_rows = call(
         design_kernel,
         [((REGRESSORS, paths_all), BF16), ((paths_all, LANES), BF16)],
-        *leads,
+        small,
         name="design",
     )
     (solved,) = call(

time: 51.7 us -> 50.8 us (0.983)
  starting transfers between devices: 23.1 us -> 22.4 us
    ppermute x23 -> x22, starting transfers between devices: 23.1 us -> 22.4 us  [swap(): return lax.ppermute(x, 'paths', [(d, d ^ mask) for d in range(n)])]
    ppermute x23 -> x22, waiting for transfers between devices: 11.8 us -> 11.5 us  [swap(): return lax.ppermute(x, 'paths', [(d, d ^ mask) for d in range(n)])]
    unnamed x14 -> x15, local copies, waits for them, and re-layouts: 2.51 us -> 2.52 us
  transfers between devices with their start and end apart: 23 -> 22, of which waited for: 8 -> 8; matrix products, arithmetic and copies ran while one was open for 1% -> 1% of each run, Pallas kernels for 15% -> 16%
where the time goes in v3:
time: 50.8 us; the launch traced here: 50.6 us
  starting transfers between devices  22.4 us (44%)
  Pallas kernels  12.8 us (25%)
  waiting for transfers between devices  11.5 us (23%)
  local copies, waits for them, and re-layouts  3.04 us (6%)
  between operations  0.79 us (2%)
    ppermute x22, starting transfers between devices, swap(): return lax.ppermute(x, 'paths', [(d, d ^ mask) for d in range(n)])  22.4 us
    pallas_call x10, Pallas kernels, call(): pl.pallas_call(kernel, out_shape=[jax.ShapeDtypeStruct(s, d) for s, d in...  12.8 us
    ppermute x22, waiting for transfers between devices, swap(): return lax.ppermute(x, 'paths', [(d, d ^ mask) for d in range(n)])  11.5 us
    unnamed x15, local copies, waits for them, and re-layouts  2.52 us
  transfers between devices with their start and end apart: 22, of which 8 were waited for; matrix products, arithmetic and copies ran while one was open for 1% of the time, Pallas kernels for 16%

profile of v3, /device:TPU:0, one launch (start us, length us, event | category | flops | bytes accessed | tf_op | source)
XLA Modules:
  0.0 50.6 jit_solution(4895611646338962728)
XLA Ops:
  0.6 4.1 %collective-permute-start.3 = (bf16[128,512]{1,0:T(8,128)(2,1)}, bf16[128,512]{1,0:T(8,128)(2,1)S(1)}, u32[]{:S(2)}, u32[]{:S(2)}) collective-permute-start(bf16[128,512]{1,0:T(8,128)(2,1)} %w_ref.1), channel_id=1, source_target_pairs={{0,8},{1,9},{2,10},{3,11},{4,12},{5,13},{6,14},{7,15},{8,0},{9,1},... | collective-permute-start | bytes 393224 | tf_op jit(solution)/shard_map/ppermute | solution.py:325
  4.7 1.5 %collective-permute-start = (bf16[128,512]{1,0:T(8,128)(2,1)}, bf16[128,512]{1,0:T(8,128)(2,1)S(1)}, u32[]{:S(2)}, u32[]{:S(2)}) collective-permute-start(bf16[128,512]{1,0:T(8,128)(2,1)} %x_ref.1), channel_id=1, source_target_pairs={{0,2},{1,3},{2,0},{3,1},{4,6},{5,7},{6,4},{7,5},{8,10},{9,11},{10,... | collective-permute-start | bytes 393224 | tf_op jit(solution)/shard_map/ppermute | solution.py:325
  6.3 1.6 %collective-permute-start.1 = (bf16[128,512]{1,0:T(8,128)(2,1)}, bf16[128,512]{1,0:T(8,128)(2,1)S(1)}, u32[]{:S(2)}, u32[]{:S(2)}) collective-permute-start(bf16[128,512]{1,0:T(8,128)(2,1)} %x_ref.1), channel_id=1, source_target_pairs={{0,4},{1,5},{2,6},{3,7},{4,0},{5,1},{6,2},{7,3},{8,12},{9,13},{10,... | collective-permute-start | bytes 393224 | tf_op jit(solution)/shard_map/ppermute | solution.py:325
  9.0 0.9 %copy-done = bf16[128,512]{1,0:T(8,128)(2,1)S(1)} copy-done((bf16[128,512]{1,0:T(8,128)(2,1)S(1)}, bf16[128,512]{1,0:T(8,128)(2,1)}, u32[]{:S(2)}) %copy-start) | copy-done | bytes 131096
  9.9 0.9 %copy-done.1 = bf16[128,512]{1,0:T(8,128)(2,1)S(1)} copy-done((bf16[128,512]{1,0:T(8,128)(2,1)S(1)}, bf16[128,512]{1,0:T(8,128)(2,1)}, u32[]{:S(2)}) %copy-start.1) | copy-done | bytes 131096
  11.5 2.0 %collective-permute-done.6 = bf16[128]{0:T(256)(128)(2,1)S(1)} collective-permute-done((bf16[128]{0:T(256)(128)(2,1)}, bf16[128]{0:T(256)(128)(2,1)S(1)}, u32[]{:S(2)}, u32[]{:S(2)}) %collective-permute-start.6) | collective-permute-done | bytes 288 | tf_op jit(solution)/shard_map/ppermute | solution.py:325
  14.5 1.2 %collective-permute-done.2.refs_3_.refs_5_ = bf16[128,512]{1,0:T(8,128)(2,1)S(1)} collective-permute-done((bf16[128,512]{1,0:T(8,128)(2,1)}, bf16[128,512]{1,0:T(8,128)(2,1)S(1)}, u32[]{:S(2)}, u32[]{:S(2)}) %collective-permute-start.2) | collective-permute-done | bytes 131104 | tf_op jit(solution)/shard_map/ppermute | solution.py:325
  15.8 1.3 %forward.1 = (bf16[512,512]{1,0:T(8,128)(2,1)S(1)}, f32[32,256]{1,0:T(8,128)S(1)}, f32[32,256]{1,0:T(8,128)S(1)}) custom-call(bf16[128,512]{1,0:T(8,128)(2,1)S(1)} %get-tuple-element.30.refs_0_.refs_2_, bf16[128,512]{1,0:T(8,128)(2,1)S(1)} %collective-permute-done.refs_1_.refs_3_, bf16[128,512]{1,0:T(8,128)(2,1)S(1)} %collective-permute-done.1.refs_2_.refs_4_, ...), custom_call_target="tpu_custom_call" | custom-call | bytes 2196480 | tf_op jit(solution)/shard_map/forward/pallas_call | solution.py:297
  17.1 1.2 %collective-permute-done.9 = f32[32,256]{1,0:T(8,128)S(1)} collective-permute-done((f32[32,256]{1,0:T(8,128)S(1)}, f32[32,256]{1,0:T(8,128)S(1)}, u32[]{:S(2)}, u32[]{:S(2)}) %collective-permute-start.9) | collective-permute-done | bytes 32800 | tf_op jit(solution)/shard_map/ppermute | solution.py:325
  18.3 1.4 %collective-permute-start.11 = (f32[32,256]{1,0:T(8,128)S(1)}, f32[32,256]{1,0:T(8,128)S(1)}, u32[]{:S(2)}, u32[]{:S(2)}) collective-permute-start(f32[32,256]{1,0:T(8,128)S(1)} %add.12), channel_id=1, source_target_pairs={{0,2},{1,3},{2,0},{3,1},{4,6},{5,7},{6,4},{7,5},{8,10},{9,11},{10,... | collective-permute-start | bytes 98312 | tf_op jit(solution)/shard_map/ppermute | solution.py:325
  19.7 2.9 %collective-permute-start.10 = (bf16[1,32,512]{2,1,0:T(8,128)(2,1)S(1)}, bf16[1,32,512]{2,1,0:T(8,128)(2,1)S(1)}, u32[]{:S(2)}, u32[]{:S(2)}) collective-permute-start(bf16[1,32,512]{2,1,0:T(8,128)(2,1)S(1)} %bitcast.10), channel_id=1, source_target_pairs={{0,8},{1,9},{2,10},{3,11},{4,12},{5,13},{6,14},{7,15},{8,0},{9,1},... | collective-permute-start | bytes 98312 | tf_op jit(solution)/shard_map/ppermute | solution.py:325
  22.6 1.4 %collective-permute-start.13 = (f32[32,256]{1,0:T(8,128)S(1)}, f32[32,256]{1,0:T(8,128)S(1)}, u32[]{:S(2)}, u32[]{:S(2)}) collective-permute-start(f32[32,256]{1,0:T(8,128)S(1)} %add.13), channel_id=1, source_target_pairs={{0,4},{1,5},{2,6},{3,7},{4,0},{5,1},{6,2},{7,3},{8,12},{9,13},{10,... | collective-permute-start | bytes 98312 | tf_op jit(solution)/shard_map/ppermute | solution.py:325
  24.7 1.9 %collective-permute-done.13 = f32[32,256]{1,0:T(8,128)S(1)} collective-permute-done((f32[32,256]{1,0:T(8,128)S(1)}, f32[32,256]{1,0:T(8,128)S(1)}, u32[]{:S(2)}, u32[]{:S(2)}) %collective-permute-start.13) | collective-permute-done | bytes 32800 | tf_op jit(solution)/shard_map/ppermute | solution.py:325
  26.6 2.4 %collective-permute-start.14 = (f32[32,256]{1,0:T(8,128)S(1)}, f32[32,256]{1,0:T(8,128)S(1)}, u32[]{:S(2)}, u32[]{:S(2)}) collective-permute-start(f32[32,256]{1,0:T(8,128)S(1)} %add.14.refs_0_), channel_id=1, source_target_pairs={{0,8},{1,9},{2,10},{3,11},{4,12},{5,13},{6,14},{7,15},{8,0},{9,1},... | collective-permute-start | bytes 98312 | tf_op jit(solution)/shard_map/ppermute | solution.py:325
  29.5 2.5 %inverse.1.inverse_ref = f32[32,32]{1,0:T(8,128)S(1)} custom-call(bf16[4,32,512]{2,1,0:T(8,128)(2,1)S(1)} %constant_dynamic-update-slice_fusion.small_ref), custom_call_target="tpu_custom_call" | custom-call | bytes 135168 | tf_op jit(solution)/shard_map/inverse/pallas_call | solution.py:297
  32.0 1.4 %solve.1.refs_0_ = f32[64,256]{1,0:T(8,128)S(1)} custom-call(f32[32,32]{1,0:T(8,128)S(1)} %inverse.1.inverse_ref, bf16[32,2048]{1,0:T(8,128)(2,1)S(1)} %get-tuple-element.41.design_ref, bf16[2048,128]{1,0:T(8,128)(2,1)S(1)} %get-tuple-element.38.rows_ref, f32[1,512]{1,0:T(1,128)S(1)} %get-tuple-element.39.thresh_ref, ...), custom_call_target="tpu_custom_call" | custom-call | bytes 794624 | tf_op jit(solution)/shard_map/solve/pallas_call | solution.py:297
  33.5 0.9 %slope.1.slope_ref = f32[512,512]{1,0:T(8,128)S(1)} custom-call(bf16[128,512]{1,0:T(8,128)(2,1)S(1)} %get-tuple-element.30.refs_0_.refs_2_, bf16[128,512]{1,0:T(8,128)(2,1)S(1)} %collective-permute-done.refs_1_.refs_3_, bf16[128,512]{1,0:T(8,128)(2,1)S(1)} %collective-permute-done.1.refs_2_.refs_4_, ...), custom_call_target="tpu_custom_call" | custom-call | bytes 2098176 | tf_op jit(solution)/shard_map/slope/pallas_call | solution.py:297
  34.8 1.4 %backward.1 = (bf16[128,512]{1,0:T(8,128)(2,1)S(1)}, bf16[128,512]{1,0:T(8,128)(2,1)S(1)}, bf16[128,512]{1,0:T(8,128)(2,1)S(1)}, bf16[128,512]{1,0:T(8,128)(2,1)...) custom-call(bf16[512,512]{1,0:T(8,128)(2,1)S(1)} %get-tuple-element., ...), custom_call_target="tpu_custom_call" | custom-call | bytes 4849664 | tf_op jit(solution)/shard_map/backward/pallas_call | solution.py:297
  37.1 2.2 %collective-permute-start.19 = (bf16[128,512]{1,0:T(8,128)(2,1)S(1)}, bf16[128,512]{1,0:T(8,128)(2,1)S(1)}, u32[]{:S(2)}, u32[]{:S(2)}) collective-permute-start(bf16[128,512]{1,0:T(8,128)(2,1)S(1)} %get-tuple-element.50), channel_id=1, source_target_pairs={{0,6},{1,7},{2,4},{3,5},{4,2},{5,3},{6,0},{7,1},{8,14},{9,15},{10,... | collective-permute-start | bytes 393224 | tf_op jit(solution)/shard_map/ppermute | solution.py:325
  39.3 1.8 %collective-permute-start.21 = (bf16[128,512]{1,0:T(8,128)(2,1)S(1)}, bf16[128,512]{1,0:T(8,128)(2,1)S(1)}, u32[]{:S(2)}, u32[]{:S(2)}) collective-permute-start(bf16[128,512]{1,0:T(8,128)(2,1)S(1)} %add_convert_fusion), channel_id=1, source_target_pairs={{0,8},{1,9},{2,10},{3,11},{4,12},{5,13},{6,14},{7,15},{8,0},{9,1},... | collective-permute-start | bytes 393224 | tf_op jit(solution)/shard_map/ppermute | solution.py:325
  41.7 3.2 %loss.1 = (f32[8,128]{1,0:T(8,128)S(1)}, f32[128,128]{1,0:T(8,128)S(1)}) custom-call(bf16[2048,128]{1,0:T(8,128)(2,1)S(1)} %get-tuple-element.38.rows_ref, f32[1,512]{1,0:T(1,128)S(1)} %get-tuple-element.39.thresh_ref, f32[1,512]{1,0:T(1,128)S(1)} %get-tuple-element.40.rate_ref, f32[64,256]{1,0:T(8,128)S(1)} %solve.1.refs_0_, ...), custom_call_target="tpu_custom_call" | custom-call | bytes 729088 | tf_op jit(solution)/shard_map/loss/pallas_call | solution.py:297
  45.4 3.4 %collective-permute-done.19.refs_3_ = bf16[128,512]{1,0:T(8,128)(2,1)S(1)} collective-permute-done((bf16[128,512]{1,0:T(8,128)(2,1)S(1)}, bf16[128,512]{1,0:T(8,128)(2,1)S(1)}, u32[]{:S(2)}, u32[]{:S(2)}) %collective-permute-start.19) | collective-permute-done | bytes 131104 | tf_op jit(solution)/shard_map/ppermute | solution.py:325
  48.8 0.9 %collective-permute-done.17.refs_1_ = bf16[128,512]{1,0:T(8,128)(2,1)S(1)} collective-permute-done((bf16[128,512]{1,0:T(8,128)(2,1)S(1)}, bf16[128,512]{1,0:T(8,128)(2,1)S(1)}, u32[]{:S(2)}, u32[]{:S(2)}) %collective-permute-start.17) | collective-permute-done | bytes 131104 | tf_op jit(solution)/shard_map/ppermute | solution.py:325
  49.7 0.9 %sums.1 = (f32[128,512]{1,0:T(8,128)}, f32[128,512]{1,0:T(8,128)}) custom-call(f32[128,128]{1,0:T(8,128)S(1)} %get-tuple-element.43.own_ref, bf16[128,512]{1,0:T(8,128)(2,1)S(1)} %get-tuple-element.45.refs_0_, bf16[128,512]{1,0:T(8,128)(2,1)S(1)} %collective-permute-done.17.refs_1_, bf16[128,512]{1,0:T(8,128)(2,1)S(1)} %collective-permute-done.18.refs_2_, ...), custom_call_target="tpu_custom_call" | custom-call | bytes 1507328 | tf_op jit(solution)/shard_map/sums/pallas_call | solution.py:297
  (52 shorter events, 6.6 us)
Async XLA Ops:
  0.6 7.7 %copy-start.2 = (s32[2048]{0:T(1024)S(1)}, s32[2048]{0:T(1024)}, u32[]{:S(2)}) copy-start(s32[2048]{0:T(1024)} %param.10) | copy-start | bytes 24580
  0.6 12.8 %collective-permute-start.3 = (bf16[128,512]{1,0:T(8,128)(2,1)}, bf16[128,512]{1,0:T(8,128)(2,1)S(1)}, u32[]{:S(2)}, u32[]{:S(2)}) collective-permute-start(bf16[128,512]{1,0:T(8,128)(2,1)} %w_ref.1), channel_id=1, source_target_pairs={{0,8},{1,9},{2,10},{3,11},{4,12},{5,13},{6,14},{7,15},{8,0},{9,1},... | collective-permute-start | bytes 393224 | tf_op jit(solution)/shard_map/ppermute | solution.py:325
  4.7 9.3 %collective-permute-start = (bf16[128,512]{1,0:T(8,128)(2,1)}, bf16[128,512]{1,0:T(8,128)(2,1)S(1)}, u32[]{:S(2)}, u32[]{:S(2)}) collective-permute-start(bf16[128,512]{1,0:T(8,128)(2,1)} %x_ref.1), channel_id=1, source_target_pairs={{0,2},{1,3},{2,0},{3,1},{4,6},{5,7},{6,4},{7,5},{8,10},{9,11},{10,... | collective-permute-start | bytes 393224 | tf_op jit(solution)/shard_map/ppermute | solution.py:325
  6.3 7.8 %collective-permute-start.1 = (bf16[128,512]{1,0:T(8,128)(2,1)}, bf16[128,512]{1,0:T(8,128)(2,1)S(1)}, u32[]{:S(2)}, u32[]{:S(2)}) collective-permute-start(bf16[128,512]{1,0:T(8,128)(2,1)} %x_ref.1), channel_id=1, source_target_pairs={{0,4},{1,5},{2,6},{3,7},{4,0},{5,1},{6,2},{7,3},{8,12},{9,13},{10,... | collective-permute-start | bytes 393224 | tf_op jit(solution)/shard_map/ppermute | solution.py:325
  7.8 7.8 %collective-permute-start.2 = (bf16[128,512]{1,0:T(8,128)(2,1)}, bf16[128,512]{1,0:T(8,128)(2,1)S(1)}, u32[]{:S(2)}, u32[]{:S(2)}) collective-permute-start(bf16[128,512]{1,0:T(8,128)(2,1)} %x_ref.1), channel_id=1, source_target_pairs={{0,6},{1,7},{2,4},{3,5},{4,2},{5,3},{6,0},{7,1},{8,14},{9,15},{10,... | collective-permute-start | bytes 393224 | tf_op jit(solution)/shard_map/ppermute | solution.py:325
  8.2 5.2 %collective-permute-start.6 = (bf16[128]{0:T(256)(128)(2,1)}, bf16[128]{0:T(256)(128)(2,1)S(1)}, u32[]{:S(2)}, u32[]{:S(2)}) collective-permute-start(bf16[128]{0:T(256)(128)(2,1)} %param.9), channel_id=1, source_target_pairs={{0,8},{1,9},{2,10},{3,11},{4,12},{5,13},{6,14},{7,15},{8,0},{9,1},... | collective-permute-start | bytes 776 | tf_op jit(solution)/shard_map/ppermute | solution.py:325
  11.5 2.5 %copy-start.5 = (bf16[128]{0:T(256)(128)(2,1)S(1)}, bf16[128]{0:T(256)(128)(2,1)}, u32[]{:S(2)}) copy-start(bf16[128]{0:T(256)(128)(2,1)} %param.9) | copy-start | bytes 772
  13.5 2.3 %collective-permute-start.4 = (bf16[128,512]{1,0:T(8,128)(2,1)S(1)}, bf16[128,512]{1,0:T(8,128)(2,1)S(1)}, u32[]{:S(2)}, u32[]{:S(2)}) collective-permute-start(bf16[128,512]{1,0:T(8,128)(2,1)S(1)} %copy-done.1), channel_id=1, source_target_pairs={{0,1},{1,0},{2,3},{3,2},{4,5},{5,4},{6,7},{7,6},{8,9},{9,8},{10,11... | collective-permute-start | bytes 393224 | tf_op jit(solution)/shard_map/ppermute | solution.py:325
  13.5 2.3 %collective-permute-start.5 = (bf16[128,512]{1,0:T(8,128)(2,1)S(1)}, bf16[128,512]{1,0:T(8,128)(2,1)S(1)}, u32[]{:S(2)}, u32[]{:S(2)}) collective-permute-start(bf16[128,512]{1,0:T(8,128)(2,1)S(1)} %collective-permute-done.3.refs_5_.refs_7_), channel_id=1, source_target_pairs={{0,1},{1,0},{2,3},{3,2},{4,5},{5,4},{6,7},{7,6},{8,9},{9,8},{10,11... | collective-permute-start | bytes 393224 | tf_op jit(solution)/shard_map/ppermute | solution.py:325
  14.0 1.8 %collective-permute-start.7 = (bf16[128]{0:T(256)(128)(2,1)S(1)}, bf16[128]{0:T(256)(128)(2,1)S(1)}, u32[]{:S(2)}, u32[]{:S(2)}) collective-permute-start(bf16[128]{0:T(256)(128)(2,1)S(1)} %copy-done.5), channel_id=1, source_target_pairs={{0,1},{1,0},{2,3},{3,2},{4,5},{5,4},{6,7},{7,6},{8,9},{9,8},{10,11... | collective-permute-start | bytes 776 | tf_op jit(solution)/shard_map/ppermute | solution.py:325
  14.1 1.7 %collective-permute-start.8 = (bf16[128]{0:T(256)(128)(2,1)S(1)}, bf16[128]{0:T(256)(128)(2,1)S(1)}, u32[]{:S(2)}, u32[]{:S(2)}) collective-permute-start(bf16[128]{0:T(256)(128)(2,1)S(1)} %collective-permute-done.6), channel_id=1, source_target_pairs={{0,1},{1,0},{2,3},{3,2},{4,5},{5,4},{6,7},{7,6},{8,9},{9,8},{10,11... | collective-permute-start | bytes 776 | tf_op jit(solution)/shard_map/ppermute | solution.py:325
  17.1 1.3 %collective-permute-start.9 = (f32[32,256]{1,0:T(8,128)S(1)}, f32[32,256]{1,0:T(8,128)S(1)}, u32[]{:S(2)}, u32[]{:S(2)}) collective-permute-start(f32[32,256]{1,0:T(8,128)S(1)} %get-tuple-element.35), channel_id=1, source_target_pairs={{0,1},{1,0},{2,3},{3,2},{4,5},{5,4},{6,7},{7,6},{8,9},{9,8},{10,11... | collective-permute-start | bytes 98312 | tf_op jit(solution)/shard_map/ppermute | solution.py:325
  18.3 4.3 %collective-permute-start.11 = (f32[32,256]{1,0:T(8,128)S(1)}, f32[32,256]{1,0:T(8,128)S(1)}, u32[]{:S(2)}, u32[]{:S(2)}) collective-permute-start(f32[32,256]{1,0:T(8,128)S(1)} %add.12), channel_id=1, source_target_pairs={{0,2},{1,3},{2,0},{3,1},{4,6},{5,7},{6,4},{7,5},{8,10},{9,11},{10,... | collective-permute-start | bytes 98312 | tf_op jit(solution)/shard_map/ppermute | solution.py:325
  19.7 4.8 %collective-permute-start.10 = (bf16[1,32,512]{2,1,0:T(8,128)(2,1)S(1)}, bf16[1,32,512]{2,1,0:T(8,128)(2,1)S(1)}, u32[]{:S(2)}, u32[]{:S(2)}) collective-permute-start(bf16[1,32,512]{2,1,0:T(8,128)(2,1)S(1)} %bitcast.10), channel_id=1, source_target_pairs={{0,8},{1,9},{2,10},{3,11},{4,12},{5,13},{6,14},{7,15},{8,0},{9,1},... | collective-permute-start | bytes 98312 | tf_op jit(solution)/shard_map/ppermute | solution.py:325
  22.6 4.0 %collective-permute-start.13 = (f32[32,256]{1,0:T(8,128)S(1)}, f32[32,256]{1,0:T(8,128)S(1)}, u32[]{:S(2)}, u32[]{:S(2)}) collective-permute-start(f32[32,256]{1,0:T(8,128)S(1)} %add.13), channel_id=1, source_target_pairs={{0,4},{1,5},{2,6},{3,7},{4,0},{5,1},{6,2},{7,3},{8,12},{9,13},{10,... | collective-permute-start | bytes 98312 | tf_op jit(solution)/shard_map/ppermute | solution.py:325
  24.6 4.4 %collective-permute-start.12 = (bf16[2,32,512]{2,1,0:T(8,128)(2,1)S(1)}, bf16[2,32,512]{2,1,0:T(8,128)(2,1)S(1)}, u32[]{:S(2)}, u32[]{:S(2)}) collective-permute-start(bf16[2,32,512]{2,1,0:T(8,128)(2,1)S(1)} %pad_maximum_fusion), channel_id=1, source_target_pairs={{0,1},{1,0},{2,3},{3,2},{4,5},{5,4},{6,7},{7,6},{8,9},{9,8},{10,11... | collective-permute-start | bytes 196616 | tf_op jit(solution)/shard_map/ppermute | solution.py:325
  26.6 5.4 %collective-permute-start.14 = (f32[32,256]{1,0:T(8,128)S(1)}, f32[32,256]{1,0:T(8,128)S(1)}, u32[]{:S(2)}, u32[]{:S(2)}) collective-permute-start(f32[32,256]{1,0:T(8,128)S(1)} %add.14.refs_0_), channel_id=1, source_target_pairs={{0,8},{1,9},{2,10},{3,11},{4,12},{5,13},{6,14},{7,15},{8,0},{9,1},... | collective-permute-start | bytes 98312 | tf_op jit(solution)/shard_map/ppermute | solution.py:325
  33.4 1.3 %collective-permute-start.15 = (f32[64,256]{1,0:T(8,128)S(1)}, f32[64,256]{1,0:T(8,128)S(1)}, u32[]{:S(2)}, u32[]{:S(2)}) collective-permute-start(f32[64,256]{1,0:T(8,128)S(1)} %solve.1.refs_0_), channel_id=1, source_target_pairs={{0,1},{1,0},{2,3},{3,2},{4,5},{5,4},{6,7},{7,6},{8,9},{9,8},{10,11... | collective-permute-start | bytes 196616 | tf_op jit(solution)/shard_map/ppermute | solution.py:325
  36.1 3.2 %collective-permute-start.16 = (bf16[128,512]{1,0:T(8,128)(2,1)S(1)}, bf16[128,512]{1,0:T(8,128)(2,1)S(1)}, u32[]{:S(2)}, u32[]{:S(2)}) collective-permute-start(bf16[128,512]{1,0:T(8,128)(2,1)S(1)} %get-tuple-element.47), channel_id=1, source_target_pairs={{0,1},{1,0},{2,3},{3,2},{4,5},{5,4},{6,7},{7,6},{8,9},{9,8},{10,11... | collective-permute-start | bytes 393224 | tf_op jit(solution)/shard_map/ppermute | solution.py:325
  36.4 9.0 %collective-permute-start.18 = (bf16[128,512]{1,0:T(8,128)(2,1)S(1)}, bf16[128,512]{1,0:T(8,128)(2,1)S(1)}, u32[]{:S(2)}, u32[]{:S(2)}) collective-permute-start(bf16[128,512]{1,0:T(8,128)(2,1)S(1)} %get-tuple-element.49), channel_id=1, source_target_pairs={{0,4},{1,5},{2,6},{3,7},{4,0},{5,1},{6,2},{7,3},{8,12},{9,13},{10,... | collective-permute-start | bytes 393224 | tf_op jit(solution)/shard_map/ppermute | solution.py:325
  37.1 11.7 %collective-permute-start.19 = (bf16[128,512]{1,0:T(8,128)(2,1)S(1)}, bf16[128,512]{1,0:T(8,128)(2,1)S(1)}, u32[]{:S(2)}, u32[]{:S(2)}) collective-permute-start(bf16[128,512]{1,0:T(8,128)(2,1)S(1)} %get-tuple-element.50), channel_id=1, source_target_pairs={{0,6},{1,7},{2,4},{3,5},{4,2},{5,3},{6,0},{7,1},{8,14},{9,15},{10,... | collective-permute-start | bytes 393224 | tf_op jit(solution)/shard_map/ppermute | solution.py:325
  39.3 9.4 %collective-permute-start.21 = (bf16[128,512]{1,0:T(8,128)(2,1)S(1)}, bf16[128,512]{1,0:T(8,128)(2,1)S(1)}, u32[]{:S(2)}, u32[]{:S(2)}) collective-permute-start(bf16[128,512]{1,0:T(8,128)(2,1)S(1)} %add_convert_fusion), channel_id=1, source_target_pairs={{0,8},{1,9},{2,10},{3,11},{4,12},{5,13},{6,14},{7,15},{8,0},{9,1},... | collective-permute-start | bytes 393224 | tf_op jit(solution)/shard_map/ppermute | solution.py:325
  41.1 7.6 %collective-permute-start.20 = (bf16[128,512]{1,0:T(8,128)(2,1)S(1)}, bf16[128,512]{1,0:T(8,128)(2,1)S(1)}, u32[]{:S(2)}, u32[]{:S(2)}) collective-permute-start(bf16[128,512]{1,0:T(8,128)(2,1)S(1)} %get-tuple-element.53), channel_id=1, source_target_pairs={{0,1},{1,0},{2,3},{3,2},{4,5},{5,4},{6,7},{7,6},{8,9},{9,8},{10,11... | collective-permute-start | bytes 393224 | tf_op jit(solution)/shard_map/ppermute | solution.py:325
  41.2 8.6 %collective-permute-start.17 = (bf16[128,512]{1,0:T(8,128)(2,1)S(1)}, bf16[128,512]{1,0:T(8,128)(2,1)S(1)}, u32[]{:S(2)}, u32[]{:S(2)}) collective-permute-start(bf16[128,512]{1,0:T(8,128)(2,1)S(1)} %get-tuple-element.48), channel_id=1, source_target_pairs={{0,2},{1,3},{2,0},{3,1},{4,6},{5,7},{6,4},{7,5},{8,10},{9,11},{10,... | collective-permute-start | bytes 393224 | tf_op jit(solution)/shard_map/ppermute | solution.py:325
  (5 other events, 3.9 us)

commit v4 on v3

--- a/solution.py
+++ b/solution.py
@@ -84,18 +84,29 @@
     def one_row(block, k):
         return jnp.broadcast_to(block[k : k + 1], shape)
 
-    for k in range(0, size, 2):
-        left = [jnp.broadcast_to(block[:, k : k + 1], shape) for block in blocks]
-        right = [jnp.broadcast_to(block[:, k + 1 : k + 2], shape) for block in blocks]
+    for k in range(0, size, 4):
         at, here = k // SUBLANES, k % SUBLANES
-        a, b = one_row(left[at], here), one_row(right[at], here)
-        c, d = one_row(left[at], here + 1), one_row(right[at], here + 1)
-        upper, lower = one_row(blocks[at], here), one_row(blocks[at], here + 1)
-        scale = 1.0 / (a * d - b * c)
-        upper, lower = (d * upper - b * lower) * scale, (a * lower - c * upper) * scale
-        blocks = [w - x * upper - y * lower for w, x, y in zip(blocks, left, right)]
-        kept = jnp.where(row == here + 1, lower, blocks[at])
-        blocks[at] = jnp.where(row == here, upper, kept)
+        columns = [
+            [jnp.broadcast_to(block[:, k + j : k + j + 1], shape) for block in blocks]
+            for j in range(4)
+        ]
+        p = [[one_row(columns[j][at], here + i) for j in range(4)] for i in range(4)]
+        r = [one_row(blocks[at], here + i) for i in range(4)]
+        for i in range(4):
+            scale = 1.0 / p[i][i]
+            r[i] = r[i] * scale
+            p[i] = [entry * scale for entry in p[i]]
+            for m in range(4):
+                if m != i:
+                    r[m] = r[m] - p[m][i] * r[i]
+                    p[m] = [x - p[m][i] * y if j > i else x for j, (x, y) in enumerate(zip(p[m], p[i]))]
+        for i, block in enumerate(blocks):
+            for j in range(4):
+                block = block - columns[j][i] * r[j]
+            if i == at:
+                for j in range(4):
+                    block = jnp.where(row == here + j, r[j], block)
+            blocks[i] = block
     return jnp.concatenate(blocks, axis=0)[:, size:]
 
 
@@ -205,7 +216,9 @@
 
     def seeds(here):
         power = jnp.exp2(jnp.minimum(dot(rows_ref[here], turn_ref[...]), 126.0))
-        seed = (1.0 / (1.0 + power)).astype(BF16)
+        below = 1.0 + power
+        seed = pl.reciprocal(below, approx=True)
+        seed = (seed * (2.0 - below * seed)).astype(BF16)
         total_ref[...] += dot(design_ref[:, here], seed)
 
     each_chunk(rows_ref.shape[0], seeds)
@@ -375,14 +388,13 @@
     )
     moment = moments[0] + swap(moments[1], SHARES - 1)
     small = after(lead, moment)[None]
-    steps = inner_bits + outer_bits[-2:0:-1]
-    for k in range(max(len(steps), outer_bits.index(0) + 1)):
-        if k < len(outer_bits):
-            if k > 0:
-                small = after(small, moment)
-            small = jnp.concatenate([small, swap(small, 1 << outer_bits[k])], axis=0)
-        if k < len(steps):
-            moment = moment + swap(moment, 1 << steps[k])
+    small = jnp.concatenate([small, swap(small, 1 << first_bit)], axis=0)
+    moment = sum(direct([moment] * inner, inner_bits), moment)
+    for bit in outer_bits[1:]:
+        small = after(small, moment)
+        small = jnp.concatenate([small, swap(small, 1 << bit)], axis=0)
+    for bit in outer_bits[-2:0:-1]:
+        moment = moment + swap(moment, 1 << bit)
     moments = [moment, swap(moment, 1 << first_bit)]
     (inverse,) = call(
         partial(inverse_kernel, RIDGE_SCALE * paths_all),

time: 50.8 us -> 50 us (0.984)
  Pallas kernels: 12.8 us -> 12 us
    pallas_call x10, Pallas kernels: 12.8 us -> 12 us  [call(): pl.pallas_call(kernel, out_shape=[jax.ShapeDtypeStruct(s, d) for s, d in...]
    ppermute x22 -> x23, starting transfers between devices: 22.4 us -> 22 us  [swap(): return lax.ppermute(x, 'paths', [(d, d ^ mask) for d in range(n)])]
    ppermute x22 -> x23, waiting for transfers between devices: 11.5 us -> 11.9 us  [swap(): return lax.ppermute(x, 'paths', [(d, d ^ mask) for d in range(n)])]
  transfers between devices with their start and end apart: 22 -> 23, of which waited for: 8 -> 9; matrix products, arithmetic and copies ran while one was open for 1% -> 1% of each run, Pallas kernels for 16% -> 14%
where the time goes in v4:
time: 50 us; the launch traced here: 49.8 us
  starting transfers between devices  22 us (44%)
  Pallas kernels  12 us (24%)
  waiting for transfers between devices  11.9 us (24%)
  local copies, waits for them, and re-layouts  3.04 us (6%)
  between operations  0.78 us (2%)
    ppermute x23, starting transfers between devices, swap(): return lax.ppermute(x, 'paths', [(d, d ^ mask) for d in range(n)])  22 us
    pallas_call x10, Pallas kernels, call(): pl.pallas_call(kernel, out_shape=[jax.ShapeDtypeStruct(s, d) for s, d in...  12 us
    ppermute x23, waiting for transfers between devices, swap(): return lax.ppermute(x, 'paths', [(d, d ^ mask) for d in range(n)])  11.9 us
    unnamed x15, local copies, waits for them, and re-layouts  2.52 us
  transfers between devices with their start and end apart: 23, of which 9 were waited for; matrix products, arithmetic and copies ran while one was open for 1% of the time, Pallas kernels for 14%

profile of v4, /device:TPU:0, one launch (start us, length us, event | category | flops | bytes accessed | tf_op | source)
XLA Modules:
  0.0 49.8 jit_solution(2479044745844975012)
XLA Ops:
  0.6 4.1 %collective-permute-start.3 = (bf16[128,512]{1,0:T(8,128)(2,1)}, bf16[128,512]{1,0:T(8,128)(2,1)S(1)}, u32[]{:S(2)}, u32[]{:S(2)}) collective-permute-start(bf16[128,512]{1,0:T(8,128)(2,1)} %w_ref.1), channel_id=1, source_target_pairs={{0,8},{1,9},{2,10},{3,11},{4,12},{5,13},{6,14},{7,15},{8,0},{9,1},... | collective-permute-start | bytes 393224 | tf_op jit(solution)/shard_map/ppermute | solution.py:338
  4.7 1.5 %collective-permute-start = (bf16[128,512]{1,0:T(8,128)(2,1)}, bf16[128,512]{1,0:T(8,128)(2,1)S(1)}, u32[]{:S(2)}, u32[]{:S(2)}) collective-permute-start(bf16[128,512]{1,0:T(8,128)(2,1)} %x_ref.1), channel_id=1, source_target_pairs={{0,2},{1,3},{2,0},{3,1},{4,6},{5,7},{6,4},{7,5},{8,10},{9,11},{10,... | collective-permute-start | bytes 393224 | tf_op jit(solution)/shard_map/ppermute | solution.py:338
  6.3 1.6 %collective-permute-start.1 = (bf16[128,512]{1,0:T(8,128)(2,1)}, bf16[128,512]{1,0:T(8,128)(2,1)S(1)}, u32[]{:S(2)}, u32[]{:S(2)}) collective-permute-start(bf16[128,512]{1,0:T(8,128)(2,1)} %x_ref.1), channel_id=1, source_target_pairs={{0,4},{1,5},{2,6},{3,7},{4,0},{5,1},{6,2},{7,3},{8,12},{9,13},{10,... | collective-permute-start | bytes 393224 | tf_op jit(solution)/shard_map/ppermute | solution.py:338
  9.0 0.9 %copy-done = bf16[128,512]{1,0:T(8,128)(2,1)S(1)} copy-done((bf16[128,512]{1,0:T(8,128)(2,1)S(1)}, bf16[128,512]{1,0:T(8,128)(2,1)}, u32[]{:S(2)}) %copy-start) | copy-done | bytes 131096
  9.9 0.9 %copy-done.1 = bf16[128,512]{1,0:T(8,128)(2,1)S(1)} copy-done((bf16[128,512]{1,0:T(8,128)(2,1)S(1)}, bf16[128,512]{1,0:T(8,128)(2,1)}, u32[]{:S(2)}) %copy-start.1) | copy-done | bytes 131096
  11.5 2.0 %collective-permute-done.6 = bf16[128]{0:T(256)(128)(2,1)S(1)} collective-permute-done((bf16[128]{0:T(256)(128)(2,1)}, bf16[128]{0:T(256)(128)(2,1)S(1)}, u32[]{:S(2)}, u32[]{:S(2)}) %collective-permute-start.6) | collective-permute-done | bytes 288 | tf_op jit(solution)/shard_map/ppermute | solution.py:338
  14.5 1.2 %collective-permute-done.2.refs_3_.refs_5_ = bf16[128,512]{1,0:T(8,128)(2,1)S(1)} collective-permute-done((bf16[128,512]{1,0:T(8,128)(2,1)}, bf16[128,512]{1,0:T(8,128)(2,1)S(1)}, u32[]{:S(2)}, u32[]{:S(2)}) %collective-permute-start.2) | collective-permute-done | bytes 131104 | tf_op jit(solution)/shard_map/ppermute | solution.py:338
  15.8 1.3 %forward.1 = (bf16[512,512]{1,0:T(8,128)(2,1)S(1)}, f32[32,256]{1,0:T(8,128)S(1)}, f32[32,256]{1,0:T(8,128)S(1)}) custom-call(bf16[128,512]{1,0:T(8,128)(2,1)S(1)} %get-tuple-element.30.refs_0_.refs_2_, bf16[128,512]{1,0:T(8,128)(2,1)S(1)} %collective-permute-done.refs_1_.refs_3_, bf16[128,512]{1,0:T(8,128)(2,1)S(1)} %collective-permute-done.1.refs_2_.refs_4_, ...), custom_call_target="tpu_custom_call" | custom-call | bytes 2196480 | tf_op jit(solution)/shard_map/forward/pallas_call | solution.py:310
  17.1 1.2 %collective-permute-done.9 = f32[32,256]{1,0:T(8,128)S(1)} collective-permute-done((f32[32,256]{1,0:T(8,128)S(1)}, f32[32,256]{1,0:T(8,128)S(1)}, u32[]{:S(2)}, u32[]{:S(2)}) %collective-permute-start.9) | collective-permute-done | bytes 32800 | tf_op jit(solution)/shard_map/ppermute | solution.py:338
  18.3 1.4 %collective-permute-start.11 = (f32[32,256]{1,0:T(8,128)S(1)}, f32[32,256]{1,0:T(8,128)S(1)}, u32[]{:S(2)}, u32[]{:S(2)}) collective-permute-start(f32[32,256]{1,0:T(8,128)S(1)} %add.15), channel_id=1, source_target_pairs={{0,2},{1,3},{2,0},{3,1},{4,6},{5,7},{6,4},{7,5},{8,10},{9,11},{10,... | collective-permute-start | bytes 98312 | tf_op jit(solution)/shard_map/ppermute | solution.py:338
  19.7 1.9 %collective-permute-start.12 = (f32[32,256]{1,0:T(8,128)S(1)}, f32[32,256]{1,0:T(8,128)S(1)}, u32[]{:S(2)}, u32[]{:S(2)}) collective-permute-start(f32[32,256]{1,0:T(8,128)S(1)} %add.15), channel_id=1, source_target_pairs={{0,4},{1,5},{2,6},{3,7},{4,0},{5,1},{6,2},{7,3},{8,12},{9,13},{10,... | collective-permute-start | bytes 98312 | tf_op jit(solution)/shard_map/ppermute | solution.py:338
  21.8 2.8 %collective-permute-start.10 = (bf16[1,32,512]{2,1,0:T(8,128)(2,1)S(1)}, bf16[1,32,512]{2,1,0:T(8,128)(2,1)S(1)}, u32[]{:S(2)}, u32[]{:S(2)}) collective-permute-start(bf16[1,32,512]{2,1,0:T(8,128)(2,1)S(1)} %bitcast.10), channel_id=1, source_target_pairs={{0,8},{1,9},{2,10},{3,11},{4,12},{5,13},{6,14},{7,15},{8,0},{9,1},... | collective-permute-start | bytes 98312 | tf_op jit(solution)/shard_map/ppermute | solution.py:338
  24.6 1.9 %collective-permute-done.13 = f32[32,256]{1,0:T(8,128)S(1)} collective-permute-done((f32[32,256]{1,0:T(8,128)S(1)}, f32[32,256]{1,0:T(8,128)S(1)}, u32[]{:S(2)}, u32[]{:S(2)}) %collective-permute-start.13) | collective-permute-done | bytes 32800 | tf_op jit(solution)/shard_map/ppermute | solution.py:338
  26.6 1.2 %collective-permute-start.15 = (f32[32,256]{1,0:T(8,128)S(1)}, f32[32,256]{1,0:T(8,128)S(1)}, u32[]{:S(2)}, u32[]{:S(2)}) collective-permute-start(f32[32,256]{1,0:T(8,128)S(1)} %add_add_fusion.refs_0_), channel_id=1, source_target_pairs={{0,8},{1,9},{2,10},{3,11},{4,12},{5,13},{6,14},{7,15},{8,0},{9,1},... | collective-permute-start | bytes 98312 | tf_op jit(solution)/shard_map/ppermute | solution.py:338
  27.9 1.2 %collective-permute-done.14 = bf16[2,32,512]{2,1,0:T(8,128)(2,1)S(1)} collective-permute-done((bf16[2,32,512]{2,1,0:T(8,128)(2,1)S(1)}, bf16[2,32,512]{2,1,0:T(8,128)(2,1)S(1)}, u32[]{:S(2)}, u32[]{:S(2)}) %collective-permute-start.14) | collective-permute-done | bytes 65568 | tf_op jit(solution)/shard_map/ppermute | solution.py:338
  29.7 1.8 %inverse.1.inverse_ref = f32[32,32]{1,0:T(8,128)S(1)} custom-call(bf16[4,32,512]{2,1,0:T(8,128)(2,1)S(1)} %constant_dynamic-update-slice_fusion.small_ref), custom_call_target="tpu_custom_call" | custom-call | bytes 135168 | tf_op jit(solution)/shard_map/inverse/pallas_call | solution.py:310
  31.4 1.4 %solve.1.refs_0_ = f32[64,256]{1,0:T(8,128)S(1)} custom-call(f32[32,32]{1,0:T(8,128)S(1)} %inverse.1.inverse_ref, bf16[32,2048]{1,0:T(8,128)(2,1)S(1)} %get-tuple-element.41.design_ref, bf16[2048,128]{1,0:T(8,128)(2,1)S(1)} %get-tuple-element.38.rows_ref, f32[1,512]{1,0:T(1,128)S(1)} %get-tuple-element.39.thresh_ref, ...), custom_call_target="tpu_custom_call" | custom-call | bytes 794624 | tf_op jit(solution)/shard_map/solve/pallas_call | solution.py:310
  33.1 0.9 %slope.1.slope_ref = f32[512,512]{1,0:T(8,128)S(1)} custom-call(bf16[128,512]{1,0:T(8,128)(2,1)S(1)} %get-tuple-element.30.refs_0_.refs_2_, bf16[128,512]{1,0:T(8,128)(2,1)S(1)} %collective-permute-done.refs_1_.refs_3_, bf16[128,512]{1,0:T(8,128)(2,1)S(1)} %collective-permute-done.1.refs_2_.refs_4_, ...), custom_call_target="tpu_custom_call" | custom-call | bytes 2098176 | tf_op jit(solution)/shard_map/slope/pallas_call | solution.py:310
  34.2 1.4 %backward.1 = (bf16[128,512]{1,0:T(8,128)(2,1)S(1)}, bf16[128,512]{1,0:T(8,128)(2,1)S(1)}, bf16[128,512]{1,0:T(8,128)(2,1)S(1)}, bf16[128,512]{1,0:T(8,128)(2,1)...) custom-call(bf16[512,512]{1,0:T(8,128)(2,1)S(1)} %get-tuple-element., ...), custom_call_target="tpu_custom_call" | custom-call | bytes 4849664 | tf_op jit(solution)/shard_map/backward/pallas_call | solution.py:310
  35.8 1.8 %collective-permute-start.19 = (bf16[128,512]{1,0:T(8,128)(2,1)S(1)}, bf16[128,512]{1,0:T(8,128)(2,1)S(1)}, u32[]{:S(2)}, u32[]{:S(2)}) collective-permute-start(bf16[128,512]{1,0:T(8,128)(2,1)S(1)} %get-tuple-element.49), channel_id=1, source_target_pairs={{0,4},{1,5},{2,6},{3,7},{4,0},{5,1},{6,2},{7,3},{8,12},{9,13},{10,... | collective-permute-start | bytes 393224 | tf_op jit(solution)/shard_map/ppermute | solution.py:338
  38.3 2.4 %collective-permute-start.22 = (bf16[128,512]{1,0:T(8,128)(2,1)S(1)}, bf16[128,512]{1,0:T(8,128)(2,1)S(1)}, u32[]{:S(2)}, u32[]{:S(2)}) collective-permute-start(bf16[128,512]{1,0:T(8,128)(2,1)S(1)} %add_convert_fusion), channel_id=1, source_target_pairs={{0,8},{1,9},{2,10},{3,11},{4,12},{5,13},{6,14},{7,15},{8,0},{9,1},... | collective-permute-start | bytes 393224 | tf_op jit(solution)/shard_map/ppermute | solution.py:338
  41.2 3.2 %loss.1 = (f32[8,128]{1,0:T(8,128)S(1)}, f32[128,128]{1,0:T(8,128)S(1)}) custom-call(bf16[2048,128]{1,0:T(8,128)(2,1)S(1)} %get-tuple-element.38.rows_ref, f32[1,512]{1,0:T(1,128)S(1)} %get-tuple-element.39.thresh_ref, f32[1,512]{1,0:T(1,128)S(1)} %get-tuple-element.40.rate_ref, f32[64,256]{1,0:T(8,128)S(1)} %solve.1.refs_0_, ...), custom_call_target="tpu_custom_call" | custom-call | bytes 729088 | tf_op jit(solution)/shard_map/loss/pallas_call | solution.py:310
  44.9 2.7 %collective-permute-done.20.refs_3_ = bf16[128,512]{1,0:T(8,128)(2,1)S(1)} collective-permute-done((bf16[128,512]{1,0:T(8,128)(2,1)S(1)}, bf16[128,512]{1,0:T(8,128)(2,1)S(1)}, u32[]{:S(2)}, u32[]{:S(2)}) %collective-permute-start.20) | collective-permute-done | bytes 131104 | tf_op jit(solution)/shard_map/ppermute | solution.py:338
  47.7 1.2 %collective-permute-done.18.refs_1_ = bf16[128,512]{1,0:T(8,128)(2,1)S(1)} collective-permute-done((bf16[128,512]{1,0:T(8,128)(2,1)S(1)}, bf16[128,512]{1,0:T(8,128)(2,1)S(1)}, u32[]{:S(2)}, u32[]{:S(2)}) %collective-permute-start.18) | collective-permute-done | bytes 131104 | tf_op jit(solution)/shard_map/ppermute | solution.py:338
  (53 shorter events, 7.2 us)
Async XLA Ops:
  0.6 7.7 %copy-start.2 = (s32[2048]{0:T(1024)S(1)}, s32[2048]{0:T(1024)}, u32[]{:S(2)}) copy-start(s32[2048]{0:T(1024)} %param.10) | copy-start | bytes 24580
  0.6 12.8 %collective-permute-start.3 = (bf16[128,512]{1,0:T(8,128)(2,1)}, bf16[128,512]{1,0:T(8,128)(2,1)S(1)}, u32[]{:S(2)}, u32[]{:S(2)}) collective-permute-start(bf16[128,512]{1,0:T(8,128)(2,1)} %w_ref.1), channel_id=1, source_target_pairs={{0,8},{1,9},{2,10},{3,11},{4,12},{5,13},{6,14},{7,15},{8,0},{9,1},... | collective-permute-start | bytes 393224 | tf_op jit(solution)/shard_map/ppermute | solution.py:338
  4.7 9.3 %collective-permute-start = (bf16[128,512]{1,0:T(8,128)(2,1)}, bf16[128,512]{1,0:T(8,128)(2,1)S(1)}, u32[]{:S(2)}, u32[]{:S(2)}) collective-permute-start(bf16[128,512]{1,0:T(8,128)(2,1)} %x_ref.1), channel_id=1, source_target_pairs={{0,2},{1,3},{2,0},{3,1},{4,6},{5,7},{6,4},{7,5},{8,10},{9,11},{10,... | collective-permute-start | bytes 393224 | tf_op jit(solution)/shard_map/ppermute | solution.py:338
  6.3 7.8 %collective-permute-start.1 = (bf16[128,512]{1,0:T(8,128)(2,1)}, bf16[128,512]{1,0:T(8,128)(2,1)S(1)}, u32[]{:S(2)}, u32[]{:S(2)}) collective-permute-start(bf16[128,512]{1,0:T(8,128)(2,1)} %x_ref.1), channel_id=1, source_target_pairs={{0,4},{1,5},{2,6},{3,7},{4,0},{5,1},{6,2},{7,3},{8,12},{9,13},{10,... | collective-permute-start | bytes 393224 | tf_op jit(solution)/shard_map/ppermute | solution.py:338
  7.8 7.8 %collective-permute-start.2 = (bf16[128,512]{1,0:T(8,128)(2,1)}, bf16[128,512]{1,0:T(8,128)(2,1)S(1)}, u32[]{:S(2)}, u32[]{:S(2)}) collective-permute-start(bf16[128,512]{1,0:T(8,128)(2,1)} %x_ref.1), channel_id=1, source_target_pairs={{0,6},{1,7},{2,4},{3,5},{4,2},{5,3},{6,0},{7,1},{8,14},{9,15},{10,... | collective-permute-start | bytes 393224 | tf_op jit(solution)/shard_map/ppermute | solution.py:338
  8.2 5.2 %collective-permute-start.6 = (bf16[128]{0:T(256)(128)(2,1)}, bf16[128]{0:T(256)(128)(2,1)S(1)}, u32[]{:S(2)}, u32[]{:S(2)}) collective-permute-start(bf16[128]{0:T(256)(128)(2,1)} %param.9), channel_id=1, source_target_pairs={{0,8},{1,9},{2,10},{3,11},{4,12},{5,13},{6,14},{7,15},{8,0},{9,1},... | collective-permute-start | bytes 776 | tf_op jit(solution)/shard_map/ppermute | solution.py:338
  13.5 2.3 %collective-permute-start.4 = (bf16[128,512]{1,0:T(8,128)(2,1)S(1)}, bf16[128,512]{1,0:T(8,128)(2,1)S(1)}, u32[]{:S(2)}, u32[]{:S(2)}) collective-permute-start(bf16[128,512]{1,0:T(8,128)(2,1)S(1)} %copy-done.1), channel_id=1, source_target_pairs={{0,1},{1,0},{2,3},{3,2},{4,5},{5,4},{6,7},{7,6},{8,9},{9,8},{10,11... | collective-permute-start | bytes 393224 | tf_op jit(solution)/shard_map/ppermute | solution.py:338
  13.5 2.3 %collective-permute-start.5 = (bf16[128,512]{1,0:T(8,128)(2,1)S(1)}, bf16[128,512]{1,0:T(8,128)(2,1)S(1)}, u32[]{:S(2)}, u32[]{:S(2)}) collective-permute-start(bf16[128,512]{1,0:T(8,128)(2,1)S(1)} %collective-permute-done.3.refs_5_.refs_7_), channel_id=1, source_target_pairs={{0,1},{1,0},{2,3},{3,2},{4,5},{5,4},{6,7},{7,6},{8,9},{9,8},{10,11... | collective-permute-start | bytes 393224 | tf_op jit(solution)/shard_map/ppermute | solution.py:338
  14.0 1.8 %collective-permute-start.7 = (bf16[128]{0:T(256)(128)(2,1)S(1)}, bf16[128]{0:T(256)(128)(2,1)S(1)}, u32[]{:S(2)}, u32[]{:S(2)}) collective-permute-start(bf16[128]{0:T(256)(128)(2,1)S(1)} %copy-done.5), channel_id=1, source_target_pairs={{0,1},{1,0},{2,3},{3,2},{4,5},{5,4},{6,7},{7,6},{8,9},{9,8},{10,11... | collective-permute-start | bytes 776 | tf_op jit(solution)/shard_map/ppermute | solution.py:338
  14.1 1.7 %collective-permute-start.8 = (bf16[128]{0:T(256)(128)(2,1)S(1)}, bf16[128]{0:T(256)(128)(2,1)S(1)}, u32[]{:S(2)}, u32[]{:S(2)}) collective-permute-start(bf16[128]{0:T(256)(128)(2,1)S(1)} %collective-permute-done.6), channel_id=1, source_target_pairs={{0,1},{1,0},{2,3},{3,2},{4,5},{5,4},{6,7},{7,6},{8,9},{9,8},{10,11... | collective-permute-start | bytes 776 | tf_op jit(solution)/shard_map/ppermute | solution.py:338
  17.1 1.3 %collective-permute-start.9 = (f32[32,256]{1,0:T(8,128)S(1)}, f32[32,256]{1,0:T(8,128)S(1)}, u32[]{:S(2)}, u32[]{:S(2)}) collective-permute-start(f32[32,256]{1,0:T(8,128)S(1)} %get-tuple-element.35), channel_id=1, source_target_pairs={{0,1},{1,0},{2,3},{3,2},{4,5},{5,4},{6,7},{7,6},{8,9},{9,8},{10,11... | collective-permute-start | bytes 98312 | tf_op jit(solution)/shard_map/ppermute | solution.py:338
  18.3 6.3 %collective-permute-start.11 = (f32[32,256]{1,0:T(8,128)S(1)}, f32[32,256]{1,0:T(8,128)S(1)}, u32[]{:S(2)}, u32[]{:S(2)}) collective-permute-start(f32[32,256]{1,0:T(8,128)S(1)} %add.15), channel_id=1, source_target_pairs={{0,2},{1,3},{2,0},{3,1},{4,6},{5,7},{6,4},{7,5},{8,10},{9,11},{10,... | collective-permute-start | bytes 98312 | tf_op jit(solution)/shard_map/ppermute | solution.py:338
  19.7 4.9 %collective-permute-start.12 = (f32[32,256]{1,0:T(8,128)S(1)}, f32[32,256]{1,0:T(8,128)S(1)}, u32[]{:S(2)}, u32[]{:S(2)}) collective-permute-start(f32[32,256]{1,0:T(8,128)S(1)} %add.15), channel_id=1, source_target_pairs={{0,4},{1,5},{2,6},{3,7},{4,0},{5,1},{6,2},{7,3},{8,12},{9,13},{10,... | collective-permute-start | bytes 98312 | tf_op jit(solution)/shard_map/ppermute | solution.py:338
  21.6 4.9 %collective-permute-start.13 = (f32[32,256]{1,0:T(8,128)S(1)}, f32[32,256]{1,0:T(8,128)S(1)}, u32[]{:S(2)}, u32[]{:S(2)}) collective-permute-start(f32[32,256]{1,0:T(8,128)S(1)} %add.15), channel_id=1, source_target_pairs={{0,6},{1,7},{2,4},{3,5},{4,2},{5,3},{6,0},{7,1},{8,14},{9,15},{10,... | collective-permute-start | bytes 98312 | tf_op jit(solution)/shard_map/ppermute | solution.py:338
  21.8 6.0 %collective-permute-start.10 = (bf16[1,32,512]{2,1,0:T(8,128)(2,1)S(1)}, bf16[1,32,512]{2,1,0:T(8,128)(2,1)S(1)}, u32[]{:S(2)}, u32[]{:S(2)}) collective-permute-start(bf16[1,32,512]{2,1,0:T(8,128)(2,1)S(1)} %bitcast.10), channel_id=1, source_target_pairs={{0,8},{1,9},{2,10},{3,11},{4,12},{5,13},{6,14},{7,15},{8,0},{9,1},... | collective-permute-start | bytes 98312 | tf_op jit(solution)/shard_map/ppermute | solution.py:338
  26.6 4.9 %collective-permute-start.15 = (f32[32,256]{1,0:T(8,128)S(1)}, f32[32,256]{1,0:T(8,128)S(1)}, u32[]{:S(2)}, u32[]{:S(2)}) collective-permute-start(f32[32,256]{1,0:T(8,128)S(1)} %add_add_fusion.refs_0_), channel_id=1, source_target_pairs={{0,8},{1,9},{2,10},{3,11},{4,12},{5,13},{6,14},{7,15},{8,0},{9,1},... | collective-permute-start | bytes 98312 | tf_op jit(solution)/shard_map/ppermute | solution.py:338
  27.8 1.3 %collective-permute-start.14 = (bf16[2,32,512]{2,1,0:T(8,128)(2,1)S(1)}, bf16[2,32,512]{2,1,0:T(8,128)(2,1)S(1)}, u32[]{:S(2)}, u32[]{:S(2)}) collective-permute-start(bf16[2,32,512]{2,1,0:T(8,128)(2,1)S(1)} %pad_maximum_fusion), channel_id=1, source_target_pairs={{0,1},{1,0},{2,3},{3,2},{4,5},{5,4},{6,7},{7,6},{8,9},{9,8},{10,11... | collective-permute-start | bytes 196616 | tf_op jit(solution)/shard_map/ppermute | solution.py:338
  32.9 1.3 %collective-permute-start.16 = (f32[64,256]{1,0:T(8,128)S(1)}, f32[64,256]{1,0:T(8,128)S(1)}, u32[]{:S(2)}, u32[]{:S(2)}) collective-permute-start(f32[64,256]{1,0:T(8,128)S(1)} %solve.1.refs_0_), channel_id=1, source_target_pairs={{0,1},{1,0},{2,3},{3,2},{4,5},{5,4},{6,7},{7,6},{8,9},{9,8},{10,11... | collective-permute-start | bytes 196616 | tf_op jit(solution)/shard_map/ppermute | solution.py:338
  35.6 2.7 %collective-permute-start.17 = (bf16[128,512]{1,0:T(8,128)(2,1)S(1)}, bf16[128,512]{1,0:T(8,128)(2,1)S(1)}, u32[]{:S(2)}, u32[]{:S(2)}) collective-permute-start(bf16[128,512]{1,0:T(8,128)(2,1)S(1)} %get-tuple-element.47), channel_id=1, source_target_pairs={{0,1},{1,0},{2,3},{3,2},{4,5},{5,4},{6,7},{7,6},{8,9},{9,8},{10,11... | collective-permute-start | bytes 393224 | tf_op jit(solution)/shard_map/ppermute | solution.py:338
  35.8 9.1 %collective-permute-start.19 = (bf16[128,512]{1,0:T(8,128)(2,1)S(1)}, bf16[128,512]{1,0:T(8,128)(2,1)S(1)}, u32[]{:S(2)}, u32[]{:S(2)}) collective-permute-start(bf16[128,512]{1,0:T(8,128)(2,1)S(1)} %get-tuple-element.49), channel_id=1, source_target_pairs={{0,4},{1,5},{2,6},{3,7},{4,0},{5,1},{6,2},{7,3},{8,12},{9,13},{10,... | collective-permute-start | bytes 393224 | tf_op jit(solution)/shard_map/ppermute | solution.py:338
  37.6 10.1 %collective-permute-start.20 = (bf16[128,512]{1,0:T(8,128)(2,1)S(1)}, bf16[128,512]{1,0:T(8,128)(2,1)S(1)}, u32[]{:S(2)}, u32[]{:S(2)}) collective-permute-start(bf16[128,512]{1,0:T(8,128)(2,1)S(1)} %get-tuple-element.50), channel_id=1, source_target_pairs={{0,6},{1,7},{2,4},{3,5},{4,2},{5,3},{6,0},{7,1},{8,14},{9,15},{10,... | collective-permute-start | bytes 393224 | tf_op jit(solution)/shard_map/ppermute | solution.py:338
  38.3 9.4 %collective-permute-start.22 = (bf16[128,512]{1,0:T(8,128)(2,1)S(1)}, bf16[128,512]{1,0:T(8,128)(2,1)S(1)}, u32[]{:S(2)}, u32[]{:S(2)}) collective-permute-start(bf16[128,512]{1,0:T(8,128)(2,1)S(1)} %add_convert_fusion), channel_id=1, source_target_pairs={{0,8},{1,9},{2,10},{3,11},{4,12},{5,13},{6,14},{7,15},{8,0},{9,1},... | collective-permute-start | bytes 393224 | tf_op jit(solution)/shard_map/ppermute | solution.py:338
  40.6 7.0 %collective-permute-start.21 = (bf16[128,512]{1,0:T(8,128)(2,1)S(1)}, bf16[128,512]{1,0:T(8,128)(2,1)S(1)}, u32[]{:S(2)}, u32[]{:S(2)}) collective-permute-start(bf16[128,512]{1,0:T(8,128)(2,1)S(1)} %get-tuple-element.53), channel_id=1, source_target_pairs={{0,1},{1,0},{2,3},{3,2},{4,5},{5,4},{6,7},{7,6},{8,9},{9,8},{10,11... | collective-permute-start | bytes 393224 | tf_op jit(solution)/shard_map/ppermute | solution.py:338
  40.6 8.3 %collective-permute-start.18 = (bf16[128,512]{1,0:T(8,128)(2,1)S(1)}, bf16[128,512]{1,0:T(8,128)(2,1)S(1)}, u32[]{:S(2)}, u32[]{:S(2)}) collective-permute-start(bf16[128,512]{1,0:T(8,128)(2,1)S(1)} %get-tuple-element.48), channel_id=1, source_target_pairs={{0,2},{1,3},{2,0},{3,1},{4,6},{5,7},{6,4},{7,5},{8,10},{9,11},{10,... | collective-permute-start | bytes 393224 | tf_op jit(solution)/shard_map/ppermute | solution.py:338
  (6 other events, 6.4 us)

commit v5 on v4

--- a/solution.py
+++ b/solution.py
@@ -230,12 +230,11 @@
     return jnp.concatenate([ref[here] for ref in refs], axis=1)
 
 
-def backward_kernel(scale, shares, paths, trades, member_ref, rows_ref, slope_ref, value_ref, *refs):
+def weight_side_kernel(scale, shares, paths, member_ref, rows_ref, slope_ref, *refs):
     solved_refs, refs = refs[:shares], refs[shares:]
-    x_refs, refs = refs[:paths], refs[paths:]
-    w_refs, refs = refs[:trades], refs[trades:]
-    weight_refs, basis_refs, slopes_ref = refs[:trades], refs[trades:-1], refs[-1]
+    x_refs, (traded_ref, slopes_ref, *weight_refs) = refs[:paths], refs[paths:]
     traded = dot(three_rows(joined(solved_refs, 0)), member_ref[...]).astype(BF16)
+    traded_ref[...] = traded
     group = slopes_ref.shape[0]
     spread = dot(rows_ref[:group], traded).astype(BF16).astype(F32)
     slopes_ref[...] = (slope_ref[...] * spread).astype(BF16)
@@ -245,12 +244,16 @@
     for part in weight_refs:
         part[...] = weight[start : start + part.shape[0]]
         start += part.shape[0]
+
+
+def basis_side_kernel(trades, value_ref, traded_ref, slopes_ref, *refs):
+    w_refs, basis_refs = refs[:trades], refs[trades:]
     weights = joined_weights(w_refs)
     start = 0
     for part in basis_refs:
         here = slice(start, start + part.shape[0])
         total = dot(slopes_ref[here], weights)
-        wide = dot(value_ref[here], traded, 1, 1)
+        wide = dot(value_ref[here], traded_ref[...], 1, 1)
         design = wide
         for k in range(1, 3):
             design = design + pltpu.roll(wide, LANES - k * REGRESSORS, 1)
@@ -387,12 +390,10 @@
         name="forward",
     )
     moment = moments[0] + swap(moments[1], SHARES - 1)
-    small = after(lead, moment)[None]
-    small = jnp.concatenate([small, swap(small, 1 << first_bit)], axis=0)
+    small = lead[None]
+    for bit in outer_bits:
+        small = jnp.concatenate([small, swap(small, 1 << bit)], axis=0)
     moment = sum(direct([moment] * inner, inner_bits), moment)
-    for bit in outer_bits[1:]:
-        small = after(small, moment)
-        small = jnp.concatenate([small, swap(small, 1 << bit)], axis=0)
     for bit in outer_bits[-2:0:-1]:
         moment = moment + swap(moment, 1 << bit)
     moments = [moment, swap(moment, 1 << first_bit)]
@@ -422,14 +423,22 @@
         *basis, *weights, *notionals,
         name="slope",
     )
-    parts = call(
-        partial(backward_kernel, 1.0 / math.sqrt(paths_all), SHARES, inner, outer),
-        [((trade_rows, features), BF16)] * outer + [((path_rows, features), BF16)] * inner,
-        member, design_rows, slope, value, *solved, *basis, *weights,
-        name="backward",
-        scratch=[pltpu.VMEM((group_paths, group_trades), BF16)],
-    )
-    terms = [[part] for part in parts[:outer]]
+    traded, slopes, *weight_parts = call(
+        partial(weight_side_kernel, 1.0 / math.sqrt(paths_all), SHARES, inner),
+        [((LANES, group_trades), BF16), ((group_paths, group_trades), BF16)]
+        + [((trade_rows, features), BF16)] * outer,
+        member, design_rows, slope, *solved, *basis,
+        name="weight_side",
+    )
+    basis_parts = list(
+        call(
+            partial(basis_side_kernel, outer),
+            [((path_rows, features), BF16)] * inner,
+            value, traded, slopes, *weights,
+            name="basis_side",
+        )
+    )
+    terms = [[part] for part in weight_parts]
     for bit in reversed(outer_bits):
         count = len(terms) // 2
         arrived = None
@@ -441,7 +450,6 @@
             arrived = swap(gone, 1 << bit)
             terms[k].append(arrived)
             if bit == outer_bits[-1] and k == count - 1:
-                basis_parts = list(parts[outer:])
                 basis_parts[1] = after(basis_parts[1], arrived)
         terms = terms[:count]
     weight_terms = terms[0]

time: 50 us -> 49.2 us (0.984)
  waiting for transfers between devices: 11.9 us -> 9.61 us
  starting transfers between devices: 22 us -> 23.3 us
    ppermute x23, waiting for transfers between devices: 11.9 us -> 9.61 us  [swap(): return lax.ppermute(x, 'paths', [(d, d ^ mask) for d in range(n)])]
    ppermute x23, starting transfers between devices: 22 us -> 23.3 us  [swap(): return lax.ppermute(x, 'paths', [(d, d ^ mask) for d in range(n)])]
    pallas_call x10 -> x11, Pallas kernels: 12 us -> 12.2 us  [call(): pl.pallas_call(kernel, out_shape=[jax.ShapeDtypeStruct(s, d) for s, d in...]
    unnamed x15 -> x14, local copies, waits for them, and re-layouts: 2.52 us -> 2.51 us
  transfers between devices with their start and end apart: 23 -> 23, of which waited for: 9 -> 9; matrix products, arithmetic and copies ran while one was open for 1% -> 1% of each run, Pallas kernels for 14% -> 16%
where the time goes in v5:
time: 49.2 us; the launch traced here: 49 us
  starting transfers between devices  23.3 us (47%)
  Pallas kernels  12.2 us (25%)
  waiting for transfers between devices  9.61 us (20%)
  local copies, waits for them, and re-layouts  3.02 us (6%)
  between operations  0.79 us (2%)
    ppermute x23, starting transfers between devices, swap(): return lax.ppermute(x, 'paths', [(d, d ^ mask) for d in range(n)])  23.3 us
    pallas_call x11, Pallas kernels, call(): pl.pallas_call(kernel, out_shape=[jax.ShapeDtypeStruct(s, d) for s, d in...  12.2 us
    ppermute x23, waiting for transfers between devices, swap(): return lax.ppermute(x, 'paths', [(d, d ^ mask) for d in range(n)])  9.61 us
    unnamed x14, local copies, waits for them, and re-layouts  2.51 us
  transfers between devices with their start and end apart: 23, of which 9 were waited for; matrix products, arithmetic and copies ran while one was open for 1% of the time, Pallas kernels for 16%

profile of v5, /device:TPU:0, one launch (start us, length us, event | category | flops | bytes accessed | tf_op | source)
XLA Modules:
  0.0 49.0 jit_solution(15828469242330428131)
XLA Ops:
  0.6 4.1 %collective-permute-start.5 = (bf16[128,512]{1,0:T(8,128)(2,1)}, bf16[128,512]{1,0:T(8,128)(2,1)S(1)}, u32[]{:S(2)}, u32[]{:S(2)}) collective-permute-start(bf16[128,512]{1,0:T(8,128)(2,1)} %w_ref.1), channel_id=1, source_target_pairs={{0,8},{1,9},{2,10},{3,11},{4,12},{5,13},{6,14},{7,15},{8,0},{9,1},... | collective-permute-start | bytes 393224 | tf_op jit(solution)/shard_map/ppermute | solution.py:341
  4.7 1.5 %collective-permute-start = (bf16[128,512]{1,0:T(8,128)(2,1)}, bf16[128,512]{1,0:T(8,128)(2,1)S(1)}, u32[]{:S(2)}, u32[]{:S(2)}) collective-permute-start(bf16[128,512]{1,0:T(8,128)(2,1)} %x_ref.1), channel_id=1, source_target_pairs={{0,2},{1,3},{2,0},{3,1},{4,6},{5,7},{6,4},{7,5},{8,10},{9,11},{10,... | collective-permute-start | bytes 393224 | tf_op jit(solution)/shard_map/ppermute | solution.py:341
  6.3 1.6 %collective-permute-start.1 = (bf16[128,512]{1,0:T(8,128)(2,1)}, bf16[128,512]{1,0:T(8,128)(2,1)S(1)}, u32[]{:S(2)}, u32[]{:S(2)}) collective-permute-start(bf16[128,512]{1,0:T(8,128)(2,1)} %x_ref.1), channel_id=1, source_target_pairs={{0,4},{1,5},{2,6},{3,7},{4,0},{5,1},{6,2},{7,3},{8,12},{9,13},{10,... | collective-permute-start | bytes 393224 | tf_op jit(solution)/shard_map/ppermute | solution.py:341
  9.0 0.9 %copy-done = bf16[128,512]{1,0:T(8,128)(2,1)S(1)} copy-done((bf16[128,512]{1,0:T(8,128)(2,1)S(1)}, bf16[128,512]{1,0:T(8,128)(2,1)}, u32[]{:S(2)}) %copy-start) | copy-done | bytes 131096
  9.9 0.9 %copy-done.1 = bf16[128,512]{1,0:T(8,128)(2,1)S(1)} copy-done((bf16[128,512]{1,0:T(8,128)(2,1)S(1)}, bf16[128,512]{1,0:T(8,128)(2,1)}, u32[]{:S(2)}) %copy-start.1) | copy-done | bytes 131096
  11.5 2.0 %collective-permute-done.8 = bf16[128]{0:T(256)(128)(2,1)S(1)} collective-permute-done((bf16[128]{0:T(256)(128)(2,1)}, bf16[128]{0:T(256)(128)(2,1)S(1)}, u32[]{:S(2)}, u32[]{:S(2)}) %collective-permute-start.8) | collective-permute-done | bytes 288 | tf_op jit(solution)/shard_map/ppermute | solution.py:341
  14.5 1.2 %collective-permute-done.2.refs_3_.refs_5_ = bf16[128,512]{1,0:T(8,128)(2,1)S(1)} collective-permute-done((bf16[128,512]{1,0:T(8,128)(2,1)}, bf16[128,512]{1,0:T(8,128)(2,1)S(1)}, u32[]{:S(2)}, u32[]{:S(2)}) %collective-permute-start.2) | collective-permute-done | bytes 131104 | tf_op jit(solution)/shard_map/ppermute | solution.py:341
  15.8 1.3 %forward.1 = (bf16[512,512]{1,0:T(8,128)(2,1)S(1)}, f32[32,256]{1,0:T(8,128)S(1)}, f32[32,256]{1,0:T(8,128)S(1)}) custom-call(bf16[128,512]{1,0:T(8,128)(2,1)S(1)} %get-tuple-element.30.refs_0_.refs_2_, bf16[128,512]{1,0:T(8,128)(2,1)S(1)} %collective-permute-done.refs_1_.refs_3_, bf16[128,512]{1,0:T(8,128)(2,1)S(1)} %collective-permute-done.1.refs_2_.refs_4_, ...), custom_call_target="tpu_custom_call" | custom-call | bytes 2196480 | tf_op jit(solution)/shard_map/forward/pallas_call | solution.py:313
  17.1 3.1 %collective-permute-start.3 = (bf16[1,32,512]{2,1,0:T(8,128)(2,1)S(1)}, bf16[1,32,512]{2,1,0:T(8,128)(2,1)S(1)}, u32[]{:S(2)}, u32[]{:S(2)}) collective-permute-start(bf16[1,32,512]{2,1,0:T(8,128)(2,1)S(1)} %bitcast.10), channel_id=1, source_target_pairs={{0,8},{1,9},{2,10},{3,11},{4,12},{5,13},{6,14},{7,15},{8,0},{9,1},... | collective-permute-start | bytes 98312 | tf_op jit(solution)/shard_map/ppermute | solution.py:341
  20.2 1.6 %collective-permute-start.12 = (f32[32,256]{1,0:T(8,128)S(1)}, f32[32,256]{1,0:T(8,128)S(1)}, u32[]{:S(2)}, u32[]{:S(2)}) collective-permute-start(f32[32,256]{1,0:T(8,128)S(1)} %add.15), channel_id=1, source_target_pairs={{0,2},{1,3},{2,0},{3,1},{4,6},{5,7},{6,4},{7,5},{8,10},{9,11},{10,... | collective-permute-start | bytes 98312 | tf_op jit(solution)/shard_map/ppermute | solution.py:341
  21.8 2.0 %collective-permute-start.14 = (f32[32,256]{1,0:T(8,128)S(1)}, f32[32,256]{1,0:T(8,128)S(1)}, u32[]{:S(2)}, u32[]{:S(2)}) collective-permute-start(f32[32,256]{1,0:T(8,128)S(1)} %add.15), channel_id=1, source_target_pairs={{0,6},{1,7},{2,4},{3,5},{4,2},{5,3},{6,0},{7,1},{8,14},{9,15},{10,... | collective-permute-start | bytes 98312 | tf_op jit(solution)/shard_map/ppermute | solution.py:341
  24.2 1.5 %collective-permute-done.13 = f32[32,256]{1,0:T(8,128)S(1)} collective-permute-done((f32[32,256]{1,0:T(8,128)S(1)}, f32[32,256]{1,0:T(8,128)S(1)}, u32[]{:S(2)}, u32[]{:S(2)}) %collective-permute-start.13) | collective-permute-done | bytes 32800 | tf_op jit(solution)/shard_map/ppermute | solution.py:341
  25.7 0.9 %collective-permute-done.14 = f32[32,256]{1,0:T(8,128)S(1)} collective-permute-done((f32[32,256]{1,0:T(8,128)S(1)}, f32[32,256]{1,0:T(8,128)S(1)}, u32[]{:S(2)}, u32[]{:S(2)}) %collective-permute-start.14) | collective-permute-done | bytes 32800 | tf_op jit(solution)/shard_map/ppermute | solution.py:341
  26.6 2.0 %collective-permute-start.15 = (f32[32,256]{1,0:T(8,128)S(1)}, f32[32,256]{1,0:T(8,128)S(1)}, u32[]{:S(2)}, u32[]{:S(2)}) collective-permute-start(f32[32,256]{1,0:T(8,128)S(1)} %add_add_fusion.refs_0_), channel_id=1, source_target_pairs={{0,8},{1,9},{2,10},{3,11},{4,12},{5,13},{6,14},{7,15},{8,0},{9,1},... | collective-permute-start | bytes 98312 | tf_op jit(solution)/shard_map/ppermute | solution.py:341
  29.2 1.8 %inverse.1.inverse_ref = f32[32,32]{1,0:T(8,128)S(1)} custom-call(bf16[4,32,512]{2,1,0:T(8,128)(2,1)S(1)} %pad_maximum_fusion.small_ref), custom_call_target="tpu_custom_call" | custom-call | bytes 135168 | tf_op jit(solution)/shard_map/inverse/pallas_call | solution.py:313
  31.5 1.4 %solve.1.refs_0_ = f32[64,256]{1,0:T(8,128)S(1)} custom-call(f32[32,32]{1,0:T(8,128)S(1)} %inverse.1.inverse_ref, bf16[32,2048]{1,0:T(8,128)(2,1)S(1)} %get-tuple-element.34.design_ref, bf16[2048,128]{1,0:T(8,128)(2,1)S(1)} %get-tuple-element.31.rows_ref, f32[1,512]{1,0:T(1,128)S(1)} %get-tuple-element.32.thresh_ref, ...), custom_call_target="tpu_custom_call" | custom-call | bytes 794624 | tf_op jit(solution)/shard_map/solve/pallas_call | solution.py:313
  33.0 0.9 %slope.1.slope_ref = f32[512,512]{1,0:T(8,128)S(1)} custom-call(bf16[128,512]{1,0:T(8,128)(2,1)S(1)} %get-tuple-element.30.refs_0_.refs_2_, bf16[128,512]{1,0:T(8,128)(2,1)S(1)} %collective-permute-done.refs_1_.refs_3_, bf16[128,512]{1,0:T(8,128)(2,1)S(1)} %collective-permute-done.1.refs_2_.refs_4_, ...), custom_call_target="tpu_custom_call" | custom-call | bytes 2098176 | tf_op jit(solution)/shard_map/slope/pallas_call | solution.py:313
  34.2 0.9 %weight_side.1 = (bf16[128,512]{1,0:T(8,128)(2,1)S(1)}, bf16[512,512]{1,0:T(8,128)(2,1)S(1)}, bf16[128,512]{1,0:T(8,128)(2,1)S(1)}, bf16[128,512]{1,0:T(8,128)(2...) custom-call(bf16[512,512]{1,0:T(8,128)(2,1)S(1)} %get-tuple-element.36.refs_13_.member_ref, ...), custom_call_target="tpu_custom_call" | custom-call | bytes 3932160 | tf_op jit(solution)/shard_map/weight_side/pallas_call | solution.py:313
  36.0 2.1 %collective-permute-start.19 = (bf16[128,512]{1,0:T(8,128)(2,1)S(1)}, bf16[128,512]{1,0:T(8,128)(2,1)S(1)}, u32[]{:S(2)}, u32[]{:S(2)}) collective-permute-start(bf16[128,512]{1,0:T(8,128)(2,1)S(1)} %get-tuple-element.49), channel_id=1, source_target_pairs={{0,4},{1,5},{2,6},{3,7},{4,0},{5,1},{6,2},{7,3},{8,12},{9,13},{10,... | collective-permute-start | bytes 393224 | tf_op jit(solution)/shard_map/ppermute | solution.py:341
  38.5 1.6 %collective-permute-start.22 = (bf16[128,512]{1,0:T(8,128)(2,1)S(1)}, bf16[128,512]{1,0:T(8,128)(2,1)S(1)}, u32[]{:S(2)}, u32[]{:S(2)}) collective-permute-start(bf16[128,512]{1,0:T(8,128)(2,1)S(1)} %add_convert_fusion), channel_id=1, source_target_pairs={{0,8},{1,9},{2,10},{3,11},{4,12},{5,13},{6,14},{7,15},{8,0},{9,1},... | collective-permute-start | bytes 393224 | tf_op jit(solution)/shard_map/ppermute | solution.py:341
  40.1 1.5 %collective-permute-start.18 = (bf16[128,512]{1,0:T(8,128)(2,1)S(1)}, bf16[128,512]{1,0:T(8,128)(2,1)S(1)}, u32[]{:S(2)}, u32[]{:S(2)}) collective-permute-start(bf16[128,512]{1,0:T(8,128)(2,1)S(1)} %get-tuple-element.48), channel_id=1, source_target_pairs={{0,2},{1,3},{2,0},{3,1},{4,6},{5,7},{6,4},{7,5},{8,10},{9,11},{10,... | collective-permute-start | bytes 393224 | tf_op jit(solution)/shard_map/ppermute | solution.py:341
  41.6 3.2 %loss.1 = (f32[8,128]{1,0:T(8,128)S(1)}, f32[128,128]{1,0:T(8,128)S(1)}) custom-call(bf16[2048,128]{1,0:T(8,128)(2,1)S(1)} %get-tuple-element.31.rows_ref, f32[1,512]{1,0:T(1,128)S(1)} %get-tuple-element.32.thresh_ref, f32[1,512]{1,0:T(1,128)S(1)} %get-tuple-element.33.rate_ref, f32[64,256]{1,0:T(8,128)S(1)} %solve.1.refs_0_, ...), custom_call_target="tpu_custom_call" | custom-call | bytes 729088 | tf_op jit(solution)/shard_map/loss/pallas_call | solution.py:313
  45.3 2.6 %collective-permute-done.20.refs_3_ = bf16[128,512]{1,0:T(8,128)(2,1)S(1)} collective-permute-done((bf16[128,512]{1,0:T(8,128)(2,1)S(1)}, bf16[128,512]{1,0:T(8,128)(2,1)S(1)}, u32[]{:S(2)}, u32[]{:S(2)}) %collective-permute-start.20) | collective-permute-done | bytes 131104 | tf_op jit(solution)/shard_map/ppermute | solution.py:341
  48.2 0.9 %sums.1 = (f32[128,512]{1,0:T(8,128)}, f32[128,512]{1,0:T(8,128)}) custom-call(f32[128,128]{1,0:T(8,128)S(1)} %get-tuple-element.41.own_ref, bf16[128,512]{1,0:T(8,128)(2,1)S(1)} %get-tuple-element.45.refs_0_, bf16[128,512]{1,0:T(8,128)(2,1)S(1)} %collective-permute-done.18.refs_1_, bf16[128,512]{1,0:T(8,128)(2,1)S(1)} %collective-permute-done.19.refs_2_, ...), custom_call_target="tpu_custom_call" | custom-call | bytes 1507328 | tf_op jit(solution)/shard_map/sums/pallas_call | solution.py:313
  (53 shorter events, 6.9 us)
Async XLA Ops:
  0.6 7.7 %copy-start.2 = (s32[2048]{0:T(1024)S(1)}, s32[2048]{0:T(1024)}, u32[]{:S(2)}) copy-start(s32[2048]{0:T(1024)} %param.10) | copy-start | bytes 24580
  0.6 12.8 %collective-permute-start.5 = (bf16[128,512]{1,0:T(8,128)(2,1)}, bf16[128,512]{1,0:T(8,128)(2,1)S(1)}, u32[]{:S(2)}, u32[]{:S(2)}) collective-permute-start(bf16[128,512]{1,0:T(8,128)(2,1)} %w_ref.1), channel_id=1, source_target_pairs={{0,8},{1,9},{2,10},{3,11},{4,12},{5,13},{6,14},{7,15},{8,0},{9,1},... | collective-permute-start | bytes 393224 | tf_op jit(solution)/shard_map/ppermute | solution.py:341
  4.7 9.3 %collective-permute-start = (bf16[128,512]{1,0:T(8,128)(2,1)}, bf16[128,512]{1,0:T(8,128)(2,1)S(1)}, u32[]{:S(2)}, u32[]{:S(2)}) collective-permute-start(bf16[128,512]{1,0:T(8,128)(2,1)} %x_ref.1), channel_id=1, source_target_pairs={{0,2},{1,3},{2,0},{3,1},{4,6},{5,7},{6,4},{7,5},{8,10},{9,11},{10,... | collective-permute-start | bytes 393224 | tf_op jit(solution)/shard_map/ppermute | solution.py:341
  6.3 7.8 %collective-permute-start.1 = (bf16[128,512]{1,0:T(8,128)(2,1)}, bf16[128,512]{1,0:T(8,128)(2,1)S(1)}, u32[]{:S(2)}, u32[]{:S(2)}) collective-permute-start(bf16[128,512]{1,0:T(8,128)(2,1)} %x_ref.1), channel_id=1, source_target_pairs={{0,4},{1,5},{2,6},{3,7},{4,0},{5,1},{6,2},{7,3},{8,12},{9,13},{10,... | collective-permute-start | bytes 393224 | tf_op jit(solution)/shard_map/ppermute | solution.py:341
  7.8 7.8 %collective-permute-start.2 = (bf16[128,512]{1,0:T(8,128)(2,1)}, bf16[128,512]{1,0:T(8,128)(2,1)S(1)}, u32[]{:S(2)}, u32[]{:S(2)}) collective-permute-start(bf16[128,512]{1,0:T(8,128)(2,1)} %x_ref.1), channel_id=1, source_target_pairs={{0,6},{1,7},{2,4},{3,5},{4,2},{5,3},{6,0},{7,1},{8,14},{9,15},{10,... | collective-permute-start | bytes 393224 | tf_op jit(solution)/shard_map/ppermute | solution.py:341
  8.2 5.2 %collective-permute-start.8 = (bf16[128]{0:T(256)(128)(2,1)}, bf16[128]{0:T(256)(128)(2,1)S(1)}, u32[]{:S(2)}, u32[]{:S(2)}) collective-permute-start(bf16[128]{0:T(256)(128)(2,1)} %param.9), channel_id=1, source_target_pairs={{0,8},{1,9},{2,10},{3,11},{4,12},{5,13},{6,14},{7,15},{8,0},{9,1},... | collective-permute-start | bytes 776 | tf_op jit(solution)/shard_map/ppermute | solution.py:341
  13.5 2.3 %collective-permute-start.6 = (bf16[128,512]{1,0:T(8,128)(2,1)S(1)}, bf16[128,512]{1,0:T(8,128)(2,1)S(1)}, u32[]{:S(2)}, u32[]{:S(2)}) collective-permute-start(bf16[128,512]{1,0:T(8,128)(2,1)S(1)} %copy-done.1), channel_id=1, source_target_pairs={{0,1},{1,0},{2,3},{3,2},{4,5},{5,4},{6,7},{7,6},{8,9},{9,8},{10,11... | collective-permute-start | bytes 393224 | tf_op jit(solution)/shard_map/ppermute | solution.py:341
  13.5 2.3 %collective-permute-start.7 = (bf16[128,512]{1,0:T(8,128)(2,1)S(1)}, bf16[128,512]{1,0:T(8,128)(2,1)S(1)}, u32[]{:S(2)}, u32[]{:S(2)}) collective-permute-start(bf16[128,512]{1,0:T(8,128)(2,1)S(1)} %collective-permute-done.5.refs_5_.refs_1_), channel_id=1, source_target_pairs={{0,1},{1,0},{2,3},{3,2},{4,5},{5,4},{6,7},{7,6},{8,9},{9,8},{10,11... | collective-permute-start | bytes 393224 | tf_op jit(solution)/shard_map/ppermute | solution.py:341
  14.0 1.8 %collective-permute-start.9 = (bf16[128]{0:T(256)(128)(2,1)S(1)}, bf16[128]{0:T(256)(128)(2,1)S(1)}, u32[]{:S(2)}, u32[]{:S(2)}) collective-permute-start(bf16[128]{0:T(256)(128)(2,1)S(1)} %copy-done.5), channel_id=1, source_target_pairs={{0,1},{1,0},{2,3},{3,2},{4,5},{5,4},{6,7},{7,6},{8,9},{9,8},{10,11... | collective-permute-start | bytes 776 | tf_op jit(solution)/shard_map/ppermute | solution.py:341
  14.1 1.7 %collective-permute-start.10 = (bf16[128]{0:T(256)(128)(2,1)S(1)}, bf16[128]{0:T(256)(128)(2,1)S(1)}, u32[]{:S(2)}, u32[]{:S(2)}) collective-permute-start(bf16[128]{0:T(256)(128)(2,1)S(1)} %collective-permute-done.8), channel_id=1, source_target_pairs={{0,1},{1,0},{2,3},{3,2},{4,5},{5,4},{6,7},{7,6},{8,9},{9,8},{10,11... | collective-permute-start | bytes 776 | tf_op jit(solution)/shard_map/ppermute | solution.py:341
  17.1 3.1 %collective-permute-start.11 = (f32[32,256]{1,0:T(8,128)S(1)}, f32[32,256]{1,0:T(8,128)S(1)}, u32[]{:S(2)}, u32[]{:S(2)}) collective-permute-start(f32[32,256]{1,0:T(8,128)S(1)} %get-tuple-element.39), channel_id=1, source_target_pairs={{0,1},{1,0},{2,3},{3,2},{4,5},{5,4},{6,7},{7,6},{8,9},{9,8},{10,11... | collective-permute-start | bytes 98312 | tf_op jit(solution)/shard_map/ppermute | solution.py:341
  17.1 6.7 %collective-permute-start.3 = (bf16[1,32,512]{2,1,0:T(8,128)(2,1)S(1)}, bf16[1,32,512]{2,1,0:T(8,128)(2,1)S(1)}, u32[]{:S(2)}, u32[]{:S(2)}) collective-permute-start(bf16[1,32,512]{2,1,0:T(8,128)(2,1)S(1)} %bitcast.10), channel_id=1, source_target_pairs={{0,8},{1,9},{2,10},{3,11},{4,12},{5,13},{6,14},{7,15},{8,0},{9,1},... | collective-permute-start | bytes 98312 | tf_op jit(solution)/shard_map/ppermute | solution.py:341
  20.2 4.0 %collective-permute-start.12 = (f32[32,256]{1,0:T(8,128)S(1)}, f32[32,256]{1,0:T(8,128)S(1)}, u32[]{:S(2)}, u32[]{:S(2)}) collective-permute-start(f32[32,256]{1,0:T(8,128)S(1)} %add.15), channel_id=1, source_target_pairs={{0,2},{1,3},{2,0},{3,1},{4,6},{5,7},{6,4},{7,5},{8,10},{9,11},{10,... | collective-permute-start | bytes 98312 | tf_op jit(solution)/shard_map/ppermute | solution.py:341
  21.8 3.9 %collective-permute-start.13 = (f32[32,256]{1,0:T(8,128)S(1)}, f32[32,256]{1,0:T(8,128)S(1)}, u32[]{:S(2)}, u32[]{:S(2)}) collective-permute-start(f32[32,256]{1,0:T(8,128)S(1)} %add.15), channel_id=1, source_target_pairs={{0,4},{1,5},{2,6},{3,7},{4,0},{5,1},{6,2},{7,3},{8,12},{9,13},{10,... | collective-permute-start | bytes 98312 | tf_op jit(solution)/shard_map/ppermute | solution.py:341
  21.8 4.8 %collective-permute-start.14 = (f32[32,256]{1,0:T(8,128)S(1)}, f32[32,256]{1,0:T(8,128)S(1)}, u32[]{:S(2)}, u32[]{:S(2)}) collective-permute-start(f32[32,256]{1,0:T(8,128)S(1)} %add.15), channel_id=1, source_target_pairs={{0,6},{1,7},{2,4},{3,5},{4,2},{5,3},{6,0},{7,1},{8,14},{9,15},{10,... | collective-permute-start | bytes 98312 | tf_op jit(solution)/shard_map/ppermute | solution.py:341
  23.8 4.8 %collective-permute-start.4 = (bf16[2,32,512]{2,1,0:T(8,128)(2,1)S(1)}, bf16[2,32,512]{2,1,0:T(8,128)(2,1)S(1)}, u32[]{:S(2)}, u32[]{:S(2)}) collective-permute-start(bf16[2,32,512]{2,1,0:T(8,128)(2,1)S(1)} %pad_maximum_fusion.1), channel_id=1, source_target_pairs={{0,1},{1,0},{2,3},{3,2},{4,5},{5,4},{6,7},{7,6},{8,9},{9,8},{10,11... | collective-permute-start | bytes 196616 | tf_op jit(solution)/shard_map/ppermute | solution.py:341
  26.6 4.9 %collective-permute-start.15 = (f32[32,256]{1,0:T(8,128)S(1)}, f32[32,256]{1,0:T(8,128)S(1)}, u32[]{:S(2)}, u32[]{:S(2)}) collective-permute-start(f32[32,256]{1,0:T(8,128)S(1)} %add_add_fusion.refs_0_), channel_id=1, source_target_pairs={{0,8},{1,9},{2,10},{3,11},{4,12},{5,13},{6,14},{7,15},{8,0},{9,1},... | collective-permute-start | bytes 98312 | tf_op jit(solution)/shard_map/ppermute | solution.py:341
  32.9 1.3 %collective-permute-start.16 = (f32[64,256]{1,0:T(8,128)S(1)}, f32[64,256]{1,0:T(8,128)S(1)}, u32[]{:S(2)}, u32[]{:S(2)}) collective-permute-start(f32[64,256]{1,0:T(8,128)S(1)} %solve.1.refs_0_), channel_id=1, source_target_pairs={{0,1},{1,0},{2,3},{3,2},{4,5},{5,4},{6,7},{7,6},{8,9},{9,8},{10,11... | collective-permute-start | bytes 196616 | tf_op jit(solution)/shard_map/ppermute | solution.py:341
  35.1 3.3 %collective-permute-start.17 = (bf16[128,512]{1,0:T(8,128)(2,1)S(1)}, bf16[128,512]{1,0:T(8,128)(2,1)S(1)}, u32[]{:S(2)}, u32[]{:S(2)}) collective-permute-start(bf16[128,512]{1,0:T(8,128)(2,1)S(1)} %get-tuple-element.47), channel_id=1, source_target_pairs={{0,1},{1,0},{2,3},{3,2},{4,5},{5,4},{6,7},{7,6},{8,9},{9,8},{10,11... | collective-permute-start | bytes 393224 | tf_op jit(solution)/shard_map/ppermute | solution.py:341
  36.0 9.3 %collective-permute-start.19 = (bf16[128,512]{1,0:T(8,128)(2,1)S(1)}, bf16[128,512]{1,0:T(8,128)(2,1)S(1)}, u32[]{:S(2)}, u32[]{:S(2)}) collective-permute-start(bf16[128,512]{1,0:T(8,128)(2,1)S(1)} %get-tuple-element.49), channel_id=1, source_target_pairs={{0,4},{1,5},{2,6},{3,7},{4,0},{5,1},{6,2},{7,3},{8,12},{9,13},{10,... | collective-permute-start | bytes 393224 | tf_op jit(solution)/shard_map/ppermute | solution.py:341
  38.1 9.8 %collective-permute-start.20 = (bf16[128,512]{1,0:T(8,128)(2,1)S(1)}, bf16[128,512]{1,0:T(8,128)(2,1)S(1)}, u32[]{:S(2)}, u32[]{:S(2)}) collective-permute-start(bf16[128,512]{1,0:T(8,128)(2,1)S(1)} %get-tuple-element.50), channel_id=1, source_target_pairs={{0,6},{1,7},{2,4},{3,5},{4,2},{5,3},{6,0},{7,1},{8,14},{9,15},{10,... | collective-permute-start | bytes 393224 | tf_op jit(solution)/shard_map/ppermute | solution.py:341
  38.5 9.4 %collective-permute-start.22 = (bf16[128,512]{1,0:T(8,128)(2,1)S(1)}, bf16[128,512]{1,0:T(8,128)(2,1)S(1)}, u32[]{:S(2)}, u32[]{:S(2)}) collective-permute-start(bf16[128,512]{1,0:T(8,128)(2,1)S(1)} %add_convert_fusion), channel_id=1, source_target_pairs={{0,8},{1,9},{2,10},{3,11},{4,12},{5,13},{6,14},{7,15},{8,0},{9,1},... | collective-permute-start | bytes 393224 | tf_op jit(solution)/shard_map/ppermute | solution.py:341
  40.1 7.8 %collective-permute-start.21 = (bf16[128,512]{1,0:T(8,128)(2,1)S(1)}, bf16[128,512]{1,0:T(8,128)(2,1)S(1)}, u32[]{:S(2)}, u32[]{:S(2)}) collective-permute-start(bf16[128,512]{1,0:T(8,128)(2,1)S(1)} %get-tuple-element.53), channel_id=1, source_target_pairs={{0,1},{1,0},{2,3},{3,2},{4,5},{5,4},{6,7},{7,6},{8,9},{9,8},{10,11... | collective-permute-start | bytes 393224 | tf_op jit(solution)/shard_map/ppermute | solution.py:341
  40.1 8.0 %collective-permute-start.18 = (bf16[128,512]{1,0:T(8,128)(2,1)S(1)}, bf16[128,512]{1,0:T(8,128)(2,1)S(1)}, u32[]{:S(2)}, u32[]{:S(2)}) collective-permute-start(bf16[128,512]{1,0:T(8,128)(2,1)S(1)} %get-tuple-element.48), channel_id=1, source_target_pairs={{0,2},{1,3},{2,0},{3,1},{4,6},{5,7},{6,4},{7,5},{8,10},{9,11},{10,... | collective-permute-start | bytes 393224 | tf_op jit(solution)/shard_map/ppermute | solution.py:341
  (6 other events, 6.4 us)

commit v6 on v5

--- a/solution.py
+++ b/solution.py
@@ -110,21 +110,25 @@
     return jnp.concatenate(blocks, axis=0)[:, size:]
 
 
+def regressors(x):
+    turned = x[:, :LANES].astype(F32).T[:REGRESSORS]
+    return jnp.where(rows(turned.shape) == CONSTANT, 1.0, turned).astype(BF16)
+
+
 def lead_kernel(*refs):
     x_refs, lead_ref = refs[:-1], refs[-1]
     start = 0
     for x in x_refs:
-        turned = x[:, :LANES].astype(F32).T[:REGRESSORS]
-        turned = jnp.where(rows(turned.shape) == CONSTANT, 1.0, turned)
-        lead_ref[:, start : start + x.shape[0]] = turned.astype(BF16)
+        lead_ref[:, start : start + x.shape[0]] = regressors(x)
         start += x.shape[0]
 
 
 def tables_kernel(
     trade_masks, me_ref, level_ref, set_ref, index_ref, rate_ref, x_ref, w_ref,
-    member_ref, thresh_out_ref, rate_out_ref, x_out_ref, w_out_ref,
+    member_ref, thresh_out_ref, rate_out_ref, x_out_ref, w_out_ref, lead_ref,
 ):
     x_out_ref[...] = x_ref[...]
+    lead_ref[...] = regressors(x_ref)
     w_out_ref[...] = w_ref[...]
     me = me_ref[0]
     shares = index_ref.shape[0]
@@ -356,7 +360,7 @@
     basis = [path_basis] + direct([path_basis] * inner, inner_bits)
     notionals = [notional, swap(notional, 1 << first_bit)]
 
-    member, thresh, rate, basis[0], own_weight = call(
+    member, thresh, rate, basis[0], own_weight, own_lead = call(
         partial(tables_kernel, masks(outer_bits)),
         [
             ((sets, group_trades), BF16),
@@ -364,6 +368,7 @@
             ((1, sets), F32),
             (path_basis.shape, BF16),
             (proxy_weight.shape, BF16),
+            ((REGRESSORS, path_rows), BF16),
         ],
         me.astype(jnp.int32).reshape(1),
         threshold_levels,
@@ -389,11 +394,21 @@
         *basis, *weights, *notionals, lead, member,
         name="forward",
     )
-    moment = moments[0] + swap(moments[1], SHARES - 1)
-    small = lead[None]
-    for bit in outer_bits:
-        small = jnp.concatenate([small, swap(small, 1 << bit)], axis=0)
-    moment = sum(direct([moment] * inner, inner_bits), moment)
+    beside = [own_lead]
+    for bit in outer_bits[:-1]:
+        beside = beside + [swap(x, 1 << bit) for x in beside]
+    beside = beside[1:]
+    moment = moments[0] + swap(after(moments[1], *beside), SHARES - 1)
+    message = jnp.concatenate([moment] + [x.astype(F32) for x in beside], axis=1)
+    arrived = [message] + direct([message] * inner, inner_bits)
+    moment = sum(x[:, :share] for x in arrived)
+    small = [lead]
+    for k in range(len(beside)):
+        start = share + k * path_rows
+        group = [x[:, start : start + path_rows].astype(BF16) for x in arrived]
+        small.append(jnp.concatenate(group, axis=1))
+    small = jnp.stack(small)
+    small = jnp.concatenate([small, swap(small, SHARES - 1)], axis=0)
     for bit in outer_bits[-2:0:-1]:
         moment = moment + swap(moment, 1 << bit)
     moments = [moment, swap(moment, 1 << first_bit)]

time: 49.2 us -> 50.9 us (1.035)
  waiting for transfers between devices: 9.61 us -> 11.6 us
    ppermute x23, waiting for transfers between devices: 9.61 us -> 11.6 us  [swap(): return lax.ppermute(x, 'paths', [(d, d ^ mask) for d in range(n)])]
  transfers between devices with their start and end apart: 23 -> 23, of which waited for: 9 -> 11; matrix products, arithmetic and copies ran while one was open for 1% -> 1% of each run, Pallas kernels for 16% -> 18%
where the time goes in v6:
time: 50.9 us; the launch traced here: 50.8 us
  starting transfers between devices  23.1 us (45%)
  Pallas kernels  12.2 us (24%)
  waiting for transfers between devices  11.6 us (23%)
  local copies, waits for them, and re-layouts  3.03 us (6%)
  between operations  0.78 us (2%)
    ppermute x23, starting transfers between devices, swap(): return lax.ppermute(x, 'paths', [(d, d ^ mask) for d in range(n)])  23.1 us
    pallas_call x11, Pallas kernels, call(): pl.pallas_call(kernel, out_shape=[jax.ShapeDtypeStruct(s, d) for s, d in...  12.2 us
    ppermute x23, waiting for transfers between devices, swap(): return lax.ppermute(x, 'paths', [(d, d ^ mask) for d in range(n)])  11.6 us
    unnamed x14, local copies, waits for them, and re-layouts  2.51 us
  transfers between devices with their start and end apart: 23, of which 11 were waited for; matrix products, arithmetic and copies ran while one was open for 1% of the time, Pallas kernels for 18%

profile of v6, /device:TPU:0, one launch (start us, length us, event | category | flops | bytes accessed | tf_op | source)
XLA Modules:
  0.0 50.8 jit_solution(15704936854082178968)
XLA Ops:
  0.6 4.1 %collective-permute-start.4 = (bf16[128,512]{1,0:T(8,128)(2,1)}, bf16[128,512]{1,0:T(8,128)(2,1)S(1)}, u32[]{:S(2)}, u32[]{:S(2)}) collective-permute-start(bf16[128,512]{1,0:T(8,128)(2,1)} %w_ref.1), channel_id=1, source_target_pairs={{0,8},{1,9},{2,10},{3,11},{4,12},{5,13},{6,14},{7,15},{8,0},{9,1},... | collective-permute-start | bytes 393224 | tf_op jit(solution)/shard_map/ppermute | solution.py:345
  4.7 1.5 %collective-permute-start = (bf16[128,512]{1,0:T(8,128)(2,1)}, bf16[128,512]{1,0:T(8,128)(2,1)S(1)}, u32[]{:S(2)}, u32[]{:S(2)}) collective-permute-start(bf16[128,512]{1,0:T(8,128)(2,1)} %x_ref.1), channel_id=1, source_target_pairs={{0,2},{1,3},{2,0},{3,1},{4,6},{5,7},{6,4},{7,5},{8,10},{9,11},{10,... | collective-permute-start | bytes 393224 | tf_op jit(solution)/shard_map/ppermute | solution.py:345
  6.3 1.6 %collective-permute-start.1 = (bf16[128,512]{1,0:T(8,128)(2,1)}, bf16[128,512]{1,0:T(8,128)(2,1)S(1)}, u32[]{:S(2)}, u32[]{:S(2)}) collective-permute-start(bf16[128,512]{1,0:T(8,128)(2,1)} %x_ref.1), channel_id=1, source_target_pairs={{0,4},{1,5},{2,6},{3,7},{4,0},{5,1},{6,2},{7,3},{8,12},{9,13},{10,... | collective-permute-start | bytes 393224 | tf_op jit(solution)/shard_map/ppermute | solution.py:345
  9.0 0.9 %copy-done = bf16[128,512]{1,0:T(8,128)(2,1)S(1)} copy-done((bf16[128,512]{1,0:T(8,128)(2,1)S(1)}, bf16[128,512]{1,0:T(8,128)(2,1)}, u32[]{:S(2)}) %copy-start) | copy-done | bytes 131096
  9.9 0.9 %copy-done.1 = bf16[128,512]{1,0:T(8,128)(2,1)S(1)} copy-done((bf16[128,512]{1,0:T(8,128)(2,1)S(1)}, bf16[128,512]{1,0:T(8,128)(2,1)}, u32[]{:S(2)}) %copy-start.1) | copy-done | bytes 131096
  11.5 1.9 %collective-permute-done.7 = bf16[128]{0:T(256)(128)(2,1)S(1)} collective-permute-done((bf16[128]{0:T(256)(128)(2,1)}, bf16[128]{0:T(256)(128)(2,1)S(1)}, u32[]{:S(2)}, u32[]{:S(2)}) %collective-permute-start.7) | collective-permute-done | bytes 288 | tf_op jit(solution)/shard_map/ppermute | solution.py:345
  14.0 3.3 %collective-permute-start.3 = (bf16[32,128]{1,0:T(8,128)(2,1)S(1)}, bf16[32,128]{1,0:T(8,128)(2,1)S(1)}, u32[]{:S(2)}, u32[]{:S(2)}) collective-permute-start(bf16[32,128]{1,0:T(8,128)(2,1)S(1)} %get-tuple-element.33), channel_id=1, source_target_pairs={{0,8},{1,9},{2,10},{3,11},{4,12},{5,13},{6,14},{7,15},{8,0},{9,1},... | collective-permute-start | bytes 24584 | tf_op jit(solution)/shard_map/ppermute | solution.py:345
  18.6 1.3 %forward.1 = (bf16[512,512]{1,0:T(8,128)(2,1)S(1)}, f32[32,256]{1,0:T(8,128)S(1)}, f32[32,256]{1,0:T(8,128)S(1)}) custom-call(bf16[128,512]{1,0:T(8,128)(2,1)S(1)} %get-tuple-element.32.refs_0_.refs_2_, bf16[128,512]{1,0:T(8,128)(2,1)S(1)} %collective-permute-done.refs_1_.refs_3_, bf16[128,512]{1,0:T(8,128)(2,1)S(1)} %collective-permute-done.1.refs_2_.refs_4_, ...), custom_call_target="tpu_custom_call" | custom-call | bytes 2196480 | tf_op jit(solution)/shard_map/forward/pallas_call | solution.py:317
  20.2 0.9 %collective-permute-done.10 = f32[32,256]{1,0:T(8,128)S(1)} collective-permute-done((f32[32,256]{1,0:T(8,128)S(1)}, f32[32,256]{1,0:T(8,128)S(1)}, u32[]{:S(2)}, u32[]{:S(2)}) %collective-permute-start.10) | collective-permute-done | bytes 32800 | tf_op jit(solution)/shard_map/ppermute | solution.py:345
  21.1 1.9 %collective-permute-start.13 = (f32[32,384]{1,0:T(8,128)S(1)}, f32[32,384]{1,0:T(8,128)S(1)}, u32[]{:S(2)}, u32[]{:S(2)}) collective-permute-start(f32[32,384]{1,0:T(8,128)S(1)} %pad_maximum_fusion.2), channel_id=1, source_target_pairs={{0,6},{1,7},{2,4},{3,5},{4,2},{5,3},{6,0},{7,1},{8,14},{9,15},{10,... | collective-permute-start | bytes 147464 | tf_op jit(solution)/shard_map/ppermute | solution.py:345
  23.0 1.1 %collective-permute-start.12 = (f32[32,384]{1,0:T(8,128)S(1)}, f32[32,384]{1,0:T(8,128)S(1)}, u32[]{:S(2)}, u32[]{:S(2)}) collective-permute-start(f32[32,384]{1,0:T(8,128)S(1)} %pad_maximum_fusion.2), channel_id=1, source_target_pairs={{0,4},{1,5},{2,6},{3,7},{4,0},{5,1},{6,2},{7,3},{8,12},{9,13},{10,... | collective-permute-start | bytes 147464 | tf_op jit(solution)/shard_map/ppermute | solution.py:345
  24.7 1.9 %collective-permute-done.13 = f32[32,384]{1,0:T(8,128)S(1)} collective-permute-done((f32[32,384]{1,0:T(8,128)S(1)}, f32[32,384]{1,0:T(8,128)S(1)}, u32[]{:S(2)}, u32[]{:S(2)}) %collective-permute-start.13) | collective-permute-done | bytes 49184 | tf_op jit(solution)/shard_map/ppermute | solution.py:345
  27.1 1.1 %collective-permute-done.11 = f32[32,384]{1,0:T(8,128)S(1)} collective-permute-done((f32[32,384]{1,0:T(8,128)S(1)}, f32[32,384]{1,0:T(8,128)S(1)}, u32[]{:S(2)}, u32[]{:S(2)}) %collective-permute-start.11) | collective-permute-done | bytes 49184 | tf_op jit(solution)/shard_map/ppermute | solution.py:345
  28.4 1.9 %collective-permute-start.15 = (f32[32,256]{1,0:T(8,128)S(1)}, f32[32,256]{1,0:T(8,128)S(1)}, u32[]{:S(2)}, u32[]{:S(2)}) collective-permute-start(f32[32,256]{1,0:T(8,128)S(1)} %slice_add_fusion.refs_0_), channel_id=1, source_target_pairs={{0,8},{1,9},{2,10},{3,11},{4,12},{5,13},{6,14},{7,15},{8,0},{9,1},... | collective-permute-start | bytes 98312 | tf_op jit(solution)/shard_map/ppermute | solution.py:345
  30.9 1.8 %inverse.1.inverse_ref = f32[32,32]{1,0:T(8,128)S(1)} custom-call(bf16[4,32,512]{2,1,0:T(8,128)(2,1)S(1)} %pad_maximum_fusion.small_ref), custom_call_target="tpu_custom_call" | custom-call | bytes 135168 | tf_op jit(solution)/shard_map/inverse/pallas_call | solution.py:317
  32.6 1.2 %collective-permute-done.15.refs_1_ = f32[32,256]{1,0:T(8,128)S(1)} collective-permute-done((f32[32,256]{1,0:T(8,128)S(1)}, f32[32,256]{1,0:T(8,128)S(1)}, u32[]{:S(2)}, u32[]{:S(2)}) %collective-permute-start.15) | collective-permute-done | bytes 32800 | tf_op jit(solution)/shard_map/ppermute | solution.py:345
  33.8 1.4 %solve.1.refs_0_ = f32[64,256]{1,0:T(8,128)S(1)} custom-call(f32[32,32]{1,0:T(8,128)S(1)} %inverse.1.inverse_ref, bf16[32,2048]{1,0:T(8,128)(2,1)S(1)} %get-tuple-element.43.design_ref, bf16[2048,128]{1,0:T(8,128)(2,1)S(1)} %get-tuple-element.40.rows_ref, f32[1,512]{1,0:T(1,128)S(1)} %get-tuple-element.41.thresh_ref, ...), custom_call_target="tpu_custom_call" | custom-call | bytes 794624 | tf_op jit(solution)/shard_map/solve/pallas_call | solution.py:317
  35.3 0.9 %slope.1.slope_ref = f32[512,512]{1,0:T(8,128)S(1)} custom-call(bf16[128,512]{1,0:T(8,128)(2,1)S(1)} %get-tuple-element.32.refs_0_.refs_2_, bf16[128,512]{1,0:T(8,128)(2,1)S(1)} %collective-permute-done.refs_1_.refs_3_, bf16[128,512]{1,0:T(8,128)(2,1)S(1)} %collective-permute-done.1.refs_2_.refs_4_, ...), custom_call_target="tpu_custom_call" | custom-call | bytes 2098176 | tf_op jit(solution)/shard_map/slope/pallas_call | solution.py:317
  36.6 0.9 %weight_side.1 = (bf16[128,512]{1,0:T(8,128)(2,1)S(1)}, bf16[512,512]{1,0:T(8,128)(2,1)S(1)}, bf16[128,512]{1,0:T(8,128)(2,1)S(1)}, bf16[128,512]{1,0:T(8,128)(2...) custom-call(bf16[512,512]{1,0:T(8,128)(2,1)S(1)} %get-tuple-element.35.refs_13_.member_ref, ...), custom_call_target="tpu_custom_call" | custom-call | bytes 3932160 | tf_op jit(solution)/shard_map/weight_side/pallas_call | solution.py:317
  38.8 1.7 %collective-permute-start.20 = (bf16[128,512]{1,0:T(8,128)(2,1)S(1)}, bf16[128,512]{1,0:T(8,128)(2,1)S(1)}, u32[]{:S(2)}, u32[]{:S(2)}) collective-permute-start(bf16[128,512]{1,0:T(8,128)(2,1)S(1)} %get-tuple-element.54), channel_id=1, source_target_pairs={{0,6},{1,7},{2,4},{3,5},{4,2},{5,3},{6,0},{7,1},{8,14},{9,15},{10,... | collective-permute-start | bytes 393224 | tf_op jit(solution)/shard_map/ppermute | solution.py:345
  40.5 1.4 %collective-permute-start.22 = (bf16[128,512]{1,0:T(8,128)(2,1)S(1)}, bf16[128,512]{1,0:T(8,128)(2,1)S(1)}, u32[]{:S(2)}, u32[]{:S(2)}) collective-permute-start(bf16[128,512]{1,0:T(8,128)(2,1)S(1)} %add_convert_fusion), channel_id=1, source_target_pairs={{0,8},{1,9},{2,10},{3,11},{4,12},{5,13},{6,14},{7,15},{8,0},{9,1},... | collective-permute-start | bytes 393224 | tf_op jit(solution)/shard_map/ppermute | solution.py:345
  41.9 1.5 %collective-permute-start.18 = (bf16[128,512]{1,0:T(8,128)(2,1)S(1)}, bf16[128,512]{1,0:T(8,128)(2,1)S(1)}, u32[]{:S(2)}, u32[]{:S(2)}) collective-permute-start(bf16[128,512]{1,0:T(8,128)(2,1)S(1)} %get-tuple-element.52), channel_id=1, source_target_pairs={{0,2},{1,3},{2,0},{3,1},{4,6},{5,7},{6,4},{7,5},{8,10},{9,11},{10,... | collective-permute-start | bytes 393224 | tf_op jit(solution)/shard_map/ppermute | solution.py:345
  43.3 3.2 %loss.1 = (f32[8,128]{1,0:T(8,128)S(1)}, f32[128,128]{1,0:T(8,128)S(1)}) custom-call(bf16[2048,128]{1,0:T(8,128)(2,1)S(1)} %get-tuple-element.40.rows_ref, f32[1,512]{1,0:T(1,128)S(1)} %get-tuple-element.41.thresh_ref, f32[1,512]{1,0:T(1,128)S(1)} %get-tuple-element.42.rate_ref, f32[64,256]{1,0:T(8,128)S(1)} %solve.1.refs_0_, ...), custom_call_target="tpu_custom_call" | custom-call | bytes 729088 | tf_op jit(solution)/shard_map/loss/pallas_call | solution.py:317
  47.6 2.3 %collective-permute-done.20.refs_3_ = bf16[128,512]{1,0:T(8,128)(2,1)S(1)} collective-permute-done((bf16[128,512]{1,0:T(8,128)(2,1)S(1)}, bf16[128,512]{1,0:T(8,128)(2,1)S(1)}, u32[]{:S(2)}, u32[]{:S(2)}) %collective-permute-start.20) | collective-permute-done | bytes 131104 | tf_op jit(solution)/shard_map/ppermute | solution.py:345
  (59 shorter events, 9.5 us)
Async XLA Ops:
  0.6 7.7 %copy-start.2 = (s32[2048]{0:T(1024)S(1)}, s32[2048]{0:T(1024)}, u32[]{:S(2)}) copy-start(s32[2048]{0:T(1024)} %param.10) | copy-start | bytes 24580
  0.6 12.8 %collective-permute-start.4 = (bf16[128,512]{1,0:T(8,128)(2,1)}, bf16[128,512]{1,0:T(8,128)(2,1)S(1)}, u32[]{:S(2)}, u32[]{:S(2)}) collective-permute-start(bf16[128,512]{1,0:T(8,128)(2,1)} %w_ref.1), channel_id=1, source_target_pairs={{0,8},{1,9},{2,10},{3,11},{4,12},{5,13},{6,14},{7,15},{8,0},{9,1},... | collective-permute-start | bytes 393224 | tf_op jit(solution)/shard_map/ppermute | solution.py:345
  4.7 9.3 %collective-permute-start = (bf16[128,512]{1,0:T(8,128)(2,1)}, bf16[128,512]{1,0:T(8,128)(2,1)S(1)}, u32[]{:S(2)}, u32[]{:S(2)}) collective-permute-start(bf16[128,512]{1,0:T(8,128)(2,1)} %x_ref.1), channel_id=1, source_target_pairs={{0,2},{1,3},{2,0},{3,1},{4,6},{5,7},{6,4},{7,5},{8,10},{9,11},{10,... | collective-permute-start | bytes 393224 | tf_op jit(solution)/shard_map/ppermute | solution.py:345
  6.3 11.0 %collective-permute-start.1 = (bf16[128,512]{1,0:T(8,128)(2,1)}, bf16[128,512]{1,0:T(8,128)(2,1)S(1)}, u32[]{:S(2)}, u32[]{:S(2)}) collective-permute-start(bf16[128,512]{1,0:T(8,128)(2,1)} %x_ref.1), channel_id=1, source_target_pairs={{0,4},{1,5},{2,6},{3,7},{4,0},{5,1},{6,2},{7,3},{8,12},{9,13},{10,... | collective-permute-start | bytes 393224 | tf_op jit(solution)/shard_map/ppermute | solution.py:345
  7.8 9.4 %collective-permute-start.2 = (bf16[128,512]{1,0:T(8,128)(2,1)}, bf16[128,512]{1,0:T(8,128)(2,1)S(1)}, u32[]{:S(2)}, u32[]{:S(2)}) collective-permute-start(bf16[128,512]{1,0:T(8,128)(2,1)} %x_ref.1), channel_id=1, source_target_pairs={{0,6},{1,7},{2,4},{3,5},{4,2},{5,3},{6,0},{7,1},{8,14},{9,15},{10,... | collective-permute-start | bytes 393224 | tf_op jit(solution)/shard_map/ppermute | solution.py:345
  8.2 5.2 %collective-permute-start.7 = (bf16[128]{0:T(256)(128)(2,1)}, bf16[128]{0:T(256)(128)(2,1)S(1)}, u32[]{:S(2)}, u32[]{:S(2)}) collective-permute-start(bf16[128]{0:T(256)(128)(2,1)} %param.9), channel_id=1, source_target_pairs={{0,8},{1,9},{2,10},{3,11},{4,12},{5,13},{6,14},{7,15},{8,0},{9,1},... | collective-permute-start | bytes 776 | tf_op jit(solution)/shard_map/ppermute | solution.py:345
  13.5 5.1 %collective-permute-start.5 = (bf16[128,512]{1,0:T(8,128)(2,1)S(1)}, bf16[128,512]{1,0:T(8,128)(2,1)S(1)}, u32[]{:S(2)}, u32[]{:S(2)}) collective-permute-start(bf16[128,512]{1,0:T(8,128)(2,1)S(1)} %copy-done.1), channel_id=1, source_target_pairs={{0,1},{1,0},{2,3},{3,2},{4,5},{5,4},{6,7},{7,6},{8,9},{9,8},{10,11... | collective-permute-start | bytes 393224 | tf_op jit(solution)/shard_map/ppermute | solution.py:345
  13.5 5.1 %collective-permute-start.6 = (bf16[128,512]{1,0:T(8,128)(2,1)S(1)}, bf16[128,512]{1,0:T(8,128)(2,1)S(1)}, u32[]{:S(2)}, u32[]{:S(2)}) collective-permute-start(bf16[128,512]{1,0:T(8,128)(2,1)S(1)} %collective-permute-done.4.refs_5_.refs_1_), channel_id=1, source_target_pairs={{0,1},{1,0},{2,3},{3,2},{4,5},{5,4},{6,7},{7,6},{8,9},{9,8},{10,11... | collective-permute-start | bytes 393224 | tf_op jit(solution)/shard_map/ppermute | solution.py:345
  14.0 5.9 %collective-permute-start.3 = (bf16[32,128]{1,0:T(8,128)(2,1)S(1)}, bf16[32,128]{1,0:T(8,128)(2,1)S(1)}, u32[]{:S(2)}, u32[]{:S(2)}) collective-permute-start(bf16[32,128]{1,0:T(8,128)(2,1)S(1)} %get-tuple-element.33), channel_id=1, source_target_pairs={{0,8},{1,9},{2,10},{3,11},{4,12},{5,13},{6,14},{7,15},{8,0},{9,1},... | collective-permute-start | bytes 24584 | tf_op jit(solution)/shard_map/ppermute | solution.py:345
  17.3 1.1 %collective-permute-start.8 = (bf16[128]{0:T(256)(128)(2,1)S(1)}, bf16[128]{0:T(256)(128)(2,1)S(1)}, u32[]{:S(2)}, u32[]{:S(2)}) collective-permute-start(bf16[128]{0:T(256)(128)(2,1)S(1)} %copy-done.5), channel_id=1, source_target_pairs={{0,1},{1,0},{2,3},{3,2},{4,5},{5,4},{6,7},{7,6},{8,9},{9,8},{10,11... | collective-permute-start | bytes 776 | tf_op jit(solution)/shard_map/ppermute | solution.py:345
  17.3 1.3 %collective-permute-start.9 = (bf16[128]{0:T(256)(128)(2,1)S(1)}, bf16[128]{0:T(256)(128)(2,1)S(1)}, u32[]{:S(2)}, u32[]{:S(2)}) collective-permute-start(bf16[128]{0:T(256)(128)(2,1)S(1)} %collective-permute-done.7), channel_id=1, source_target_pairs={{0,1},{1,0},{2,3},{3,2},{4,5},{5,4},{6,7},{7,6},{8,9},{9,8},{10,11... | collective-permute-start | bytes 776 | tf_op jit(solution)/shard_map/ppermute | solution.py:345
  19.9 1.3 %collective-permute-start.10 = (f32[32,256]{1,0:T(8,128)S(1)}, f32[32,256]{1,0:T(8,128)S(1)}, u32[]{:S(2)}, u32[]{:S(2)}) collective-permute-start(f32[32,256]{1,0:T(8,128)S(1)} %get-tuple-element.39), channel_id=1, source_target_pairs={{0,1},{1,0},{2,3},{3,2},{4,5},{5,4},{6,7},{7,6},{8,9},{9,8},{10,11... | collective-permute-start | bytes 98312 | tf_op jit(solution)/shard_map/ppermute | solution.py:345
  21.1 5.4 %collective-permute-start.13 = (f32[32,384]{1,0:T(8,128)S(1)}, f32[32,384]{1,0:T(8,128)S(1)}, u32[]{:S(2)}, u32[]{:S(2)}) collective-permute-start(f32[32,384]{1,0:T(8,128)S(1)} %pad_maximum_fusion.2), channel_id=1, source_target_pairs={{0,6},{1,7},{2,4},{3,5},{4,2},{5,3},{6,0},{7,1},{8,14},{9,15},{10,... | collective-permute-start | bytes 147464 | tf_op jit(solution)/shard_map/ppermute | solution.py:345
  23.0 4.1 %collective-permute-start.12 = (f32[32,384]{1,0:T(8,128)S(1)}, f32[32,384]{1,0:T(8,128)S(1)}, u32[]{:S(2)}, u32[]{:S(2)}) collective-permute-start(f32[32,384]{1,0:T(8,128)S(1)} %pad_maximum_fusion.2), channel_id=1, source_target_pairs={{0,4},{1,5},{2,6},{3,7},{4,0},{5,1},{6,2},{7,3},{8,12},{9,13},{10,... | collective-permute-start | bytes 147464 | tf_op jit(solution)/shard_map/ppermute | solution.py:345
  24.2 4.1 %collective-permute-start.11 = (f32[32,384]{1,0:T(8,128)S(1)}, f32[32,384]{1,0:T(8,128)S(1)}, u32[]{:S(2)}, u32[]{:S(2)}) collective-permute-start(f32[32,384]{1,0:T(8,128)S(1)} %pad_maximum_fusion.2), channel_id=1, source_target_pairs={{0,2},{1,3},{2,0},{3,1},{4,6},{5,7},{6,4},{7,5},{8,10},{9,11},{10,... | collective-permute-start | bytes 147464 | tf_op jit(solution)/shard_map/ppermute | solution.py:345
  28.3 2.0 %collective-permute-start.14 = (bf16[2,32,512]{2,1,0:T(8,128)(2,1)S(1)}, bf16[2,32,512]{2,1,0:T(8,128)(2,1)S(1)}, u32[]{:S(2)}, u32[]{:S(2)}) collective-permute-start(bf16[2,32,512]{2,1,0:T(8,128)(2,1)S(1)} %pad_maximum_fusion.1), channel_id=1, source_target_pairs={{0,1},{1,0},{2,3},{3,2},{4,5},{5,4},{6,7},{7,6},{8,9},{9,8},{10,11... | collective-permute-start | bytes 196616 | tf_op jit(solution)/shard_map/ppermute | solution.py:345
  28.4 5.5 %collective-permute-start.15 = (f32[32,256]{1,0:T(8,128)S(1)}, f32[32,256]{1,0:T(8,128)S(1)}, u32[]{:S(2)}, u32[]{:S(2)}) collective-permute-start(f32[32,256]{1,0:T(8,128)S(1)} %slice_add_fusion.refs_0_), channel_id=1, source_target_pairs={{0,8},{1,9},{2,10},{3,11},{4,12},{5,13},{6,14},{7,15},{8,0},{9,1},... | collective-permute-start | bytes 98312 | tf_op jit(solution)/shard_map/ppermute | solution.py:345
  35.3 1.3 %collective-permute-start.16 = (f32[64,256]{1,0:T(8,128)S(1)}, f32[64,256]{1,0:T(8,128)S(1)}, u32[]{:S(2)}, u32[]{:S(2)}) collective-permute-start(f32[64,256]{1,0:T(8,128)S(1)} %solve.1.refs_0_), channel_id=1, source_target_pairs={{0,1},{1,0},{2,3},{3,2},{4,5},{5,4},{6,7},{7,6},{8,9},{9,8},{10,11... | collective-permute-start | bytes 196616 | tf_op jit(solution)/shard_map/ppermute | solution.py:345
  37.5 3.0 %collective-permute-start.17 = (bf16[128,512]{1,0:T(8,128)(2,1)S(1)}, bf16[128,512]{1,0:T(8,128)(2,1)S(1)}, u32[]{:S(2)}, u32[]{:S(2)}) collective-permute-start(bf16[128,512]{1,0:T(8,128)(2,1)S(1)} %get-tuple-element.51), channel_id=1, source_target_pairs={{0,1},{1,0},{2,3},{3,2},{4,5},{5,4},{6,7},{7,6},{8,9},{9,8},{10,11... | collective-permute-start | bytes 393224 | tf_op jit(solution)/shard_map/ppermute | solution.py:345
  38.4 9.2 %collective-permute-start.19 = (bf16[128,512]{1,0:T(8,128)(2,1)S(1)}, bf16[128,512]{1,0:T(8,128)(2,1)S(1)}, u32[]{:S(2)}, u32[]{:S(2)}) collective-permute-start(bf16[128,512]{1,0:T(8,128)(2,1)S(1)} %get-tuple-element.53), channel_id=1, source_target_pairs={{0,4},{1,5},{2,6},{3,7},{4,0},{5,1},{6,2},{7,3},{8,12},{9,13},{10,... | collective-permute-start | bytes 393224 | tf_op jit(solution)/shard_map/ppermute | solution.py:345
  38.8 11.1 %collective-permute-start.20 = (bf16[128,512]{1,0:T(8,128)(2,1)S(1)}, bf16[128,512]{1,0:T(8,128)(2,1)S(1)}, u32[]{:S(2)}, u32[]{:S(2)}) collective-permute-start(bf16[128,512]{1,0:T(8,128)(2,1)S(1)} %get-tuple-element.54), channel_id=1, source_target_pairs={{0,6},{1,7},{2,4},{3,5},{4,2},{5,3},{6,0},{7,1},{8,14},{9,15},{10,... | collective-permute-start | bytes 393224 | tf_op jit(solution)/shard_map/ppermute | solution.py:345
  40.5 9.4 %collective-permute-start.22 = (bf16[128,512]{1,0:T(8,128)(2,1)S(1)}, bf16[128,512]{1,0:T(8,128)(2,1)S(1)}, u32[]{:S(2)}, u32[]{:S(2)}) collective-permute-start(bf16[128,512]{1,0:T(8,128)(2,1)S(1)} %add_convert_fusion), channel_id=1, source_target_pairs={{0,8},{1,9},{2,10},{3,11},{4,12},{5,13},{6,14},{7,15},{8,0},{9,1},... | collective-permute-start | bytes 393224 | tf_op jit(solution)/shard_map/ppermute | solution.py:345
  41.8 8.0 %collective-permute-start.21 = (bf16[128,512]{1,0:T(8,128)(2,1)S(1)}, bf16[128,512]{1,0:T(8,128)(2,1)S(1)}, u32[]{:S(2)}, u32[]{:S(2)}) collective-permute-start(bf16[128,512]{1,0:T(8,128)(2,1)S(1)} %get-tuple-element.57), channel_id=1, source_target_pairs={{0,1},{1,0},{2,3},{3,2},{4,5},{5,4},{6,7},{7,6},{8,9},{9,8},{10,11... | collective-permute-start | bytes 393224 | tf_op jit(solution)/shard_map/ppermute | solution.py:345
  41.9 8.0 %collective-permute-start.18 = (bf16[128,512]{1,0:T(8,128)(2,1)S(1)}, bf16[128,512]{1,0:T(8,128)(2,1)S(1)}, u32[]{:S(2)}, u32[]{:S(2)}) collective-permute-start(bf16[128,512]{1,0:T(8,128)(2,1)S(1)} %get-tuple-element.52), channel_id=1, source_target_pairs={{0,2},{1,3},{2,0},{3,1},{4,6},{5,7},{6,4},{7,5},{8,10},{9,11},{10,... | collective-permute-start | bytes 393224 | tf_op jit(solution)/shard_map/ppermute | solution.py:345
  (6 other events, 9.6 us)

commit v7 on v5

--- a/solution.py
+++ b/solution.py
@@ -390,13 +390,13 @@
         name="forward",
     )
     moment = moments[0] + swap(moments[1], SHARES - 1)
-    small = lead[None]
-    for bit in outer_bits:
-        small = jnp.concatenate([small, swap(small, 1 << bit)], axis=0)
-    moment = sum(direct([moment] * inner, inner_bits), moment)
-    for bit in outer_bits[-2:0:-1]:
-        moment = moment + swap(moment, 1 << bit)
-    moments = [moment, swap(moment, 1 << first_bit)]
+    lead = after(lead, moment)
+    leads = [lead] + direct([lead] * outer, outer_bits)
+    for bit in outer_bits[:-1]:
+        there = swap(moment, 1 << bit)
+        moment = moment + there
+    small = jnp.stack(leads)
+    moments = [moment] + direct([moment] * inner, inner_bits)
     (inverse,) = call(
         partial(inverse_kernel, RIDGE_SCALE * paths_all),
         [((REGRESSORS, REGRESSORS), F32)],

time: 49.2 us -> 48.7 us (0.990)
    ppermute x23 -> x24, waiting for transfers between devices: 9.61 us -> 9.19 us  [swap(): return lax.ppermute(x, 'paths', [(d, d ^ mask) for d in range(n)])]
    ppermute x23 -> x24, starting transfers between devices: 23.3 us -> 23.3 us  [swap(): return lax.ppermute(x, 'paths', [(d, d ^ mask) for d in range(n)])]
  transfers between devices with their start and end apart: 23 -> 24, of which waited for: 9 -> 8; matrix products, arithmetic and copies ran while one was open for 1% -> 1% of each run, Pallas kernels for 16% -> 16%
where the time goes in v7:
time: 48.7 us; the launch traced here: 48.5 us
  starting transfers between devices  23.3 us (48%)
  Pallas kernels  12.2 us (25%)
  waiting for transfers between devices  9.19 us (19%)
  local copies, waits for them, and re-layouts  3.02 us (6%)
  between operations  0.78 us (2%)
    ppermute x24, starting transfers between devices, swap(): return lax.ppermute(x, 'paths', [(d, d ^ mask) for d in range(n)])  23.3 us
    pallas_call x11, Pallas kernels, call(): pl.pallas_call(kernel, out_shape=[jax.ShapeDtypeStruct(s, d) for s, d in...  12.2 us
    ppermute x24, waiting for transfers between devices, swap(): return lax.ppermute(x, 'paths', [(d, d ^ mask) for d in range(n)])  9.19 us
    unnamed x14, local copies, waits for them, and re-layouts  2.51 us
  transfers between devices with their start and end apart: 24, of which 8 were waited for; matrix products, arithmetic and copies ran while one was open for 1% of the time, Pallas kernels for 16%

profile of v7, /device:TPU:0, one launch (start us, length us, event | category | flops | bytes accessed | tf_op | source)
XLA Modules:
  0.0 48.5 jit_solution(5900827520544324732)
XLA Ops:
  0.6 4.1 %collective-permute-start.3 = (bf16[128,512]{1,0:T(8,128)(2,1)}, bf16[128,512]{1,0:T(8,128)(2,1)S(1)}, u32[]{:S(2)}, u32[]{:S(2)}) collective-permute-start(bf16[128,512]{1,0:T(8,128)(2,1)} %w_ref.1), channel_id=1, source_target_pairs={{0,8},{1,9},{2,10},{3,11},{4,12},{5,13},{6,14},{7,15},{8,0},{9,1},... | collective-permute-start | bytes 393224 | tf_op jit(solution)/shard_map/ppermute | solution.py:341
  4.7 1.5 %collective-permute-start = (bf16[128,512]{1,0:T(8,128)(2,1)}, bf16[128,512]{1,0:T(8,128)(2,1)S(1)}, u32[]{:S(2)}, u32[]{:S(2)}) collective-permute-start(bf16[128,512]{1,0:T(8,128)(2,1)} %x_ref.1), channel_id=1, source_target_pairs={{0,2},{1,3},{2,0},{3,1},{4,6},{5,7},{6,4},{7,5},{8,10},{9,11},{10,... | collective-permute-start | bytes 393224 | tf_op jit(solution)/shard_map/ppermute | solution.py:341
  6.3 1.6 %collective-permute-start.1 = (bf16[128,512]{1,0:T(8,128)(2,1)}, bf16[128,512]{1,0:T(8,128)(2,1)S(1)}, u32[]{:S(2)}, u32[]{:S(2)}) collective-permute-start(bf16[128,512]{1,0:T(8,128)(2,1)} %x_ref.1), channel_id=1, source_target_pairs={{0,4},{1,5},{2,6},{3,7},{4,0},{5,1},{6,2},{7,3},{8,12},{9,13},{10,... | collective-permute-start | bytes 393224 | tf_op jit(solution)/shard_map/ppermute | solution.py:341
  9.0 0.9 %copy-done = bf16[128,512]{1,0:T(8,128)(2,1)S(1)} copy-done((bf16[128,512]{1,0:T(8,128)(2,1)S(1)}, bf16[128,512]{1,0:T(8,128)(2,1)}, u32[]{:S(2)}) %copy-start) | copy-done | bytes 131096
  9.9 0.9 %copy-done.1 = bf16[128,512]{1,0:T(8,128)(2,1)S(1)} copy-done((bf16[128,512]{1,0:T(8,128)(2,1)S(1)}, bf16[128,512]{1,0:T(8,128)(2,1)}, u32[]{:S(2)}) %copy-start.1) | copy-done | bytes 131096
  11.5 2.0 %collective-permute-done.6 = bf16[128]{0:T(256)(128)(2,1)S(1)} collective-permute-done((bf16[128]{0:T(256)(128)(2,1)}, bf16[128]{0:T(256)(128)(2,1)S(1)}, u32[]{:S(2)}, u32[]{:S(2)}) %collective-permute-start.6) | collective-permute-done | bytes 288 | tf_op jit(solution)/shard_map/ppermute | solution.py:341
  14.5 1.2 %collective-permute-done.2.refs_3_.refs_5_ = bf16[128,512]{1,0:T(8,128)(2,1)S(1)} collective-permute-done((bf16[128,512]{1,0:T(8,128)(2,1)}, bf16[128,512]{1,0:T(8,128)(2,1)S(1)}, u32[]{:S(2)}, u32[]{:S(2)}) %collective-permute-start.2) | collective-permute-done | bytes 131104 | tf_op jit(solution)/shard_map/ppermute | solution.py:341
  15.8 1.3 %forward.1 = (bf16[512,512]{1,0:T(8,128)(2,1)S(1)}, f32[32,256]{1,0:T(8,128)S(1)}, f32[32,256]{1,0:T(8,128)S(1)}) custom-call(bf16[128,512]{1,0:T(8,128)(2,1)S(1)} %get-tuple-element.31.refs_0_.refs_2_, bf16[128,512]{1,0:T(8,128)(2,1)S(1)} %collective-permute-done.refs_1_.refs_3_, bf16[128,512]{1,0:T(8,128)(2,1)S(1)} %collective-permute-done.1.refs_2_.refs_4_, ...), custom_call_target="tpu_custom_call" | custom-call | bytes 2196480 | tf_op jit(solution)/shard_map/forward/pallas_call | solution.py:313
  17.1 1.2 %collective-permute-done.9 = f32[32,256]{1,0:T(8,128)S(1)} collective-permute-done((f32[32,256]{1,0:T(8,128)S(1)}, f32[32,256]{1,0:T(8,128)S(1)}, u32[]{:S(2)}, u32[]{:S(2)}) %collective-permute-start.9) | collective-permute-done | bytes 32800 | tf_op jit(solution)/shard_map/ppermute | solution.py:341
  18.3 2.8 %collective-permute-start.13 = (f32[32,256]{1,0:T(8,128)S(1)}, f32[32,256]{1,0:T(8,128)S(1)}, u32[]{:S(2)}, u32[]{:S(2)}) collective-permute-start(f32[32,256]{1,0:T(8,128)S(1)} %add.9), channel_id=1, source_target_pairs={{0,8},{1,9},{2,10},{3,11},{4,12},{5,13},{6,14},{7,15},{8,0},{9,1},... | collective-permute-start | bytes 98312 | tf_op jit(solution)/shard_map/ppermute | solution.py:341
  21.4 2.8 %collective-permute-start.10 = (bf16[32,512]{1,0:T(8,128)(2,1)S(1)}, bf16[32,512]{1,0:T(8,128)(2,1)S(1)}, u32[]{:S(2)}, u32[]{:S(2)}) collective-permute-start(bf16[32,512]{1,0:T(8,128)(2,1)S(1)} %lead.1.refs_12_), channel_id=1, source_target_pairs={{0,8},{1,9},{2,10},{3,11},{4,12},{5,13},{6,14},{7,15},{8,0},{9,1},... | collective-permute-start | bytes 98312 | tf_op jit(solution)/shard_map/ppermute | solution.py:341
  24.2 1.5 %collective-permute-start.14 = (f32[32,256]{1,0:T(8,128)S(1)}, f32[32,256]{1,0:T(8,128)S(1)}, u32[]{:S(2)}, u32[]{:S(2)}) collective-permute-start(f32[32,256]{1,0:T(8,128)S(1)} %add.10.refs_0_), channel_id=1, source_target_pairs={{0,2},{1,3},{2,0},{3,1},{4,6},{5,7},{6,4},{7,5},{8,10},{9,11},{10,... | collective-permute-start | bytes 98312 | tf_op jit(solution)/shard_map/ppermute | solution.py:341
  26.5 1.3 %collective-permute-start.16 = (f32[32,256]{1,0:T(8,128)S(1)}, f32[32,256]{1,0:T(8,128)S(1)}, u32[]{:S(2)}, u32[]{:S(2)}) collective-permute-start(f32[32,256]{1,0:T(8,128)S(1)} %add.10.refs_0_), channel_id=1, source_target_pairs={{0,6},{1,7},{2,4},{3,5},{4,2},{5,3},{6,0},{7,1},{8,14},{9,15},{10,... | collective-permute-start | bytes 98312 | tf_op jit(solution)/shard_map/ppermute | solution.py:341
  28.3 1.8 %inverse.1.inverse_ref = f32[32,32]{1,0:T(8,128)S(1)} custom-call(bf16[4,32,512]{2,1,0:T(8,128)(2,1)S(1)} %pad_maximum_fusion.small_ref), custom_call_target="tpu_custom_call" | custom-call | bytes 135168 | tf_op jit(solution)/shard_map/inverse/pallas_call | solution.py:313
  30.1 1.2 %collective-permute-done.16.refs_3_ = f32[32,256]{1,0:T(8,128)S(1)} collective-permute-done((f32[32,256]{1,0:T(8,128)S(1)}, f32[32,256]{1,0:T(8,128)S(1)}, u32[]{:S(2)}, u32[]{:S(2)}) %collective-permute-start.16) | collective-permute-done | bytes 32800 | tf_op jit(solution)/shard_map/ppermute | solution.py:341
  31.3 1.4 %solve.1.refs_0_ = f32[64,256]{1,0:T(8,128)S(1)} custom-call(f32[32,32]{1,0:T(8,128)S(1)} %inverse.1.inverse_ref, bf16[32,2048]{1,0:T(8,128)(2,1)S(1)} %get-tuple-element.41.design_ref, bf16[2048,128]{1,0:T(8,128)(2,1)S(1)} %get-tuple-element.38.rows_ref, f32[1,512]{1,0:T(1,128)S(1)} %get-tuple-element.39.thresh_ref, ...), custom_call_target="tpu_custom_call" | custom-call | bytes 860160 | tf_op jit(solution)/shard_map/solve/pallas_call | solution.py:313
  32.8 0.9 %slope.1.slope_ref = f32[512,512]{1,0:T(8,128)S(1)} custom-call(bf16[128,512]{1,0:T(8,128)(2,1)S(1)} %get-tuple-element.31.refs_0_.refs_2_, bf16[128,512]{1,0:T(8,128)(2,1)S(1)} %collective-permute-done.refs_1_.refs_3_, bf16[128,512]{1,0:T(8,128)(2,1)S(1)} %collective-permute-done.1.refs_2_.refs_4_, ...), custom_call_target="tpu_custom_call" | custom-call | bytes 2098176 | tf_op jit(solution)/shard_map/slope/pallas_call | solution.py:313
  34.0 0.9 %weight_side.1 = (bf16[128,512]{1,0:T(8,128)(2,1)S(1)}, bf16[512,512]{1,0:T(8,128)(2,1)S(1)}, bf16[128,512]{1,0:T(8,128)(2,1)S(1)}, bf16[128,512]{1,0:T(8,128)(2...) custom-call(bf16[512,512]{1,0:T(8,128)(2,1)S(1)} %get-tuple-element.33.refs_13_.member_ref, ...), custom_call_target="tpu_custom_call" | custom-call | bytes 3932160 | tf_op jit(solution)/shard_map/weight_side/pallas_call | solution.py:313
  35.8 1.4 %collective-permute-start.20 = (bf16[128,512]{1,0:T(8,128)(2,1)S(1)}, bf16[128,512]{1,0:T(8,128)(2,1)S(1)}, u32[]{:S(2)}, u32[]{:S(2)}) collective-permute-start(bf16[128,512]{1,0:T(8,128)(2,1)S(1)} %get-tuple-element.51), channel_id=1, source_target_pairs={{0,4},{1,5},{2,6},{3,7},{4,0},{5,1},{6,2},{7,3},{8,12},{9,13},{10,... | collective-permute-start | bytes 393224 | tf_op jit(solution)/shard_map/ppermute | solution.py:341
  37.9 1.8 %collective-permute-start.23 = (bf16[128,512]{1,0:T(8,128)(2,1)S(1)}, bf16[128,512]{1,0:T(8,128)(2,1)S(1)}, u32[]{:S(2)}, u32[]{:S(2)}) collective-permute-start(bf16[128,512]{1,0:T(8,128)(2,1)S(1)} %add_convert_fusion), channel_id=1, source_target_pairs={{0,8},{1,9},{2,10},{3,11},{4,12},{5,13},{6,14},{7,15},{8,0},{9,1},... | collective-permute-start | bytes 393224 | tf_op jit(solution)/shard_map/ppermute | solution.py:341
  39.7 1.1 %collective-permute-start.19 = (bf16[128,512]{1,0:T(8,128)(2,1)S(1)}, bf16[128,512]{1,0:T(8,128)(2,1)S(1)}, u32[]{:S(2)}, u32[]{:S(2)}) collective-permute-start(bf16[128,512]{1,0:T(8,128)(2,1)S(1)} %get-tuple-element.50), channel_id=1, source_target_pairs={{0,2},{1,3},{2,0},{3,1},{4,6},{5,7},{6,4},{7,5},{8,10},{9,11},{10,... | collective-permute-start | bytes 393224 | tf_op jit(solution)/shard_map/ppermute | solution.py:341
  40.8 3.2 %loss.1 = (f32[8,128]{1,0:T(8,128)S(1)}, f32[128,128]{1,0:T(8,128)S(1)}) custom-call(bf16[2048,128]{1,0:T(8,128)(2,1)S(1)} %get-tuple-element.38.rows_ref, f32[1,512]{1,0:T(1,128)S(1)} %get-tuple-element.39.thresh_ref, f32[1,512]{1,0:T(1,128)S(1)} %get-tuple-element.40.rate_ref, f32[64,256]{1,0:T(8,128)S(1)} %solve.1.refs_0_, ...), custom_call_target="tpu_custom_call" | custom-call | bytes 729088 | tf_op jit(solution)/shard_map/loss/pallas_call | solution.py:313
  45.0 2.3 %collective-permute-done.21.refs_3_ = bf16[128,512]{1,0:T(8,128)(2,1)S(1)} collective-permute-done((bf16[128,512]{1,0:T(8,128)(2,1)S(1)}, bf16[128,512]{1,0:T(8,128)(2,1)S(1)}, u32[]{:S(2)}, u32[]{:S(2)}) %collective-permute-start.21) | collective-permute-done | bytes 131104 | tf_op jit(solution)/shard_map/ppermute | solution.py:341
  47.7 0.9 %sums.1 = (f32[128,512]{1,0:T(8,128)}, f32[128,512]{1,0:T(8,128)}) custom-call(f32[128,128]{1,0:T(8,128)S(1)} %get-tuple-element.43.own_ref, bf16[128,512]{1,0:T(8,128)(2,1)S(1)} %get-tuple-element.47.refs_0_, bf16[128,512]{1,0:T(8,128)(2,1)S(1)} %collective-permute-done.19.refs_1_, bf16[128,512]{1,0:T(8,128)(2,1)S(1)} %collective-permute-done.20.refs_2_, ...), custom_call_target="tpu_custom_call" | custom-call | bytes 1507328 | tf_op jit(solution)/shard_map/sums/pallas_call | solution.py:313
  (54 shorter events, 8.0 us)
Async XLA Ops:
  0.6 12.8 %collective-permute-start.3 = (bf16[128,512]{1,0:T(8,128)(2,1)}, bf16[128,512]{1,0:T(8,128)(2,1)S(1)}, u32[]{:S(2)}, u32[]{:S(2)}) collective-permute-start(bf16[128,512]{1,0:T(8,128)(2,1)} %w_ref.1), channel_id=1, source_target_pairs={{0,8},{1,9},{2,10},{3,11},{4,12},{5,13},{6,14},{7,15},{8,0},{9,1},... | collective-permute-start | bytes 393224 | tf_op jit(solution)/shard_map/ppermute | solution.py:341
  4.7 9.3 %collective-permute-start = (bf16[128,512]{1,0:T(8,128)(2,1)}, bf16[128,512]{1,0:T(8,128)(2,1)S(1)}, u32[]{:S(2)}, u32[]{:S(2)}) collective-permute-start(bf16[128,512]{1,0:T(8,128)(2,1)} %x_ref.1), channel_id=1, source_target_pairs={{0,2},{1,3},{2,0},{3,1},{4,6},{5,7},{6,4},{7,5},{8,10},{9,11},{10,... | collective-permute-start | bytes 393224 | tf_op jit(solution)/shard_map/ppermute | solution.py:341
  6.3 7.8 %collective-permute-start.1 = (bf16[128,512]{1,0:T(8,128)(2,1)}, bf16[128,512]{1,0:T(8,128)(2,1)S(1)}, u32[]{:S(2)}, u32[]{:S(2)}) collective-permute-start(bf16[128,512]{1,0:T(8,128)(2,1)} %x_ref.1), channel_id=1, source_target_pairs={{0,4},{1,5},{2,6},{3,7},{4,0},{5,1},{6,2},{7,3},{8,12},{9,13},{10,... | collective-permute-start | bytes 393224 | tf_op jit(solution)/shard_map/ppermute | solution.py:341
  7.8 7.8 %collective-permute-start.2 = (bf16[128,512]{1,0:T(8,128)(2,1)}, bf16[128,512]{1,0:T(8,128)(2,1)S(1)}, u32[]{:S(2)}, u32[]{:S(2)}) collective-permute-start(bf16[128,512]{1,0:T(8,128)(2,1)} %x_ref.1), channel_id=1, source_target_pairs={{0,6},{1,7},{2,4},{3,5},{4,2},{5,3},{6,0},{7,1},{8,14},{9,15},{10,... | collective-permute-start | bytes 393224 | tf_op jit(solution)/shard_map/ppermute | solution.py:341
  8.2 5.2 %collective-permute-start.6 = (bf16[128]{0:T(256)(128)(2,1)}, bf16[128]{0:T(256)(128)(2,1)S(1)}, u32[]{:S(2)}, u32[]{:S(2)}) collective-permute-start(bf16[128]{0:T(256)(128)(2,1)} %param.9), channel_id=1, source_target_pairs={{0,8},{1,9},{2,10},{3,11},{4,12},{5,13},{6,14},{7,15},{8,0},{9,1},... | collective-permute-start | bytes 776 | tf_op jit(solution)/shard_map/ppermute | solution.py:341
  13.5 2.3 %collective-permute-start.4 = (bf16[128,512]{1,0:T(8,128)(2,1)S(1)}, bf16[128,512]{1,0:T(8,128)(2,1)S(1)}, u32[]{:S(2)}, u32[]{:S(2)}) collective-permute-start(bf16[128,512]{1,0:T(8,128)(2,1)S(1)} %copy-done.1), channel_id=1, source_target_pairs={{0,1},{1,0},{2,3},{3,2},{4,5},{5,4},{6,7},{7,6},{8,9},{9,8},{10,11... | collective-permute-start | bytes 393224 | tf_op jit(solution)/shard_map/ppermute | solution.py:341
  13.5 2.3 %collective-permute-start.5 = (bf16[128,512]{1,0:T(8,128)(2,1)S(1)}, bf16[128,512]{1,0:T(8,128)(2,1)S(1)}, u32[]{:S(2)}, u32[]{:S(2)}) collective-permute-start(bf16[128,512]{1,0:T(8,128)(2,1)S(1)} %collective-permute-done.3.refs_5_.refs_1_), channel_id=1, source_target_pairs={{0,1},{1,0},{2,3},{3,2},{4,5},{5,4},{6,7},{7,6},{8,9},{9,8},{10,11... | collective-permute-start | bytes 393224 | tf_op jit(solution)/shard_map/ppermute | solution.py:341
  14.0 1.8 %collective-permute-start.7 = (bf16[128]{0:T(256)(128)(2,1)S(1)}, bf16[128]{0:T(256)(128)(2,1)S(1)}, u32[]{:S(2)}, u32[]{:S(2)}) collective-permute-start(bf16[128]{0:T(256)(128)(2,1)S(1)} %copy-done.5), channel_id=1, source_target_pairs={{0,1},{1,0},{2,3},{3,2},{4,5},{5,4},{6,7},{7,6},{8,9},{9,8},{10,11... | collective-permute-start | bytes 776 | tf_op jit(solution)/shard_map/ppermute | solution.py:341
  14.1 1.7 %collective-permute-start.8 = (bf16[128]{0:T(256)(128)(2,1)S(1)}, bf16[128]{0:T(256)(128)(2,1)S(1)}, u32[]{:S(2)}, u32[]{:S(2)}) collective-permute-start(bf16[128]{0:T(256)(128)(2,1)S(1)} %collective-permute-done.6), channel_id=1, source_target_pairs={{0,1},{1,0},{2,3},{3,2},{4,5},{5,4},{6,7},{7,6},{8,9},{9,8},{10,11... | collective-permute-start | bytes 776 | tf_op jit(solution)/shard_map/ppermute | solution.py:341
  17.1 1.3 %collective-permute-start.9 = (f32[32,256]{1,0:T(8,128)S(1)}, f32[32,256]{1,0:T(8,128)S(1)}, u32[]{:S(2)}, u32[]{:S(2)}) collective-permute-start(f32[32,256]{1,0:T(8,128)S(1)} %get-tuple-element.36), channel_id=1, source_target_pairs={{0,1},{1,0},{2,3},{3,2},{4,5},{5,4},{6,7},{7,6},{8,9},{9,8},{10,11... | collective-permute-start | bytes 98312 | tf_op jit(solution)/shard_map/ppermute | solution.py:341
  18.3 5.8 %collective-permute-start.13 = (f32[32,256]{1,0:T(8,128)S(1)}, f32[32,256]{1,0:T(8,128)S(1)}, u32[]{:S(2)}, u32[]{:S(2)}) collective-permute-start(f32[32,256]{1,0:T(8,128)S(1)} %add.9), channel_id=1, source_target_pairs={{0,8},{1,9},{2,10},{3,11},{4,12},{5,13},{6,14},{7,15},{8,0},{9,1},... | collective-permute-start | bytes 98312 | tf_op jit(solution)/shard_map/ppermute | solution.py:341
  21.1 5.3 %collective-permute-start.11 = (bf16[32,512]{1,0:T(8,128)(2,1)S(1)}, bf16[32,512]{1,0:T(8,128)(2,1)S(1)}, u32[]{:S(2)}, u32[]{:S(2)}) collective-permute-start(bf16[32,512]{1,0:T(8,128)(2,1)S(1)} %lead.1.refs_12_), channel_id=1, source_target_pairs={{0,1},{1,0},{2,3},{3,2},{4,5},{5,4},{6,7},{7,6},{8,9},{9,8},{10,11... | collective-permute-start | bytes 98312 | tf_op jit(solution)/shard_map/ppermute | solution.py:341
  21.1 6.6 %collective-permute-start.12 = (bf16[32,512]{1,0:T(8,128)(2,1)S(1)}, bf16[32,512]{1,0:T(8,128)(2,1)S(1)}, u32[]{:S(2)}, u32[]{:S(2)}) collective-permute-start(bf16[32,512]{1,0:T(8,128)(2,1)S(1)} %lead.1.refs_12_), channel_id=1, source_target_pairs={{0,9},{1,8},{2,11},{3,10},{4,13},{5,12},{6,15},{7,14},{8,1},{9,0},... | collective-permute-start | bytes 98312 | tf_op jit(solution)/shard_map/ppermute | solution.py:341
  21.4 6.4 %collective-permute-start.10 = (bf16[32,512]{1,0:T(8,128)(2,1)S(1)}, bf16[32,512]{1,0:T(8,128)(2,1)S(1)}, u32[]{:S(2)}, u32[]{:S(2)}) collective-permute-start(bf16[32,512]{1,0:T(8,128)(2,1)S(1)} %lead.1.refs_12_), channel_id=1, source_target_pairs={{0,8},{1,9},{2,10},{3,11},{4,12},{5,13},{6,14},{7,15},{8,0},{9,1},... | collective-permute-start | bytes 98312 | tf_op jit(solution)/shard_map/ppermute | solution.py:341
  24.2 5.9 %collective-permute-start.14 = (f32[32,256]{1,0:T(8,128)S(1)}, f32[32,256]{1,0:T(8,128)S(1)}, u32[]{:S(2)}, u32[]{:S(2)}) collective-permute-start(f32[32,256]{1,0:T(8,128)S(1)} %add.10.refs_0_), channel_id=1, source_target_pairs={{0,2},{1,3},{2,0},{3,1},{4,6},{5,7},{6,4},{7,5},{8,10},{9,11},{10,... | collective-permute-start | bytes 98312 | tf_op jit(solution)/shard_map/ppermute | solution.py:341
  25.7 4.3 %collective-permute-start.15 = (f32[32,256]{1,0:T(8,128)S(1)}, f32[32,256]{1,0:T(8,128)S(1)}, u32[]{:S(2)}, u32[]{:S(2)}) collective-permute-start(f32[32,256]{1,0:T(8,128)S(1)} %add.10.refs_0_), channel_id=1, source_target_pairs={{0,4},{1,5},{2,6},{3,7},{4,0},{5,1},{6,2},{7,3},{8,12},{9,13},{10,... | collective-permute-start | bytes 98312 | tf_op jit(solution)/shard_map/ppermute | solution.py:341
  26.5 4.8 %collective-permute-start.16 = (f32[32,256]{1,0:T(8,128)S(1)}, f32[32,256]{1,0:T(8,128)S(1)}, u32[]{:S(2)}, u32[]{:S(2)}) collective-permute-start(f32[32,256]{1,0:T(8,128)S(1)} %add.10.refs_0_), channel_id=1, source_target_pairs={{0,6},{1,7},{2,4},{3,5},{4,2},{5,3},{6,0},{7,1},{8,14},{9,15},{10,... | collective-permute-start | bytes 98312 | tf_op jit(solution)/shard_map/ppermute | solution.py:341
  32.7 1.3 %collective-permute-start.17 = (f32[64,256]{1,0:T(8,128)S(1)}, f32[64,256]{1,0:T(8,128)S(1)}, u32[]{:S(2)}, u32[]{:S(2)}) collective-permute-start(f32[64,256]{1,0:T(8,128)S(1)} %solve.1.refs_0_), channel_id=1, source_target_pairs={{0,1},{1,0},{2,3},{3,2},{4,5},{5,4},{6,7},{7,6},{8,9},{9,8},{10,11... | collective-permute-start | bytes 196616 | tf_op jit(solution)/shard_map/ppermute | solution.py:341
  34.9 2.9 %collective-permute-start.18 = (bf16[128,512]{1,0:T(8,128)(2,1)S(1)}, bf16[128,512]{1,0:T(8,128)(2,1)S(1)}, u32[]{:S(2)}, u32[]{:S(2)}) collective-permute-start(bf16[128,512]{1,0:T(8,128)(2,1)S(1)} %get-tuple-element.49), channel_id=1, source_target_pairs={{0,1},{1,0},{2,3},{3,2},{4,5},{5,4},{6,7},{7,6},{8,9},{9,8},{10,11... | collective-permute-start | bytes 393224 | tf_op jit(solution)/shard_map/ppermute | solution.py:341
  35.8 9.2 %collective-permute-start.20 = (bf16[128,512]{1,0:T(8,128)(2,1)S(1)}, bf16[128,512]{1,0:T(8,128)(2,1)S(1)}, u32[]{:S(2)}, u32[]{:S(2)}) collective-permute-start(bf16[128,512]{1,0:T(8,128)(2,1)S(1)} %get-tuple-element.51), channel_id=1, source_target_pairs={{0,4},{1,5},{2,6},{3,7},{4,0},{5,1},{6,2},{7,3},{8,12},{9,13},{10,... | collective-permute-start | bytes 393224 | tf_op jit(solution)/shard_map/ppermute | solution.py:341
  37.2 10.1 %collective-permute-start.21 = (bf16[128,512]{1,0:T(8,128)(2,1)S(1)}, bf16[128,512]{1,0:T(8,128)(2,1)S(1)}, u32[]{:S(2)}, u32[]{:S(2)}) collective-permute-start(bf16[128,512]{1,0:T(8,128)(2,1)S(1)} %get-tuple-element.52), channel_id=1, source_target_pairs={{0,6},{1,7},{2,4},{3,5},{4,2},{5,3},{6,0},{7,1},{8,14},{9,15},{10,... | collective-permute-start | bytes 393224 | tf_op jit(solution)/shard_map/ppermute | solution.py:341
  37.9 9.4 %collective-permute-start.23 = (bf16[128,512]{1,0:T(8,128)(2,1)S(1)}, bf16[128,512]{1,0:T(8,128)(2,1)S(1)}, u32[]{:S(2)}, u32[]{:S(2)}) collective-permute-start(bf16[128,512]{1,0:T(8,128)(2,1)S(1)} %add_convert_fusion), channel_id=1, source_target_pairs={{0,8},{1,9},{2,10},{3,11},{4,12},{5,13},{6,14},{7,15},{8,0},{9,1},... | collective-permute-start | bytes 393224 | tf_op jit(solution)/shard_map/ppermute | solution.py:341
  39.7 7.6 %collective-permute-start.22 = (bf16[128,512]{1,0:T(8,128)(2,1)S(1)}, bf16[128,512]{1,0:T(8,128)(2,1)S(1)}, u32[]{:S(2)}, u32[]{:S(2)}) collective-permute-start(bf16[128,512]{1,0:T(8,128)(2,1)S(1)} %get-tuple-element.55), channel_id=1, source_target_pairs={{0,1},{1,0},{2,3},{3,2},{4,5},{5,4},{6,7},{7,6},{8,9},{9,8},{10,11... | collective-permute-start | bytes 393224 | tf_op jit(solution)/shard_map/ppermute | solution.py:341
  39.7 8.0 %collective-permute-start.19 = (bf16[128,512]{1,0:T(8,128)(2,1)S(1)}, bf16[128,512]{1,0:T(8,128)(2,1)S(1)}, u32[]{:S(2)}, u32[]{:S(2)}) collective-permute-start(bf16[128,512]{1,0:T(8,128)(2,1)S(1)} %get-tuple-element.50), channel_id=1, source_target_pairs={{0,2},{1,3},{2,0},{3,1},{4,6},{5,7},{6,4},{7,5},{8,10},{9,11},{10,... | collective-permute-start | bytes 393224 | tf_op jit(solution)/shard_map/ppermute | solution.py:341
  (7 other events, 14.1 us)

commit v8 on v7

--- a/solution.py
+++ b/solution.py
@@ -64,14 +64,13 @@
     return jnp.where(x >= 0.0, 1.0, small) / (1.0 + small)
 
 
-def each_chunk(size, step):
+def each_chunk(size, step, first):
     count = size // CHUNK
 
     def body(i, carry):
-        step(pl.ds(pl.multiple_of(i * CHUNK, CHUNK), CHUNK))
-        return carry
-
-    lax.fori_loop(0, count, body, 0, unroll=count <= 8)
+        return step(carry, pl.ds(pl.multiple_of(i * CHUNK, CHUNK), CHUNK))
+
+    return lax.fori_loop(0, count, body, first, unroll=count <= 8)
 
 
 def invert(matrix):
@@ -201,7 +200,7 @@
 def solve_kernel(
     terms, inverse_ref, design_ref, rows_ref, thresh_ref, rate_ref, *refs
 ):
-    solved_ref, turn_ref, total_ref = refs[terms:]
+    solved_ref, turn_ref = refs[terms:]
     moment = refs[0][...]
     for ref in refs[1:terms]:
         moment = moment + ref[...]
@@ -212,17 +211,16 @@
     is_constant = rows(coeffs.shape) == CONSTANT
     shifted = coeffs - jnp.where(is_constant, thresh_ref[:, :size], 0.0)
     turn_ref[...] = three_rows(-LOG2_E * shifted)
-    total_ref[...] = jnp.zeros(total_ref.shape, F32)
-
-    def seeds(here):
+
+    def seeds(total, here):
         power = jnp.exp2(jnp.minimum(dot(rows_ref[here], turn_ref[...]), 126.0))
         below = 1.0 + power
         seed = pl.reciprocal(below, approx=True)
         seed = (seed * (2.0 - below * seed)).astype(BF16)
-        total_ref[...] += dot(design_ref[:, here], seed)
-
-    each_chunk(rows_ref.shape[0], seeds)
-    solved_ref[:REGRESSORS] = dot(inverse, total_ref[...] * rate_ref[:, :size], precision=PRECISE)
+        return total + dot(design_ref[:, here], seed)
+
+    total = each_chunk(rows_ref.shape[0], seeds, jnp.zeros((REGRESSORS, size), F32))
+    solved_ref[:REGRESSORS] = dot(inverse, total * rate_ref[:, :size], precision=PRECISE)
 
 
 def joined(refs, part):
@@ -264,20 +262,19 @@
 
 
 def loss_kernel(rows_ref, thresh_ref, rate_ref, *refs):
-    solved_refs, (loss_ref, own_ref, split_ref, total_ref) = refs[:-4], refs[-4:]
+    solved_refs, (loss_ref, own_ref, split_ref) = refs[:-3], refs[-3:]
     adjoint = joined(solved_refs, 0)
     coeffs = joined(solved_refs, 1)
     thresh = thresh_ref[...]
     rate = rate_ref[...]
     split_ref[...] = three_rows(coeffs)
-    total_ref[...] = jnp.zeros(total_ref.shape, F32)
-
-    def losses(here):
+
+    def losses(total, here):
         loss = softplus(dot(rows_ref[here], split_ref[...]) - thresh)
-        total_ref[...] += jnp.sum(loss.reshape(-1, *total_ref.shape), axis=0)
-
-    each_chunk(rows_ref.shape[0], losses)
-    summed = jnp.sum(jnp.sum(total_ref[...] * rate, axis=0, keepdims=True), axis=1, keepdims=True)
+        return total + jnp.sum(loss.reshape(-1, *total.shape), axis=0)
+
+    total = each_chunk(rows_ref.shape[0], losses, jnp.zeros((SUBLANES, coeffs.shape[1]), F32))
+    summed = jnp.sum(jnp.sum(total * rate, axis=0, keepdims=True), axis=1, keepdims=True)
     loss_ref[...] = jnp.broadcast_to(
         summed / (rows_ref.shape[0] * coeffs.shape[1]), loss_ref.shape
     )
@@ -348,16 +345,18 @@
     def after(x, *others):
         return lax.optimization_barrier((x, *others))[0]
 
-    def direct(slots, bits):
-        return [swap(x, mask) for x, mask in zip(slots[1:], masks(bits)[1:])]
-
+    def direct(slots, masks):
+        return [swap(x, mask) for x, mask in zip(slots[1:], masks[1:])]
+
+    outer_masks = masks(outer_bits)
+    inner_masks = [0] + masks(inner_bits)[:0:-1]
     first_bit = outer_bits[0]
     weights = [proxy_weight, swap(proxy_weight, 1 << first_bit)]
-    basis = [path_basis] + direct([path_basis] * inner, inner_bits)
+    basis = [path_basis] + direct([path_basis] * inner, inner_masks)
     notionals = [notional, swap(notional, 1 << first_bit)]
 
     member, thresh, rate, basis[0], own_weight = call(
-        partial(tables_kernel, masks(outer_bits)),
+        partial(tables_kernel, outer_masks),
         [
             ((sets, group_trades), BF16),
             ((1, sets), F32),
@@ -391,12 +390,12 @@
     )
     moment = moments[0] + swap(moments[1], SHARES - 1)
     lead = after(lead, moment)
-    leads = [lead] + direct([lead] * outer, outer_bits)
+    leads = [lead] + direct([lead] * outer, outer_masks)
     for bit in outer_bits[:-1]:
         there = swap(moment, 1 << bit)
         moment = moment + there
     small = jnp.stack(leads)
-    moments = [moment] + direct([moment] * inner, inner_bits)
+    moments = [moment] + direct([moment] * inner, inner_masks)
     (inverse,) = call(
         partial(inverse_kernel, RIDGE_SCALE * paths_all),
         [((REGRESSORS, REGRESSORS), F32)],
@@ -414,7 +413,7 @@
         [((2 * REGRESSORS, share), F32)],
         inverse, design_all, design_rows, thresh, rate, *moments,
         name="solve",
-        scratch=[pltpu.VMEM((LANES, share), BF16), pltpu.VMEM((REGRESSORS, share), F32)],
+        scratch=[pltpu.VMEM((LANES, share), BF16)],
     )
     solved = [solved, swap(solved, SHARES - 1)]
     (slope,) = call(
@@ -450,16 +449,16 @@
             arrived = swap(gone, 1 << bit)
             terms[k].append(arrived)
             if bit == outer_bits[-1] and k == count - 1:
-                basis_parts[1] = after(basis_parts[1], arrived)
+                basis_parts[-1] = after(basis_parts[-1], arrived)
         terms = terms[:count]
     weight_terms = terms[0]
-    basis_terms = [basis_parts[0]] + direct(basis_parts, inner_bits)
+    basis_terms = [basis_parts[0]] + direct(basis_parts, inner_masks)
     loss, own_adjoint = call(
         loss_kernel,
         [((8, LANES), F32), ((path_rows, LANES), F32)],
         design_rows, thresh, rate, *solved,
         name="loss",
-        scratch=[pltpu.VMEM((LANES, sets), BF16), pltpu.VMEM((8, sets), F32)],
+        scratch=[pltpu.VMEM((LANES, sets), BF16)],
     )
     basis_adjoint, weight_adjoint = call(
         partial(sum_kernel, len(basis_terms)),

time: 48.7 us -> 48.2 us (0.990)
  transfers between devices with their start and end apart: 24 -> 24, of which waited for: 8 -> 9; matrix products, arithmetic and copies ran while one was open for 1% -> 1% of each run, Pallas kernels for 16% -> 16%
where the time goes in v8:
time: 48.2 us; the launch traced here: 48.1 us
  starting transfers between devices  23 us (48%)
  Pallas kernels  12.2 us (25%)
  waiting for transfers between devices  9 us (19%)
  local copies, waits for them, and re-layouts  3.02 us (6%)
  between operations  0.76 us (2%)
    ppermute x24, starting transfers between devices, swap(): return lax.ppermute(x, 'paths', [(d, d ^ mask) for d in range(n)])  23 us
    pallas_call x11, Pallas kernels, call(): pl.pallas_call(kernel, out_shape=[jax.ShapeDtypeStruct(s, d) for s, d in...  12.2 us
    ppermute x24, waiting for transfers between devices, swap(): return lax.ppermute(x, 'paths', [(d, d ^ mask) for d in range(n)])  9 us
    unnamed x14, local copies, waits for them, and re-layouts  2.51 us
  transfers between devices with their start and end apart: 24, of which 9 were waited for; matrix products, arithmetic and copies ran while one was open for 1% of the time, Pallas kernels for 16%

profile of v8, /device:TPU:0, one launch (start us, length us, event | category | flops | bytes accessed | tf_op | source)
XLA Modules:
  0.0 48.1 jit_solution(1430387699787598260)
XLA Ops:
  0.6 4.1 %collective-permute-start.3 = (bf16[128,512]{1,0:T(8,128)(2,1)}, bf16[128,512]{1,0:T(8,128)(2,1)S(1)}, u32[]{:S(2)}, u32[]{:S(2)}) collective-permute-start(bf16[128,512]{1,0:T(8,128)(2,1)} %w_ref.1), channel_id=1, source_target_pairs={{0,8},{1,9},{2,10},{3,11},{4,12},{5,13},{6,14},{7,15},{8,0},{9,1},... | collective-permute-start | bytes 393224 | tf_op jit(solution)/shard_map/ppermute | solution.py:338
  4.7 2.5 %collective-permute-start = (bf16[128,512]{1,0:T(8,128)(2,1)}, bf16[128,512]{1,0:T(8,128)(2,1)S(1)}, u32[]{:S(2)}, u32[]{:S(2)}) collective-permute-start(bf16[128,512]{1,0:T(8,128)(2,1)} %x_ref.1), channel_id=1, source_target_pairs={{0,6},{1,7},{2,4},{3,5},{4,2},{5,3},{6,0},{7,1},{8,14},{9,15},{10,... | collective-permute-start | bytes 393224 | tf_op jit(solution)/shard_map/ppermute | solution.py:338
  9.0 0.9 %copy-done = bf16[128,512]{1,0:T(8,128)(2,1)S(1)} copy-done((bf16[128,512]{1,0:T(8,128)(2,1)S(1)}, bf16[128,512]{1,0:T(8,128)(2,1)}, u32[]{:S(2)}) %copy-start) | copy-done | bytes 131096
  9.9 0.9 %copy-done.1 = bf16[128,512]{1,0:T(8,128)(2,1)S(1)} copy-done((bf16[128,512]{1,0:T(8,128)(2,1)S(1)}, bf16[128,512]{1,0:T(8,128)(2,1)}, u32[]{:S(2)}) %copy-start.1) | copy-done | bytes 131096
  11.5 2.0 %collective-permute-done.6 = bf16[128]{0:T(256)(128)(2,1)S(1)} collective-permute-done((bf16[128]{0:T(256)(128)(2,1)}, bf16[128]{0:T(256)(128)(2,1)S(1)}, u32[]{:S(2)}, u32[]{:S(2)}) %collective-permute-start.6) | collective-permute-done | bytes 288 | tf_op jit(solution)/shard_map/ppermute | solution.py:338
  14.1 1.2 %collective-permute-done.1.refs_2_.refs_4_ = bf16[128,512]{1,0:T(8,128)(2,1)S(1)} collective-permute-done((bf16[128,512]{1,0:T(8,128)(2,1)}, bf16[128,512]{1,0:T(8,128)(2,1)S(1)}, u32[]{:S(2)}, u32[]{:S(2)}) %collective-permute-start.1) | collective-permute-done | bytes 131104 | tf_op jit(solution)/shard_map/ppermute | solution.py:338
  15.4 1.0 %collective-permute-done.8 = bf16[128]{0:T(256)(128)(2,1)S(1)} collective-permute-done((bf16[128]{0:T(256)(128)(2,1)S(1)}, bf16[128]{0:T(256)(128)(2,1)S(1)}, u32[]{:S(2)}, u32[]{:S(2)}) %collective-permute-start.8) | collective-permute-done | bytes 288 | tf_op jit(solution)/shard_map/ppermute | solution.py:338
  16.5 1.3 %forward.1 = (bf16[512,512]{1,0:T(8,128)(2,1)S(1)}, f32[32,256]{1,0:T(8,128)S(1)}, f32[32,256]{1,0:T(8,128)S(1)}) custom-call(bf16[128,512]{1,0:T(8,128)(2,1)S(1)} %get-tuple-element.31.refs_0_.refs_2_, bf16[128,512]{1,0:T(8,128)(2,1)S(1)} %collective-permute-done.refs_1_.refs_3_, bf16[128,512]{1,0:T(8,128)(2,1)S(1)} %collective-permute-done.1.refs_2_.refs_4_, ...), custom_call_target="tpu_custom_call" | custom-call | bytes 2196480 | tf_op jit(solution)/shard_map/forward/pallas_call | solution.py:310
  18.0 1.0 %collective-permute-done.9 = f32[32,256]{1,0:T(8,128)S(1)} collective-permute-done((f32[32,256]{1,0:T(8,128)S(1)}, f32[32,256]{1,0:T(8,128)S(1)}, u32[]{:S(2)}, u32[]{:S(2)}) %collective-permute-start.9) | collective-permute-done | bytes 32800 | tf_op jit(solution)/shard_map/ppermute | solution.py:338
  19.0 2.2 %collective-permute-start.13 = (f32[32,256]{1,0:T(8,128)S(1)}, f32[32,256]{1,0:T(8,128)S(1)}, u32[]{:S(2)}, u32[]{:S(2)}) collective-permute-start(f32[32,256]{1,0:T(8,128)S(1)} %add.9), channel_id=1, source_target_pairs={{0,8},{1,9},{2,10},{3,11},{4,12},{5,13},{6,14},{7,15},{8,0},{9,1},... | collective-permute-start | bytes 98312 | tf_op jit(solution)/shard_map/ppermute | solution.py:338
  22.0 2.2 %collective-permute-start.10 = (bf16[32,512]{1,0:T(8,128)(2,1)S(1)}, bf16[32,512]{1,0:T(8,128)(2,1)S(1)}, u32[]{:S(2)}, u32[]{:S(2)}) collective-permute-start(bf16[32,512]{1,0:T(8,128)(2,1)S(1)} %lead.1.refs_12_), channel_id=1, source_target_pairs={{0,8},{1,9},{2,10},{3,11},{4,12},{5,13},{6,14},{7,15},{8,0},{9,1},... | collective-permute-start | bytes 98312 | tf_op jit(solution)/shard_map/ppermute | solution.py:338
  24.4 1.5 %collective-permute-start.14 = (f32[32,256]{1,0:T(8,128)S(1)}, f32[32,256]{1,0:T(8,128)S(1)}, u32[]{:S(2)}, u32[]{:S(2)}) collective-permute-start(f32[32,256]{1,0:T(8,128)S(1)} %add.10.refs_0_), channel_id=1, source_target_pairs={{0,6},{1,7},{2,4},{3,5},{4,2},{5,3},{6,0},{7,1},{8,14},{9,15},{10,... | collective-permute-start | bytes 98312 | tf_op jit(solution)/shard_map/ppermute | solution.py:338
  25.9 1.3 %collective-permute-start.15 = (f32[32,256]{1,0:T(8,128)S(1)}, f32[32,256]{1,0:T(8,128)S(1)}, u32[]{:S(2)}, u32[]{:S(2)}) collective-permute-start(f32[32,256]{1,0:T(8,128)S(1)} %add.10.refs_0_), channel_id=1, source_target_pairs={{0,4},{1,5},{2,6},{3,7},{4,0},{5,1},{6,2},{7,3},{8,12},{9,13},{10,... | collective-permute-start | bytes 98312 | tf_op jit(solution)/shard_map/ppermute | solution.py:338
  28.5 1.8 %inverse.1.inverse_ref = f32[32,32]{1,0:T(8,128)S(1)} custom-call(bf16[4,32,512]{2,1,0:T(8,128)(2,1)S(1)} %pad_maximum_fusion.small_ref), custom_call_target="tpu_custom_call" | custom-call | bytes 135168 | tf_op jit(solution)/shard_map/inverse/pallas_call | solution.py:310
  31.1 1.5 %solve.1.refs_0_ = f32[64,256]{1,0:T(8,128)S(1)} custom-call(f32[32,32]{1,0:T(8,128)S(1)} %inverse.1.inverse_ref, bf16[32,2048]{1,0:T(8,128)(2,1)S(1)} %get-tuple-element.41.design_ref, bf16[2048,128]{1,0:T(8,128)(2,1)S(1)} %get-tuple-element.38.rows_ref, f32[1,512]{1,0:T(1,128)S(1)} %get-tuple-element.39.thresh_ref, ...), custom_call_target="tpu_custom_call" | custom-call | bytes 860160 | tf_op jit(solution)/shard_map/solve/pallas_call | solution.py:310
  32.6 0.9 %slope.1.slope_ref = f32[512,512]{1,0:T(8,128)S(1)} custom-call(bf16[128,512]{1,0:T(8,128)(2,1)S(1)} %get-tuple-element.31.refs_0_.refs_2_, bf16[128,512]{1,0:T(8,128)(2,1)S(1)} %collective-permute-done.refs_1_.refs_3_, bf16[128,512]{1,0:T(8,128)(2,1)S(1)} %collective-permute-done.1.refs_2_.refs_4_, ...), custom_call_target="tpu_custom_call" | custom-call | bytes 2098176 | tf_op jit(solution)/shard_map/slope/pallas_call | solution.py:310
  33.8 0.9 %weight_side.1 = (bf16[128,512]{1,0:T(8,128)(2,1)S(1)}, bf16[512,512]{1,0:T(8,128)(2,1)S(1)}, bf16[128,512]{1,0:T(8,128)(2,1)S(1)}, bf16[128,512]{1,0:T(8,128)(2...) custom-call(bf16[512,512]{1,0:T(8,128)(2,1)S(1)} %get-tuple-element.33.refs_13_.member_ref, ...), custom_call_target="tpu_custom_call" | custom-call | bytes 3932160 | tf_op jit(solution)/shard_map/weight_side/pallas_call | solution.py:310
  35.6 1.0 %collective-permute-start.18 = (bf16[128,512]{1,0:T(8,128)(2,1)S(1)}, bf16[128,512]{1,0:T(8,128)(2,1)S(1)}, u32[]{:S(2)}, u32[]{:S(2)}) collective-permute-start(bf16[128,512]{1,0:T(8,128)(2,1)S(1)} %get-tuple-element.48), channel_id=1, source_target_pairs={{0,6},{1,7},{2,4},{3,5},{4,2},{5,3},{6,0},{7,1},{8,14},{9,15},{10,... | collective-permute-start | bytes 393224 | tf_op jit(solution)/shard_map/ppermute | solution.py:338
  36.6 1.2 %collective-permute-start.19 = (bf16[128,512]{1,0:T(8,128)(2,1)S(1)}, bf16[128,512]{1,0:T(8,128)(2,1)S(1)}, u32[]{:S(2)}, u32[]{:S(2)}) collective-permute-start(bf16[128,512]{1,0:T(8,128)(2,1)S(1)} %get-tuple-element.49), channel_id=1, source_target_pairs={{0,4},{1,5},{2,6},{3,7},{4,0},{5,1},{6,2},{7,3},{8,12},{9,13},{10,... | collective-permute-start | bytes 393224 | tf_op jit(solution)/shard_map/ppermute | solution.py:338
  37.9 2.0 %collective-permute-start.23 = (bf16[128,512]{1,0:T(8,128)(2,1)S(1)}, bf16[128,512]{1,0:T(8,128)(2,1)S(1)}, u32[]{:S(2)}, u32[]{:S(2)}) collective-permute-start(bf16[128,512]{1,0:T(8,128)(2,1)S(1)} %add_convert_fusion), channel_id=1, source_target_pairs={{0,8},{1,9},{2,10},{3,11},{4,12},{5,13},{6,14},{7,15},{8,0},{9,1},... | collective-permute-start | bytes 393224 | tf_op jit(solution)/shard_map/ppermute | solution.py:338
  39.9 1.3 %collective-permute-start.21 = (bf16[128,512]{1,0:T(8,128)(2,1)S(1)}, bf16[128,512]{1,0:T(8,128)(2,1)S(1)}, u32[]{:S(2)}, u32[]{:S(2)}) collective-permute-start(bf16[128,512]{1,0:T(8,128)(2,1)S(1)} %get-tuple-element.52), channel_id=1, source_target_pairs={{0,2},{1,3},{2,0},{3,1},{4,6},{5,7},{6,4},{7,5},{8,10},{9,11},{10,... | collective-permute-start | bytes 393224 | tf_op jit(solution)/shard_map/ppermute | solution.py:338
  41.2 3.2 %loss.1 = (f32[8,128]{1,0:T(8,128)S(1)}, f32[128,128]{1,0:T(8,128)S(1)}) custom-call(bf16[2048,128]{1,0:T(8,128)(2,1)S(1)} %get-tuple-element.38.rows_ref, f32[1,512]{1,0:T(1,128)S(1)} %get-tuple-element.39.thresh_ref, f32[1,512]{1,0:T(1,128)S(1)} %get-tuple-element.40.rate_ref, f32[64,256]{1,0:T(8,128)S(1)} %solve.1.refs_0_, ...), custom_call_target="tpu_custom_call" | custom-call | bytes 729088 | tf_op jit(solution)/shard_map/loss/pallas_call | solution.py:310
  45.7 1.5 %collective-permute-done.19.refs_2_ = bf16[128,512]{1,0:T(8,128)(2,1)S(1)} collective-permute-done((bf16[128,512]{1,0:T(8,128)(2,1)S(1)}, bf16[128,512]{1,0:T(8,128)(2,1)S(1)}, u32[]{:S(2)}, u32[]{:S(2)}) %collective-permute-start.19) | collective-permute-done | bytes 131104 | tf_op jit(solution)/shard_map/ppermute | solution.py:338
  47.2 0.9 %sums.1 = (f32[128,512]{1,0:T(8,128)}, f32[128,512]{1,0:T(8,128)}) custom-call(f32[128,128]{1,0:T(8,128)S(1)} %get-tuple-element.43.own_ref, bf16[128,512]{1,0:T(8,128)(2,1)S(1)} %get-tuple-element.47.refs_0_, bf16[128,512]{1,0:T(8,128)(2,1)S(1)} %collective-permute-done.18.refs_1_, bf16[128,512]{1,0:T(8,128)(2,1)S(1)} %collective-permute-done.19.refs_2_, ...), custom_call_target="tpu_custom_call" | custom-call | bytes 1507328 | tf_op jit(solution)/shard_map/sums/pallas_call | solution.py:310
  (54 shorter events, 9.2 us)
Async XLA Ops:
  0.6 12.9 %collective-permute-start.3 = (bf16[128,512]{1,0:T(8,128)(2,1)}, bf16[128,512]{1,0:T(8,128)(2,1)S(1)}, u32[]{:S(2)}, u32[]{:S(2)}) collective-permute-start(bf16[128,512]{1,0:T(8,128)(2,1)} %w_ref.1), channel_id=1, source_target_pairs={{0,8},{1,9},{2,10},{3,11},{4,12},{5,13},{6,14},{7,15},{8,0},{9,1},... | collective-permute-start | bytes 393224 | tf_op jit(solution)/shard_map/ppermute | solution.py:338
  4.7 9.3 %collective-permute-start = (bf16[128,512]{1,0:T(8,128)(2,1)}, bf16[128,512]{1,0:T(8,128)(2,1)S(1)}, u32[]{:S(2)}, u32[]{:S(2)}) collective-permute-start(bf16[128,512]{1,0:T(8,128)(2,1)} %x_ref.1), channel_id=1, source_target_pairs={{0,6},{1,7},{2,4},{3,5},{4,2},{5,3},{6,0},{7,1},{8,14},{9,15},{10,... | collective-permute-start | bytes 393224 | tf_op jit(solution)/shard_map/ppermute | solution.py:338
  7.3 8.1 %collective-permute-start.1 = (bf16[128,512]{1,0:T(8,128)(2,1)}, bf16[128,512]{1,0:T(8,128)(2,1)S(1)}, u32[]{:S(2)}, u32[]{:S(2)}) collective-permute-start(bf16[128,512]{1,0:T(8,128)(2,1)} %x_ref.1), channel_id=1, source_target_pairs={{0,4},{1,5},{2,6},{3,7},{4,0},{5,1},{6,2},{7,3},{8,12},{9,13},{10,... | collective-permute-start | bytes 393224 | tf_op jit(solution)/shard_map/ppermute | solution.py:338
  7.7 7.6 %collective-permute-start.2 = (bf16[128,512]{1,0:T(8,128)(2,1)}, bf16[128,512]{1,0:T(8,128)(2,1)S(1)}, u32[]{:S(2)}, u32[]{:S(2)}) collective-permute-start(bf16[128,512]{1,0:T(8,128)(2,1)} %x_ref.1), channel_id=1, source_target_pairs={{0,2},{1,3},{2,0},{3,1},{4,6},{5,7},{6,4},{7,5},{8,10},{9,11},{10,... | collective-permute-start | bytes 393224 | tf_op jit(solution)/shard_map/ppermute | solution.py:338
  8.2 5.3 %collective-permute-start.6 = (bf16[128]{0:T(256)(128)(2,1)}, bf16[128]{0:T(256)(128)(2,1)S(1)}, u32[]{:S(2)}, u32[]{:S(2)}) collective-permute-start(bf16[128]{0:T(256)(128)(2,1)} %param.9), channel_id=1, source_target_pairs={{0,8},{1,9},{2,10},{3,11},{4,12},{5,13},{6,14},{7,15},{8,0},{9,1},... | collective-permute-start | bytes 776 | tf_op jit(solution)/shard_map/ppermute | solution.py:338
  13.5 2.9 %collective-permute-start.4 = (bf16[128,512]{1,0:T(8,128)(2,1)S(1)}, bf16[128,512]{1,0:T(8,128)(2,1)S(1)}, u32[]{:S(2)}, u32[]{:S(2)}) collective-permute-start(bf16[128,512]{1,0:T(8,128)(2,1)S(1)} %copy-done.1), channel_id=1, source_target_pairs={{0,1},{1,0},{2,3},{3,2},{4,5},{5,4},{6,7},{7,6},{8,9},{9,8},{10,11... | collective-permute-start | bytes 393224 | tf_op jit(solution)/shard_map/ppermute | solution.py:338
  13.5 2.9 %collective-permute-start.5 = (bf16[128,512]{1,0:T(8,128)(2,1)S(1)}, bf16[128,512]{1,0:T(8,128)(2,1)S(1)}, u32[]{:S(2)}, u32[]{:S(2)}) collective-permute-start(bf16[128,512]{1,0:T(8,128)(2,1)S(1)} %collective-permute-done.3.refs_5_.refs_1_), channel_id=1, source_target_pairs={{0,1},{1,0},{2,3},{3,2},{4,5},{5,4},{6,7},{7,6},{8,9},{9,8},{10,11... | collective-permute-start | bytes 393224 | tf_op jit(solution)/shard_map/ppermute | solution.py:338
  14.1 1.4 %collective-permute-start.7 = (bf16[128]{0:T(256)(128)(2,1)S(1)}, bf16[128]{0:T(256)(128)(2,1)S(1)}, u32[]{:S(2)}, u32[]{:S(2)}) collective-permute-start(bf16[128]{0:T(256)(128)(2,1)S(1)} %copy-done.5), channel_id=1, source_target_pairs={{0,1},{1,0},{2,3},{3,2},{4,5},{5,4},{6,7},{7,6},{8,9},{9,8},{10,11... | collective-permute-start | bytes 776 | tf_op jit(solution)/shard_map/ppermute | solution.py:338
  15.3 1.1 %collective-permute-start.8 = (bf16[128]{0:T(256)(128)(2,1)S(1)}, bf16[128]{0:T(256)(128)(2,1)S(1)}, u32[]{:S(2)}, u32[]{:S(2)}) collective-permute-start(bf16[128]{0:T(256)(128)(2,1)S(1)} %collective-permute-done.6), channel_id=1, source_target_pairs={{0,1},{1,0},{2,3},{3,2},{4,5},{5,4},{6,7},{7,6},{8,9},{9,8},{10,11... | collective-permute-start | bytes 776 | tf_op jit(solution)/shard_map/ppermute | solution.py:338
  17.7 1.3 %collective-permute-start.9 = (f32[32,256]{1,0:T(8,128)S(1)}, f32[32,256]{1,0:T(8,128)S(1)}, u32[]{:S(2)}, u32[]{:S(2)}) collective-permute-start(f32[32,256]{1,0:T(8,128)S(1)} %get-tuple-element.36), channel_id=1, source_target_pairs={{0,1},{1,0},{2,3},{3,2},{4,5},{5,4},{6,7},{7,6},{8,9},{9,8},{10,11... | collective-permute-start | bytes 98312 | tf_op jit(solution)/shard_map/ppermute | solution.py:338
  19.0 5.4 %collective-permute-start.13 = (f32[32,256]{1,0:T(8,128)S(1)}, f32[32,256]{1,0:T(8,128)S(1)}, u32[]{:S(2)}, u32[]{:S(2)}) collective-permute-start(f32[32,256]{1,0:T(8,128)S(1)} %add.9), channel_id=1, source_target_pairs={{0,8},{1,9},{2,10},{3,11},{4,12},{5,13},{6,14},{7,15},{8,0},{9,1},... | collective-permute-start | bytes 98312 | tf_op jit(solution)/shard_map/ppermute | solution.py:338
  21.2 6.0 %collective-permute-start.11 = (bf16[32,512]{1,0:T(8,128)(2,1)S(1)}, bf16[32,512]{1,0:T(8,128)(2,1)S(1)}, u32[]{:S(2)}, u32[]{:S(2)}) collective-permute-start(bf16[32,512]{1,0:T(8,128)(2,1)S(1)} %lead.1.refs_12_), channel_id=1, source_target_pairs={{0,1},{1,0},{2,3},{3,2},{4,5},{5,4},{6,7},{7,6},{8,9},{9,8},{10,11... | collective-permute-start | bytes 98312 | tf_op jit(solution)/shard_map/ppermute | solution.py:338
  21.2 6.7 %collective-permute-start.12 = (bf16[32,512]{1,0:T(8,128)(2,1)S(1)}, bf16[32,512]{1,0:T(8,128)(2,1)S(1)}, u32[]{:S(2)}, u32[]{:S(2)}) collective-permute-start(bf16[32,512]{1,0:T(8,128)(2,1)S(1)} %lead.1.refs_12_), channel_id=1, source_target_pairs={{0,9},{1,8},{2,11},{3,10},{4,13},{5,12},{6,15},{7,14},{8,1},{9,0},... | collective-permute-start | bytes 98312 | tf_op jit(solution)/shard_map/ppermute | solution.py:338
  22.0 5.9 %collective-permute-start.10 = (bf16[32,512]{1,0:T(8,128)(2,1)S(1)}, bf16[32,512]{1,0:T(8,128)(2,1)S(1)}, u32[]{:S(2)}, u32[]{:S(2)}) collective-permute-start(bf16[32,512]{1,0:T(8,128)(2,1)S(1)} %lead.1.refs_12_), channel_id=1, source_target_pairs={{0,8},{1,9},{2,10},{3,11},{4,12},{5,13},{6,14},{7,15},{8,0},{9,1},... | collective-permute-start | bytes 98312 | tf_op jit(solution)/shard_map/ppermute | solution.py:338
  24.4 5.8 %collective-permute-start.14 = (f32[32,256]{1,0:T(8,128)S(1)}, f32[32,256]{1,0:T(8,128)S(1)}, u32[]{:S(2)}, u32[]{:S(2)}) collective-permute-start(f32[32,256]{1,0:T(8,128)S(1)} %add.10.refs_0_), channel_id=1, source_target_pairs={{0,6},{1,7},{2,4},{3,5},{4,2},{5,3},{6,0},{7,1},{8,14},{9,15},{10,... | collective-permute-start | bytes 98312 | tf_op jit(solution)/shard_map/ppermute | solution.py:338
  25.9 4.4 %collective-permute-start.15 = (f32[32,256]{1,0:T(8,128)S(1)}, f32[32,256]{1,0:T(8,128)S(1)}, u32[]{:S(2)}, u32[]{:S(2)}) collective-permute-start(f32[32,256]{1,0:T(8,128)S(1)} %add.10.refs_0_), channel_id=1, source_target_pairs={{0,4},{1,5},{2,6},{3,7},{4,0},{5,1},{6,2},{7,3},{8,12},{9,13},{10,... | collective-permute-start | bytes 98312 | tf_op jit(solution)/shard_map/ppermute | solution.py:338
  27.2 3.9 %collective-permute-start.16 = (f32[32,256]{1,0:T(8,128)S(1)}, f32[32,256]{1,0:T(8,128)S(1)}, u32[]{:S(2)}, u32[]{:S(2)}) collective-permute-start(f32[32,256]{1,0:T(8,128)S(1)} %add.10.refs_0_), channel_id=1, source_target_pairs={{0,2},{1,3},{2,0},{3,1},{4,6},{5,7},{6,4},{7,5},{8,10},{9,11},{10,... | collective-permute-start | bytes 98312 | tf_op jit(solution)/shard_map/ppermute | solution.py:338
  32.6 1.3 %collective-permute-start.17 = (f32[64,256]{1,0:T(8,128)S(1)}, f32[64,256]{1,0:T(8,128)S(1)}, u32[]{:S(2)}, u32[]{:S(2)}) collective-permute-start(f32[64,256]{1,0:T(8,128)S(1)} %solve.1.refs_0_), channel_id=1, source_target_pairs={{0,1},{1,0},{2,3},{3,2},{4,5},{5,4},{6,7},{7,6},{8,9},{9,8},{10,11... | collective-permute-start | bytes 196616 | tf_op jit(solution)/shard_map/ppermute | solution.py:338
  34.7 3.1 %collective-permute-start.20 = (bf16[128,512]{1,0:T(8,128)(2,1)S(1)}, bf16[128,512]{1,0:T(8,128)(2,1)S(1)}, u32[]{:S(2)}, u32[]{:S(2)}) collective-permute-start(bf16[128,512]{1,0:T(8,128)(2,1)S(1)} %get-tuple-element.51), channel_id=1, source_target_pairs={{0,1},{1,0},{2,3},{3,2},{4,5},{5,4},{6,7},{7,6},{8,9},{9,8},{10,11... | collective-permute-start | bytes 393224 | tf_op jit(solution)/shard_map/ppermute | solution.py:338
  35.6 10.1 %collective-permute-start.18 = (bf16[128,512]{1,0:T(8,128)(2,1)S(1)}, bf16[128,512]{1,0:T(8,128)(2,1)S(1)}, u32[]{:S(2)}, u32[]{:S(2)}) collective-permute-start(bf16[128,512]{1,0:T(8,128)(2,1)S(1)} %get-tuple-element.48), channel_id=1, source_target_pairs={{0,6},{1,7},{2,4},{3,5},{4,2},{5,3},{6,0},{7,1},{8,14},{9,15},{10,... | collective-permute-start | bytes 393224 | tf_op jit(solution)/shard_map/ppermute | solution.py:338
  36.6 10.6 %collective-permute-start.19 = (bf16[128,512]{1,0:T(8,128)(2,1)S(1)}, bf16[128,512]{1,0:T(8,128)(2,1)S(1)}, u32[]{:S(2)}, u32[]{:S(2)}) collective-permute-start(bf16[128,512]{1,0:T(8,128)(2,1)S(1)} %get-tuple-element.49), channel_id=1, source_target_pairs={{0,4},{1,5},{2,6},{3,7},{4,0},{5,1},{6,2},{7,3},{8,12},{9,13},{10,... | collective-permute-start | bytes 393224 | tf_op jit(solution)/shard_map/ppermute | solution.py:338
  37.9 9.3 %collective-permute-start.23 = (bf16[128,512]{1,0:T(8,128)(2,1)S(1)}, bf16[128,512]{1,0:T(8,128)(2,1)S(1)}, u32[]{:S(2)}, u32[]{:S(2)}) collective-permute-start(bf16[128,512]{1,0:T(8,128)(2,1)S(1)} %add_convert_fusion), channel_id=1, source_target_pairs={{0,8},{1,9},{2,10},{3,11},{4,12},{5,13},{6,14},{7,15},{8,0},{9,1},... | collective-permute-start | bytes 393224 | tf_op jit(solution)/shard_map/ppermute | solution.py:338
  39.9 7.3 %collective-permute-start.22 = (bf16[128,512]{1,0:T(8,128)(2,1)S(1)}, bf16[128,512]{1,0:T(8,128)(2,1)S(1)}, u32[]{:S(2)}, u32[]{:S(2)}) collective-permute-start(bf16[128,512]{1,0:T(8,128)(2,1)S(1)} %get-tuple-element.55), channel_id=1, source_target_pairs={{0,1},{1,0},{2,3},{3,2},{4,5},{5,4},{6,7},{7,6},{8,9},{9,8},{10,11... | collective-permute-start | bytes 393224 | tf_op jit(solution)/shard_map/ppermute | solution.py:338
  39.9 7.3 %collective-permute-start.21 = (bf16[128,512]{1,0:T(8,128)(2,1)S(1)}, bf16[128,512]{1,0:T(8,128)(2,1)S(1)}, u32[]{:S(2)}, u32[]{:S(2)}) collective-permute-start(bf16[128,512]{1,0:T(8,128)(2,1)S(1)} %get-tuple-element.52), channel_id=1, source_target_pairs={{0,2},{1,3},{2,0},{3,1},{4,6},{5,7},{6,4},{7,5},{8,10},{9,11},{10,... | collective-permute-start | bytes 393224 | tf_op jit(solution)/shard_map/ppermute | solution.py:338
  (7 other events, 14.1 us)

commit v9 on v8

--- a/solution.py
+++ b/solution.py
@@ -80,7 +80,7 @@
     blocks = [work[i : i + SUBLANES] for i in range(0, size, SUBLANES)]
     row = rows(shape)
 
-    def one_row(block, k):
+    def row_of(block, k):
         return jnp.broadcast_to(block[k : k + 1], shape)
 
     for k in range(0, size, 4):
@@ -89,8 +89,8 @@
             [jnp.broadcast_to(block[:, k + j : k + j + 1], shape) for block in blocks]
             for j in range(4)
         ]
-        p = [[one_row(columns[j][at], here + i) for j in range(4)] for i in range(4)]
-        r = [one_row(blocks[at], here + i) for i in range(4)]
+        p = [[row_of(columns[j][at], here + i) for j in range(4)] for i in range(4)]
+        r = [row_of(blocks[at], here + i) for i in range(4)]
         for i in range(4):
             scale = 1.0 / p[i][i]
             r[i] = r[i] * scale
@@ -121,8 +121,9 @@
 
 def tables_kernel(
     trade_masks, me_ref, level_ref, set_ref, index_ref, rate_ref, x_ref, w_ref,
-    member_ref, thresh_out_ref, rate_out_ref, x_out_ref, w_out_ref,
+    notional_ref, member_ref, thresh_out_ref, rate_out_ref, x_out_ref, w_out_ref, notional_out_ref,
 ):
+    notional_out_ref[...] = notional_ref[...]
     x_out_ref[...] = x_ref[...]
     w_out_ref[...] = w_ref[...]
     me = me_ref[0]
@@ -167,14 +168,15 @@
     return jnp.concatenate([ref[...] for ref in refs], axis=0)
 
 
-def joined_notionals(refs):
-    return jnp.concatenate([ref[...].astype(F32) for ref in refs], axis=1)
+def one_row(ref):
+    wide = ref[...].astype(F32)
+    return jnp.concatenate([wide[k : k + 1] for k in range(wide.shape[0])], axis=1)
 
 
 def forward_kernel(paths, trades, *refs):
     x_refs, refs = refs[:paths], refs[paths:]
-    weights, notional = joined_weights(refs[:trades]), joined_notionals(refs[trades : 2 * trades])
-    lead_ref, member_ref, value_ref, *moment_refs = refs[2 * trades :]
+    weights, notional = joined_weights(refs[:trades]), one_row(refs[trades])
+    lead_ref, member_ref, value_ref, *moment_refs = refs[trades + 1 :]
     start = 0
     for x in x_refs:
         pre_act = dot(x[...], weights, 1, 1)
@@ -190,7 +192,7 @@
 
 def slope_kernel(paths, trades, *refs):
     x_refs, refs, slope_ref = refs[:paths], refs[paths:], refs[-1]
-    weights, notional = joined_weights(refs[:trades]), joined_notionals(refs[trades : 2 * trades])
+    weights, notional = joined_weights(refs[:trades]), one_row(refs[trades])
     start = 0
     for x in x_refs:
         slope_ref[start : start + x.shape[0]] = notional * sigmoid(dot(x[...], weights, 1, 1))
@@ -288,22 +290,40 @@
     own_ref[...] = jnp.where(lanes(design.shape) < CONSTANT, design, 0.0)
 
 
-def total(refs):
-    out = refs[0][...].astype(F32)
-    for ref in refs[1:]:
-        out = out + ref[...].astype(F32)
-    return out
-
-
 def sum_kernel(first, own_ref, *refs):
-    basis_ref, weight_ref = refs[-2:]
-    basis = total(refs[:first])
-    basis_ref[:, :LANES] = basis[:, :LANES] + own_ref[...]
-    basis_ref[:, LANES:] = basis[:, LANES:]
-    weight_ref[...] = total(refs[first:-2])
-
-
-def call(kernel, outs, *args, name, flops=0, scratch=(), scalars=0):
+    *terms, basis_ref, weight_ref, basis_scratch, weight_scratch, sems = refs
+
+    def total(refs, here):
+        out = refs[0][here].astype(F32)
+        for ref in refs[1:]:
+            out = out + ref[here].astype(F32)
+        return out
+
+    copies = []
+
+    def send(source, target, here):
+        copy = pltpu.make_async_copy(source.at[here], target.at[here], sems.at[len(copies)])
+        copy.start()
+        copies.append(copy)
+
+    parts = sems.shape[0] // 2
+    for k in range(parts):
+        size = weight_ref.shape[0] // parts
+        here = slice(k * size, (k + 1) * size)
+        weight_scratch[here] = total(terms[first:], here)
+        send(weight_scratch, weight_ref, pl.ds(k * size, size))
+    for k in range(parts):
+        size = basis_ref.shape[0] // parts
+        here = slice(k * size, (k + 1) * size)
+        basis = total(terms[:first], here)
+        basis_scratch[here, :LANES] = basis[:, :LANES] + own_ref[here]
+        basis_scratch[here, LANES:] = basis[:, LANES:]
+        send(basis_scratch, basis_ref, pl.ds(k * size, size))
+    for copy in copies:
+        copy.wait()
+
+
+def call(kernel, outs, *args, name, flops=0, scratch=(), scalars=0, far=False):
     size = sum(a.size * a.dtype.itemsize for a in args) + sum(
         math.prod(s) * jnp.dtype(d).itemsize for s, d in outs
     )
@@ -312,7 +332,7 @@
         out_shape=[jax.ShapeDtypeStruct(s, d) for s, d in outs],
         in_specs=[pl.BlockSpec(memory_space=pltpu.SMEM)] * scalars
         + [pl.BlockSpec(memory_space=pltpu.VMEM)] * (len(args) - scalars),
-        out_specs=[pl.BlockSpec(memory_space=pltpu.VMEM)] * len(outs),
+        out_specs=[pl.BlockSpec(memory_space=pl.ANY if far else pltpu.VMEM)] * len(outs),
         scratch_shapes=scratch,
         compiler_params=pltpu.CompilerParams(vmem_limit_bytes=VMEM_BYTES),
         cost_estimate=pl.CostEstimate(flops=int(flops), bytes_accessed=int(size), transcendentals=0),
@@ -353,9 +373,9 @@
     first_bit = outer_bits[0]
     weights = [proxy_weight, swap(proxy_weight, 1 << first_bit)]
     basis = [path_basis] + direct([path_basis] * inner, inner_masks)
-    notionals = [notional, swap(notional, 1 << first_bit)]
-
-    member, thresh, rate, basis[0], own_weight = call(
+    notionals = [notional[None, :], swap(notional, 1 << first_bit)[None, :]]
+
+    member, thresh, rate, basis[0], own_weight, notionals[0] = call(
         partial(tables_kernel, outer_masks),
         [
             ((sets, group_trades), BF16),
@@ -363,6 +383,7 @@
             ((1, sets), F32),
             (path_basis.shape, BF16),
             (proxy_weight.shape, BF16),
+            ((1, trade_rows), BF16),
         ],
         me.astype(jnp.int32).reshape(1),
         threshold_levels,
@@ -371,21 +392,22 @@
         loss_rate.reshape(SHARES, 1, share),
         path_basis,
         proxy_weight,
+        notionals[0],
         name="tables",
         scalars=2,
     )
+    notionals = after(jnp.concatenate(notionals, axis=0), basis[-1])
     for bit in outer_bits[1:]:
         weights = weights + [
             swap(w if k else after(w, member), 1 << bit) for k, w in enumerate(weights)
         ]
-        notionals = notionals + [swap(x, 1 << bit) for x in notionals]
+        notionals = jnp.concatenate([notionals, swap(notionals, 1 << bit)], axis=0)
     weights[0] = own_weight
-    notionals = [x[None, :] for x in notionals]
     (lead,) = call(lead_kernel, [((REGRESSORS, group_paths), BF16)], *basis, name="lead")
     value, *moments = call(
         partial(forward_kernel, inner, outer),
         [((group_paths, group_trades), BF16)] + [((REGRESSORS, share), F32)] * SHARES,
-        *basis, *weights, *notionals, lead, member,
+        *basis, *weights, notionals, lead, member,
         name="forward",
     )
     moment = moments[0] + swap(moments[1], SHARES - 1)
@@ -419,7 +441,7 @@
     (slope,) = call(
         partial(slope_kernel, inner, outer),
         [((group_paths, group_trades), F32)],
-        *basis, *weights, *notionals,
+        *basis, *weights, notionals,
         name="slope",
     )
     traded, slopes, *weight_parts = call(
@@ -460,11 +482,18 @@
         name="loss",
         scratch=[pltpu.VMEM((LANES, sets), BF16)],
     )
+    parts = 4 if trade_rows % (4 * SUBLANES * 2) == 0 else 1
     basis_adjoint, weight_adjoint = call(
         partial(sum_kernel, len(basis_terms)),
         [((path_rows, features), F32), ((trade_rows, features), F32)],
         own_adjoint, *basis_terms, *weight_terms,
         name="sums",
+        scratch=[
+            pltpu.VMEM((path_rows, features), F32),
+            pltpu.VMEM((trade_rows, features), F32),
+            pltpu.SemaphoreType.DMA((2 * parts,)),
+        ],
+        far=True,
     )
     return (loss[0, :1], basis_adjoint, weight_adjoint)
 

time: 48.2 us -> 48.1 us (level)
  waiting for transfers between devices: 9 us -> 8.46 us
    ppermute x24 -> x23, waiting for transfers between devices: 9 us -> 8.46 us  [swap(): return lax.ppermute(x, 'paths', [(d, d ^ mask) for d in range(n)])]
    ppermute x24 -> x23, starting transfers between devices: 23 us -> 23.3 us  [swap(): return lax.ppermute(x, 'paths', [(d, d ^ mask) for d in range(n)])]
  transfers between devices with their start and end apart: 24 -> 23, of which waited for: 9 -> 8; matrix products, arithmetic and copies ran while one was open for 1% -> 1% of each run, Pallas kernels for 16% -> 16%
where the time goes in v9:
time: 48.1 us; the launch traced here: 47.9 us
  starting transfers between devices  23.3 us (48%)
  Pallas kernels  12.2 us (25%)
  waiting for transfers between devices  8.46 us (18%)
  local copies, waits for them, and re-layouts  3.04 us (6%)
  between operations  0.79 us (2%)
    ppermute x23, starting transfers between devices, swap(): return lax.ppermute(x, 'paths', [(d, d ^ mask) for d in range(n)])  23.3 us
    pallas_call x11, Pallas kernels, call(): pl.pallas_call(kernel, out_shape=[jax.ShapeDtypeStruct(s, d) for s, d in...  12.2 us
    ppermute x23, waiting for transfers between devices, swap(): return lax.ppermute(x, 'paths', [(d, d ^ mask) for d in range(n)])  8.46 us
    unnamed x14, local copies, waits for them, and re-layouts  2.52 us
  transfers between devices with their start and end apart: 23, of which 8 were waited for; matrix products, arithmetic and copies ran while one was open for 1% of the time, Pallas kernels for 16%

profile of v9, /device:TPU:0, one launch (start us, length us, event | category | flops | bytes accessed | tf_op | source)
XLA Modules:
  0.0 47.9 jit_solution(2691883327606353120)
XLA Ops:
  0.6 4.1 %collective-permute-start.3 = (bf16[128,512]{1,0:T(8,128)(2,1)}, bf16[128,512]{1,0:T(8,128)(2,1)S(1)}, u32[]{:S(2)}, u32[]{:S(2)}) collective-permute-start(bf16[128,512]{1,0:T(8,128)(2,1)} %w_ref.1), channel_id=1, source_target_pairs={{0,8},{1,9},{2,10},{3,11},{4,12},{5,13},{6,14},{7,15},{8,0},{9,1},... | collective-permute-start | bytes 393224 | tf_op jit(solution)/shard_map/ppermute | solution.py:358
  4.7 1.5 %collective-permute-start.2 = (bf16[128,512]{1,0:T(8,128)(2,1)}, bf16[128,512]{1,0:T(8,128)(2,1)S(1)}, u32[]{:S(2)}, u32[]{:S(2)}) collective-permute-start(bf16[128,512]{1,0:T(8,128)(2,1)} %x_ref.1), channel_id=1, source_target_pairs={{0,2},{1,3},{2,0},{3,1},{4,6},{5,7},{6,4},{7,5},{8,10},{9,11},{10,... | collective-permute-start | bytes 393224 | tf_op jit(solution)/shard_map/ppermute | solution.py:358
  6.3 1.5 %collective-permute-start = (bf16[128,512]{1,0:T(8,128)(2,1)}, bf16[128,512]{1,0:T(8,128)(2,1)S(1)}, u32[]{:S(2)}, u32[]{:S(2)}) collective-permute-start(bf16[128,512]{1,0:T(8,128)(2,1)} %x_ref.1), channel_id=1, source_target_pairs={{0,6},{1,7},{2,4},{3,5},{4,2},{5,3},{6,0},{7,1},{8,14},{9,15},{10,... | collective-permute-start | bytes 393224 | tf_op jit(solution)/shard_map/ppermute | solution.py:358
  9.0 0.9 %copy-done = bf16[128,512]{1,0:T(8,128)(2,1)S(1)} copy-done((bf16[128,512]{1,0:T(8,128)(2,1)S(1)}, bf16[128,512]{1,0:T(8,128)(2,1)}, u32[]{:S(2)}) %copy-start) | copy-done | bytes 131096
  9.9 0.9 %copy-done.1 = bf16[128,512]{1,0:T(8,128)(2,1)S(1)} copy-done((bf16[128,512]{1,0:T(8,128)(2,1)S(1)}, bf16[128,512]{1,0:T(8,128)(2,1)}, u32[]{:S(2)}) %copy-start.1) | copy-done | bytes 131096
  11.5 2.0 %collective-permute-done.6 = bf16[128]{0:T(256)(128)(2,1)S(1)} collective-permute-done((bf16[128]{0:T(256)(128)(2,1)}, bf16[128]{0:T(256)(128)(2,1)S(1)}, u32[]{:S(2)}, u32[]{:S(2)}) %collective-permute-start.6) | collective-permute-done | bytes 288 | tf_op jit(solution)/shard_map/ppermute | solution.py:358
  15.7 1.3 %forward.1 = (bf16[512,512]{1,0:T(8,128)(2,1)S(1)}, f32[32,256]{1,0:T(8,128)S(1)}, f32[32,256]{1,0:T(8,128)S(1)}) custom-call(bf16[128,512]{1,0:T(8,128)(2,1)S(1)} %get-tuple-element.33.refs_0_.refs_2_, bf16[128,512]{1,0:T(8,128)(2,1)S(1)} %collective-permute-done.refs_1_.refs_3_, bf16[128,512]{1,0:T(8,128)(2,1)S(1)} %collective-permute-done.1.refs_2_.refs_4_, ...), custom_call_target="tpu_custom_call" | custom-call | bytes 2196480 | tf_op jit(solution)/shard_map/forward/pallas_call | solution.py:330
  17.0 1.3 %collective-permute-done.8 = f32[32,256]{1,0:T(8,128)S(1)} collective-permute-done((f32[32,256]{1,0:T(8,128)S(1)}, f32[32,256]{1,0:T(8,128)S(1)}, u32[]{:S(2)}, u32[]{:S(2)}) %collective-permute-start.8) | collective-permute-done | bytes 32800 | tf_op jit(solution)/shard_map/ppermute | solution.py:358
  18.2 2.8 %collective-permute-start.12 = (f32[32,256]{1,0:T(8,128)S(1)}, f32[32,256]{1,0:T(8,128)S(1)}, u32[]{:S(2)}, u32[]{:S(2)}) collective-permute-start(f32[32,256]{1,0:T(8,128)S(1)} %add.9), channel_id=1, source_target_pairs={{0,8},{1,9},{2,10},{3,11},{4,12},{5,13},{6,14},{7,15},{8,0},{9,1},... | collective-permute-start | bytes 98312 | tf_op jit(solution)/shard_map/ppermute | solution.py:358
  21.2 2.9 %collective-permute-start.11 = (bf16[32,512]{1,0:T(8,128)(2,1)S(1)}, bf16[32,512]{1,0:T(8,128)(2,1)S(1)}, u32[]{:S(2)}, u32[]{:S(2)}) collective-permute-start(bf16[32,512]{1,0:T(8,128)(2,1)S(1)} %lead.1.refs_9_), channel_id=1, source_target_pairs={{0,9},{1,8},{2,11},{3,10},{4,13},{5,12},{6,15},{7,14},{8,1},{9,0},... | collective-permute-start | bytes 98312 | tf_op jit(solution)/shard_map/ppermute | solution.py:358
  24.1 1.8 %collective-permute-start.13 = (f32[32,256]{1,0:T(8,128)S(1)}, f32[32,256]{1,0:T(8,128)S(1)}, u32[]{:S(2)}, u32[]{:S(2)}) collective-permute-start(f32[32,256]{1,0:T(8,128)S(1)} %add.10.refs_0_), channel_id=1, source_target_pairs={{0,6},{1,7},{2,4},{3,5},{4,2},{5,3},{6,0},{7,1},{8,14},{9,15},{10,... | collective-permute-start | bytes 98312 | tf_op jit(solution)/shard_map/ppermute | solution.py:358
  25.9 1.2 %collective-permute-start.14 = (f32[32,256]{1,0:T(8,128)S(1)}, f32[32,256]{1,0:T(8,128)S(1)}, u32[]{:S(2)}, u32[]{:S(2)}) collective-permute-start(f32[32,256]{1,0:T(8,128)S(1)} %add.10.refs_0_), channel_id=1, source_target_pairs={{0,4},{1,5},{2,6},{3,7},{4,0},{5,1},{6,2},{7,3},{8,12},{9,13},{10,... | collective-permute-start | bytes 98312 | tf_op jit(solution)/shard_map/ppermute | solution.py:358
  28.3 1.8 %inverse.1.inverse_ref = f32[32,32]{1,0:T(8,128)S(1)} custom-call(bf16[4,32,512]{2,1,0:T(8,128)(2,1)S(1)} %pad_maximum_fusion.small_ref), custom_call_target="tpu_custom_call" | custom-call | bytes 135168 | tf_op jit(solution)/shard_map/inverse/pallas_call | solution.py:330
  30.1 1.0 %collective-permute-done.15.refs_3_ = f32[32,256]{1,0:T(8,128)S(1)} collective-permute-done((f32[32,256]{1,0:T(8,128)S(1)}, f32[32,256]{1,0:T(8,128)S(1)}, u32[]{:S(2)}, u32[]{:S(2)}) %collective-permute-start.15) | collective-permute-done | bytes 32800 | tf_op jit(solution)/shard_map/ppermute | solution.py:358
  31.1 1.5 %solve.1.refs_0_ = f32[64,256]{1,0:T(8,128)S(1)} custom-call(f32[32,32]{1,0:T(8,128)S(1)} %inverse.1.inverse_ref, bf16[32,2048]{1,0:T(8,128)(2,1)S(1)} %get-tuple-element.45.design_ref, bf16[2048,128]{1,0:T(8,128)(2,1)S(1)} %get-tuple-element.42.rows_ref, f32[1,512]{1,0:T(1,128)S(1)} %get-tuple-element.43.thresh_ref, ...), custom_call_target="tpu_custom_call" | custom-call | bytes 860160 | tf_op jit(solution)/shard_map/solve/pallas_call | solution.py:330
  32.5 0.9 %slope.1.slope_ref = f32[512,512]{1,0:T(8,128)S(1)} custom-call(bf16[128,512]{1,0:T(8,128)(2,1)S(1)} %get-tuple-element.33.refs_0_.refs_2_, bf16[128,512]{1,0:T(8,128)(2,1)S(1)} %collective-permute-done.refs_1_.refs_3_, bf16[128,512]{1,0:T(8,128)(2,1)S(1)} %collective-permute-done.1.refs_2_.refs_4_, ...), custom_call_target="tpu_custom_call" | custom-call | bytes 2098176 | tf_op jit(solution)/shard_map/slope/pallas_call | solution.py:330
  33.8 0.9 %weight_side.1 = (bf16[128,512]{1,0:T(8,128)(2,1)S(1)}, bf16[512,512]{1,0:T(8,128)(2,1)S(1)}, bf16[128,512]{1,0:T(8,128)(2,1)S(1)}, bf16[128,512]{1,0:T(8,128)(2...) custom-call(bf16[512,512]{1,0:T(8,128)(2,1)S(1)} %get-tuple-element.35.refs_10_.member_ref, ...), custom_call_target="tpu_custom_call" | custom-call | bytes 3932160 | tf_op jit(solution)/shard_map/weight_side/pallas_call | solution.py:330
  36.4 1.3 %collective-permute-start.18 = (bf16[128,512]{1,0:T(8,128)(2,1)S(1)}, bf16[128,512]{1,0:T(8,128)(2,1)S(1)}, u32[]{:S(2)}, u32[]{:S(2)}) collective-permute-start(bf16[128,512]{1,0:T(8,128)(2,1)S(1)} %get-tuple-element.53), channel_id=1, source_target_pairs={{0,4},{1,5},{2,6},{3,7},{4,0},{5,1},{6,2},{7,3},{8,12},{9,13},{10,... | collective-permute-start | bytes 393224 | tf_op jit(solution)/shard_map/ppermute | solution.py:358
  37.8 1.7 %collective-permute-start.22 = (bf16[128,512]{1,0:T(8,128)(2,1)S(1)}, bf16[128,512]{1,0:T(8,128)(2,1)S(1)}, u32[]{:S(2)}, u32[]{:S(2)}) collective-permute-start(bf16[128,512]{1,0:T(8,128)(2,1)S(1)} %add_convert_fusion), channel_id=1, source_target_pairs={{0,8},{1,9},{2,10},{3,11},{4,12},{5,13},{6,14},{7,15},{8,0},{9,1},... | collective-permute-start | bytes 393224 | tf_op jit(solution)/shard_map/ppermute | solution.py:358
  39.5 1.5 %collective-permute-start.20 = (bf16[128,512]{1,0:T(8,128)(2,1)S(1)}, bf16[128,512]{1,0:T(8,128)(2,1)S(1)}, u32[]{:S(2)}, u32[]{:S(2)}) collective-permute-start(bf16[128,512]{1,0:T(8,128)(2,1)S(1)} %get-tuple-element.56), channel_id=1, source_target_pairs={{0,2},{1,3},{2,0},{3,1},{4,6},{5,7},{6,4},{7,5},{8,10},{9,11},{10,... | collective-permute-start | bytes 393224 | tf_op jit(solution)/shard_map/ppermute | solution.py:358
  41.0 3.2 %loss.1 = (f32[8,128]{1,0:T(8,128)S(1)}, f32[128,128]{1,0:T(8,128)S(1)}) custom-call(bf16[2048,128]{1,0:T(8,128)(2,1)S(1)} %get-tuple-element.42.rows_ref, f32[1,512]{1,0:T(1,128)S(1)} %get-tuple-element.43.thresh_ref, f32[1,512]{1,0:T(1,128)S(1)} %get-tuple-element.44.rate_ref, f32[64,256]{1,0:T(8,128)S(1)} %solve.1.refs_0_, ...), custom_call_target="tpu_custom_call" | custom-call | bytes 729088 | tf_op jit(solution)/shard_map/loss/pallas_call | solution.py:330
  44.7 1.0 %collective-permute-done.17.refs_1_ = bf16[128,512]{1,0:T(8,128)(2,1)S(1)} collective-permute-done((bf16[128,512]{1,0:T(8,128)(2,1)S(1)}, bf16[128,512]{1,0:T(8,128)(2,1)S(1)}, u32[]{:S(2)}, u32[]{:S(2)}) %collective-permute-start.17) | collective-permute-done | bytes 131104 | tf_op jit(solution)/shard_map/ppermute | solution.py:358
  45.7 1.4 %collective-permute-done.18.refs_2_ = bf16[128,512]{1,0:T(8,128)(2,1)S(1)} collective-permute-done((bf16[128,512]{1,0:T(8,128)(2,1)S(1)}, bf16[128,512]{1,0:T(8,128)(2,1)S(1)}, u32[]{:S(2)}, u32[]{:S(2)}) %collective-permute-start.18) | collective-permute-done | bytes 131104 | tf_op jit(solution)/shard_map/ppermute | solution.py:358
  47.1 0.9 %sums.1 = (f32[128,512]{1,0:T(8,128)}, f32[128,512]{1,0:T(8,128)}) custom-call(f32[128,128]{1,0:T(8,128)S(1)} %get-tuple-element.47.own_ref, bf16[128,512]{1,0:T(8,128)(2,1)S(1)} %get-tuple-element.51.refs_0_, bf16[128,512]{1,0:T(8,128)(2,1)S(1)} %collective-permute-done.17.refs_1_, bf16[128,512]{1,0:T(8,128)(2,1)S(1)} %collective-permute-done.18.refs_2_, ...), custom_call_target="tpu_custom_call" | custom-call | bytes 1507328 | tf_op jit(solution)/shard_map/sums/pallas_call | solution.py:330
  (54 shorter events, 7.9 us)
Async XLA Ops:
  0.6 7.7 %copy-start.2 = (s32[2048]{0:T(1024)S(1)}, s32[2048]{0:T(1024)}, u32[]{:S(2)}) copy-start(s32[2048]{0:T(1024)} %param.10) | copy-start | bytes 24580
  0.6 12.9 %collective-permute-start.3 = (bf16[128,512]{1,0:T(8,128)(2,1)}, bf16[128,512]{1,0:T(8,128)(2,1)S(1)}, u32[]{:S(2)}, u32[]{:S(2)}) collective-permute-start(bf16[128,512]{1,0:T(8,128)(2,1)} %w_ref.1), channel_id=1, source_target_pairs={{0,8},{1,9},{2,10},{3,11},{4,12},{5,13},{6,14},{7,15},{8,0},{9,1},... | collective-permute-start | bytes 393224 | tf_op jit(solution)/shard_map/ppermute | solution.py:358
  4.7 9.3 %collective-permute-start.2 = (bf16[128,512]{1,0:T(8,128)(2,1)}, bf16[128,512]{1,0:T(8,128)(2,1)S(1)}, u32[]{:S(2)}, u32[]{:S(2)}) collective-permute-start(bf16[128,512]{1,0:T(8,128)(2,1)} %x_ref.1), channel_id=1, source_target_pairs={{0,2},{1,3},{2,0},{3,1},{4,6},{5,7},{6,4},{7,5},{8,10},{9,11},{10,... | collective-permute-start | bytes 393224 | tf_op jit(solution)/shard_map/ppermute | solution.py:358
  6.3 8.5 %collective-permute-start = (bf16[128,512]{1,0:T(8,128)(2,1)}, bf16[128,512]{1,0:T(8,128)(2,1)S(1)}, u32[]{:S(2)}, u32[]{:S(2)}) collective-permute-start(bf16[128,512]{1,0:T(8,128)(2,1)} %x_ref.1), channel_id=1, source_target_pairs={{0,6},{1,7},{2,4},{3,5},{4,2},{5,3},{6,0},{7,1},{8,14},{9,15},{10,... | collective-permute-start | bytes 393224 | tf_op jit(solution)/shard_map/ppermute | solution.py:358
  7.8 7.8 %collective-permute-start.1 = (bf16[128,512]{1,0:T(8,128)(2,1)}, bf16[128,512]{1,0:T(8,128)(2,1)S(1)}, u32[]{:S(2)}, u32[]{:S(2)}) collective-permute-start(bf16[128,512]{1,0:T(8,128)(2,1)} %x_ref.1), channel_id=1, source_target_pairs={{0,4},{1,5},{2,6},{3,7},{4,0},{5,1},{6,2},{7,3},{8,12},{9,13},{10,... | collective-permute-start | bytes 393224 | tf_op jit(solution)/shard_map/ppermute | solution.py:358
  8.2 5.3 %collective-permute-start.6 = (bf16[128]{0:T(256)(128)(2,1)}, bf16[128]{0:T(256)(128)(2,1)S(1)}, u32[]{:S(2)}, u32[]{:S(2)}) collective-permute-start(bf16[128]{0:T(256)(128)(2,1)} %param.9), channel_id=1, source_target_pairs={{0,8},{1,9},{2,10},{3,11},{4,12},{5,13},{6,14},{7,15},{8,0},{9,1},... | collective-permute-start | bytes 776 | tf_op jit(solution)/shard_map/ppermute | solution.py:358
  13.5 2.1 %collective-permute-start.4 = (bf16[128,512]{1,0:T(8,128)(2,1)S(1)}, bf16[128,512]{1,0:T(8,128)(2,1)S(1)}, u32[]{:S(2)}, u32[]{:S(2)}) collective-permute-start(bf16[128,512]{1,0:T(8,128)(2,1)S(1)} %copy-done.1), channel_id=1, source_target_pairs={{0,1},{1,0},{2,3},{3,2},{4,5},{5,4},{6,7},{7,6},{8,9},{9,8},{10,11... | collective-permute-start | bytes 393224 | tf_op jit(solution)/shard_map/ppermute | solution.py:358
  13.5 2.1 %collective-permute-start.5 = (bf16[128,512]{1,0:T(8,128)(2,1)S(1)}, bf16[128,512]{1,0:T(8,128)(2,1)S(1)}, u32[]{:S(2)}, u32[]{:S(2)}) collective-permute-start(bf16[128,512]{1,0:T(8,128)(2,1)S(1)} %collective-permute-done.3.refs_5_.refs_1_), channel_id=1, source_target_pairs={{0,1},{1,0},{2,3},{3,2},{4,5},{5,4},{6,7},{7,6},{8,9},{9,8},{10,11... | collective-permute-start | bytes 393224 | tf_op jit(solution)/shard_map/ppermute | solution.py:358
  14.1 1.6 %collective-permute-start.7 = (bf16[2,128]{1,0:T(2,128)(2,1)S(1)}, bf16[2,128]{1,0:T(2,128)(2,1)S(1)}, u32[]{:S(2)}, u32[]{:S(2)}) collective-permute-start(bf16[2,128]{1,0:T(2,128)(2,1)S(1)} %pad_maximum_fusion.2), channel_id=1, source_target_pairs={{0,1},{1,0},{2,3},{3,2},{4,5},{5,4},{6,7},{7,6},{8,9},{9,8},{10,11... | collective-permute-start | bytes 1544 | tf_op jit(solution)/shard_map/ppermute | solution.py:358
  17.0 1.3 %collective-permute-start.8 = (f32[32,256]{1,0:T(8,128)S(1)}, f32[32,256]{1,0:T(8,128)S(1)}, u32[]{:S(2)}, u32[]{:S(2)}) collective-permute-start(f32[32,256]{1,0:T(8,128)S(1)} %get-tuple-element.40), channel_id=1, source_target_pairs={{0,1},{1,0},{2,3},{3,2},{4,5},{5,4},{6,7},{7,6},{8,9},{9,8},{10,11... | collective-permute-start | bytes 98312 | tf_op jit(solution)/shard_map/ppermute | solution.py:358
  18.2 5.9 %collective-permute-start.12 = (f32[32,256]{1,0:T(8,128)S(1)}, f32[32,256]{1,0:T(8,128)S(1)}, u32[]{:S(2)}, u32[]{:S(2)}) collective-permute-start(f32[32,256]{1,0:T(8,128)S(1)} %add.9), channel_id=1, source_target_pairs={{0,8},{1,9},{2,10},{3,11},{4,12},{5,13},{6,14},{7,15},{8,0},{9,1},... | collective-permute-start | bytes 98312 | tf_op jit(solution)/shard_map/ppermute | solution.py:358
  21.1 6.1 %collective-permute-start.9 = (bf16[32,512]{1,0:T(8,128)(2,1)S(1)}, bf16[32,512]{1,0:T(8,128)(2,1)S(1)}, u32[]{:S(2)}, u32[]{:S(2)}) collective-permute-start(bf16[32,512]{1,0:T(8,128)(2,1)S(1)} %lead.1.refs_9_), channel_id=1, source_target_pairs={{0,8},{1,9},{2,10},{3,11},{4,12},{5,13},{6,14},{7,15},{8,0},{9,1},... | collective-permute-start | bytes 98312 | tf_op jit(solution)/shard_map/ppermute | solution.py:358
  21.2 6.6 %collective-permute-start.10 = (bf16[32,512]{1,0:T(8,128)(2,1)S(1)}, bf16[32,512]{1,0:T(8,128)(2,1)S(1)}, u32[]{:S(2)}, u32[]{:S(2)}) collective-permute-start(bf16[32,512]{1,0:T(8,128)(2,1)S(1)} %lead.1.refs_9_), channel_id=1, source_target_pairs={{0,1},{1,0},{2,3},{3,2},{4,5},{5,4},{6,7},{7,6},{8,9},{9,8},{10,11... | collective-permute-start | bytes 98312 | tf_op jit(solution)/shard_map/ppermute | solution.py:358
  21.2 6.6 %collective-permute-start.11 = (bf16[32,512]{1,0:T(8,128)(2,1)S(1)}, bf16[32,512]{1,0:T(8,128)(2,1)S(1)}, u32[]{:S(2)}, u32[]{:S(2)}) collective-permute-start(bf16[32,512]{1,0:T(8,128)(2,1)S(1)} %lead.1.refs_9_), channel_id=1, source_target_pairs={{0,9},{1,8},{2,11},{3,10},{4,13},{5,12},{6,15},{7,14},{8,1},{9,0},... | collective-permute-start | bytes 98312 | tf_op jit(solution)/shard_map/ppermute | solution.py:358
  24.1 6.0 %collective-permute-start.13 = (f32[32,256]{1,0:T(8,128)S(1)}, f32[32,256]{1,0:T(8,128)S(1)}, u32[]{:S(2)}, u32[]{:S(2)}) collective-permute-start(f32[32,256]{1,0:T(8,128)S(1)} %add.10.refs_0_), channel_id=1, source_target_pairs={{0,6},{1,7},{2,4},{3,5},{4,2},{5,3},{6,0},{7,1},{8,14},{9,15},{10,... | collective-permute-start | bytes 98312 | tf_op jit(solution)/shard_map/ppermute | solution.py:358
  25.9 4.2 %collective-permute-start.14 = (f32[32,256]{1,0:T(8,128)S(1)}, f32[32,256]{1,0:T(8,128)S(1)}, u32[]{:S(2)}, u32[]{:S(2)}) collective-permute-start(f32[32,256]{1,0:T(8,128)S(1)} %add.10.refs_0_), channel_id=1, source_target_pairs={{0,4},{1,5},{2,6},{3,7},{4,0},{5,1},{6,2},{7,3},{8,12},{9,13},{10,... | collective-permute-start | bytes 98312 | tf_op jit(solution)/shard_map/ppermute | solution.py:358
  27.2 3.9 %collective-permute-start.15 = (f32[32,256]{1,0:T(8,128)S(1)}, f32[32,256]{1,0:T(8,128)S(1)}, u32[]{:S(2)}, u32[]{:S(2)}) collective-permute-start(f32[32,256]{1,0:T(8,128)S(1)} %add.10.refs_0_), channel_id=1, source_target_pairs={{0,2},{1,3},{2,0},{3,1},{4,6},{5,7},{6,4},{7,5},{8,10},{9,11},{10,... | collective-permute-start | bytes 98312 | tf_op jit(solution)/shard_map/ppermute | solution.py:358
  32.5 1.3 %collective-permute-start.16 = (f32[64,256]{1,0:T(8,128)S(1)}, f32[64,256]{1,0:T(8,128)S(1)}, u32[]{:S(2)}, u32[]{:S(2)}) collective-permute-start(f32[64,256]{1,0:T(8,128)S(1)} %solve.1.refs_0_), channel_id=1, source_target_pairs={{0,1},{1,0},{2,3},{3,2},{4,5},{5,4},{6,7},{7,6},{8,9},{9,8},{10,11... | collective-permute-start | bytes 196616 | tf_op jit(solution)/shard_map/ppermute | solution.py:358
  34.7 3.0 %collective-permute-start.19 = (bf16[128,512]{1,0:T(8,128)(2,1)S(1)}, bf16[128,512]{1,0:T(8,128)(2,1)S(1)}, u32[]{:S(2)}, u32[]{:S(2)}) collective-permute-start(bf16[128,512]{1,0:T(8,128)(2,1)S(1)} %get-tuple-element.55), channel_id=1, source_target_pairs={{0,1},{1,0},{2,3},{3,2},{4,5},{5,4},{6,7},{7,6},{8,9},{9,8},{10,11... | collective-permute-start | bytes 393224 | tf_op jit(solution)/shard_map/ppermute | solution.py:358
  35.6 10.1 %collective-permute-start.17 = (bf16[128,512]{1,0:T(8,128)(2,1)S(1)}, bf16[128,512]{1,0:T(8,128)(2,1)S(1)}, u32[]{:S(2)}, u32[]{:S(2)}) collective-permute-start(bf16[128,512]{1,0:T(8,128)(2,1)S(1)} %get-tuple-element.52), channel_id=1, source_target_pairs={{0,6},{1,7},{2,4},{3,5},{4,2},{5,3},{6,0},{7,1},{8,14},{9,15},{10,... | collective-permute-start | bytes 393224 | tf_op jit(solution)/shard_map/ppermute | solution.py:358
  36.4 10.7 %collective-permute-start.18 = (bf16[128,512]{1,0:T(8,128)(2,1)S(1)}, bf16[128,512]{1,0:T(8,128)(2,1)S(1)}, u32[]{:S(2)}, u32[]{:S(2)}) collective-permute-start(bf16[128,512]{1,0:T(8,128)(2,1)S(1)} %get-tuple-element.53), channel_id=1, source_target_pairs={{0,4},{1,5},{2,6},{3,7},{4,0},{5,1},{6,2},{7,3},{8,12},{9,13},{10,... | collective-permute-start | bytes 393224 | tf_op jit(solution)/shard_map/ppermute | solution.py:358
  37.8 9.3 %collective-permute-start.22 = (bf16[128,512]{1,0:T(8,128)(2,1)S(1)}, bf16[128,512]{1,0:T(8,128)(2,1)S(1)}, u32[]{:S(2)}, u32[]{:S(2)}) collective-permute-start(bf16[128,512]{1,0:T(8,128)(2,1)S(1)} %add_convert_fusion), channel_id=1, source_target_pairs={{0,8},{1,9},{2,10},{3,11},{4,12},{5,13},{6,14},{7,15},{8,0},{9,1},... | collective-permute-start | bytes 393224 | tf_op jit(solution)/shard_map/ppermute | solution.py:358
  39.5 7.6 %collective-permute-start.21 = (bf16[128,512]{1,0:T(8,128)(2,1)S(1)}, bf16[128,512]{1,0:T(8,128)(2,1)S(1)}, u32[]{:S(2)}, u32[]{:S(2)}) collective-permute-start(bf16[128,512]{1,0:T(8,128)(2,1)S(1)} %get-tuple-element.59), channel_id=1, source_target_pairs={{0,1},{1,0},{2,3},{3,2},{4,5},{5,4},{6,7},{7,6},{8,9},{9,8},{10,11... | collective-permute-start | bytes 393224 | tf_op jit(solution)/shard_map/ppermute | solution.py:358
  39.5 7.6 %collective-permute-start.20 = (bf16[128,512]{1,0:T(8,128)(2,1)S(1)}, bf16[128,512]{1,0:T(8,128)(2,1)S(1)}, u32[]{:S(2)}, u32[]{:S(2)}) collective-permute-start(bf16[128,512]{1,0:T(8,128)(2,1)S(1)} %get-tuple-element.56), channel_id=1, source_target_pairs={{0,2},{1,3},{2,0},{3,1},{4,6},{5,7},{6,4},{7,5},{8,10},{9,11},{10,... | collective-permute-start | bytes 393224 | tf_op jit(solution)/shard_map/ppermute | solution.py:358
  (6 other events, 4.6 us)

commit v10 on v9

--- a/solution.py
+++ b/solution.py
@@ -246,10 +246,10 @@
         start += part.shape[0]
 
 
-def basis_side_kernel(trades, value_ref, traded_ref, slopes_ref, *refs):
+def basis_side_kernel(trades, first, value_ref, traded_ref, slopes_ref, *refs):
     w_refs, basis_refs = refs[:trades], refs[trades:]
     weights = joined_weights(w_refs)
-    start = 0
+    start = first
     for part in basis_refs:
         here = slice(start, start + part.shape[0])
         total = dot(slopes_ref[here], weights)
@@ -396,7 +396,7 @@
         name="tables",
         scalars=2,
     )
-    notionals = after(jnp.concatenate(notionals, axis=0), basis[-1])
+    notionals = after(jnp.concatenate(notionals, axis=0), weights[1])
     for bit in outer_bits[1:]:
         weights = weights + [
             swap(w if k else after(w, member), 1 << bit) for k, w in enumerate(weights)
@@ -451,15 +451,8 @@
         member, design_rows, slope, *solved, *basis,
         name="weight_side",
     )
-    basis_parts = list(
-        call(
-            partial(basis_side_kernel, outer),
-            [((path_rows, features), BF16)] * inner,
-            value, traded, slopes, *weights,
-            name="basis_side",
-        )
-    )
     terms = [[part] for part in weight_parts]
+    core_step = None
     for bit in reversed(outer_bits):
         count = len(terms) // 2
         arrived = None
@@ -470,11 +463,23 @@
                 gone = after(gone, arrived)
             arrived = swap(gone, 1 << bit)
             terms[k].append(arrived)
-            if bit == outer_bits[-1] and k == count - 1:
-                basis_parts[-1] = after(basis_parts[-1], arrived)
+            if core_step is None:
+                core_step = arrived
         terms = terms[:count]
     weight_terms = terms[0]
-    basis_terms = [basis_parts[0]] + direct(basis_parts, inner_masks)
+
+    def basis_side(first, last, slopes):
+        return call(
+            partial(basis_side_kernel, outer, first * path_rows),
+            [((path_rows, features), BF16)] * (last - first),
+            value, traded, slopes, *weights,
+            name="basis_side",
+        )
+
+    far = list(basis_side(1, inner - 1, slopes))
+    late = after(slopes, core_step)
+    own, near = basis_side(0, 1, late)[0], basis_side(inner - 1, inner, late)[0]
+    basis_terms = [own] + direct([own] + far + [near], inner_masks)
     loss, own_adjoint = call(
         loss_kernel,
         [((8, LANES), F32), ((path_rows, LANES), F32)],

time: 48.1 us -> 47.8 us (level)
  waiting for transfers between devices: 8.46 us -> 7.4 us
  Pallas kernels: 12.2 us -> 12.7 us
    ppermute x23, waiting for transfers between devices: 8.46 us -> 7.4 us  [swap(): return lax.ppermute(x, 'paths', [(d, d ^ mask) for d in range(n)])]
    pallas_call x11 -> x13, Pallas kernels: 12.2 us -> 12.7 us  [call(): pl.pallas_call(kernel, out_shape=[jax.ShapeDtypeStruct(s, d) for s, d in...]
  transfers between devices with their start and end apart: 23 -> 23, of which waited for: 8 -> 7; matrix products, arithmetic and copies ran while one was open for 1% -> 1% of each run, Pallas kernels for 16% -> 17%
where the time goes in v10:
time: 47.8 us; the launch traced here: 47.6 us
  starting transfers between devices  23.6 us (49%)
  Pallas kernels  12.7 us (27%)
  waiting for transfers between devices  7.4 us (15%)
  local copies, waits for them, and re-layouts  3.04 us (6%)
  between operations  0.8 us (2%)
    ppermute x23, starting transfers between devices, swap(): return lax.ppermute(x, 'paths', [(d, d ^ mask) for d in range(n)])  23.6 us
    pallas_call x13, Pallas kernels, call(): pl.pallas_call(kernel, out_shape=[jax.ShapeDtypeStruct(s, d) for s, d in...  12.7 us
    ppermute x23, waiting for transfers between devices, swap(): return lax.ppermute(x, 'paths', [(d, d ^ mask) for d in range(n)])  7.4 us
    unnamed x14, local copies, waits for them, and re-layouts  2.52 us
  transfers between devices with their start and end apart: 23, of which 7 were waited for; matrix products, arithmetic and copies ran while one was open for 1% of the time, Pallas kernels for 17%

profile of v10, /device:TPU:0, one launch (start us, length us, event | category | flops | bytes accessed | tf_op | source)
XLA Modules:
  0.0 47.6 jit_solution(14688268779243808732)
XLA Ops:
  0.6 4.1 %collective-permute-start.3 = (bf16[128,512]{1,0:T(8,128)(2,1)}, bf16[128,512]{1,0:T(8,128)(2,1)S(1)}, u32[]{:S(2)}, u32[]{:S(2)}) collective-permute-start(bf16[128,512]{1,0:T(8,128)(2,1)} %w_ref.1), channel_id=1, source_target_pairs={{0,8},{1,9},{2,10},{3,11},{4,12},{5,13},{6,14},{7,15},{8,0},{9,1},... | collective-permute-start | bytes 393224 | tf_op jit(solution)/shard_map/ppermute | solution.py:358
  4.7 2.5 %collective-permute-start = (bf16[128,512]{1,0:T(8,128)(2,1)}, bf16[128,512]{1,0:T(8,128)(2,1)S(1)}, u32[]{:S(2)}, u32[]{:S(2)}) collective-permute-start(bf16[128,512]{1,0:T(8,128)(2,1)} %x_ref.1), channel_id=1, source_target_pairs={{0,6},{1,7},{2,4},{3,5},{4,2},{5,3},{6,0},{7,1},{8,14},{9,15},{10,... | collective-permute-start | bytes 393224 | tf_op jit(solution)/shard_map/ppermute | solution.py:358
  9.0 0.9 %copy-done = bf16[128,512]{1,0:T(8,128)(2,1)S(1)} copy-done((bf16[128,512]{1,0:T(8,128)(2,1)S(1)}, bf16[128,512]{1,0:T(8,128)(2,1)}, u32[]{:S(2)}) %copy-start) | copy-done | bytes 131096
  9.9 0.9 %copy-done.1 = bf16[128,512]{1,0:T(8,128)(2,1)S(1)} copy-done((bf16[128,512]{1,0:T(8,128)(2,1)S(1)}, bf16[128,512]{1,0:T(8,128)(2,1)}, u32[]{:S(2)}) %copy-start.1) | copy-done | bytes 131096
  11.5 2.0 %collective-permute-done.6 = bf16[128]{0:T(256)(128)(2,1)S(1)} collective-permute-done((bf16[128]{0:T(256)(128)(2,1)}, bf16[128]{0:T(256)(128)(2,1)S(1)}, u32[]{:S(2)}, u32[]{:S(2)}) %collective-permute-start.6) | collective-permute-done | bytes 288 | tf_op jit(solution)/shard_map/ppermute | solution.py:358
  14.1 1.2 %collective-permute-done.1.refs_2_.refs_4_ = bf16[128,512]{1,0:T(8,128)(2,1)S(1)} collective-permute-done((bf16[128,512]{1,0:T(8,128)(2,1)}, bf16[128,512]{1,0:T(8,128)(2,1)S(1)}, u32[]{:S(2)}, u32[]{:S(2)}) %collective-permute-start.1) | collective-permute-done | bytes 131104 | tf_op jit(solution)/shard_map/ppermute | solution.py:358
  15.5 1.3 %forward.1 = (bf16[512,512]{1,0:T(8,128)(2,1)S(1)}, f32[32,256]{1,0:T(8,128)S(1)}, f32[32,256]{1,0:T(8,128)S(1)}) custom-call(bf16[128,512]{1,0:T(8,128)(2,1)S(1)} %get-tuple-element.31.refs_0_.refs_2_, bf16[128,512]{1,0:T(8,128)(2,1)S(1)} %collective-permute-done.refs_1_.refs_3_, bf16[128,512]{1,0:T(8,128)(2,1)S(1)} %collective-permute-done.1.refs_2_.refs_4_, ...), custom_call_target="tpu_custom_call" | custom-call | bytes 2196480 | tf_op jit(solution)/shard_map/forward/pallas_call | solution.py:330
  16.8 1.2 %collective-permute-done.8 = f32[32,256]{1,0:T(8,128)S(1)} collective-permute-done((f32[32,256]{1,0:T(8,128)S(1)}, f32[32,256]{1,0:T(8,128)S(1)}, u32[]{:S(2)}, u32[]{:S(2)}) %collective-permute-start.8) | collective-permute-done | bytes 32800 | tf_op jit(solution)/shard_map/ppermute | solution.py:358
  18.0 3.1 %collective-permute-start.12 = (f32[32,256]{1,0:T(8,128)S(1)}, f32[32,256]{1,0:T(8,128)S(1)}, u32[]{:S(2)}, u32[]{:S(2)}) collective-permute-start(f32[32,256]{1,0:T(8,128)S(1)} %add.9), channel_id=1, source_target_pairs={{0,8},{1,9},{2,10},{3,11},{4,12},{5,13},{6,14},{7,15},{8,0},{9,1},... | collective-permute-start | bytes 98312 | tf_op jit(solution)/shard_map/ppermute | solution.py:358
  21.1 3.0 %collective-permute-start.11 = (bf16[32,512]{1,0:T(8,128)(2,1)S(1)}, bf16[32,512]{1,0:T(8,128)(2,1)S(1)}, u32[]{:S(2)}, u32[]{:S(2)}) collective-permute-start(bf16[32,512]{1,0:T(8,128)(2,1)S(1)} %lead.1.refs_9_), channel_id=1, source_target_pairs={{0,9},{1,8},{2,11},{3,10},{4,13},{5,12},{6,15},{7,14},{8,1},{9,0},... | collective-permute-start | bytes 98312 | tf_op jit(solution)/shard_map/ppermute | solution.py:358
  24.1 1.7 %collective-permute-start.13 = (f32[32,256]{1,0:T(8,128)S(1)}, f32[32,256]{1,0:T(8,128)S(1)}, u32[]{:S(2)}, u32[]{:S(2)}) collective-permute-start(f32[32,256]{1,0:T(8,128)S(1)} %add.10.refs_0_), channel_id=1, source_target_pairs={{0,6},{1,7},{2,4},{3,5},{4,2},{5,3},{6,0},{7,1},{8,14},{9,15},{10,... | collective-permute-start | bytes 98312 | tf_op jit(solution)/shard_map/ppermute | solution.py:358
  25.8 1.3 %collective-permute-start.14 = (f32[32,256]{1,0:T(8,128)S(1)}, f32[32,256]{1,0:T(8,128)S(1)}, u32[]{:S(2)}, u32[]{:S(2)}) collective-permute-start(f32[32,256]{1,0:T(8,128)S(1)} %add.10.refs_0_), channel_id=1, source_target_pairs={{0,4},{1,5},{2,6},{3,7},{4,0},{5,1},{6,2},{7,3},{8,12},{9,13},{10,... | collective-permute-start | bytes 98312 | tf_op jit(solution)/shard_map/ppermute | solution.py:358
  28.2 1.8 %inverse.1.inverse_ref = f32[32,32]{1,0:T(8,128)S(1)} custom-call(bf16[4,32,512]{2,1,0:T(8,128)(2,1)S(1)} %pad_maximum_fusion.small_ref), custom_call_target="tpu_custom_call" | custom-call | bytes 135168 | tf_op jit(solution)/shard_map/inverse/pallas_call | solution.py:330
  30.0 1.0 %collective-permute-done.15.refs_3_ = f32[32,256]{1,0:T(8,128)S(1)} collective-permute-done((f32[32,256]{1,0:T(8,128)S(1)}, f32[32,256]{1,0:T(8,128)S(1)}, u32[]{:S(2)}, u32[]{:S(2)}) %collective-permute-start.15) | collective-permute-done | bytes 32800 | tf_op jit(solution)/shard_map/ppermute | solution.py:358
  31.0 1.5 %solve.1.refs_0_ = f32[64,256]{1,0:T(8,128)S(1)} custom-call(f32[32,32]{1,0:T(8,128)S(1)} %inverse.1.inverse_ref, bf16[32,2048]{1,0:T(8,128)(2,1)S(1)} %get-tuple-element.43.design_ref, bf16[2048,128]{1,0:T(8,128)(2,1)S(1)} %get-tuple-element.40.rows_ref, f32[1,512]{1,0:T(1,128)S(1)} %get-tuple-element.41.thresh_ref, ...), custom_call_target="tpu_custom_call" | custom-call | bytes 860160 | tf_op jit(solution)/shard_map/solve/pallas_call | solution.py:330
  32.5 0.9 %slope.1.slope_ref = f32[512,512]{1,0:T(8,128)S(1)} custom-call(bf16[128,512]{1,0:T(8,128)(2,1)S(1)} %get-tuple-element.31.refs_0_.refs_2_, bf16[128,512]{1,0:T(8,128)(2,1)S(1)} %collective-permute-done.refs_1_.refs_3_, bf16[128,512]{1,0:T(8,128)(2,1)S(1)} %collective-permute-done.1.refs_2_.refs_4_, ...), custom_call_target="tpu_custom_call" | custom-call | bytes 2098176 | tf_op jit(solution)/shard_map/slope/pallas_call | solution.py:330
  33.7 0.9 %weight_side.1 = (bf16[128,512]{1,0:T(8,128)(2,1)S(1)}, bf16[512,512]{1,0:T(8,128)(2,1)S(1)}, bf16[128,512]{1,0:T(8,128)(2,1)S(1)}, bf16[128,512]{1,0:T(8,128)(2...) custom-call(bf16[512,512]{1,0:T(8,128)(2,1)S(1)} %get-tuple-element.33.refs_10_.member_ref, ...), custom_call_target="tpu_custom_call" | custom-call | bytes 3932160 | tf_op jit(solution)/shard_map/weight_side/pallas_call | solution.py:330
  35.3 1.1 %collective-permute-start.18 = (bf16[128,512]{1,0:T(8,128)(2,1)S(1)}, bf16[128,512]{1,0:T(8,128)(2,1)S(1)}, u32[]{:S(2)}, u32[]{:S(2)}) collective-permute-start(bf16[128,512]{1,0:T(8,128)(2,1)S(1)} %get-tuple-element.51), channel_id=1, source_target_pairs={{0,6},{1,7},{2,4},{3,5},{4,2},{5,3},{6,0},{7,1},{8,14},{9,15},{10,... | collective-permute-start | bytes 393224 | tf_op jit(solution)/shard_map/ppermute | solution.py:358
  36.4 1.0 %collective-permute-start.19 = (bf16[128,512]{1,0:T(8,128)(2,1)S(1)}, bf16[128,512]{1,0:T(8,128)(2,1)S(1)}, u32[]{:S(2)}, u32[]{:S(2)}) collective-permute-start(bf16[128,512]{1,0:T(8,128)(2,1)S(1)} %get-tuple-element.52), channel_id=1, source_target_pairs={{0,4},{1,5},{2,6},{3,7},{4,0},{5,1},{6,2},{7,3},{8,12},{9,13},{10,... | collective-permute-start | bytes 393224 | tf_op jit(solution)/shard_map/ppermute | solution.py:358
  37.5 1.8 %collective-permute-start.22 = (bf16[128,512]{1,0:T(8,128)(2,1)S(1)}, bf16[128,512]{1,0:T(8,128)(2,1)S(1)}, u32[]{:S(2)}, u32[]{:S(2)}) collective-permute-start(bf16[128,512]{1,0:T(8,128)(2,1)S(1)} %add_convert_fusion), channel_id=1, source_target_pairs={{0,8},{1,9},{2,10},{3,11},{4,12},{5,13},{6,14},{7,15},{8,0},{9,1},... | collective-permute-start | bytes 393224 | tf_op jit(solution)/shard_map/ppermute | solution.py:358
  39.6 1.5 %collective-permute-start.20 = (bf16[128,512]{1,0:T(8,128)(2,1)S(1)}, bf16[128,512]{1,0:T(8,128)(2,1)S(1)}, u32[]{:S(2)}, u32[]{:S(2)}) collective-permute-start(bf16[128,512]{1,0:T(8,128)(2,1)S(1)} %basis_side.5), channel_id=1, source_target_pairs={{0,2},{1,3},{2,0},{3,1},{4,6},{5,7},{6,4},{7,5},{8,10},{9,11},{10,... | collective-permute-start | bytes 393224 | tf_op jit(solution)/shard_map/ppermute | solution.py:358
  41.1 3.2 %loss.1 = (f32[8,128]{1,0:T(8,128)S(1)}, f32[128,128]{1,0:T(8,128)S(1)}) custom-call(bf16[2048,128]{1,0:T(8,128)(2,1)S(1)} %get-tuple-element.40.rows_ref, f32[1,512]{1,0:T(1,128)S(1)} %get-tuple-element.41.thresh_ref, f32[1,512]{1,0:T(1,128)S(1)} %get-tuple-element.42.rate_ref, f32[64,256]{1,0:T(8,128)S(1)} %solve.1.refs_0_, ...), custom_call_target="tpu_custom_call" | custom-call | bytes 729088 | tf_op jit(solution)/shard_map/loss/pallas_call | solution.py:330
  45.4 1.4 %collective-permute-done.19.refs_2_ = bf16[128,512]{1,0:T(8,128)(2,1)S(1)} collective-permute-done((bf16[128,512]{1,0:T(8,128)(2,1)S(1)}, bf16[128,512]{1,0:T(8,128)(2,1)S(1)}, u32[]{:S(2)}, u32[]{:S(2)}) %collective-permute-start.19) | collective-permute-done | bytes 131104 | tf_op jit(solution)/shard_map/ppermute | solution.py:358
  46.8 0.9 %sums.1 = (f32[128,512]{1,0:T(8,128)}, f32[128,512]{1,0:T(8,128)}) custom-call(f32[128,128]{1,0:T(8,128)S(1)} %get-tuple-element.45.own_ref, bf16[128,512]{1,0:T(8,128)(2,1)S(1)} %basis_side.3.refs_0_, bf16[128,512]{1,0:T(8,128)(2,1)S(1)} %collective-permute-done.18.refs_1_, bf16[128,512]{1,0:T(8,128)(2,1)S(1)} %collective-permute-done.19.refs_2_, ...), custom_call_target="tpu_custom_call" | custom-call | bytes 1507328 | tf_op jit(solution)/shard_map/sums/pallas_call | solution.py:330
  (56 shorter events, 6.9 us)
Async XLA Ops:
  0.6 7.7 %copy-start.2 = (s32[2048]{0:T(1024)S(1)}, s32[2048]{0:T(1024)}, u32[]{:S(2)}) copy-start(s32[2048]{0:T(1024)} %param.10) | copy-start | bytes 24580
  0.6 12.9 %collective-permute-start.3 = (bf16[128,512]{1,0:T(8,128)(2,1)}, bf16[128,512]{1,0:T(8,128)(2,1)S(1)}, u32[]{:S(2)}, u32[]{:S(2)}) collective-permute-start(bf16[128,512]{1,0:T(8,128)(2,1)} %w_ref.1), channel_id=1, source_target_pairs={{0,8},{1,9},{2,10},{3,11},{4,12},{5,13},{6,14},{7,15},{8,0},{9,1},... | collective-permute-start | bytes 393224 | tf_op jit(solution)/shard_map/ppermute | solution.py:358
  4.7 9.3 %collective-permute-start = (bf16[128,512]{1,0:T(8,128)(2,1)}, bf16[128,512]{1,0:T(8,128)(2,1)S(1)}, u32[]{:S(2)}, u32[]{:S(2)}) collective-permute-start(bf16[128,512]{1,0:T(8,128)(2,1)} %x_ref.1), channel_id=1, source_target_pairs={{0,6},{1,7},{2,4},{3,5},{4,2},{5,3},{6,0},{7,1},{8,14},{9,15},{10,... | collective-permute-start | bytes 393224 | tf_op jit(solution)/shard_map/ppermute | solution.py:358
  7.3 8.1 %collective-permute-start.1 = (bf16[128,512]{1,0:T(8,128)(2,1)}, bf16[128,512]{1,0:T(8,128)(2,1)S(1)}, u32[]{:S(2)}, u32[]{:S(2)}) collective-permute-start(bf16[128,512]{1,0:T(8,128)(2,1)} %x_ref.1), channel_id=1, source_target_pairs={{0,4},{1,5},{2,6},{3,7},{4,0},{5,1},{6,2},{7,3},{8,12},{9,13},{10,... | collective-permute-start | bytes 393224 | tf_op jit(solution)/shard_map/ppermute | solution.py:358
  7.7 7.6 %collective-permute-start.2 = (bf16[128,512]{1,0:T(8,128)(2,1)}, bf16[128,512]{1,0:T(8,128)(2,1)S(1)}, u32[]{:S(2)}, u32[]{:S(2)}) collective-permute-start(bf16[128,512]{1,0:T(8,128)(2,1)} %x_ref.1), channel_id=1, source_target_pairs={{0,2},{1,3},{2,0},{3,1},{4,6},{5,7},{6,4},{7,5},{8,10},{9,11},{10,... | collective-permute-start | bytes 393224 | tf_op jit(solution)/shard_map/ppermute | solution.py:358
  8.2 5.3 %collective-permute-start.6 = (bf16[128]{0:T(256)(128)(2,1)}, bf16[128]{0:T(256)(128)(2,1)S(1)}, u32[]{:S(2)}, u32[]{:S(2)}) collective-permute-start(bf16[128]{0:T(256)(128)(2,1)} %param.9), channel_id=1, source_target_pairs={{0,8},{1,9},{2,10},{3,11},{4,12},{5,13},{6,14},{7,15},{8,0},{9,1},... | collective-permute-start | bytes 776 | tf_op jit(solution)/shard_map/ppermute | solution.py:358
  13.5 1.9 %collective-permute-start.4 = (bf16[128,512]{1,0:T(8,128)(2,1)S(1)}, bf16[128,512]{1,0:T(8,128)(2,1)S(1)}, u32[]{:S(2)}, u32[]{:S(2)}) collective-permute-start(bf16[128,512]{1,0:T(8,128)(2,1)S(1)} %copy-done.1), channel_id=1, source_target_pairs={{0,1},{1,0},{2,3},{3,2},{4,5},{5,4},{6,7},{7,6},{8,9},{9,8},{10,11... | collective-permute-start | bytes 393224 | tf_op jit(solution)/shard_map/ppermute | solution.py:358
  13.5 1.9 %collective-permute-start.5 = (bf16[128,512]{1,0:T(8,128)(2,1)S(1)}, bf16[128,512]{1,0:T(8,128)(2,1)S(1)}, u32[]{:S(2)}, u32[]{:S(2)}) collective-permute-start(bf16[128,512]{1,0:T(8,128)(2,1)S(1)} %collective-permute-done.3.refs_5_.refs_1_), channel_id=1, source_target_pairs={{0,1},{1,0},{2,3},{3,2},{4,5},{5,4},{6,7},{7,6},{8,9},{9,8},{10,11... | collective-permute-start | bytes 393224 | tf_op jit(solution)/shard_map/ppermute | solution.py:358
  14.1 1.4 %collective-permute-start.7 = (bf16[2,128]{1,0:T(2,128)(2,1)S(1)}, bf16[2,128]{1,0:T(2,128)(2,1)S(1)}, u32[]{:S(2)}, u32[]{:S(2)}) collective-permute-start(bf16[2,128]{1,0:T(2,128)(2,1)S(1)} %pad_maximum_fusion.2), channel_id=1, source_target_pairs={{0,1},{1,0},{2,3},{3,2},{4,5},{5,4},{6,7},{7,6},{8,9},{9,8},{10,11... | collective-permute-start | bytes 1544 | tf_op jit(solution)/shard_map/ppermute | solution.py:358
  16.7 1.3 %collective-permute-start.8 = (f32[32,256]{1,0:T(8,128)S(1)}, f32[32,256]{1,0:T(8,128)S(1)}, u32[]{:S(2)}, u32[]{:S(2)}) collective-permute-start(f32[32,256]{1,0:T(8,128)S(1)} %get-tuple-element.38), channel_id=1, source_target_pairs={{0,1},{1,0},{2,3},{3,2},{4,5},{5,4},{6,7},{7,6},{8,9},{9,8},{10,11... | collective-permute-start | bytes 98312 | tf_op jit(solution)/shard_map/ppermute | solution.py:358
  18.0 6.1 %collective-permute-start.12 = (f32[32,256]{1,0:T(8,128)S(1)}, f32[32,256]{1,0:T(8,128)S(1)}, u32[]{:S(2)}, u32[]{:S(2)}) collective-permute-start(f32[32,256]{1,0:T(8,128)S(1)} %add.9), channel_id=1, source_target_pairs={{0,8},{1,9},{2,10},{3,11},{4,12},{5,13},{6,14},{7,15},{8,0},{9,1},... | collective-permute-start | bytes 98312 | tf_op jit(solution)/shard_map/ppermute | solution.py:358
  21.1 6.0 %collective-permute-start.9 = (bf16[32,512]{1,0:T(8,128)(2,1)S(1)}, bf16[32,512]{1,0:T(8,128)(2,1)S(1)}, u32[]{:S(2)}, u32[]{:S(2)}) collective-permute-start(bf16[32,512]{1,0:T(8,128)(2,1)S(1)} %lead.1.refs_9_), channel_id=1, source_target_pairs={{0,8},{1,9},{2,10},{3,11},{4,12},{5,13},{6,14},{7,15},{8,0},{9,1},... | collective-permute-start | bytes 98312 | tf_op jit(solution)/shard_map/ppermute | solution.py:358
  21.1 6.5 %collective-permute-start.10 = (bf16[32,512]{1,0:T(8,128)(2,1)S(1)}, bf16[32,512]{1,0:T(8,128)(2,1)S(1)}, u32[]{:S(2)}, u32[]{:S(2)}) collective-permute-start(bf16[32,512]{1,0:T(8,128)(2,1)S(1)} %lead.1.refs_9_), channel_id=1, source_target_pairs={{0,1},{1,0},{2,3},{3,2},{4,5},{5,4},{6,7},{7,6},{8,9},{9,8},{10,11... | collective-permute-start | bytes 98312 | tf_op jit(solution)/shard_map/ppermute | solution.py:358
  21.1 6.5 %collective-permute-start.11 = (bf16[32,512]{1,0:T(8,128)(2,1)S(1)}, bf16[32,512]{1,0:T(8,128)(2,1)S(1)}, u32[]{:S(2)}, u32[]{:S(2)}) collective-permute-start(bf16[32,512]{1,0:T(8,128)(2,1)S(1)} %lead.1.refs_9_), channel_id=1, source_target_pairs={{0,9},{1,8},{2,11},{3,10},{4,13},{5,12},{6,15},{7,14},{8,1},{9,0},... | collective-permute-start | bytes 98312 | tf_op jit(solution)/shard_map/ppermute | solution.py:358
  24.1 5.9 %collective-permute-start.13 = (f32[32,256]{1,0:T(8,128)S(1)}, f32[32,256]{1,0:T(8,128)S(1)}, u32[]{:S(2)}, u32[]{:S(2)}) collective-permute-start(f32[32,256]{1,0:T(8,128)S(1)} %add.10.refs_0_), channel_id=1, source_target_pairs={{0,6},{1,7},{2,4},{3,5},{4,2},{5,3},{6,0},{7,1},{8,14},{9,15},{10,... | collective-permute-start | bytes 98312 | tf_op jit(solution)/shard_map/ppermute | solution.py:358
  25.8 4.2 %collective-permute-start.14 = (f32[32,256]{1,0:T(8,128)S(1)}, f32[32,256]{1,0:T(8,128)S(1)}, u32[]{:S(2)}, u32[]{:S(2)}) collective-permute-start(f32[32,256]{1,0:T(8,128)S(1)} %add.10.refs_0_), channel_id=1, source_target_pairs={{0,4},{1,5},{2,6},{3,7},{4,0},{5,1},{6,2},{7,3},{8,12},{9,13},{10,... | collective-permute-start | bytes 98312 | tf_op jit(solution)/shard_map/ppermute | solution.py:358
  27.1 3.9 %collective-permute-start.15 = (f32[32,256]{1,0:T(8,128)S(1)}, f32[32,256]{1,0:T(8,128)S(1)}, u32[]{:S(2)}, u32[]{:S(2)}) collective-permute-start(f32[32,256]{1,0:T(8,128)S(1)} %add.10.refs_0_), channel_id=1, source_target_pairs={{0,2},{1,3},{2,0},{3,1},{4,6},{5,7},{6,4},{7,5},{8,10},{9,11},{10,... | collective-permute-start | bytes 98312 | tf_op jit(solution)/shard_map/ppermute | solution.py:358
  32.5 1.3 %collective-permute-start.16 = (f32[64,256]{1,0:T(8,128)S(1)}, f32[64,256]{1,0:T(8,128)S(1)}, u32[]{:S(2)}, u32[]{:S(2)}) collective-permute-start(f32[64,256]{1,0:T(8,128)S(1)} %solve.1.refs_0_), channel_id=1, source_target_pairs={{0,1},{1,0},{2,3},{3,2},{4,5},{5,4},{6,7},{7,6},{8,9},{9,8},{10,11... | collective-permute-start | bytes 196616 | tf_op jit(solution)/shard_map/ppermute | solution.py:358
  34.6 2.8 %collective-permute-start.17 = (bf16[128,512]{1,0:T(8,128)(2,1)S(1)}, bf16[128,512]{1,0:T(8,128)(2,1)S(1)}, u32[]{:S(2)}, u32[]{:S(2)}) collective-permute-start(bf16[128,512]{1,0:T(8,128)(2,1)S(1)} %get-tuple-element.49), channel_id=1, source_target_pairs={{0,1},{1,0},{2,3},{3,2},{4,5},{5,4},{6,7},{7,6},{8,9},{9,8},{10,11... | collective-permute-start | bytes 393224 | tf_op jit(solution)/shard_map/ppermute | solution.py:358
  35.3 10.1 %collective-permute-start.18 = (bf16[128,512]{1,0:T(8,128)(2,1)S(1)}, bf16[128,512]{1,0:T(8,128)(2,1)S(1)}, u32[]{:S(2)}, u32[]{:S(2)}) collective-permute-start(bf16[128,512]{1,0:T(8,128)(2,1)S(1)} %get-tuple-element.51), channel_id=1, source_target_pairs={{0,6},{1,7},{2,4},{3,5},{4,2},{5,3},{6,0},{7,1},{8,14},{9,15},{10,... | collective-permute-start | bytes 393224 | tf_op jit(solution)/shard_map/ppermute | solution.py:358
  36.4 10.4 %collective-permute-start.19 = (bf16[128,512]{1,0:T(8,128)(2,1)S(1)}, bf16[128,512]{1,0:T(8,128)(2,1)S(1)}, u32[]{:S(2)}, u32[]{:S(2)}) collective-permute-start(bf16[128,512]{1,0:T(8,128)(2,1)S(1)} %get-tuple-element.52), channel_id=1, source_target_pairs={{0,4},{1,5},{2,6},{3,7},{4,0},{5,1},{6,2},{7,3},{8,12},{9,13},{10,... | collective-permute-start | bytes 393224 | tf_op jit(solution)/shard_map/ppermute | solution.py:358
  37.5 9.3 %collective-permute-start.22 = (bf16[128,512]{1,0:T(8,128)(2,1)S(1)}, bf16[128,512]{1,0:T(8,128)(2,1)S(1)}, u32[]{:S(2)}, u32[]{:S(2)}) collective-permute-start(bf16[128,512]{1,0:T(8,128)(2,1)S(1)} %add_convert_fusion), channel_id=1, source_target_pairs={{0,8},{1,9},{2,10},{3,11},{4,12},{5,13},{6,14},{7,15},{8,0},{9,1},... | collective-permute-start | bytes 393224 | tf_op jit(solution)/shard_map/ppermute | solution.py:358
  39.2 7.5 %collective-permute-start.21 = (bf16[128,512]{1,0:T(8,128)(2,1)S(1)}, bf16[128,512]{1,0:T(8,128)(2,1)S(1)}, u32[]{:S(2)}, u32[]{:S(2)}) collective-permute-start(bf16[128,512]{1,0:T(8,128)(2,1)S(1)} %get-tuple-element.55), channel_id=1, source_target_pairs={{0,1},{1,0},{2,3},{3,2},{4,5},{5,4},{6,7},{7,6},{8,9},{9,8},{10,11... | collective-permute-start | bytes 393224 | tf_op jit(solution)/shard_map/ppermute | solution.py:358
  39.6 7.2 %collective-permute-start.20 = (bf16[128,512]{1,0:T(8,128)(2,1)S(1)}, bf16[128,512]{1,0:T(8,128)(2,1)S(1)}, u32[]{:S(2)}, u32[]{:S(2)}) collective-permute-start(bf16[128,512]{1,0:T(8,128)(2,1)S(1)} %basis_side.5), channel_id=1, source_target_pairs={{0,2},{1,3},{2,0},{3,1},{4,6},{5,7},{6,4},{7,5},{8,10},{9,11},{10,... | collective-permute-start | bytes 393224 | tf_op jit(solution)/shard_map/ppermute | solution.py:358
  (6 other events, 4.6 us)

commit v11 on v10

--- a/solution.py
+++ b/solution.py
@@ -410,13 +410,10 @@
         *basis, *weights, notionals, lead, member,
         name="forward",
     )
-    moment = moments[0] + swap(moments[1], SHARES - 1)
-    lead = after(lead, moment)
-    leads = [lead] + direct([lead] * outer, outer_masks)
-    for bit in outer_bits[:-1]:
-        there = swap(moment, 1 << bit)
-        moment = moment + there
-    small = jnp.stack(leads)
+    sent = [moments[mask & (SHARES - 1)] for mask in outer_masks]
+    moment = sum(direct(sent, outer_masks), moments[0])
+    lead = after(lead, value)
+    small = jnp.stack([lead] + direct([lead] * outer, outer_masks))
     moments = [moment] + direct([moment] * inner, inner_masks)
     (inverse,) = call(
         partial(inverse_kernel, RIDGE_SCALE * paths_all),

time: 47.8 us -> 48.2 us (level)
  starting transfers between devices: 23.6 us -> 24.1 us
    ppermute x23 -> x24, starting transfers between devices: 23.6 us -> 24.1 us  [swap(): return lax.ppermute(x, 'paths', [(d, d ^ mask) for d in range(n)])]
    ppermute x23 -> x24, waiting for transfers between devices: 7.4 us -> 7.29 us  [swap(): return lax.ppermute(x, 'paths', [(d, d ^ mask) for d in range(n)])]
  transfers between devices with their start and end apart: 23 -> 24, of which waited for: 7 -> 7; matrix products, arithmetic and copies ran while one was open for 1% -> 1% of each run, Pallas kernels for 17% -> 17%
where the time goes in v11:
time: 48.2 us; the launch traced here: 48 us
  starting transfers between devices  24.1 us (50%)
  Pallas kernels  12.7 us (26%)
  waiting for transfers between devices  7.29 us (15%)
  local copies, waits for them, and re-layouts  3.04 us (6%)
  between operations  0.8 us (2%)
    ppermute x24, starting transfers between devices, swap(): return lax.ppermute(x, 'paths', [(d, d ^ mask) for d in range(n)])  24.1 us
    pallas_call x13, Pallas kernels, call(): pl.pallas_call(kernel, out_shape=[jax.ShapeDtypeStruct(s, d) for s, d in...  12.7 us
    ppermute x24, waiting for transfers between devices, swap(): return lax.ppermute(x, 'paths', [(d, d ^ mask) for d in range(n)])  7.29 us
    unnamed x14, local copies, waits for them, and re-layouts  2.52 us
  transfers between devices with their start and end apart: 24, of which 7 were waited for; matrix products, arithmetic and copies ran while one was open for 1% of the time, Pallas kernels for 17%

profile of v11, /device:TPU:0, one launch (start us, length us, event | category | flops | bytes accessed | tf_op | source)
XLA Modules:
  0.0 48.0 jit_solution(3460732679797646314)
XLA Ops:
  0.6 4.1 %collective-permute-start.3 = (bf16[128,512]{1,0:T(8,128)(2,1)}, bf16[128,512]{1,0:T(8,128)(2,1)S(1)}, u32[]{:S(2)}, u32[]{:S(2)}) collective-permute-start(bf16[128,512]{1,0:T(8,128)(2,1)} %w_ref.1), channel_id=1, source_target_pairs={{0,8},{1,9},{2,10},{3,11},{4,12},{5,13},{6,14},{7,15},{8,0},{9,1},... | collective-permute-start | bytes 393224 | tf_op jit(solution)/shard_map/ppermute | solution.py:358
  4.7 2.5 %collective-permute-start = (bf16[128,512]{1,0:T(8,128)(2,1)}, bf16[128,512]{1,0:T(8,128)(2,1)S(1)}, u32[]{:S(2)}, u32[]{:S(2)}) collective-permute-start(bf16[128,512]{1,0:T(8,128)(2,1)} %x_ref.1), channel_id=1, source_target_pairs={{0,6},{1,7},{2,4},{3,5},{4,2},{5,3},{6,0},{7,1},{8,14},{9,15},{10,... | collective-permute-start | bytes 393224 | tf_op jit(solution)/shard_map/ppermute | solution.py:358
  9.0 0.9 %copy-done = bf16[128,512]{1,0:T(8,128)(2,1)S(1)} copy-done((bf16[128,512]{1,0:T(8,128)(2,1)S(1)}, bf16[128,512]{1,0:T(8,128)(2,1)}, u32[]{:S(2)}) %copy-start) | copy-done | bytes 131096
  9.9 0.9 %copy-done.1 = bf16[128,512]{1,0:T(8,128)(2,1)S(1)} copy-done((bf16[128,512]{1,0:T(8,128)(2,1)S(1)}, bf16[128,512]{1,0:T(8,128)(2,1)}, u32[]{:S(2)}) %copy-start.1) | copy-done | bytes 131096
  11.5 2.0 %collective-permute-done.6 = bf16[128]{0:T(256)(128)(2,1)S(1)} collective-permute-done((bf16[128]{0:T(256)(128)(2,1)}, bf16[128]{0:T(256)(128)(2,1)S(1)}, u32[]{:S(2)}, u32[]{:S(2)}) %collective-permute-start.6) | collective-permute-done | bytes 288 | tf_op jit(solution)/shard_map/ppermute | solution.py:358
  14.1 1.2 %collective-permute-done.1.refs_2_.refs_4_ = bf16[128,512]{1,0:T(8,128)(2,1)S(1)} collective-permute-done((bf16[128,512]{1,0:T(8,128)(2,1)}, bf16[128,512]{1,0:T(8,128)(2,1)S(1)}, u32[]{:S(2)}, u32[]{:S(2)}) %collective-permute-start.1) | collective-permute-done | bytes 131104 | tf_op jit(solution)/shard_map/ppermute | solution.py:358
  15.5 1.3 %forward.1 = (bf16[512,512]{1,0:T(8,128)(2,1)S(1)}, f32[32,256]{1,0:T(8,128)S(1)}, f32[32,256]{1,0:T(8,128)S(1)}) custom-call(bf16[128,512]{1,0:T(8,128)(2,1)S(1)} %get-tuple-element.31.refs_0_.refs_2_, bf16[128,512]{1,0:T(8,128)(2,1)S(1)} %collective-permute-done.refs_1_.refs_3_, bf16[128,512]{1,0:T(8,128)(2,1)S(1)} %collective-permute-done.1.refs_2_.refs_4_, ...), custom_call_target="tpu_custom_call" | custom-call | bytes 2196480 | tf_op jit(solution)/shard_map/forward/pallas_call | solution.py:330
  16.7 3.1 %collective-permute-start.11 = (f32[32,256]{1,0:T(8,128)S(1)}, f32[32,256]{1,0:T(8,128)S(1)}, u32[]{:S(2)}, u32[]{:S(2)}) collective-permute-start(f32[32,256]{1,0:T(8,128)S(1)} %get-tuple-element.43), channel_id=1, source_target_pairs={{0,8},{1,9},{2,10},{3,11},{4,12},{5,13},{6,14},{7,15},{8,0},{9,1},... | collective-permute-start | bytes 98312 | tf_op jit(solution)/shard_map/ppermute | solution.py:358
  20.0 2.9 %collective-permute-start.8 = (bf16[32,512]{1,0:T(8,128)(2,1)S(1)}, bf16[32,512]{1,0:T(8,128)(2,1)S(1)}, u32[]{:S(2)}, u32[]{:S(2)}) collective-permute-start(bf16[32,512]{1,0:T(8,128)(2,1)S(1)} %lead.1.refs_9_), channel_id=1, source_target_pairs={{0,8},{1,9},{2,10},{3,11},{4,12},{5,13},{6,14},{7,15},{8,0},{9,1},... | collective-permute-start | bytes 98312 | tf_op jit(solution)/shard_map/ppermute | solution.py:358
  23.3 1.1 %collective-permute-done.13 = f32[32,256]{1,0:T(8,128)S(1)} collective-permute-done((f32[32,256]{1,0:T(8,128)S(1)}, f32[32,256]{1,0:T(8,128)S(1)}, u32[]{:S(2)}, u32[]{:S(2)}) %collective-permute-start.13) | collective-permute-done | bytes 32800 | tf_op jit(solution)/shard_map/ppermute | solution.py:358
  24.5 1.5 %collective-permute-start.14 = (f32[32,256]{1,0:T(8,128)S(1)}, f32[32,256]{1,0:T(8,128)S(1)}, u32[]{:S(2)}, u32[]{:S(2)}) collective-permute-start(f32[32,256]{1,0:T(8,128)S(1)} %add_add_fusion.refs_0_), channel_id=1, source_target_pairs={{0,6},{1,7},{2,4},{3,5},{4,2},{5,3},{6,0},{7,1},{8,14},{9,15},{10,... | collective-permute-start | bytes 98312 | tf_op jit(solution)/shard_map/ppermute | solution.py:358
  25.9 1.2 %collective-permute-start.15 = (f32[32,256]{1,0:T(8,128)S(1)}, f32[32,256]{1,0:T(8,128)S(1)}, u32[]{:S(2)}, u32[]{:S(2)}) collective-permute-start(f32[32,256]{1,0:T(8,128)S(1)} %add_add_fusion.refs_0_), channel_id=1, source_target_pairs={{0,4},{1,5},{2,6},{3,7},{4,0},{5,1},{6,2},{7,3},{8,12},{9,13},{10,... | collective-permute-start | bytes 98312 | tf_op jit(solution)/shard_map/ppermute | solution.py:358
  27.2 0.9 %collective-permute-start.16 = (f32[32,256]{1,0:T(8,128)S(1)}, f32[32,256]{1,0:T(8,128)S(1)}, u32[]{:S(2)}, u32[]{:S(2)}) collective-permute-start(f32[32,256]{1,0:T(8,128)S(1)} %add_add_fusion.refs_0_), channel_id=1, source_target_pairs={{0,2},{1,3},{2,0},{3,1},{4,6},{5,7},{6,4},{7,5},{8,10},{9,11},{10,... | collective-permute-start | bytes 98312 | tf_op jit(solution)/shard_map/ppermute | solution.py:358
  28.6 1.8 %inverse.1.inverse_ref = f32[32,32]{1,0:T(8,128)S(1)} custom-call(bf16[4,32,512]{2,1,0:T(8,128)(2,1)S(1)} %pad_maximum_fusion.small_ref), custom_call_target="tpu_custom_call" | custom-call | bytes 135168 | tf_op jit(solution)/shard_map/inverse/pallas_call | solution.py:330
  31.1 1.5 %solve.1.refs_0_ = f32[64,256]{1,0:T(8,128)S(1)} custom-call(f32[32,32]{1,0:T(8,128)S(1)} %inverse.1.inverse_ref, bf16[32,2048]{1,0:T(8,128)(2,1)S(1)} %get-tuple-element.42.design_ref, bf16[2048,128]{1,0:T(8,128)(2,1)S(1)} %get-tuple-element.39.rows_ref, f32[1,512]{1,0:T(1,128)S(1)} %get-tuple-element.40.thresh_ref, ...), custom_call_target="tpu_custom_call" | custom-call | bytes 860160 | tf_op jit(solution)/shard_map/solve/pallas_call | solution.py:330
  32.5 0.9 %slope.1.slope_ref = f32[512,512]{1,0:T(8,128)S(1)} custom-call(bf16[128,512]{1,0:T(8,128)(2,1)S(1)} %get-tuple-element.31.refs_0_.refs_2_, bf16[128,512]{1,0:T(8,128)(2,1)S(1)} %collective-permute-done.refs_1_.refs_3_, bf16[128,512]{1,0:T(8,128)(2,1)S(1)} %collective-permute-done.1.refs_2_.refs_4_, ...), custom_call_target="tpu_custom_call" | custom-call | bytes 2098176 | tf_op jit(solution)/shard_map/slope/pallas_call | solution.py:330
  33.8 0.9 %weight_side.1 = (bf16[128,512]{1,0:T(8,128)(2,1)S(1)}, bf16[512,512]{1,0:T(8,128)(2,1)S(1)}, bf16[128,512]{1,0:T(8,128)(2,1)S(1)}, bf16[128,512]{1,0:T(8,128)(2...) custom-call(bf16[512,512]{1,0:T(8,128)(2,1)S(1)} %get-tuple-element.33.refs_10_.member_ref, ...), custom_call_target="tpu_custom_call" | custom-call | bytes 3932160 | tf_op jit(solution)/shard_map/weight_side/pallas_call | solution.py:330
  35.4 0.8 %collective-permute-start.19 = (bf16[128,512]{1,0:T(8,128)(2,1)S(1)}, bf16[128,512]{1,0:T(8,128)(2,1)S(1)}, u32[]{:S(2)}, u32[]{:S(2)}) collective-permute-start(bf16[128,512]{1,0:T(8,128)(2,1)S(1)} %get-tuple-element.51), channel_id=1, source_target_pairs={{0,6},{1,7},{2,4},{3,5},{4,2},{5,3},{6,0},{7,1},{8,14},{9,15},{10,... | collective-permute-start | bytes 393224 | tf_op jit(solution)/shard_map/ppermute | solution.py:358
  36.2 1.6 %collective-permute-start.20 = (bf16[128,512]{1,0:T(8,128)(2,1)S(1)}, bf16[128,512]{1,0:T(8,128)(2,1)S(1)}, u32[]{:S(2)}, u32[]{:S(2)}) collective-permute-start(bf16[128,512]{1,0:T(8,128)(2,1)S(1)} %get-tuple-element.52), channel_id=1, source_target_pairs={{0,4},{1,5},{2,6},{3,7},{4,0},{5,1},{6,2},{7,3},{8,12},{9,13},{10,... | collective-permute-start | bytes 393224 | tf_op jit(solution)/shard_map/ppermute | solution.py:358
  37.8 1.6 %collective-permute-start.23 = (bf16[128,512]{1,0:T(8,128)(2,1)S(1)}, bf16[128,512]{1,0:T(8,128)(2,1)S(1)}, u32[]{:S(2)}, u32[]{:S(2)}) collective-permute-start(bf16[128,512]{1,0:T(8,128)(2,1)S(1)} %add_convert_fusion), channel_id=1, source_target_pairs={{0,8},{1,9},{2,10},{3,11},{4,12},{5,13},{6,14},{7,15},{8,0},{9,1},... | collective-permute-start | bytes 393224 | tf_op jit(solution)/shard_map/ppermute | solution.py:358
  39.7 1.5 %collective-permute-start.21 = (bf16[128,512]{1,0:T(8,128)(2,1)S(1)}, bf16[128,512]{1,0:T(8,128)(2,1)S(1)}, u32[]{:S(2)}, u32[]{:S(2)}) collective-permute-start(bf16[128,512]{1,0:T(8,128)(2,1)S(1)} %basis_side.5), channel_id=1, source_target_pairs={{0,2},{1,3},{2,0},{3,1},{4,6},{5,7},{6,4},{7,5},{8,10},{9,11},{10,... | collective-permute-start | bytes 393224 | tf_op jit(solution)/shard_map/ppermute | solution.py:358
  41.2 3.2 %loss.1 = (f32[8,128]{1,0:T(8,128)S(1)}, f32[128,128]{1,0:T(8,128)S(1)}) custom-call(bf16[2048,128]{1,0:T(8,128)(2,1)S(1)} %get-tuple-element.39.rows_ref, f32[1,512]{1,0:T(1,128)S(1)} %get-tuple-element.40.thresh_ref, f32[1,512]{1,0:T(1,128)S(1)} %get-tuple-element.41.rate_ref, f32[64,256]{1,0:T(8,128)S(1)} %solve.1.refs_0_, ...), custom_call_target="tpu_custom_call" | custom-call | bytes 729088 | tf_op jit(solution)/shard_map/loss/pallas_call | solution.py:330
  45.5 1.6 %collective-permute-done.20.refs_2_ = bf16[128,512]{1,0:T(8,128)(2,1)S(1)} collective-permute-done((bf16[128,512]{1,0:T(8,128)(2,1)S(1)}, bf16[128,512]{1,0:T(8,128)(2,1)S(1)}, u32[]{:S(2)}, u32[]{:S(2)}) %collective-permute-start.20) | collective-permute-done | bytes 131104 | tf_op jit(solution)/shard_map/ppermute | solution.py:358
  47.1 0.9 %sums.1 = (f32[128,512]{1,0:T(8,128)}, f32[128,512]{1,0:T(8,128)}) custom-call(f32[128,128]{1,0:T(8,128)S(1)} %get-tuple-element.46.own_ref, bf16[128,512]{1,0:T(8,128)(2,1)S(1)} %basis_side.3.refs_0_, bf16[128,512]{1,0:T(8,128)(2,1)S(1)} %collective-permute-done.19.refs_1_, bf16[128,512]{1,0:T(8,128)(2,1)S(1)} %collective-permute-done.20.refs_2_, ...), custom_call_target="tpu_custom_call" | custom-call | bytes 1507328 | tf_op jit(solution)/shard_map/sums/pallas_call | solution.py:330
  (57 shorter events, 7.5 us)
Async XLA Ops:
  0.6 12.9 %collective-permute-start.3 = (bf16[128,512]{1,0:T(8,128)(2,1)}, bf16[128,512]{1,0:T(8,128)(2,1)S(1)}, u32[]{:S(2)}, u32[]{:S(2)}) collective-permute-start(bf16[128,512]{1,0:T(8,128)(2,1)} %w_ref.1), channel_id=1, source_target_pairs={{0,8},{1,9},{2,10},{3,11},{4,12},{5,13},{6,14},{7,15},{8,0},{9,1},... | collective-permute-start | bytes 393224 | tf_op jit(solution)/shard_map/ppermute | solution.py:358
  4.7 9.3 %collective-permute-start = (bf16[128,512]{1,0:T(8,128)(2,1)}, bf16[128,512]{1,0:T(8,128)(2,1)S(1)}, u32[]{:S(2)}, u32[]{:S(2)}) collective-permute-start(bf16[128,512]{1,0:T(8,128)(2,1)} %x_ref.1), channel_id=1, source_target_pairs={{0,6},{1,7},{2,4},{3,5},{4,2},{5,3},{6,0},{7,1},{8,14},{9,15},{10,... | collective-permute-start | bytes 393224 | tf_op jit(solution)/shard_map/ppermute | solution.py:358
  7.3 8.1 %collective-permute-start.1 = (bf16[128,512]{1,0:T(8,128)(2,1)}, bf16[128,512]{1,0:T(8,128)(2,1)S(1)}, u32[]{:S(2)}, u32[]{:S(2)}) collective-permute-start(bf16[128,512]{1,0:T(8,128)(2,1)} %x_ref.1), channel_id=1, source_target_pairs={{0,4},{1,5},{2,6},{3,7},{4,0},{5,1},{6,2},{7,3},{8,12},{9,13},{10,... | collective-permute-start | bytes 393224 | tf_op jit(solution)/shard_map/ppermute | solution.py:358
  7.7 7.6 %collective-permute-start.2 = (bf16[128,512]{1,0:T(8,128)(2,1)}, bf16[128,512]{1,0:T(8,128)(2,1)S(1)}, u32[]{:S(2)}, u32[]{:S(2)}) collective-permute-start(bf16[128,512]{1,0:T(8,128)(2,1)} %x_ref.1), channel_id=1, source_target_pairs={{0,2},{1,3},{2,0},{3,1},{4,6},{5,7},{6,4},{7,5},{8,10},{9,11},{10,... | collective-permute-start | bytes 393224 | tf_op jit(solution)/shard_map/ppermute | solution.py:358
  8.2 5.3 %collective-permute-start.6 = (bf16[128]{0:T(256)(128)(2,1)}, bf16[128]{0:T(256)(128)(2,1)S(1)}, u32[]{:S(2)}, u32[]{:S(2)}) collective-permute-start(bf16[128]{0:T(256)(128)(2,1)} %param.9), channel_id=1, source_target_pairs={{0,8},{1,9},{2,10},{3,11},{4,12},{5,13},{6,14},{7,15},{8,0},{9,1},... | collective-permute-start | bytes 776 | tf_op jit(solution)/shard_map/ppermute | solution.py:358
  13.5 1.9 %collective-permute-start.4 = (bf16[128,512]{1,0:T(8,128)(2,1)S(1)}, bf16[128,512]{1,0:T(8,128)(2,1)S(1)}, u32[]{:S(2)}, u32[]{:S(2)}) collective-permute-start(bf16[128,512]{1,0:T(8,128)(2,1)S(1)} %copy-done.1), channel_id=1, source_target_pairs={{0,1},{1,0},{2,3},{3,2},{4,5},{5,4},{6,7},{7,6},{8,9},{9,8},{10,11... | collective-permute-start | bytes 393224 | tf_op jit(solution)/shard_map/ppermute | solution.py:358
  13.5 1.9 %collective-permute-start.5 = (bf16[128,512]{1,0:T(8,128)(2,1)S(1)}, bf16[128,512]{1,0:T(8,128)(2,1)S(1)}, u32[]{:S(2)}, u32[]{:S(2)}) collective-permute-start(bf16[128,512]{1,0:T(8,128)(2,1)S(1)} %collective-permute-done.3.refs_5_.refs_1_), channel_id=1, source_target_pairs={{0,1},{1,0},{2,3},{3,2},{4,5},{5,4},{6,7},{7,6},{8,9},{9,8},{10,11... | collective-permute-start | bytes 393224 | tf_op jit(solution)/shard_map/ppermute | solution.py:358
  14.1 1.4 %collective-permute-start.7 = (bf16[2,128]{1,0:T(2,128)(2,1)S(1)}, bf16[2,128]{1,0:T(2,128)(2,1)S(1)}, u32[]{:S(2)}, u32[]{:S(2)}) collective-permute-start(bf16[2,128]{1,0:T(2,128)(2,1)S(1)} %pad_maximum_fusion.2), channel_id=1, source_target_pairs={{0,1},{1,0},{2,3},{3,2},{4,5},{5,4},{6,7},{7,6},{8,9},{9,8},{10,11... | collective-permute-start | bytes 1544 | tf_op jit(solution)/shard_map/ppermute | solution.py:358
  16.7 6.2 %collective-permute-start.11 = (f32[32,256]{1,0:T(8,128)S(1)}, f32[32,256]{1,0:T(8,128)S(1)}, u32[]{:S(2)}, u32[]{:S(2)}) collective-permute-start(f32[32,256]{1,0:T(8,128)S(1)} %get-tuple-element.43), channel_id=1, source_target_pairs={{0,8},{1,9},{2,10},{3,11},{4,12},{5,13},{6,14},{7,15},{8,0},{9,1},... | collective-permute-start | bytes 98312 | tf_op jit(solution)/shard_map/ppermute | solution.py:358
  19.8 3.5 %collective-permute-start.12 = (f32[32,256]{1,0:T(8,128)S(1)}, f32[32,256]{1,0:T(8,128)S(1)}, u32[]{:S(2)}, u32[]{:S(2)}) collective-permute-start(f32[32,256]{1,0:T(8,128)S(1)} %get-tuple-element.44), channel_id=1, source_target_pairs={{0,1},{1,0},{2,3},{3,2},{4,5},{5,4},{6,7},{7,6},{8,9},{9,8},{10,11... | collective-permute-start | bytes 98312 | tf_op jit(solution)/shard_map/ppermute | solution.py:358
  19.9 4.6 %collective-permute-start.13 = (f32[32,256]{1,0:T(8,128)S(1)}, f32[32,256]{1,0:T(8,128)S(1)}, u32[]{:S(2)}, u32[]{:S(2)}) collective-permute-start(f32[32,256]{1,0:T(8,128)S(1)} %get-tuple-element.44), channel_id=1, source_target_pairs={{0,9},{1,8},{2,11},{3,10},{4,13},{5,12},{6,15},{7,14},{8,1},{9,0},... | collective-permute-start | bytes 98312 | tf_op jit(solution)/shard_map/ppermute | solution.py:358
  20.0 7.2 %collective-permute-start.8 = (bf16[32,512]{1,0:T(8,128)(2,1)S(1)}, bf16[32,512]{1,0:T(8,128)(2,1)S(1)}, u32[]{:S(2)}, u32[]{:S(2)}) collective-permute-start(bf16[32,512]{1,0:T(8,128)(2,1)S(1)} %lead.1.refs_9_), channel_id=1, source_target_pairs={{0,8},{1,9},{2,10},{3,11},{4,12},{5,13},{6,14},{7,15},{8,0},{9,1},... | collective-permute-start | bytes 98312 | tf_op jit(solution)/shard_map/ppermute | solution.py:358
  22.9 5.1 %collective-permute-start.9 = (bf16[32,512]{1,0:T(8,128)(2,1)S(1)}, bf16[32,512]{1,0:T(8,128)(2,1)S(1)}, u32[]{:S(2)}, u32[]{:S(2)}) collective-permute-start(bf16[32,512]{1,0:T(8,128)(2,1)S(1)} %lead.1.refs_9_), channel_id=1, source_target_pairs={{0,1},{1,0},{2,3},{3,2},{4,5},{5,4},{6,7},{7,6},{8,9},{9,8},{10,11... | collective-permute-start | bytes 98312 | tf_op jit(solution)/shard_map/ppermute | solution.py:358
  22.9 5.1 %collective-permute-start.10 = (bf16[32,512]{1,0:T(8,128)(2,1)S(1)}, bf16[32,512]{1,0:T(8,128)(2,1)S(1)}, u32[]{:S(2)}, u32[]{:S(2)}) collective-permute-start(bf16[32,512]{1,0:T(8,128)(2,1)S(1)} %lead.1.refs_9_), channel_id=1, source_target_pairs={{0,9},{1,8},{2,11},{3,10},{4,13},{5,12},{6,15},{7,14},{8,1},{9,0},... | collective-permute-start | bytes 98312 | tf_op jit(solution)/shard_map/ppermute | solution.py:358
  24.5 5.9 %collective-permute-start.14 = (f32[32,256]{1,0:T(8,128)S(1)}, f32[32,256]{1,0:T(8,128)S(1)}, u32[]{:S(2)}, u32[]{:S(2)}) collective-permute-start(f32[32,256]{1,0:T(8,128)S(1)} %add_add_fusion.refs_0_), channel_id=1, source_target_pairs={{0,6},{1,7},{2,4},{3,5},{4,2},{5,3},{6,0},{7,1},{8,14},{9,15},{10,... | collective-permute-start | bytes 98312 | tf_op jit(solution)/shard_map/ppermute | solution.py:358
  25.9 4.4 %collective-permute-start.15 = (f32[32,256]{1,0:T(8,128)S(1)}, f32[32,256]{1,0:T(8,128)S(1)}, u32[]{:S(2)}, u32[]{:S(2)}) collective-permute-start(f32[32,256]{1,0:T(8,128)S(1)} %add_add_fusion.refs_0_), channel_id=1, source_target_pairs={{0,4},{1,5},{2,6},{3,7},{4,0},{5,1},{6,2},{7,3},{8,12},{9,13},{10,... | collective-permute-start | bytes 98312 | tf_op jit(solution)/shard_map/ppermute | solution.py:358
  27.2 3.9 %collective-permute-start.16 = (f32[32,256]{1,0:T(8,128)S(1)}, f32[32,256]{1,0:T(8,128)S(1)}, u32[]{:S(2)}, u32[]{:S(2)}) collective-permute-start(f32[32,256]{1,0:T(8,128)S(1)} %add_add_fusion.refs_0_), channel_id=1, source_target_pairs={{0,2},{1,3},{2,0},{3,1},{4,6},{5,7},{6,4},{7,5},{8,10},{9,11},{10,... | collective-permute-start | bytes 98312 | tf_op jit(solution)/shard_map/ppermute | solution.py:358
  32.5 1.3 %collective-permute-start.17 = (f32[64,256]{1,0:T(8,128)S(1)}, f32[64,256]{1,0:T(8,128)S(1)}, u32[]{:S(2)}, u32[]{:S(2)}) collective-permute-start(f32[64,256]{1,0:T(8,128)S(1)} %solve.1.refs_0_), channel_id=1, source_target_pairs={{0,1},{1,0},{2,3},{3,2},{4,5},{5,4},{6,7},{7,6},{8,9},{9,8},{10,11... | collective-permute-start | bytes 196616 | tf_op jit(solution)/shard_map/ppermute | solution.py:358
  34.7 3.1 %collective-permute-start.18 = (bf16[128,512]{1,0:T(8,128)(2,1)S(1)}, bf16[128,512]{1,0:T(8,128)(2,1)S(1)}, u32[]{:S(2)}, u32[]{:S(2)}) collective-permute-start(bf16[128,512]{1,0:T(8,128)(2,1)S(1)} %get-tuple-element.49), channel_id=1, source_target_pairs={{0,1},{1,0},{2,3},{3,2},{4,5},{5,4},{6,7},{7,6},{8,9},{9,8},{10,11... | collective-permute-start | bytes 393224 | tf_op jit(solution)/shard_map/ppermute | solution.py:358
  35.4 10.1 %collective-permute-start.19 = (bf16[128,512]{1,0:T(8,128)(2,1)S(1)}, bf16[128,512]{1,0:T(8,128)(2,1)S(1)}, u32[]{:S(2)}, u32[]{:S(2)}) collective-permute-start(bf16[128,512]{1,0:T(8,128)(2,1)S(1)} %get-tuple-element.51), channel_id=1, source_target_pairs={{0,6},{1,7},{2,4},{3,5},{4,2},{5,3},{6,0},{7,1},{8,14},{9,15},{10,... | collective-permute-start | bytes 393224 | tf_op jit(solution)/shard_map/ppermute | solution.py:358
  36.2 10.9 %collective-permute-start.20 = (bf16[128,512]{1,0:T(8,128)(2,1)S(1)}, bf16[128,512]{1,0:T(8,128)(2,1)S(1)}, u32[]{:S(2)}, u32[]{:S(2)}) collective-permute-start(bf16[128,512]{1,0:T(8,128)(2,1)S(1)} %get-tuple-element.52), channel_id=1, source_target_pairs={{0,4},{1,5},{2,6},{3,7},{4,0},{5,1},{6,2},{7,3},{8,12},{9,13},{10,... | collective-permute-start | bytes 393224 | tf_op jit(solution)/shard_map/ppermute | solution.py:358
  37.8 9.3 %collective-permute-start.23 = (bf16[128,512]{1,0:T(8,128)(2,1)S(1)}, bf16[128,512]{1,0:T(8,128)(2,1)S(1)}, u32[]{:S(2)}, u32[]{:S(2)}) collective-permute-start(bf16[128,512]{1,0:T(8,128)(2,1)S(1)} %add_convert_fusion), channel_id=1, source_target_pairs={{0,8},{1,9},{2,10},{3,11},{4,12},{5,13},{6,14},{7,15},{8,0},{9,1},... | collective-permute-start | bytes 393224 | tf_op jit(solution)/shard_map/ppermute | solution.py:358
  39.4 7.7 %collective-permute-start.22 = (bf16[128,512]{1,0:T(8,128)(2,1)S(1)}, bf16[128,512]{1,0:T(8,128)(2,1)S(1)}, u32[]{:S(2)}, u32[]{:S(2)}) collective-permute-start(bf16[128,512]{1,0:T(8,128)(2,1)S(1)} %get-tuple-element.55), channel_id=1, source_target_pairs={{0,1},{1,0},{2,3},{3,2},{4,5},{5,4},{6,7},{7,6},{8,9},{9,8},{10,11... | collective-permute-start | bytes 393224 | tf_op jit(solution)/shard_map/ppermute | solution.py:358
  39.7 7.4 %collective-permute-start.21 = (bf16[128,512]{1,0:T(8,128)(2,1)S(1)}, bf16[128,512]{1,0:T(8,128)(2,1)S(1)}, u32[]{:S(2)}, u32[]{:S(2)}) collective-permute-start(bf16[128,512]{1,0:T(8,128)(2,1)S(1)} %basis_side.5), channel_id=1, source_target_pairs={{0,2},{1,3},{2,0},{3,1},{4,6},{5,7},{6,4},{7,5},{8,10},{9,11},{10,... | collective-permute-start | bytes 393224 | tf_op jit(solution)/shard_map/ppermute | solution.py:358
  (7 other events, 12.3 us)

commit v12 on v10

--- a/solution.py
+++ b/solution.py
@@ -399,7 +399,7 @@
     notionals = after(jnp.concatenate(notionals, axis=0), weights[1])
     for bit in outer_bits[1:]:
         weights = weights + [
-            swap(w if k else after(w, member), 1 << bit) for k, w in enumerate(weights)
+            swap(after(w, basis[-2] if k else member), 1 << bit) for k, w in enumerate(weights)
         ]
         notionals = jnp.concatenate([notionals, swap(notionals, 1 << bit)], axis=0)
     weights[0] = own_weight

time: 47.8 us -> 47.3 us (0.990)
  starting transfers between devices: 23.6 us -> 22.4 us
  waiting for transfers between devices: 7.4 us -> 7.99 us
    ppermute x23, starting transfers between devices: 23.6 us -> 22.4 us  [swap(): return lax.ppermute(x, 'paths', [(d, d ^ mask) for d in range(n)])]
    ppermute x23, waiting for transfers between devices: 7.4 us -> 7.99 us  [swap(): return lax.ppermute(x, 'paths', [(d, d ^ mask) for d in range(n)])]
  transfers between devices with their start and end apart: 23 -> 23, of which waited for: 7 -> 8; matrix products, arithmetic and copies ran while one was open for 1% -> 1% of each run, Pallas kernels for 17% -> 17%
where the time goes in v12:
time: 47.3 us; the launch traced here: 47.1 us
  starting transfers between devices  22.4 us (47%)
  Pallas kernels  12.7 us (27%)
  waiting for transfers between devices  7.99 us (17%)
  local copies, waits for them, and re-layouts  3.04 us (6%)
  between operations  0.82 us (2%)
    ppermute x23, starting transfers between devices, swap(): return lax.ppermute(x, 'paths', [(d, d ^ mask) for d in range(n)])  22.4 us
    pallas_call x13, Pallas kernels, call(): pl.pallas_call(kernel, out_shape=[jax.ShapeDtypeStruct(s, d) for s, d in...  12.7 us
    ppermute x23, waiting for transfers between devices, swap(): return lax.ppermute(x, 'paths', [(d, d ^ mask) for d in range(n)])  7.99 us
    unnamed x14, local copies, waits for them, and re-layouts  2.52 us
  transfers between devices with their start and end apart: 23, of which 8 were waited for; matrix products, arithmetic and copies ran while one was open for 1% of the time, Pallas kernels for 17%

profile of v12, /device:TPU:0, one launch (start us, length us, event | category | flops | bytes accessed | tf_op | source)
XLA Modules:
  0.0 47.1 jit_solution(9094979539597605999)
XLA Ops:
  0.6 4.1 %collective-permute-start.3 = (bf16[128,512]{1,0:T(8,128)(2,1)}, bf16[128,512]{1,0:T(8,128)(2,1)S(1)}, u32[]{:S(2)}, u32[]{:S(2)}) collective-permute-start(bf16[128,512]{1,0:T(8,128)(2,1)} %w_ref.1), channel_id=1, source_target_pairs={{0,8},{1,9},{2,10},{3,11},{4,12},{5,13},{6,14},{7,15},{8,0},{9,1},... | collective-permute-start | bytes 393224 | tf_op jit(solution)/shard_map/ppermute | solution.py:358
  4.7 1.6 %collective-permute-start.1 = (bf16[128,512]{1,0:T(8,128)(2,1)}, bf16[128,512]{1,0:T(8,128)(2,1)S(1)}, u32[]{:S(2)}, u32[]{:S(2)}) collective-permute-start(bf16[128,512]{1,0:T(8,128)(2,1)} %x_ref.1), channel_id=1, source_target_pairs={{0,4},{1,5},{2,6},{3,7},{4,0},{5,1},{6,2},{7,3},{8,12},{9,13},{10,... | collective-permute-start | bytes 393224 | tf_op jit(solution)/shard_map/ppermute | solution.py:358
  6.3 1.4 %collective-permute-start = (bf16[128,512]{1,0:T(8,128)(2,1)}, bf16[128,512]{1,0:T(8,128)(2,1)S(1)}, u32[]{:S(2)}, u32[]{:S(2)}) collective-permute-start(bf16[128,512]{1,0:T(8,128)(2,1)} %x_ref.1), channel_id=1, source_target_pairs={{0,6},{1,7},{2,4},{3,5},{4,2},{5,3},{6,0},{7,1},{8,14},{9,15},{10,... | collective-permute-start | bytes 393224 | tf_op jit(solution)/shard_map/ppermute | solution.py:358
  9.0 0.9 %copy-done = bf16[128,512]{1,0:T(8,128)(2,1)S(1)} copy-done((bf16[128,512]{1,0:T(8,128)(2,1)S(1)}, bf16[128,512]{1,0:T(8,128)(2,1)}, u32[]{:S(2)}) %copy-start) | copy-done | bytes 131096
  9.9 0.9 %copy-done.1 = bf16[128,512]{1,0:T(8,128)(2,1)S(1)} copy-done((bf16[128,512]{1,0:T(8,128)(2,1)S(1)}, bf16[128,512]{1,0:T(8,128)(2,1)}, u32[]{:S(2)}) %copy-start.1) | copy-done | bytes 131096
  11.6 0.9 %collective-permute-done.1.refs_2_.refs_4_ = bf16[128,512]{1,0:T(8,128)(2,1)S(1)} collective-permute-done((bf16[128,512]{1,0:T(8,128)(2,1)}, bf16[128,512]{1,0:T(8,128)(2,1)S(1)}, u32[]{:S(2)}, u32[]{:S(2)}) %collective-permute-start.1) | collective-permute-done | bytes 131104 | tf_op jit(solution)/shard_map/ppermute | solution.py:358
  12.6 0.9 %collective-permute-done.6 = bf16[128]{0:T(256)(128)(2,1)S(1)} collective-permute-done((bf16[128]{0:T(256)(128)(2,1)}, bf16[128]{0:T(256)(128)(2,1)S(1)}, u32[]{:S(2)}, u32[]{:S(2)}) %collective-permute-start.6) | collective-permute-done | bytes 288 | tf_op jit(solution)/shard_map/ppermute | solution.py:358
  13.5 1.9 %collective-permute-done.refs_1_.refs_3_ = bf16[128,512]{1,0:T(8,128)(2,1)S(1)} collective-permute-done((bf16[128,512]{1,0:T(8,128)(2,1)}, bf16[128,512]{1,0:T(8,128)(2,1)S(1)}, u32[]{:S(2)}, u32[]{:S(2)}) %collective-permute-start) | collective-permute-done | bytes 131104 | tf_op jit(solution)/shard_map/ppermute | solution.py:358
  15.5 1.3 %forward.1 = (bf16[512,512]{1,0:T(8,128)(2,1)S(1)}, f32[32,256]{1,0:T(8,128)S(1)}, f32[32,256]{1,0:T(8,128)S(1)}) custom-call(bf16[128,512]{1,0:T(8,128)(2,1)S(1)} %get-tuple-element.32.refs_0_.refs_2_, bf16[128,512]{1,0:T(8,128)(2,1)S(1)} %collective-permute-done.refs_1_.refs_3_, bf16[128,512]{1,0:T(8,128)(2,1)S(1)} %collective-permute-done.1.refs_2_.refs_4_, ...), custom_call_target="tpu_custom_call" | custom-call | bytes 2196480 | tf_op jit(solution)/shard_map/forward/pallas_call | solution.py:330
  16.8 1.2 %collective-permute-done.8 = f32[32,256]{1,0:T(8,128)S(1)} collective-permute-done((f32[32,256]{1,0:T(8,128)S(1)}, f32[32,256]{1,0:T(8,128)S(1)}, u32[]{:S(2)}, u32[]{:S(2)}) %collective-permute-start.8) | collective-permute-done | bytes 32800 | tf_op jit(solution)/shard_map/ppermute | solution.py:358
  18.1 2.5 %collective-permute-start.12 = (f32[32,256]{1,0:T(8,128)S(1)}, f32[32,256]{1,0:T(8,128)S(1)}, u32[]{:S(2)}, u32[]{:S(2)}) collective-permute-start(f32[32,256]{1,0:T(8,128)S(1)} %add.9), channel_id=1, source_target_pairs={{0,8},{1,9},{2,10},{3,11},{4,12},{5,13},{6,14},{7,15},{8,0},{9,1},... | collective-permute-start | bytes 98312 | tf_op jit(solution)/shard_map/ppermute | solution.py:358
  21.0 2.6 %collective-permute-start.11 = (bf16[32,512]{1,0:T(8,128)(2,1)S(1)}, bf16[32,512]{1,0:T(8,128)(2,1)S(1)}, u32[]{:S(2)}, u32[]{:S(2)}) collective-permute-start(bf16[32,512]{1,0:T(8,128)(2,1)S(1)} %lead.1.refs_9_), channel_id=1, source_target_pairs={{0,9},{1,8},{2,11},{3,10},{4,13},{5,12},{6,15},{7,14},{8,1},{9,0},... | collective-permute-start | bytes 98312 | tf_op jit(solution)/shard_map/ppermute | solution.py:358
  23.6 1.8 %collective-permute-start.13 = (f32[32,256]{1,0:T(8,128)S(1)}, f32[32,256]{1,0:T(8,128)S(1)}, u32[]{:S(2)}, u32[]{:S(2)}) collective-permute-start(f32[32,256]{1,0:T(8,128)S(1)} %add.10.refs_0_), channel_id=1, source_target_pairs={{0,6},{1,7},{2,4},{3,5},{4,2},{5,3},{6,0},{7,1},{8,14},{9,15},{10,... | collective-permute-start | bytes 98312 | tf_op jit(solution)/shard_map/ppermute | solution.py:358
  25.4 1.2 %collective-permute-start.14 = (f32[32,256]{1,0:T(8,128)S(1)}, f32[32,256]{1,0:T(8,128)S(1)}, u32[]{:S(2)}, u32[]{:S(2)}) collective-permute-start(f32[32,256]{1,0:T(8,128)S(1)} %add.10.refs_0_), channel_id=1, source_target_pairs={{0,4},{1,5},{2,6},{3,7},{4,0},{5,1},{6,2},{7,3},{8,12},{9,13},{10,... | collective-permute-start | bytes 98312 | tf_op jit(solution)/shard_map/ppermute | solution.py:358
  27.7 1.8 %inverse.1.inverse_ref = f32[32,32]{1,0:T(8,128)S(1)} custom-call(bf16[4,32,512]{2,1,0:T(8,128)(2,1)S(1)} %pad_maximum_fusion.small_ref), custom_call_target="tpu_custom_call" | custom-call | bytes 135168 | tf_op jit(solution)/shard_map/inverse/pallas_call | solution.py:330
  29.5 1.1 %collective-permute-done.15.refs_3_ = f32[32,256]{1,0:T(8,128)S(1)} collective-permute-done((f32[32,256]{1,0:T(8,128)S(1)}, f32[32,256]{1,0:T(8,128)S(1)}, u32[]{:S(2)}, u32[]{:S(2)}) %collective-permute-start.15) | collective-permute-done | bytes 32800 | tf_op jit(solution)/shard_map/ppermute | solution.py:358
  30.5 1.5 %solve.1.refs_0_ = f32[64,256]{1,0:T(8,128)S(1)} custom-call(f32[32,32]{1,0:T(8,128)S(1)} %inverse.1.inverse_ref, bf16[32,2048]{1,0:T(8,128)(2,1)S(1)} %get-tuple-element.45.design_ref, bf16[2048,128]{1,0:T(8,128)(2,1)S(1)} %get-tuple-element.42.rows_ref, f32[1,512]{1,0:T(1,128)S(1)} %get-tuple-element.43.thresh_ref, ...), custom_call_target="tpu_custom_call" | custom-call | bytes 860160 | tf_op jit(solution)/shard_map/solve/pallas_call | solution.py:330
  32.0 0.9 %slope.1.slope_ref = f32[512,512]{1,0:T(8,128)S(1)} custom-call(bf16[128,512]{1,0:T(8,128)(2,1)S(1)} %get-tuple-element.32.refs_0_.refs_2_, bf16[128,512]{1,0:T(8,128)(2,1)S(1)} %collective-permute-done.refs_1_.refs_3_, bf16[128,512]{1,0:T(8,128)(2,1)S(1)} %collective-permute-done.1.refs_2_.refs_4_, ...), custom_call_target="tpu_custom_call" | custom-call | bytes 2098176 | tf_op jit(solution)/shard_map/slope/pallas_call | solution.py:330
  33.2 0.9 %weight_side.1 = (bf16[128,512]{1,0:T(8,128)(2,1)S(1)}, bf16[512,512]{1,0:T(8,128)(2,1)S(1)}, bf16[128,512]{1,0:T(8,128)(2,1)S(1)}, bf16[128,512]{1,0:T(8,128)(2...) custom-call(bf16[512,512]{1,0:T(8,128)(2,1)S(1)} %get-tuple-element.34.refs_10_.member_ref, ...), custom_call_target="tpu_custom_call" | custom-call | bytes 3932160 | tf_op jit(solution)/shard_map/weight_side/pallas_call | solution.py:330
  34.8 1.2 %collective-permute-start.18 = (bf16[128,512]{1,0:T(8,128)(2,1)S(1)}, bf16[128,512]{1,0:T(8,128)(2,1)S(1)}, u32[]{:S(2)}, u32[]{:S(2)}) collective-permute-start(bf16[128,512]{1,0:T(8,128)(2,1)S(1)} %get-tuple-element.53), channel_id=1, source_target_pairs={{0,6},{1,7},{2,4},{3,5},{4,2},{5,3},{6,0},{7,1},{8,14},{9,15},{10,... | collective-permute-start | bytes 393224 | tf_op jit(solution)/shard_map/ppermute | solution.py:358
  36.9 1.9 %collective-permute-start.22 = (bf16[128,512]{1,0:T(8,128)(2,1)S(1)}, bf16[128,512]{1,0:T(8,128)(2,1)S(1)}, u32[]{:S(2)}, u32[]{:S(2)}) collective-permute-start(bf16[128,512]{1,0:T(8,128)(2,1)S(1)} %add_convert_fusion), channel_id=1, source_target_pairs={{0,8},{1,9},{2,10},{3,11},{4,12},{5,13},{6,14},{7,15},{8,0},{9,1},... | collective-permute-start | bytes 393224 | tf_op jit(solution)/shard_map/ppermute | solution.py:358
  39.2 1.5 %collective-permute-start.20 = (bf16[128,512]{1,0:T(8,128)(2,1)S(1)}, bf16[128,512]{1,0:T(8,128)(2,1)S(1)}, u32[]{:S(2)}, u32[]{:S(2)}) collective-permute-start(bf16[128,512]{1,0:T(8,128)(2,1)S(1)} %basis_side.5), channel_id=1, source_target_pairs={{0,2},{1,3},{2,0},{3,1},{4,6},{5,7},{6,4},{7,5},{8,10},{9,11},{10,... | collective-permute-start | bytes 393224 | tf_op jit(solution)/shard_map/ppermute | solution.py:358
  40.6 3.2 %loss.1 = (f32[8,128]{1,0:T(8,128)S(1)}, f32[128,128]{1,0:T(8,128)S(1)}) custom-call(bf16[2048,128]{1,0:T(8,128)(2,1)S(1)} %get-tuple-element.42.rows_ref, f32[1,512]{1,0:T(1,128)S(1)} %get-tuple-element.43.thresh_ref, f32[1,512]{1,0:T(1,128)S(1)} %get-tuple-element.44.rate_ref, f32[64,256]{1,0:T(8,128)S(1)} %solve.1.refs_0_, ...), custom_call_target="tpu_custom_call" | custom-call | bytes 729088 | tf_op jit(solution)/shard_map/loss/pallas_call | solution.py:330
  44.9 1.3 %collective-permute-done.19.refs_2_ = bf16[128,512]{1,0:T(8,128)(2,1)S(1)} collective-permute-done((bf16[128,512]{1,0:T(8,128)(2,1)S(1)}, bf16[128,512]{1,0:T(8,128)(2,1)S(1)}, u32[]{:S(2)}, u32[]{:S(2)}) %collective-permute-start.19) | collective-permute-done | bytes 131104 | tf_op jit(solution)/shard_map/ppermute | solution.py:358
  (56 shorter events, 7.9 us)
Async XLA Ops:
  0.6 7.7 %copy-start.2 = (s32[2048]{0:T(1024)S(1)}, s32[2048]{0:T(1024)}, u32[]{:S(2)}) copy-start(s32[2048]{0:T(1024)} %param.10) | copy-start | bytes 24580
  0.6 10.9 %collective-permute-start.3 = (bf16[128,512]{1,0:T(8,128)(2,1)}, bf16[128,512]{1,0:T(8,128)(2,1)S(1)}, u32[]{:S(2)}, u32[]{:S(2)}) collective-permute-start(bf16[128,512]{1,0:T(8,128)(2,1)} %w_ref.1), channel_id=1, source_target_pairs={{0,8},{1,9},{2,10},{3,11},{4,12},{5,13},{6,14},{7,15},{8,0},{9,1},... | collective-permute-start | bytes 393224 | tf_op jit(solution)/shard_map/ppermute | solution.py:358
  4.7 7.8 %collective-permute-start.1 = (bf16[128,512]{1,0:T(8,128)(2,1)}, bf16[128,512]{1,0:T(8,128)(2,1)S(1)}, u32[]{:S(2)}, u32[]{:S(2)}) collective-permute-start(bf16[128,512]{1,0:T(8,128)(2,1)} %x_ref.1), channel_id=1, source_target_pairs={{0,4},{1,5},{2,6},{3,7},{4,0},{5,1},{6,2},{7,3},{8,12},{9,13},{10,... | collective-permute-start | bytes 393224 | tf_op jit(solution)/shard_map/ppermute | solution.py:358
  6.3 9.1 %collective-permute-start = (bf16[128,512]{1,0:T(8,128)(2,1)}, bf16[128,512]{1,0:T(8,128)(2,1)S(1)}, u32[]{:S(2)}, u32[]{:S(2)}) collective-permute-start(bf16[128,512]{1,0:T(8,128)(2,1)} %x_ref.1), channel_id=1, source_target_pairs={{0,6},{1,7},{2,4},{3,5},{4,2},{5,3},{6,0},{7,1},{8,14},{9,15},{10,... | collective-permute-start | bytes 393224 | tf_op jit(solution)/shard_map/ppermute | solution.py:358
  7.7 7.7 %collective-permute-start.2 = (bf16[128,512]{1,0:T(8,128)(2,1)}, bf16[128,512]{1,0:T(8,128)(2,1)S(1)}, u32[]{:S(2)}, u32[]{:S(2)}) collective-permute-start(bf16[128,512]{1,0:T(8,128)(2,1)} %x_ref.1), channel_id=1, source_target_pairs={{0,2},{1,3},{2,0},{3,1},{4,6},{5,7},{6,4},{7,5},{8,10},{9,11},{10,... | collective-permute-start | bytes 393224 | tf_op jit(solution)/shard_map/ppermute | solution.py:358
  8.2 5.3 %collective-permute-start.6 = (bf16[128]{0:T(256)(128)(2,1)}, bf16[128]{0:T(256)(128)(2,1)S(1)}, u32[]{:S(2)}, u32[]{:S(2)}) collective-permute-start(bf16[128]{0:T(256)(128)(2,1)} %param.9), channel_id=1, source_target_pairs={{0,8},{1,9},{2,10},{3,11},{4,12},{5,13},{6,14},{7,15},{8,0},{9,1},... | collective-permute-start | bytes 776 | tf_op jit(solution)/shard_map/ppermute | solution.py:358
  11.5 4.0 %collective-permute-start.4 = (bf16[128,512]{1,0:T(8,128)(2,1)S(1)}, bf16[128,512]{1,0:T(8,128)(2,1)S(1)}, u32[]{:S(2)}, u32[]{:S(2)}) collective-permute-start(bf16[128,512]{1,0:T(8,128)(2,1)S(1)} %copy-done.1), channel_id=1, source_target_pairs={{0,1},{1,0},{2,3},{3,2},{4,5},{5,4},{6,7},{7,6},{8,9},{9,8},{10,11... | collective-permute-start | bytes 393224 | tf_op jit(solution)/shard_map/ppermute | solution.py:358
  12.6 3.0 %collective-permute-start.5 = (bf16[128,512]{1,0:T(8,128)(2,1)S(1)}, bf16[128,512]{1,0:T(8,128)(2,1)S(1)}, u32[]{:S(2)}, u32[]{:S(2)}) collective-permute-start(bf16[128,512]{1,0:T(8,128)(2,1)S(1)} %collective-permute-done.3.refs_5_.refs_1_), channel_id=1, source_target_pairs={{0,1},{1,0},{2,3},{3,2},{4,5},{5,4},{6,7},{7,6},{8,9},{9,8},{10,11... | collective-permute-start | bytes 393224 | tf_op jit(solution)/shard_map/ppermute | solution.py:358
  13.5 2.0 %collective-permute-start.7 = (bf16[2,128]{1,0:T(2,128)(2,1)S(1)}, bf16[2,128]{1,0:T(2,128)(2,1)S(1)}, u32[]{:S(2)}, u32[]{:S(2)}) collective-permute-start(bf16[2,128]{1,0:T(2,128)(2,1)S(1)} %pad_maximum_fusion.2), channel_id=1, source_target_pairs={{0,1},{1,0},{2,3},{3,2},{4,5},{5,4},{6,7},{7,6},{8,9},{9,8},{10,11... | collective-permute-start | bytes 1544 | tf_op jit(solution)/shard_map/ppermute | solution.py:358
  16.8 1.3 %collective-permute-start.8 = (f32[32,256]{1,0:T(8,128)S(1)}, f32[32,256]{1,0:T(8,128)S(1)}, u32[]{:S(2)}, u32[]{:S(2)}) collective-permute-start(f32[32,256]{1,0:T(8,128)S(1)} %get-tuple-element.40), channel_id=1, source_target_pairs={{0,1},{1,0},{2,3},{3,2},{4,5},{5,4},{6,7},{7,6},{8,9},{9,8},{10,11... | collective-permute-start | bytes 98312 | tf_op jit(solution)/shard_map/ppermute | solution.py:358
  18.1 5.5 %collective-permute-start.12 = (f32[32,256]{1,0:T(8,128)S(1)}, f32[32,256]{1,0:T(8,128)S(1)}, u32[]{:S(2)}, u32[]{:S(2)}) collective-permute-start(f32[32,256]{1,0:T(8,128)S(1)} %add.9), channel_id=1, source_target_pairs={{0,8},{1,9},{2,10},{3,11},{4,12},{5,13},{6,14},{7,15},{8,0},{9,1},... | collective-permute-start | bytes 98312 | tf_op jit(solution)/shard_map/ppermute | solution.py:358
  20.5 6.1 %collective-permute-start.9 = (bf16[32,512]{1,0:T(8,128)(2,1)S(1)}, bf16[32,512]{1,0:T(8,128)(2,1)S(1)}, u32[]{:S(2)}, u32[]{:S(2)}) collective-permute-start(bf16[32,512]{1,0:T(8,128)(2,1)S(1)} %lead.1.refs_9_), channel_id=1, source_target_pairs={{0,8},{1,9},{2,10},{3,11},{4,12},{5,13},{6,14},{7,15},{8,0},{9,1},... | collective-permute-start | bytes 98312 | tf_op jit(solution)/shard_map/ppermute | solution.py:358
  21.0 6.2 %collective-permute-start.10 = (bf16[32,512]{1,0:T(8,128)(2,1)S(1)}, bf16[32,512]{1,0:T(8,128)(2,1)S(1)}, u32[]{:S(2)}, u32[]{:S(2)}) collective-permute-start(bf16[32,512]{1,0:T(8,128)(2,1)S(1)} %lead.1.refs_9_), channel_id=1, source_target_pairs={{0,1},{1,0},{2,3},{3,2},{4,5},{5,4},{6,7},{7,6},{8,9},{9,8},{10,11... | collective-permute-start | bytes 98312 | tf_op jit(solution)/shard_map/ppermute | solution.py:358
  21.0 6.2 %collective-permute-start.11 = (bf16[32,512]{1,0:T(8,128)(2,1)S(1)}, bf16[32,512]{1,0:T(8,128)(2,1)S(1)}, u32[]{:S(2)}, u32[]{:S(2)}) collective-permute-start(bf16[32,512]{1,0:T(8,128)(2,1)S(1)} %lead.1.refs_9_), channel_id=1, source_target_pairs={{0,9},{1,8},{2,11},{3,10},{4,13},{5,12},{6,15},{7,14},{8,1},{9,0},... | collective-permute-start | bytes 98312 | tf_op jit(solution)/shard_map/ppermute | solution.py:358
  23.6 5.9 %collective-permute-start.13 = (f32[32,256]{1,0:T(8,128)S(1)}, f32[32,256]{1,0:T(8,128)S(1)}, u32[]{:S(2)}, u32[]{:S(2)}) collective-permute-start(f32[32,256]{1,0:T(8,128)S(1)} %add.10.refs_0_), channel_id=1, source_target_pairs={{0,6},{1,7},{2,4},{3,5},{4,2},{5,3},{6,0},{7,1},{8,14},{9,15},{10,... | collective-permute-start | bytes 98312 | tf_op jit(solution)/shard_map/ppermute | solution.py:358
  25.4 4.1 %collective-permute-start.14 = (f32[32,256]{1,0:T(8,128)S(1)}, f32[32,256]{1,0:T(8,128)S(1)}, u32[]{:S(2)}, u32[]{:S(2)}) collective-permute-start(f32[32,256]{1,0:T(8,128)S(1)} %add.10.refs_0_), channel_id=1, source_target_pairs={{0,4},{1,5},{2,6},{3,7},{4,0},{5,1},{6,2},{7,3},{8,12},{9,13},{10,... | collective-permute-start | bytes 98312 | tf_op jit(solution)/shard_map/ppermute | solution.py:358
  26.6 3.9 %collective-permute-start.15 = (f32[32,256]{1,0:T(8,128)S(1)}, f32[32,256]{1,0:T(8,128)S(1)}, u32[]{:S(2)}, u32[]{:S(2)}) collective-permute-start(f32[32,256]{1,0:T(8,128)S(1)} %add.10.refs_0_), channel_id=1, source_target_pairs={{0,2},{1,3},{2,0},{3,1},{4,6},{5,7},{6,4},{7,5},{8,10},{9,11},{10,... | collective-permute-start | bytes 98312 | tf_op jit(solution)/shard_map/ppermute | solution.py:358
  32.0 1.3 %collective-permute-start.16 = (f32[64,256]{1,0:T(8,128)S(1)}, f32[64,256]{1,0:T(8,128)S(1)}, u32[]{:S(2)}, u32[]{:S(2)}) collective-permute-start(f32[64,256]{1,0:T(8,128)S(1)} %solve.1.refs_0_), channel_id=1, source_target_pairs={{0,1},{1,0},{2,3},{3,2},{4,5},{5,4},{6,7},{7,6},{8,9},{9,8},{10,11... | collective-permute-start | bytes 196616 | tf_op jit(solution)/shard_map/ppermute | solution.py:358
  34.1 2.7 %collective-permute-start.17 = (bf16[128,512]{1,0:T(8,128)(2,1)S(1)}, bf16[128,512]{1,0:T(8,128)(2,1)S(1)}, u32[]{:S(2)}, u32[]{:S(2)}) collective-permute-start(bf16[128,512]{1,0:T(8,128)(2,1)S(1)} %get-tuple-element.51), channel_id=1, source_target_pairs={{0,1},{1,0},{2,3},{3,2},{4,5},{5,4},{6,7},{7,6},{8,9},{9,8},{10,11... | collective-permute-start | bytes 393224 | tf_op jit(solution)/shard_map/ppermute | solution.py:358
  34.8 10.1 %collective-permute-start.18 = (bf16[128,512]{1,0:T(8,128)(2,1)S(1)}, bf16[128,512]{1,0:T(8,128)(2,1)S(1)}, u32[]{:S(2)}, u32[]{:S(2)}) collective-permute-start(bf16[128,512]{1,0:T(8,128)(2,1)S(1)} %get-tuple-element.53), channel_id=1, source_target_pairs={{0,6},{1,7},{2,4},{3,5},{4,2},{5,3},{6,0},{7,1},{8,14},{9,15},{10,... | collective-permute-start | bytes 393224 | tf_op jit(solution)/shard_map/ppermute | solution.py:358
  36.0 10.2 %collective-permute-start.19 = (bf16[128,512]{1,0:T(8,128)(2,1)S(1)}, bf16[128,512]{1,0:T(8,128)(2,1)S(1)}, u32[]{:S(2)}, u32[]{:S(2)}) collective-permute-start(bf16[128,512]{1,0:T(8,128)(2,1)S(1)} %get-tuple-element.54), channel_id=1, source_target_pairs={{0,4},{1,5},{2,6},{3,7},{4,0},{5,1},{6,2},{7,3},{8,12},{9,13},{10,... | collective-permute-start | bytes 393224 | tf_op jit(solution)/shard_map/ppermute | solution.py:358
  36.9 9.3 %collective-permute-start.22 = (bf16[128,512]{1,0:T(8,128)(2,1)S(1)}, bf16[128,512]{1,0:T(8,128)(2,1)S(1)}, u32[]{:S(2)}, u32[]{:S(2)}) collective-permute-start(bf16[128,512]{1,0:T(8,128)(2,1)S(1)} %add_convert_fusion), channel_id=1, source_target_pairs={{0,8},{1,9},{2,10},{3,11},{4,12},{5,13},{6,14},{7,15},{8,0},{9,1},... | collective-permute-start | bytes 393224 | tf_op jit(solution)/shard_map/ppermute | solution.py:358
  38.8 7.4 %collective-permute-start.21 = (bf16[128,512]{1,0:T(8,128)(2,1)S(1)}, bf16[128,512]{1,0:T(8,128)(2,1)S(1)}, u32[]{:S(2)}, u32[]{:S(2)}) collective-permute-start(bf16[128,512]{1,0:T(8,128)(2,1)S(1)} %get-tuple-element.57), channel_id=1, source_target_pairs={{0,1},{1,0},{2,3},{3,2},{4,5},{5,4},{6,7},{7,6},{8,9},{9,8},{10,11... | collective-permute-start | bytes 393224 | tf_op jit(solution)/shard_map/ppermute | solution.py:358
  39.2 7.1 %collective-permute-start.20 = (bf16[128,512]{1,0:T(8,128)(2,1)S(1)}, bf16[128,512]{1,0:T(8,128)(2,1)S(1)}, u32[]{:S(2)}, u32[]{:S(2)}) collective-permute-start(bf16[128,512]{1,0:T(8,128)(2,1)S(1)} %basis_side.5), channel_id=1, source_target_pairs={{0,2},{1,3},{2,0},{3,1},{4,6},{5,7},{6,4},{7,5},{8,10},{9,11},{10,... | collective-permute-start | bytes 393224 | tf_op jit(solution)/shard_map/ppermute | solution.py:358
  (6 other events, 4.6 us)

commit v13 on v12

--- a/solution.py
+++ b/solution.py
@@ -479,7 +479,9 @@
     far = list(basis_side(1, inner - 1, slopes))
     late = after(slopes, core_step)
     own, near = basis_side(0, 1, late)[0], basis_side(inner - 1, inner, late)[0]
-    basis_terms = [own] + direct([own] + far + [near], inner_masks)
+    arrived = direct([own] + far + [near], inner_masks)
+    hops = [bin(mask).count("1") for mask in inner_masks[1:]]
+    basis_terms = [own] + [arrived[k] for k in sorted(range(len(hops)), key=lambda k: hops[k])]
     loss, own_adjoint = call(
         loss_kernel,
         [((8, LANES), F32), ((path_rows, LANES), F32)],

time: 47.3 us -> 48.3 us (1.021)
  waiting for transfers between devices: 7.99 us -> 9.07 us
    ppermute x23, waiting for transfers between devices: 7.99 us -> 9.07 us  [swap(): return lax.ppermute(x, 'paths', [(d, d ^ mask) for d in range(n)])]
where the time goes in v13:
time: 48.3 us; the launch traced here: 48.2 us
  starting transfers between devices  22.4 us (46%)
  Pallas kernels  12.7 us (26%)
  waiting for transfers between devices  9.07 us (19%)
  local copies, waits for them, and re-layouts  3.04 us (6%)
  between operations  0.82 us (2%)
    ppermute x23, starting transfers between devices, swap(): return lax.ppermute(x, 'paths', [(d, d ^ mask) for d in range(n)])  22.4 us
    pallas_call x13, Pallas kernels, call(): pl.pallas_call(kernel, out_shape=[jax.ShapeDtypeStruct(s, d) for s, d in...  12.7 us
    ppermute x23, waiting for transfers between devices, swap(): return lax.ppermute(x, 'paths', [(d, d ^ mask) for d in range(n)])  9.07 us
    unnamed x14, local copies, waits for them, and re-layouts  2.52 us
  transfers between devices with their start and end apart: 23, of which 8 were waited for; matrix products, arithmetic and copies ran while one was open for 1% of the time, Pallas kernels for 17%

profile of v13, /device:TPU:0, one launch (start us, length us, event | category | flops | bytes accessed | tf_op | source)
XLA Modules:
  0.0 48.2 jit_solution(2789097768610900417)
XLA Ops:
  0.6 4.1 %collective-permute-start.3 = (bf16[128,512]{1,0:T(8,128)(2,1)}, bf16[128,512]{1,0:T(8,128)(2,1)S(1)}, u32[]{:S(2)}, u32[]{:S(2)}) collective-permute-start(bf16[128,512]{1,0:T(8,128)(2,1)} %w_ref.1), channel_id=1, source_target_pairs={{0,8},{1,9},{2,10},{3,11},{4,12},{5,13},{6,14},{7,15},{8,0},{9,1},... | collective-permute-start | bytes 393224 | tf_op jit(solution)/shard_map/ppermute | solution.py:358
  4.7 1.6 %collective-permute-start.1 = (bf16[128,512]{1,0:T(8,128)(2,1)}, bf16[128,512]{1,0:T(8,128)(2,1)S(1)}, u32[]{:S(2)}, u32[]{:S(2)}) collective-permute-start(bf16[128,512]{1,0:T(8,128)(2,1)} %x_ref.1), channel_id=1, source_target_pairs={{0,4},{1,5},{2,6},{3,7},{4,0},{5,1},{6,2},{7,3},{8,12},{9,13},{10,... | collective-permute-start | bytes 393224 | tf_op jit(solution)/shard_map/ppermute | solution.py:358
  6.3 1.4 %collective-permute-start = (bf16[128,512]{1,0:T(8,128)(2,1)}, bf16[128,512]{1,0:T(8,128)(2,1)S(1)}, u32[]{:S(2)}, u32[]{:S(2)}) collective-permute-start(bf16[128,512]{1,0:T(8,128)(2,1)} %x_ref.1), channel_id=1, source_target_pairs={{0,6},{1,7},{2,4},{3,5},{4,2},{5,3},{6,0},{7,1},{8,14},{9,15},{10,... | collective-permute-start | bytes 393224 | tf_op jit(solution)/shard_map/ppermute | solution.py:358
  9.0 0.9 %copy-done = bf16[128,512]{1,0:T(8,128)(2,1)S(1)} copy-done((bf16[128,512]{1,0:T(8,128)(2,1)S(1)}, bf16[128,512]{1,0:T(8,128)(2,1)}, u32[]{:S(2)}) %copy-start) | copy-done | bytes 131096
  9.9 0.9 %copy-done.1 = bf16[128,512]{1,0:T(8,128)(2,1)S(1)} copy-done((bf16[128,512]{1,0:T(8,128)(2,1)S(1)}, bf16[128,512]{1,0:T(8,128)(2,1)}, u32[]{:S(2)}) %copy-start.1) | copy-done | bytes 131096
  11.6 0.9 %collective-permute-done.1.refs_2_.refs_4_ = bf16[128,512]{1,0:T(8,128)(2,1)S(1)} collective-permute-done((bf16[128,512]{1,0:T(8,128)(2,1)}, bf16[128,512]{1,0:T(8,128)(2,1)S(1)}, u32[]{:S(2)}, u32[]{:S(2)}) %collective-permute-start.1) | collective-permute-done | bytes 131104 | tf_op jit(solution)/shard_map/ppermute | solution.py:358
  12.6 0.9 %collective-permute-done.6 = bf16[128]{0:T(256)(128)(2,1)S(1)} collective-permute-done((bf16[128]{0:T(256)(128)(2,1)}, bf16[128]{0:T(256)(128)(2,1)S(1)}, u32[]{:S(2)}, u32[]{:S(2)}) %collective-permute-start.6) | collective-permute-done | bytes 288 | tf_op jit(solution)/shard_map/ppermute | solution.py:358
  13.5 1.9 %collective-permute-done.refs_1_.refs_3_ = bf16[128,512]{1,0:T(8,128)(2,1)S(1)} collective-permute-done((bf16[128,512]{1,0:T(8,128)(2,1)}, bf16[128,512]{1,0:T(8,128)(2,1)S(1)}, u32[]{:S(2)}, u32[]{:S(2)}) %collective-permute-start) | collective-permute-done | bytes 131104 | tf_op jit(solution)/shard_map/ppermute | solution.py:358
  15.5 1.3 %forward.1 = (bf16[512,512]{1,0:T(8,128)(2,1)S(1)}, f32[32,256]{1,0:T(8,128)S(1)}, f32[32,256]{1,0:T(8,128)S(1)}) custom-call(bf16[128,512]{1,0:T(8,128)(2,1)S(1)} %get-tuple-element.32.refs_0_.refs_2_, bf16[128,512]{1,0:T(8,128)(2,1)S(1)} %collective-permute-done.refs_1_.refs_3_, bf16[128,512]{1,0:T(8,128)(2,1)S(1)} %collective-permute-done.1.refs_2_.refs_4_, ...), custom_call_target="tpu_custom_call" | custom-call | bytes 2196480 | tf_op jit(solution)/shard_map/forward/pallas_call | solution.py:330
  16.8 1.2 %collective-permute-done.8 = f32[32,256]{1,0:T(8,128)S(1)} collective-permute-done((f32[32,256]{1,0:T(8,128)S(1)}, f32[32,256]{1,0:T(8,128)S(1)}, u32[]{:S(2)}, u32[]{:S(2)}) %collective-permute-start.8) | collective-permute-done | bytes 32800 | tf_op jit(solution)/shard_map/ppermute | solution.py:358
  18.1 2.5 %collective-permute-start.12 = (f32[32,256]{1,0:T(8,128)S(1)}, f32[32,256]{1,0:T(8,128)S(1)}, u32[]{:S(2)}, u32[]{:S(2)}) collective-permute-start(f32[32,256]{1,0:T(8,128)S(1)} %add.9), channel_id=1, source_target_pairs={{0,8},{1,9},{2,10},{3,11},{4,12},{5,13},{6,14},{7,15},{8,0},{9,1},... | collective-permute-start | bytes 98312 | tf_op jit(solution)/shard_map/ppermute | solution.py:358
  21.0 2.6 %collective-permute-start.11 = (bf16[32,512]{1,0:T(8,128)(2,1)S(1)}, bf16[32,512]{1,0:T(8,128)(2,1)S(1)}, u32[]{:S(2)}, u32[]{:S(2)}) collective-permute-start(bf16[32,512]{1,0:T(8,128)(2,1)S(1)} %lead.1.refs_9_), channel_id=1, source_target_pairs={{0,9},{1,8},{2,11},{3,10},{4,13},{5,12},{6,15},{7,14},{8,1},{9,0},... | collective-permute-start | bytes 98312 | tf_op jit(solution)/shard_map/ppermute | solution.py:358
  23.6 1.8 %collective-permute-start.13 = (f32[32,256]{1,0:T(8,128)S(1)}, f32[32,256]{1,0:T(8,128)S(1)}, u32[]{:S(2)}, u32[]{:S(2)}) collective-permute-start(f32[32,256]{1,0:T(8,128)S(1)} %add.10.refs_0_), channel_id=1, source_target_pairs={{0,6},{1,7},{2,4},{3,5},{4,2},{5,3},{6,0},{7,1},{8,14},{9,15},{10,... | collective-permute-start | bytes 98312 | tf_op jit(solution)/shard_map/ppermute | solution.py:358
  25.4 1.2 %collective-permute-start.14 = (f32[32,256]{1,0:T(8,128)S(1)}, f32[32,256]{1,0:T(8,128)S(1)}, u32[]{:S(2)}, u32[]{:S(2)}) collective-permute-start(f32[32,256]{1,0:T(8,128)S(1)} %add.10.refs_0_), channel_id=1, source_target_pairs={{0,4},{1,5},{2,6},{3,7},{4,0},{5,1},{6,2},{7,3},{8,12},{9,13},{10,... | collective-permute-start | bytes 98312 | tf_op jit(solution)/shard_map/ppermute | solution.py:358
  27.7 1.8 %inverse.1.inverse_ref = f32[32,32]{1,0:T(8,128)S(1)} custom-call(bf16[4,32,512]{2,1,0:T(8,128)(2,1)S(1)} %pad_maximum_fusion.small_ref), custom_call_target="tpu_custom_call" | custom-call | bytes 135168 | tf_op jit(solution)/shard_map/inverse/pallas_call | solution.py:330
  29.5 1.1 %collective-permute-done.15.refs_3_ = f32[32,256]{1,0:T(8,128)S(1)} collective-permute-done((f32[32,256]{1,0:T(8,128)S(1)}, f32[32,256]{1,0:T(8,128)S(1)}, u32[]{:S(2)}, u32[]{:S(2)}) %collective-permute-start.15) | collective-permute-done | bytes 32800 | tf_op jit(solution)/shard_map/ppermute | solution.py:358
  30.5 1.5 %solve.1.refs_0_ = f32[64,256]{1,0:T(8,128)S(1)} custom-call(f32[32,32]{1,0:T(8,128)S(1)} %inverse.1.inverse_ref, bf16[32,2048]{1,0:T(8,128)(2,1)S(1)} %get-tuple-element.45.design_ref, bf16[2048,128]{1,0:T(8,128)(2,1)S(1)} %get-tuple-element.42.rows_ref, f32[1,512]{1,0:T(1,128)S(1)} %get-tuple-element.43.thresh_ref, ...), custom_call_target="tpu_custom_call" | custom-call | bytes 860160 | tf_op jit(solution)/shard_map/solve/pallas_call | solution.py:330
  33.2 0.9 %weight_side.1 = (bf16[128,512]{1,0:T(8,128)(2,1)S(1)}, bf16[512,512]{1,0:T(8,128)(2,1)S(1)}, bf16[128,512]{1,0:T(8,128)(2,1)S(1)}, bf16[128,512]{1,0:T(8,128)(2...) custom-call(bf16[512,512]{1,0:T(8,128)(2,1)S(1)} %get-tuple-element.34.refs_10_.member_ref, ...), custom_call_target="tpu_custom_call" | custom-call | bytes 3932160 | tf_op jit(solution)/shard_map/weight_side/pallas_call | solution.py:330
  35.7 1.2 %collective-permute-start.20 = (bf16[128,512]{1,0:T(8,128)(2,1)S(1)}, bf16[128,512]{1,0:T(8,128)(2,1)S(1)}, u32[]{:S(2)}, u32[]{:S(2)}) collective-permute-start(bf16[128,512]{1,0:T(8,128)(2,1)S(1)} %get-tuple-element.54), channel_id=1, source_target_pairs={{0,6},{1,7},{2,4},{3,5},{4,2},{5,3},{6,0},{7,1},{8,14},{9,15},{10,... | collective-permute-start | bytes 393224 | tf_op jit(solution)/shard_map/ppermute | solution.py:358
  36.9 2.0 %collective-permute-start.22 = (bf16[128,512]{1,0:T(8,128)(2,1)S(1)}, bf16[128,512]{1,0:T(8,128)(2,1)S(1)}, u32[]{:S(2)}, u32[]{:S(2)}) collective-permute-start(bf16[128,512]{1,0:T(8,128)(2,1)S(1)} %add_convert_fusion), channel_id=1, source_target_pairs={{0,8},{1,9},{2,10},{3,11},{4,12},{5,13},{6,14},{7,15},{8,0},{9,1},... | collective-permute-start | bytes 393224 | tf_op jit(solution)/shard_map/ppermute | solution.py:358
  39.2 1.4 %collective-permute-start.19 = (bf16[128,512]{1,0:T(8,128)(2,1)S(1)}, bf16[128,512]{1,0:T(8,128)(2,1)S(1)}, u32[]{:S(2)}, u32[]{:S(2)}) collective-permute-start(bf16[128,512]{1,0:T(8,128)(2,1)S(1)} %basis_side.5), channel_id=1, source_target_pairs={{0,2},{1,3},{2,0},{3,1},{4,6},{5,7},{6,4},{7,5},{8,10},{9,11},{10,... | collective-permute-start | bytes 393224 | tf_op jit(solution)/shard_map/ppermute | solution.py:358
  40.6 3.2 %loss.1 = (f32[8,128]{1,0:T(8,128)S(1)}, f32[128,128]{1,0:T(8,128)S(1)}) custom-call(bf16[2048,128]{1,0:T(8,128)(2,1)S(1)} %get-tuple-element.42.rows_ref, f32[1,512]{1,0:T(1,128)S(1)} %get-tuple-element.43.thresh_ref, f32[1,512]{1,0:T(1,128)S(1)} %get-tuple-element.44.rate_ref, f32[64,256]{1,0:T(8,128)S(1)} %solve.1.refs_0_, ...), custom_call_target="tpu_custom_call" | custom-call | bytes 729088 | tf_op jit(solution)/shard_map/loss/pallas_call | solution.py:330
  44.7 1.6 %collective-permute-done.20.refs_3_ = bf16[128,512]{1,0:T(8,128)(2,1)S(1)} collective-permute-done((bf16[128,512]{1,0:T(8,128)(2,1)S(1)}, bf16[128,512]{1,0:T(8,128)(2,1)S(1)}, u32[]{:S(2)}, u32[]{:S(2)}) %collective-permute-start.20) | collective-permute-done | bytes 131104 | tf_op jit(solution)/shard_map/ppermute | solution.py:358
  46.3 1.0 %collective-permute-done.19.refs_2_ = bf16[128,512]{1,0:T(8,128)(2,1)S(1)} collective-permute-done((bf16[128,512]{1,0:T(8,128)(2,1)S(1)}, bf16[128,512]{1,0:T(8,128)(2,1)S(1)}, u32[]{:S(2)}, u32[]{:S(2)}) %collective-permute-start.19) | collective-permute-done | bytes 131104 | tf_op jit(solution)/shard_map/ppermute | solution.py:358
  (56 shorter events, 8.6 us)
Async XLA Ops:
  0.6 7.7 %copy-start.2 = (s32[2048]{0:T(1024)S(1)}, s32[2048]{0:T(1024)}, u32[]{:S(2)}) copy-start(s32[2048]{0:T(1024)} %param.10) | copy-start | bytes 24580
  0.6 10.9 %collective-permute-start.3 = (bf16[128,512]{1,0:T(8,128)(2,1)}, bf16[128,512]{1,0:T(8,128)(2,1)S(1)}, u32[]{:S(2)}, u32[]{:S(2)}) collective-permute-start(bf16[128,512]{1,0:T(8,128)(2,1)} %w_ref.1), channel_id=1, source_target_pairs={{0,8},{1,9},{2,10},{3,11},{4,12},{5,13},{6,14},{7,15},{8,0},{9,1},... | collective-permute-start | bytes 393224 | tf_op jit(solution)/shard_map/ppermute | solution.py:358
  4.7 7.8 %collective-permute-start.1 = (bf16[128,512]{1,0:T(8,128)(2,1)}, bf16[128,512]{1,0:T(8,128)(2,1)S(1)}, u32[]{:S(2)}, u32[]{:S(2)}) collective-permute-start(bf16[128,512]{1,0:T(8,128)(2,1)} %x_ref.1), channel_id=1, source_target_pairs={{0,4},{1,5},{2,6},{3,7},{4,0},{5,1},{6,2},{7,3},{8,12},{9,13},{10,... | collective-permute-start | bytes 393224 | tf_op jit(solution)/shard_map/ppermute | solution.py:358
  6.3 9.1 %collective-permute-start = (bf16[128,512]{1,0:T(8,128)(2,1)}, bf16[128,512]{1,0:T(8,128)(2,1)S(1)}, u32[]{:S(2)}, u32[]{:S(2)}) collective-permute-start(bf16[128,512]{1,0:T(8,128)(2,1)} %x_ref.1), channel_id=1, source_target_pairs={{0,6},{1,7},{2,4},{3,5},{4,2},{5,3},{6,0},{7,1},{8,14},{9,15},{10,... | collective-permute-start | bytes 393224 | tf_op jit(solution)/shard_map/ppermute | solution.py:358
  7.7 7.7 %collective-permute-start.2 = (bf16[128,512]{1,0:T(8,128)(2,1)}, bf16[128,512]{1,0:T(8,128)(2,1)S(1)}, u32[]{:S(2)}, u32[]{:S(2)}) collective-permute-start(bf16[128,512]{1,0:T(8,128)(2,1)} %x_ref.1), channel_id=1, source_target_pairs={{0,2},{1,3},{2,0},{3,1},{4,6},{5,7},{6,4},{7,5},{8,10},{9,11},{10,... | collective-permute-start | bytes 393224 | tf_op jit(solution)/shard_map/ppermute | solution.py:358
  8.2 5.3 %collective-permute-start.6 = (bf16[128]{0:T(256)(128)(2,1)}, bf16[128]{0:T(256)(128)(2,1)S(1)}, u32[]{:S(2)}, u32[]{:S(2)}) collective-permute-start(bf16[128]{0:T(256)(128)(2,1)} %param.9), channel_id=1, source_target_pairs={{0,8},{1,9},{2,10},{3,11},{4,12},{5,13},{6,14},{7,15},{8,0},{9,1},... | collective-permute-start | bytes 776 | tf_op jit(solution)/shard_map/ppermute | solution.py:358
  11.5 4.0 %collective-permute-start.4 = (bf16[128,512]{1,0:T(8,128)(2,1)S(1)}, bf16[128,512]{1,0:T(8,128)(2,1)S(1)}, u32[]{:S(2)}, u32[]{:S(2)}) collective-permute-start(bf16[128,512]{1,0:T(8,128)(2,1)S(1)} %copy-done.1), channel_id=1, source_target_pairs={{0,1},{1,0},{2,3},{3,2},{4,5},{5,4},{6,7},{7,6},{8,9},{9,8},{10,11... | collective-permute-start | bytes 393224 | tf_op jit(solution)/shard_map/ppermute | solution.py:358
  12.6 3.0 %collective-permute-start.5 = (bf16[128,512]{1,0:T(8,128)(2,1)S(1)}, bf16[128,512]{1,0:T(8,128)(2,1)S(1)}, u32[]{:S(2)}, u32[]{:S(2)}) collective-permute-start(bf16[128,512]{1,0:T(8,128)(2,1)S(1)} %collective-permute-done.3.refs_5_.refs_1_), channel_id=1, source_target_pairs={{0,1},{1,0},{2,3},{3,2},{4,5},{5,4},{6,7},{7,6},{8,9},{9,8},{10,11... | collective-permute-start | bytes 393224 | tf_op jit(solution)/shard_map/ppermute | solution.py:358
  13.5 2.0 %collective-permute-start.7 = (bf16[2,128]{1,0:T(2,128)(2,1)S(1)}, bf16[2,128]{1,0:T(2,128)(2,1)S(1)}, u32[]{:S(2)}, u32[]{:S(2)}) collective-permute-start(bf16[2,128]{1,0:T(2,128)(2,1)S(1)} %pad_maximum_fusion.2), channel_id=1, source_target_pairs={{0,1},{1,0},{2,3},{3,2},{4,5},{5,4},{6,7},{7,6},{8,9},{9,8},{10,11... | collective-permute-start | bytes 1544 | tf_op jit(solution)/shard_map/ppermute | solution.py:358
  16.8 1.3 %collective-permute-start.8 = (f32[32,256]{1,0:T(8,128)S(1)}, f32[32,256]{1,0:T(8,128)S(1)}, u32[]{:S(2)}, u32[]{:S(2)}) collective-permute-start(f32[32,256]{1,0:T(8,128)S(1)} %get-tuple-element.40), channel_id=1, source_target_pairs={{0,1},{1,0},{2,3},{3,2},{4,5},{5,4},{6,7},{7,6},{8,9},{9,8},{10,11... | collective-permute-start | bytes 98312 | tf_op jit(solution)/shard_map/ppermute | solution.py:358
  18.1 5.5 %collective-permute-start.12 = (f32[32,256]{1,0:T(8,128)S(1)}, f32[32,256]{1,0:T(8,128)S(1)}, u32[]{:S(2)}, u32[]{:S(2)}) collective-permute-start(f32[32,256]{1,0:T(8,128)S(1)} %add.9), channel_id=1, source_target_pairs={{0,8},{1,9},{2,10},{3,11},{4,12},{5,13},{6,14},{7,15},{8,0},{9,1},... | collective-permute-start | bytes 98312 | tf_op jit(solution)/shard_map/ppermute | solution.py:358
  20.5 6.1 %collective-permute-start.9 = (bf16[32,512]{1,0:T(8,128)(2,1)S(1)}, bf16[32,512]{1,0:T(8,128)(2,1)S(1)}, u32[]{:S(2)}, u32[]{:S(2)}) collective-permute-start(bf16[32,512]{1,0:T(8,128)(2,1)S(1)} %lead.1.refs_9_), channel_id=1, source_target_pairs={{0,8},{1,9},{2,10},{3,11},{4,12},{5,13},{6,14},{7,15},{8,0},{9,1},... | collective-permute-start | bytes 98312 | tf_op jit(solution)/shard_map/ppermute | solution.py:358
  21.0 6.2 %collective-permute-start.10 = (bf16[32,512]{1,0:T(8,128)(2,1)S(1)}, bf16[32,512]{1,0:T(8,128)(2,1)S(1)}, u32[]{:S(2)}, u32[]{:S(2)}) collective-permute-start(bf16[32,512]{1,0:T(8,128)(2,1)S(1)} %lead.1.refs_9_), channel_id=1, source_target_pairs={{0,1},{1,0},{2,3},{3,2},{4,5},{5,4},{6,7},{7,6},{8,9},{9,8},{10,11... | collective-permute-start | bytes 98312 | tf_op jit(solution)/shard_map/ppermute | solution.py:358
  21.0 6.2 %collective-permute-start.11 = (bf16[32,512]{1,0:T(8,128)(2,1)S(1)}, bf16[32,512]{1,0:T(8,128)(2,1)S(1)}, u32[]{:S(2)}, u32[]{:S(2)}) collective-permute-start(bf16[32,512]{1,0:T(8,128)(2,1)S(1)} %lead.1.refs_9_), channel_id=1, source_target_pairs={{0,9},{1,8},{2,11},{3,10},{4,13},{5,12},{6,15},{7,14},{8,1},{9,0},... | collective-permute-start | bytes 98312 | tf_op jit(solution)/shard_map/ppermute | solution.py:358
  23.6 5.9 %collective-permute-start.13 = (f32[32,256]{1,0:T(8,128)S(1)}, f32[32,256]{1,0:T(8,128)S(1)}, u32[]{:S(2)}, u32[]{:S(2)}) collective-permute-start(f32[32,256]{1,0:T(8,128)S(1)} %add.10.refs_0_), channel_id=1, source_target_pairs={{0,6},{1,7},{2,4},{3,5},{4,2},{5,3},{6,0},{7,1},{8,14},{9,15},{10,... | collective-permute-start | bytes 98312 | tf_op jit(solution)/shard_map/ppermute | solution.py:358
  25.4 4.1 %collective-permute-start.14 = (f32[32,256]{1,0:T(8,128)S(1)}, f32[32,256]{1,0:T(8,128)S(1)}, u32[]{:S(2)}, u32[]{:S(2)}) collective-permute-start(f32[32,256]{1,0:T(8,128)S(1)} %add.10.refs_0_), channel_id=1, source_target_pairs={{0,4},{1,5},{2,6},{3,7},{4,0},{5,1},{6,2},{7,3},{8,12},{9,13},{10,... | collective-permute-start | bytes 98312 | tf_op jit(solution)/shard_map/ppermute | solution.py:358
  26.6 3.9 %collective-permute-start.15 = (f32[32,256]{1,0:T(8,128)S(1)}, f32[32,256]{1,0:T(8,128)S(1)}, u32[]{:S(2)}, u32[]{:S(2)}) collective-permute-start(f32[32,256]{1,0:T(8,128)S(1)} %add.10.refs_0_), channel_id=1, source_target_pairs={{0,2},{1,3},{2,0},{3,1},{4,6},{5,7},{6,4},{7,5},{8,10},{9,11},{10,... | collective-permute-start | bytes 98312 | tf_op jit(solution)/shard_map/ppermute | solution.py:358
  32.0 1.3 %collective-permute-start.16 = (f32[64,256]{1,0:T(8,128)S(1)}, f32[64,256]{1,0:T(8,128)S(1)}, u32[]{:S(2)}, u32[]{:S(2)}) collective-permute-start(f32[64,256]{1,0:T(8,128)S(1)} %solve.1.refs_0_), channel_id=1, source_target_pairs={{0,1},{1,0},{2,3},{3,2},{4,5},{5,4},{6,7},{7,6},{8,9},{9,8},{10,11... | collective-permute-start | bytes 196616 | tf_op jit(solution)/shard_map/ppermute | solution.py:358
  34.1 2.7 %collective-permute-start.17 = (bf16[128,512]{1,0:T(8,128)(2,1)S(1)}, bf16[128,512]{1,0:T(8,128)(2,1)S(1)}, u32[]{:S(2)}, u32[]{:S(2)}) collective-permute-start(bf16[128,512]{1,0:T(8,128)(2,1)S(1)} %get-tuple-element.51), channel_id=1, source_target_pairs={{0,1},{1,0},{2,3},{3,2},{4,5},{5,4},{6,7},{7,6},{8,9},{9,8},{10,11... | collective-permute-start | bytes 393224 | tf_op jit(solution)/shard_map/ppermute | solution.py:358
  34.8 9.9 %collective-permute-start.18 = (bf16[128,512]{1,0:T(8,128)(2,1)S(1)}, bf16[128,512]{1,0:T(8,128)(2,1)S(1)}, u32[]{:S(2)}, u32[]{:S(2)}) collective-permute-start(bf16[128,512]{1,0:T(8,128)(2,1)S(1)} %get-tuple-element.53), channel_id=1, source_target_pairs={{0,4},{1,5},{2,6},{3,7},{4,0},{5,1},{6,2},{7,3},{8,12},{9,13},{10,... | collective-permute-start | bytes 393224 | tf_op jit(solution)/shard_map/ppermute | solution.py:358
  35.7 10.6 %collective-permute-start.20 = (bf16[128,512]{1,0:T(8,128)(2,1)S(1)}, bf16[128,512]{1,0:T(8,128)(2,1)S(1)}, u32[]{:S(2)}, u32[]{:S(2)}) collective-permute-start(bf16[128,512]{1,0:T(8,128)(2,1)S(1)} %get-tuple-element.54), channel_id=1, source_target_pairs={{0,6},{1,7},{2,4},{3,5},{4,2},{5,3},{6,0},{7,1},{8,14},{9,15},{10,... | collective-permute-start | bytes 393224 | tf_op jit(solution)/shard_map/ppermute | solution.py:358
  36.9 9.4 %collective-permute-start.22 = (bf16[128,512]{1,0:T(8,128)(2,1)S(1)}, bf16[128,512]{1,0:T(8,128)(2,1)S(1)}, u32[]{:S(2)}, u32[]{:S(2)}) collective-permute-start(bf16[128,512]{1,0:T(8,128)(2,1)S(1)} %add_convert_fusion), channel_id=1, source_target_pairs={{0,8},{1,9},{2,10},{3,11},{4,12},{5,13},{6,14},{7,15},{8,0},{9,1},... | collective-permute-start | bytes 393224 | tf_op jit(solution)/shard_map/ppermute | solution.py:358
  38.9 7.4 %collective-permute-start.21 = (bf16[128,512]{1,0:T(8,128)(2,1)S(1)}, bf16[128,512]{1,0:T(8,128)(2,1)S(1)}, u32[]{:S(2)}, u32[]{:S(2)}) collective-permute-start(bf16[128,512]{1,0:T(8,128)(2,1)S(1)} %get-tuple-element.57), channel_id=1, source_target_pairs={{0,1},{1,0},{2,3},{3,2},{4,5},{5,4},{6,7},{7,6},{8,9},{9,8},{10,11... | collective-permute-start | bytes 393224 | tf_op jit(solution)/shard_map/ppermute | solution.py:358
  39.2 8.1 %collective-permute-start.19 = (bf16[128,512]{1,0:T(8,128)(2,1)S(1)}, bf16[128,512]{1,0:T(8,128)(2,1)S(1)}, u32[]{:S(2)}, u32[]{:S(2)}) collective-permute-start(bf16[128,512]{1,0:T(8,128)(2,1)S(1)} %basis_side.5), channel_id=1, source_target_pairs={{0,2},{1,3},{2,0},{3,1},{4,6},{5,7},{6,4},{7,5},{8,10},{9,11},{10,... | collective-permute-start | bytes 393224 | tf_op jit(solution)/shard_map/ppermute | solution.py:358
  (6 other events, 4.6 us)

commit v14 on v12

--- a/solution.py
+++ b/solution.py
@@ -107,16 +107,6 @@
                     block = jnp.where(row == here + j, r[j], block)
             blocks[i] = block
     return jnp.concatenate(blocks, axis=0)[:, size:]
-
-
-def lead_kernel(*refs):
-    x_refs, lead_ref = refs[:-1], refs[-1]
-    start = 0
-    for x in x_refs:
-        turned = x[:, :LANES].astype(F32).T[:REGRESSORS]
-        turned = jnp.where(rows(turned.shape) == CONSTANT, 1.0, turned)
-        lead_ref[:, start : start + x.shape[0]] = turned.astype(BF16)
-        start += x.shape[0]
 
 
 def tables_kernel(
@@ -176,11 +166,14 @@
 def forward_kernel(paths, trades, *refs):
     x_refs, refs = refs[:paths], refs[paths:]
     weights, notional = joined_weights(refs[:trades]), one_row(refs[trades])
-    lead_ref, member_ref, value_ref, *moment_refs = refs[trades + 1 :]
+    member_ref, value_ref, lead_ref, *moment_refs = refs[trades + 1 :]
     start = 0
     for x in x_refs:
         pre_act = dot(x[...], weights, 1, 1)
         value_ref[start : start + x.shape[0]] = (notional * softplus(pre_act)).astype(BF16)
+        turned = x[:, :LANES].astype(F32).T[:REGRESSORS]
+        turned = jnp.where(rows(turned.shape) == CONSTANT, 1.0, turned)
+        lead_ref[:, start : start + x.shape[0]] = turned.astype(BF16)
         start += x.shape[0]
     trade_moment = dot(lead_ref[...], value_ref[...])
     parts = dot(three(trade_moment, 0), member_ref[...], 1, 1)
@@ -403,11 +396,11 @@
         ]
         notionals = jnp.concatenate([notionals, swap(notionals, 1 << bit)], axis=0)
     weights[0] = own_weight
-    (lead,) = call(lead_kernel, [((REGRESSORS, group_paths), BF16)], *basis, name="lead")
-    value, *moments = call(
+    value, lead, *moments = call(
         partial(forward_kernel, inner, outer),
-        [((group_paths, group_trades), BF16)] + [((REGRESSORS, share), F32)] * SHARES,
-        *basis, *weights, notionals, lead, member,
+        [((group_paths, group_trades), BF16), ((REGRESSORS, group_paths), BF16)]
+        + [((REGRESSORS, share), F32)] * SHARES,
+        *basis, *weights, notionals, member,
         name="forward",
     )
     moment = moments[0] + swap(moments[1], SHARES - 1)

time: 47.3 us -> 47.3 us (level)
    pallas_call x13 -> x12, Pallas kernels: 12.7 us -> 12.6 us  [call(): pl.pallas_call(kernel, out_shape=[jax.ShapeDtypeStruct(s, d) for s, d in...]
  transfers between devices with their start and end apart: 23 -> 23, of which waited for: 8 -> 9; matrix products, arithmetic and copies ran while one was open for 1% -> 1% of each run, Pallas kernels for 17% -> 17%
where the time goes in v14:
time: 47.3 us; the launch traced here: 47.1 us
  starting transfers between devices  22.6 us (48%)
  Pallas kernels  12.6 us (27%)
  waiting for transfers between devices  7.99 us (17%)
  local copies, waits for them, and re-layouts  3.04 us (6%)
  between operations  0.79 us (2%)
    ppermute x23, starting transfers between devices, swap(): return lax.ppermute(x, 'paths', [(d, d ^ mask) for d in range(n)])  22.6 us
    pallas_call x12, Pallas kernels, call(): pl.pallas_call(kernel, out_shape=[jax.ShapeDtypeStruct(s, d) for s, d in...  12.6 us
    ppermute x23, waiting for transfers between devices, swap(): return lax.ppermute(x, 'paths', [(d, d ^ mask) for d in range(n)])  7.99 us
    unnamed x14, local copies, waits for them, and re-layouts  2.52 us
  transfers between devices with their start and end apart: 23, of which 9 were waited for; matrix products, arithmetic and copies ran while one was open for 1% of the time, Pallas kernels for 17%

profile of v14, /device:TPU:0, one launch (start us, length us, event | category | flops | bytes accessed | tf_op | source)
XLA Modules:
  0.0 47.1 jit_solution(11377570842808222965)
XLA Ops:
  0.6 4.1 %collective-permute-start.3 = (bf16[128,512]{1,0:T(8,128)(2,1)}, bf16[128,512]{1,0:T(8,128)(2,1)S(1)}, u32[]{:S(2)}, u32[]{:S(2)}) collective-permute-start(bf16[128,512]{1,0:T(8,128)(2,1)} %w_ref.1), channel_id=1, source_target_pairs={{0,8},{1,9},{2,10},{3,11},{4,12},{5,13},{6,14},{7,15},{8,0},{9,1},... | collective-permute-start | bytes 393224 | tf_op jit(solution)/shard_map/ppermute | solution.py:351
  4.7 1.6 %collective-permute-start.1 = (bf16[128,512]{1,0:T(8,128)(2,1)}, bf16[128,512]{1,0:T(8,128)(2,1)S(1)}, u32[]{:S(2)}, u32[]{:S(2)}) collective-permute-start(bf16[128,512]{1,0:T(8,128)(2,1)} %x_ref.1), channel_id=1, source_target_pairs={{0,4},{1,5},{2,6},{3,7},{4,0},{5,1},{6,2},{7,3},{8,12},{9,13},{10,... | collective-permute-start | bytes 393224 | tf_op jit(solution)/shard_map/ppermute | solution.py:351
  6.3 1.4 %collective-permute-start = (bf16[128,512]{1,0:T(8,128)(2,1)}, bf16[128,512]{1,0:T(8,128)(2,1)S(1)}, u32[]{:S(2)}, u32[]{:S(2)}) collective-permute-start(bf16[128,512]{1,0:T(8,128)(2,1)} %x_ref.1), channel_id=1, source_target_pairs={{0,6},{1,7},{2,4},{3,5},{4,2},{5,3},{6,0},{7,1},{8,14},{9,15},{10,... | collective-permute-start | bytes 393224 | tf_op jit(solution)/shard_map/ppermute | solution.py:351
  9.0 0.9 %copy-done = bf16[128,512]{1,0:T(8,128)(2,1)S(1)} copy-done((bf16[128,512]{1,0:T(8,128)(2,1)S(1)}, bf16[128,512]{1,0:T(8,128)(2,1)}, u32[]{:S(2)}) %copy-start) | copy-done | bytes 131096
  9.9 0.9 %copy-done.1 = bf16[128,512]{1,0:T(8,128)(2,1)S(1)} copy-done((bf16[128,512]{1,0:T(8,128)(2,1)S(1)}, bf16[128,512]{1,0:T(8,128)(2,1)}, u32[]{:S(2)}) %copy-start.1) | copy-done | bytes 131096
  11.6 0.9 %collective-permute-done.1.refs_2_.refs_4_ = bf16[128,512]{1,0:T(8,128)(2,1)S(1)} collective-permute-done((bf16[128,512]{1,0:T(8,128)(2,1)}, bf16[128,512]{1,0:T(8,128)(2,1)S(1)}, u32[]{:S(2)}, u32[]{:S(2)}) %collective-permute-start.1) | collective-permute-done | bytes 131104 | tf_op jit(solution)/shard_map/ppermute | solution.py:351
  12.6 0.9 %collective-permute-done.6 = bf16[128]{0:T(256)(128)(2,1)S(1)} collective-permute-done((bf16[128]{0:T(256)(128)(2,1)}, bf16[128]{0:T(256)(128)(2,1)S(1)}, u32[]{:S(2)}, u32[]{:S(2)}) %collective-permute-start.6) | collective-permute-done | bytes 288 | tf_op jit(solution)/shard_map/ppermute | solution.py:351
  13.5 1.1 %collective-permute-done.7 = bf16[2,128]{1,0:T(2,128)(2,1)S(1)} collective-permute-done((bf16[2,128]{1,0:T(2,128)(2,1)S(1)}, bf16[2,128]{1,0:T(2,128)(2,1)S(1)}, u32[]{:S(2)}, u32[]{:S(2)}) %collective-permute-start.7) | collective-permute-done | bytes 544 | tf_op jit(solution)/shard_map/ppermute | solution.py:351
  15.4 1.3 %forward.1 = (bf16[512,512]{1,0:T(8,128)(2,1)S(1)}, bf16[32,512]{1,0:T(8,128)(2,1)S(1)}, f32[32,256]{1,0:T(8,128)S(1)}, f32[32,256]{1,0:T(8,128)S(1)}) custom-call(bf16[128,512]{1,0:T(8,128)(2,1)S(1)} %get-tuple-element.33.refs_0_.refs_2_, bf16[128,512]{1,0:T(8,128)(2,1)S(1)} %collective-permute-done.refs_1_.refs_3_, ...), custom_call_target="tpu_custom_call" | custom-call | bytes 2196480 | tf_op jit(solution)/shard_map/forward/pallas_call | solution.py:323
  16.7 1.3 %collective-permute-done.8 = f32[32,256]{1,0:T(8,128)S(1)} collective-permute-done((f32[32,256]{1,0:T(8,128)S(1)}, f32[32,256]{1,0:T(8,128)S(1)}, u32[]{:S(2)}, u32[]{:S(2)}) %collective-permute-start.8) | collective-permute-done | bytes 32800 | tf_op jit(solution)/shard_map/ppermute | solution.py:351
  17.9 2.6 %collective-permute-start.12 = (f32[32,256]{1,0:T(8,128)S(1)}, f32[32,256]{1,0:T(8,128)S(1)}, u32[]{:S(2)}, u32[]{:S(2)}) collective-permute-start(f32[32,256]{1,0:T(8,128)S(1)} %add.9), channel_id=1, source_target_pairs={{0,8},{1,9},{2,10},{3,11},{4,12},{5,13},{6,14},{7,15},{8,0},{9,1},... | collective-permute-start | bytes 98312 | tf_op jit(solution)/shard_map/ppermute | solution.py:351
  20.9 2.7 %collective-permute-start.11 = (bf16[32,512]{1,0:T(8,128)(2,1)S(1)}, bf16[32,512]{1,0:T(8,128)(2,1)S(1)}, u32[]{:S(2)}, u32[]{:S(2)}) collective-permute-start(bf16[32,512]{1,0:T(8,128)(2,1)S(1)} %get-tuple-element.43), channel_id=1, source_target_pairs={{0,9},{1,8},{2,11},{3,10},{4,13},{5,12},{6,15},{7,14},{8,1},{9,0},... | collective-permute-start | bytes 98312 | tf_op jit(solution)/shard_map/ppermute | solution.py:351
  23.6 1.8 %collective-permute-start.13 = (f32[32,256]{1,0:T(8,128)S(1)}, f32[32,256]{1,0:T(8,128)S(1)}, u32[]{:S(2)}, u32[]{:S(2)}) collective-permute-start(f32[32,256]{1,0:T(8,128)S(1)} %add.10.refs_0_), channel_id=1, source_target_pairs={{0,6},{1,7},{2,4},{3,5},{4,2},{5,3},{6,0},{7,1},{8,14},{9,15},{10,... | collective-permute-start | bytes 98312 | tf_op jit(solution)/shard_map/ppermute | solution.py:351
  25.4 1.2 %collective-permute-start.14 = (f32[32,256]{1,0:T(8,128)S(1)}, f32[32,256]{1,0:T(8,128)S(1)}, u32[]{:S(2)}, u32[]{:S(2)}) collective-permute-start(f32[32,256]{1,0:T(8,128)S(1)} %add.10.refs_0_), channel_id=1, source_target_pairs={{0,4},{1,5},{2,6},{3,7},{4,0},{5,1},{6,2},{7,3},{8,12},{9,13},{10,... | collective-permute-start | bytes 98312 | tf_op jit(solution)/shard_map/ppermute | solution.py:351
  27.7 1.8 %inverse.1.inverse_ref = f32[32,32]{1,0:T(8,128)S(1)} custom-call(bf16[4,32,512]{2,1,0:T(8,128)(2,1)S(1)} %pad_maximum_fusion.small_ref), custom_call_target="tpu_custom_call" | custom-call | bytes 135168 | tf_op jit(solution)/shard_map/inverse/pallas_call | solution.py:323
  29.5 1.1 %collective-permute-done.15.refs_3_ = f32[32,256]{1,0:T(8,128)S(1)} collective-permute-done((f32[32,256]{1,0:T(8,128)S(1)}, f32[32,256]{1,0:T(8,128)S(1)}, u32[]{:S(2)}, u32[]{:S(2)}) %collective-permute-start.15) | collective-permute-done | bytes 32800 | tf_op jit(solution)/shard_map/ppermute | solution.py:351
  30.5 1.5 %solve.1.refs_0_ = f32[64,256]{1,0:T(8,128)S(1)} custom-call(f32[32,32]{1,0:T(8,128)S(1)} %inverse.1.inverse_ref, bf16[32,2048]{1,0:T(8,128)(2,1)S(1)} %get-tuple-element.47.design_ref, bf16[2048,128]{1,0:T(8,128)(2,1)S(1)} %get-tuple-element.44.rows_ref, f32[1,512]{1,0:T(1,128)S(1)} %get-tuple-element.45.thresh_ref, ...), custom_call_target="tpu_custom_call" | custom-call | bytes 860160 | tf_op jit(solution)/shard_map/solve/pallas_call | solution.py:323
  33.3 0.9 %weight_side.1 = (bf16[128,512]{1,0:T(8,128)(2,1)S(1)}, bf16[512,512]{1,0:T(8,128)(2,1)S(1)}, bf16[128,512]{1,0:T(8,128)(2,1)S(1)}, bf16[128,512]{1,0:T(8,128)(2...) custom-call(bf16[512,512]{1,0:T(8,128)(2,1)S(1)} %get-tuple-element.35.refs_9_.member_ref, ...), custom_call_target="tpu_custom_call" | custom-call | bytes 3932160 | tf_op jit(solution)/shard_map/weight_side/pallas_call | solution.py:323
  34.9 1.1 %collective-permute-start.18 = (bf16[128,512]{1,0:T(8,128)(2,1)S(1)}, bf16[128,512]{1,0:T(8,128)(2,1)S(1)}, u32[]{:S(2)}, u32[]{:S(2)}) collective-permute-start(bf16[128,512]{1,0:T(8,128)(2,1)S(1)} %get-tuple-element.55), channel_id=1, source_target_pairs={{0,6},{1,7},{2,4},{3,5},{4,2},{5,3},{6,0},{7,1},{8,14},{9,15},{10,... | collective-permute-start | bytes 393224 | tf_op jit(solution)/shard_map/ppermute | solution.py:351
  35.9 1.0 %collective-permute-start.19 = (bf16[128,512]{1,0:T(8,128)(2,1)S(1)}, bf16[128,512]{1,0:T(8,128)(2,1)S(1)}, u32[]{:S(2)}, u32[]{:S(2)}) collective-permute-start(bf16[128,512]{1,0:T(8,128)(2,1)S(1)} %get-tuple-element.56), channel_id=1, source_target_pairs={{0,4},{1,5},{2,6},{3,7},{4,0},{5,1},{6,2},{7,3},{8,12},{9,13},{10,... | collective-permute-start | bytes 393224 | tf_op jit(solution)/shard_map/ppermute | solution.py:351
  36.9 1.8 %collective-permute-start.22 = (bf16[128,512]{1,0:T(8,128)(2,1)S(1)}, bf16[128,512]{1,0:T(8,128)(2,1)S(1)}, u32[]{:S(2)}, u32[]{:S(2)}) collective-permute-start(bf16[128,512]{1,0:T(8,128)(2,1)S(1)} %add_convert_fusion), channel_id=1, source_target_pairs={{0,8},{1,9},{2,10},{3,11},{4,12},{5,13},{6,14},{7,15},{8,0},{9,1},... | collective-permute-start | bytes 393224 | tf_op jit(solution)/shard_map/ppermute | solution.py:351
  39.1 1.6 %collective-permute-start.20 = (bf16[128,512]{1,0:T(8,128)(2,1)S(1)}, bf16[128,512]{1,0:T(8,128)(2,1)S(1)}, u32[]{:S(2)}, u32[]{:S(2)}) collective-permute-start(bf16[128,512]{1,0:T(8,128)(2,1)S(1)} %basis_side.5), channel_id=1, source_target_pairs={{0,2},{1,3},{2,0},{3,1},{4,6},{5,7},{6,4},{7,5},{8,10},{9,11},{10,... | collective-permute-start | bytes 393224 | tf_op jit(solution)/shard_map/ppermute | solution.py:351
  40.7 3.2 %loss.1 = (f32[8,128]{1,0:T(8,128)S(1)}, f32[128,128]{1,0:T(8,128)S(1)}) custom-call(bf16[2048,128]{1,0:T(8,128)(2,1)S(1)} %get-tuple-element.44.rows_ref, f32[1,512]{1,0:T(1,128)S(1)} %get-tuple-element.45.thresh_ref, f32[1,512]{1,0:T(1,128)S(1)} %get-tuple-element.46.rate_ref, f32[64,256]{1,0:T(8,128)S(1)} %solve.1.refs_0_, ...), custom_call_target="tpu_custom_call" | custom-call | bytes 729088 | tf_op jit(solution)/shard_map/loss/pallas_call | solution.py:323
  44.9 1.3 %collective-permute-done.19.refs_2_ = bf16[128,512]{1,0:T(8,128)(2,1)S(1)} collective-permute-done((bf16[128,512]{1,0:T(8,128)(2,1)S(1)}, bf16[128,512]{1,0:T(8,128)(2,1)S(1)}, u32[]{:S(2)}, u32[]{:S(2)}) %collective-permute-start.19) | collective-permute-done | bytes 131104 | tf_op jit(solution)/shard_map/ppermute | solution.py:351
  (55 shorter events, 8.5 us)
Async XLA Ops:
  0.6 7.7 %copy-start.2 = (s32[2048]{0:T(1024)S(1)}, s32[2048]{0:T(1024)}, u32[]{:S(2)}) copy-start(s32[2048]{0:T(1024)} %param.10) | copy-start | bytes 24580
  0.6 10.9 %collective-permute-start.3 = (bf16[128,512]{1,0:T(8,128)(2,1)}, bf16[128,512]{1,0:T(8,128)(2,1)S(1)}, u32[]{:S(2)}, u32[]{:S(2)}) collective-permute-start(bf16[128,512]{1,0:T(8,128)(2,1)} %w_ref.1), channel_id=1, source_target_pairs={{0,8},{1,9},{2,10},{3,11},{4,12},{5,13},{6,14},{7,15},{8,0},{9,1},... | collective-permute-start | bytes 393224 | tf_op jit(solution)/shard_map/ppermute | solution.py:351
  4.7 7.8 %collective-permute-start.1 = (bf16[128,512]{1,0:T(8,128)(2,1)}, bf16[128,512]{1,0:T(8,128)(2,1)S(1)}, u32[]{:S(2)}, u32[]{:S(2)}) collective-permute-start(bf16[128,512]{1,0:T(8,128)(2,1)} %x_ref.1), channel_id=1, source_target_pairs={{0,4},{1,5},{2,6},{3,7},{4,0},{5,1},{6,2},{7,3},{8,12},{9,13},{10,... | collective-permute-start | bytes 393224 | tf_op jit(solution)/shard_map/ppermute | solution.py:351
  6.3 9.1 %collective-permute-start = (bf16[128,512]{1,0:T(8,128)(2,1)}, bf16[128,512]{1,0:T(8,128)(2,1)S(1)}, u32[]{:S(2)}, u32[]{:S(2)}) collective-permute-start(bf16[128,512]{1,0:T(8,128)(2,1)} %x_ref.1), channel_id=1, source_target_pairs={{0,6},{1,7},{2,4},{3,5},{4,2},{5,3},{6,0},{7,1},{8,14},{9,15},{10,... | collective-permute-start | bytes 393224 | tf_op jit(solution)/shard_map/ppermute | solution.py:351
  7.7 7.7 %collective-permute-start.2 = (bf16[128,512]{1,0:T(8,128)(2,1)}, bf16[128,512]{1,0:T(8,128)(2,1)S(1)}, u32[]{:S(2)}, u32[]{:S(2)}) collective-permute-start(bf16[128,512]{1,0:T(8,128)(2,1)} %x_ref.1), channel_id=1, source_target_pairs={{0,2},{1,3},{2,0},{3,1},{4,6},{5,7},{6,4},{7,5},{8,10},{9,11},{10,... | collective-permute-start | bytes 393224 | tf_op jit(solution)/shard_map/ppermute | solution.py:351
  8.2 5.3 %collective-permute-start.6 = (bf16[128]{0:T(256)(128)(2,1)}, bf16[128]{0:T(256)(128)(2,1)S(1)}, u32[]{:S(2)}, u32[]{:S(2)}) collective-permute-start(bf16[128]{0:T(256)(128)(2,1)} %param.9), channel_id=1, source_target_pairs={{0,8},{1,9},{2,10},{3,11},{4,12},{5,13},{6,14},{7,15},{8,0},{9,1},... | collective-permute-start | bytes 776 | tf_op jit(solution)/shard_map/ppermute | solution.py:351
  11.5 3.1 %collective-permute-start.4 = (bf16[128,512]{1,0:T(8,128)(2,1)S(1)}, bf16[128,512]{1,0:T(8,128)(2,1)S(1)}, u32[]{:S(2)}, u32[]{:S(2)}) collective-permute-start(bf16[128,512]{1,0:T(8,128)(2,1)S(1)} %copy-done), channel_id=1, source_target_pairs={{0,1},{1,0},{2,3},{3,2},{4,5},{5,4},{6,7},{7,6},{8,9},{9,8},{10,11... | collective-permute-start | bytes 393224 | tf_op jit(solution)/shard_map/ppermute | solution.py:351
  12.6 2.8 %collective-permute-start.5 = (bf16[128,512]{1,0:T(8,128)(2,1)S(1)}, bf16[128,512]{1,0:T(8,128)(2,1)S(1)}, u32[]{:S(2)}, u32[]{:S(2)}) collective-permute-start(bf16[128,512]{1,0:T(8,128)(2,1)S(1)} %collective-permute-done.3.refs_5_.refs_1_), channel_id=1, source_target_pairs={{0,1},{1,0},{2,3},{3,2},{4,5},{5,4},{6,7},{7,6},{8,9},{9,8},{10,11... | collective-permute-start | bytes 393224 | tf_op jit(solution)/shard_map/ppermute | solution.py:351
  13.5 1.1 %collective-permute-start.7 = (bf16[2,128]{1,0:T(2,128)(2,1)S(1)}, bf16[2,128]{1,0:T(2,128)(2,1)S(1)}, u32[]{:S(2)}, u32[]{:S(2)}) collective-permute-start(bf16[2,128]{1,0:T(2,128)(2,1)S(1)} %pad_maximum_fusion.2), channel_id=1, source_target_pairs={{0,1},{1,0},{2,3},{3,2},{4,5},{5,4},{6,7},{7,6},{8,9},{9,8},{10,11... | collective-permute-start | bytes 1544 | tf_op jit(solution)/shard_map/ppermute | solution.py:351
  16.7 1.3 %collective-permute-start.8 = (f32[32,256]{1,0:T(8,128)S(1)}, f32[32,256]{1,0:T(8,128)S(1)}, u32[]{:S(2)}, u32[]{:S(2)}) collective-permute-start(f32[32,256]{1,0:T(8,128)S(1)} %get-tuple-element.42), channel_id=1, source_target_pairs={{0,1},{1,0},{2,3},{3,2},{4,5},{5,4},{6,7},{7,6},{8,9},{9,8},{10,11... | collective-permute-start | bytes 98312 | tf_op jit(solution)/shard_map/ppermute | solution.py:351
  17.9 5.6 %collective-permute-start.12 = (f32[32,256]{1,0:T(8,128)S(1)}, f32[32,256]{1,0:T(8,128)S(1)}, u32[]{:S(2)}, u32[]{:S(2)}) collective-permute-start(f32[32,256]{1,0:T(8,128)S(1)} %add.9), channel_id=1, source_target_pairs={{0,8},{1,9},{2,10},{3,11},{4,12},{5,13},{6,14},{7,15},{8,0},{9,1},... | collective-permute-start | bytes 98312 | tf_op jit(solution)/shard_map/ppermute | solution.py:351
  20.5 6.1 %collective-permute-start.9 = (bf16[32,512]{1,0:T(8,128)(2,1)S(1)}, bf16[32,512]{1,0:T(8,128)(2,1)S(1)}, u32[]{:S(2)}, u32[]{:S(2)}) collective-permute-start(bf16[32,512]{1,0:T(8,128)(2,1)S(1)} %get-tuple-element.43), channel_id=1, source_target_pairs={{0,8},{1,9},{2,10},{3,11},{4,12},{5,13},{6,14},{7,15},{8,0},{9,1},... | collective-permute-start | bytes 98312 | tf_op jit(solution)/shard_map/ppermute | solution.py:351
  20.9 6.3 %collective-permute-start.10 = (bf16[32,512]{1,0:T(8,128)(2,1)S(1)}, bf16[32,512]{1,0:T(8,128)(2,1)S(1)}, u32[]{:S(2)}, u32[]{:S(2)}) collective-permute-start(bf16[32,512]{1,0:T(8,128)(2,1)S(1)} %get-tuple-element.43), channel_id=1, source_target_pairs={{0,1},{1,0},{2,3},{3,2},{4,5},{5,4},{6,7},{7,6},{8,9},{9,8},{10,11... | collective-permute-start | bytes 98312 | tf_op jit(solution)/shard_map/ppermute | solution.py:351
  20.9 6.3 %collective-permute-start.11 = (bf16[32,512]{1,0:T(8,128)(2,1)S(1)}, bf16[32,512]{1,0:T(8,128)(2,1)S(1)}, u32[]{:S(2)}, u32[]{:S(2)}) collective-permute-start(bf16[32,512]{1,0:T(8,128)(2,1)S(1)} %get-tuple-element.43), channel_id=1, source_target_pairs={{0,9},{1,8},{2,11},{3,10},{4,13},{5,12},{6,15},{7,14},{8,1},{9,0},... | collective-permute-start | bytes 98312 | tf_op jit(solution)/shard_map/ppermute | solution.py:351
  23.6 5.9 %collective-permute-start.13 = (f32[32,256]{1,0:T(8,128)S(1)}, f32[32,256]{1,0:T(8,128)S(1)}, u32[]{:S(2)}, u32[]{:S(2)}) collective-permute-start(f32[32,256]{1,0:T(8,128)S(1)} %add.10.refs_0_), channel_id=1, source_target_pairs={{0,6},{1,7},{2,4},{3,5},{4,2},{5,3},{6,0},{7,1},{8,14},{9,15},{10,... | collective-permute-start | bytes 98312 | tf_op jit(solution)/shard_map/ppermute | solution.py:351
  25.4 4.0 %collective-permute-start.14 = (f32[32,256]{1,0:T(8,128)S(1)}, f32[32,256]{1,0:T(8,128)S(1)}, u32[]{:S(2)}, u32[]{:S(2)}) collective-permute-start(f32[32,256]{1,0:T(8,128)S(1)} %add.10.refs_0_), channel_id=1, source_target_pairs={{0,4},{1,5},{2,6},{3,7},{4,0},{5,1},{6,2},{7,3},{8,12},{9,13},{10,... | collective-permute-start | bytes 98312 | tf_op jit(solution)/shard_map/ppermute | solution.py:351
  26.6 3.9 %collective-permute-start.15 = (f32[32,256]{1,0:T(8,128)S(1)}, f32[32,256]{1,0:T(8,128)S(1)}, u32[]{:S(2)}, u32[]{:S(2)}) collective-permute-start(f32[32,256]{1,0:T(8,128)S(1)} %add.10.refs_0_), channel_id=1, source_target_pairs={{0,2},{1,3},{2,0},{3,1},{4,6},{5,7},{6,4},{7,5},{8,10},{9,11},{10,... | collective-permute-start | bytes 98312 | tf_op jit(solution)/shard_map/ppermute | solution.py:351
  32.0 1.3 %collective-permute-start.16 = (f32[64,256]{1,0:T(8,128)S(1)}, f32[64,256]{1,0:T(8,128)S(1)}, u32[]{:S(2)}, u32[]{:S(2)}) collective-permute-start(f32[64,256]{1,0:T(8,128)S(1)} %solve.1.refs_0_), channel_id=1, source_target_pairs={{0,1},{1,0},{2,3},{3,2},{4,5},{5,4},{6,7},{7,6},{8,9},{9,8},{10,11... | collective-permute-start | bytes 196616 | tf_op jit(solution)/shard_map/ppermute | solution.py:351
  34.2 2.7 %collective-permute-start.17 = (bf16[128,512]{1,0:T(8,128)(2,1)S(1)}, bf16[128,512]{1,0:T(8,128)(2,1)S(1)}, u32[]{:S(2)}, u32[]{:S(2)}) collective-permute-start(bf16[128,512]{1,0:T(8,128)(2,1)S(1)} %get-tuple-element.53), channel_id=1, source_target_pairs={{0,1},{1,0},{2,3},{3,2},{4,5},{5,4},{6,7},{7,6},{8,9},{9,8},{10,11... | collective-permute-start | bytes 393224 | tf_op jit(solution)/shard_map/ppermute | solution.py:351
  34.9 10.1 %collective-permute-start.18 = (bf16[128,512]{1,0:T(8,128)(2,1)S(1)}, bf16[128,512]{1,0:T(8,128)(2,1)S(1)}, u32[]{:S(2)}, u32[]{:S(2)}) collective-permute-start(bf16[128,512]{1,0:T(8,128)(2,1)S(1)} %get-tuple-element.55), channel_id=1, source_target_pairs={{0,6},{1,7},{2,4},{3,5},{4,2},{5,3},{6,0},{7,1},{8,14},{9,15},{10,... | collective-permute-start | bytes 393224 | tf_op jit(solution)/shard_map/ppermute | solution.py:351
  35.9 10.3 %collective-permute-start.19 = (bf16[128,512]{1,0:T(8,128)(2,1)S(1)}, bf16[128,512]{1,0:T(8,128)(2,1)S(1)}, u32[]{:S(2)}, u32[]{:S(2)}) collective-permute-start(bf16[128,512]{1,0:T(8,128)(2,1)S(1)} %get-tuple-element.56), channel_id=1, source_target_pairs={{0,4},{1,5},{2,6},{3,7},{4,0},{5,1},{6,2},{7,3},{8,12},{9,13},{10,... | collective-permute-start | bytes 393224 | tf_op jit(solution)/shard_map/ppermute | solution.py:351
  36.9 9.3 %collective-permute-start.22 = (bf16[128,512]{1,0:T(8,128)(2,1)S(1)}, bf16[128,512]{1,0:T(8,128)(2,1)S(1)}, u32[]{:S(2)}, u32[]{:S(2)}) collective-permute-start(bf16[128,512]{1,0:T(8,128)(2,1)S(1)} %add_convert_fusion), channel_id=1, source_target_pairs={{0,8},{1,9},{2,10},{3,11},{4,12},{5,13},{6,14},{7,15},{8,0},{9,1},... | collective-permute-start | bytes 393224 | tf_op jit(solution)/shard_map/ppermute | solution.py:351
  38.7 7.5 %collective-permute-start.21 = (bf16[128,512]{1,0:T(8,128)(2,1)S(1)}, bf16[128,512]{1,0:T(8,128)(2,1)S(1)}, u32[]{:S(2)}, u32[]{:S(2)}) collective-permute-start(bf16[128,512]{1,0:T(8,128)(2,1)S(1)} %get-tuple-element.59), channel_id=1, source_target_pairs={{0,1},{1,0},{2,3},{3,2},{4,5},{5,4},{6,7},{7,6},{8,9},{9,8},{10,11... | collective-permute-start | bytes 393224 | tf_op jit(solution)/shard_map/ppermute | solution.py:351
  39.1 7.2 %collective-permute-start.20 = (bf16[128,512]{1,0:T(8,128)(2,1)S(1)}, bf16[128,512]{1,0:T(8,128)(2,1)S(1)}, u32[]{:S(2)}, u32[]{:S(2)}) collective-permute-start(bf16[128,512]{1,0:T(8,128)(2,1)S(1)} %basis_side.5), channel_id=1, source_target_pairs={{0,2},{1,3},{2,0},{3,1},{4,6},{5,7},{6,4},{7,5},{8,10},{9,11},{10,... | collective-permute-start | bytes 393224 | tf_op jit(solution)/shard_map/ppermute | solution.py:351
  (6 other events, 4.6 us)

commit v15 on v14

--- a/solution.py
+++ b/solution.py
@@ -15,7 +15,7 @@
 BF16 = jnp.bfloat16
 LANES = 128
 SUBLANES = 8
-CHUNK = 256
+CHUNK = 512
 VMEM_BYTES = 48 * 1024 * 1024
 LOG2_E = math.log2(math.e)
 SHARES = 2

time: 47.3 us -> 47 us (level)
  no operation moved by 1% of the time
where the time goes in v15:
time: 47 us; the launch traced here: 46.8 us
  starting transfers between devices  22.6 us (48%)
  Pallas kernels  12.3 us (26%)
  waiting for transfers between devices  8.02 us (17%)
  local copies, waits for them, and re-layouts  3.04 us (6%)
  between operations  0.79 us (2%)
    ppermute x23, starting transfers between devices, swap(): return lax.ppermute(x, 'paths', [(d, d ^ mask) for d in range(n)])  22.6 us
    pallas_call x12, Pallas kernels, call(): pl.pallas_call(kernel, out_shape=[jax.ShapeDtypeStruct(s, d) for s, d in...  12.3 us
    ppermute x23, waiting for transfers between devices, swap(): return lax.ppermute(x, 'paths', [(d, d ^ mask) for d in range(n)])  8.02 us
    unnamed x14, local copies, waits for them, and re-layouts  2.52 us
  transfers between devices with their start and end apart: 23, of which 9 were waited for; matrix products, arithmetic and copies ran while one was open for 1% of the time, Pallas kernels for 17%

profile of v15, /device:TPU:0, one launch (start us, length us, event | category | flops | bytes accessed | tf_op | source)
XLA Modules:
  0.0 46.8 jit_solution(16785969069688113023)
XLA Ops:
  0.6 4.1 %collective-permute-start.3 = (bf16[128,512]{1,0:T(8,128)(2,1)}, bf16[128,512]{1,0:T(8,128)(2,1)S(1)}, u32[]{:S(2)}, u32[]{:S(2)}) collective-permute-start(bf16[128,512]{1,0:T(8,128)(2,1)} %w_ref.1), channel_id=1, source_target_pairs={{0,8},{1,9},{2,10},{3,11},{4,12},{5,13},{6,14},{7,15},{8,0},{9,1},... | collective-permute-start | bytes 393224 | tf_op jit(solution)/shard_map/ppermute | solution.py:351
  4.7 1.6 %collective-permute-start.1 = (bf16[128,512]{1,0:T(8,128)(2,1)}, bf16[128,512]{1,0:T(8,128)(2,1)S(1)}, u32[]{:S(2)}, u32[]{:S(2)}) collective-permute-start(bf16[128,512]{1,0:T(8,128)(2,1)} %x_ref.1), channel_id=1, source_target_pairs={{0,4},{1,5},{2,6},{3,7},{4,0},{5,1},{6,2},{7,3},{8,12},{9,13},{10,... | collective-permute-start | bytes 393224 | tf_op jit(solution)/shard_map/ppermute | solution.py:351
  6.3 1.4 %collective-permute-start = (bf16[128,512]{1,0:T(8,128)(2,1)}, bf16[128,512]{1,0:T(8,128)(2,1)S(1)}, u32[]{:S(2)}, u32[]{:S(2)}) collective-permute-start(bf16[128,512]{1,0:T(8,128)(2,1)} %x_ref.1), channel_id=1, source_target_pairs={{0,6},{1,7},{2,4},{3,5},{4,2},{5,3},{6,0},{7,1},{8,14},{9,15},{10,... | collective-permute-start | bytes 393224 | tf_op jit(solution)/shard_map/ppermute | solution.py:351
  9.0 0.9 %copy-done = bf16[128,512]{1,0:T(8,128)(2,1)S(1)} copy-done((bf16[128,512]{1,0:T(8,128)(2,1)S(1)}, bf16[128,512]{1,0:T(8,128)(2,1)}, u32[]{:S(2)}) %copy-start) | copy-done | bytes 131096
  9.9 0.9 %copy-done.1 = bf16[128,512]{1,0:T(8,128)(2,1)S(1)} copy-done((bf16[128,512]{1,0:T(8,128)(2,1)S(1)}, bf16[128,512]{1,0:T(8,128)(2,1)}, u32[]{:S(2)}) %copy-start.1) | copy-done | bytes 131096
  11.6 0.9 %collective-permute-done.1.refs_2_.refs_4_ = bf16[128,512]{1,0:T(8,128)(2,1)S(1)} collective-permute-done((bf16[128,512]{1,0:T(8,128)(2,1)}, bf16[128,512]{1,0:T(8,128)(2,1)S(1)}, u32[]{:S(2)}, u32[]{:S(2)}) %collective-permute-start.1) | collective-permute-done | bytes 131104 | tf_op jit(solution)/shard_map/ppermute | solution.py:351
  12.6 0.9 %collective-permute-done.6 = bf16[128]{0:T(256)(128)(2,1)S(1)} collective-permute-done((bf16[128]{0:T(256)(128)(2,1)}, bf16[128]{0:T(256)(128)(2,1)S(1)}, u32[]{:S(2)}, u32[]{:S(2)}) %collective-permute-start.6) | collective-permute-done | bytes 288 | tf_op jit(solution)/shard_map/ppermute | solution.py:351
  13.5 1.1 %collective-permute-done.7 = bf16[2,128]{1,0:T(2,128)(2,1)S(1)} collective-permute-done((bf16[2,128]{1,0:T(2,128)(2,1)S(1)}, bf16[2,128]{1,0:T(2,128)(2,1)S(1)}, u32[]{:S(2)}, u32[]{:S(2)}) %collective-permute-start.7) | collective-permute-done | bytes 544 | tf_op jit(solution)/shard_map/ppermute | solution.py:351
  15.4 1.3 %forward.1 = (bf16[512,512]{1,0:T(8,128)(2,1)S(1)}, bf16[32,512]{1,0:T(8,128)(2,1)S(1)}, f32[32,256]{1,0:T(8,128)S(1)}, f32[32,256]{1,0:T(8,128)S(1)}) custom-call(bf16[128,512]{1,0:T(8,128)(2,1)S(1)} %get-tuple-element.33.refs_0_.refs_2_, bf16[128,512]{1,0:T(8,128)(2,1)S(1)} %collective-permute-done.refs_1_.refs_3_, ...), custom_call_target="tpu_custom_call" | custom-call | bytes 2196480 | tf_op jit(solution)/shard_map/forward/pallas_call | solution.py:323
  16.7 1.3 %collective-permute-done.8 = f32[32,256]{1,0:T(8,128)S(1)} collective-permute-done((f32[32,256]{1,0:T(8,128)S(1)}, f32[32,256]{1,0:T(8,128)S(1)}, u32[]{:S(2)}, u32[]{:S(2)}) %collective-permute-start.8) | collective-permute-done | bytes 32800 | tf_op jit(solution)/shard_map/ppermute | solution.py:351
  17.9 2.6 %collective-permute-start.12 = (f32[32,256]{1,0:T(8,128)S(1)}, f32[32,256]{1,0:T(8,128)S(1)}, u32[]{:S(2)}, u32[]{:S(2)}) collective-permute-start(f32[32,256]{1,0:T(8,128)S(1)} %add.9), channel_id=1, source_target_pairs={{0,8},{1,9},{2,10},{3,11},{4,12},{5,13},{6,14},{7,15},{8,0},{9,1},... | collective-permute-start | bytes 98312 | tf_op jit(solution)/shard_map/ppermute | solution.py:351
  20.9 2.7 %collective-permute-start.11 = (bf16[32,512]{1,0:T(8,128)(2,1)S(1)}, bf16[32,512]{1,0:T(8,128)(2,1)S(1)}, u32[]{:S(2)}, u32[]{:S(2)}) collective-permute-start(bf16[32,512]{1,0:T(8,128)(2,1)S(1)} %get-tuple-element.43), channel_id=1, source_target_pairs={{0,9},{1,8},{2,11},{3,10},{4,13},{5,12},{6,15},{7,14},{8,1},{9,0},... | collective-permute-start | bytes 98312 | tf_op jit(solution)/shard_map/ppermute | solution.py:351
  23.6 1.8 %collective-permute-start.13 = (f32[32,256]{1,0:T(8,128)S(1)}, f32[32,256]{1,0:T(8,128)S(1)}, u32[]{:S(2)}, u32[]{:S(2)}) collective-permute-start(f32[32,256]{1,0:T(8,128)S(1)} %add.10.refs_0_), channel_id=1, source_target_pairs={{0,6},{1,7},{2,4},{3,5},{4,2},{5,3},{6,0},{7,1},{8,14},{9,15},{10,... | collective-permute-start | bytes 98312 | tf_op jit(solution)/shard_map/ppermute | solution.py:351
  25.4 1.2 %collective-permute-start.14 = (f32[32,256]{1,0:T(8,128)S(1)}, f32[32,256]{1,0:T(8,128)S(1)}, u32[]{:S(2)}, u32[]{:S(2)}) collective-permute-start(f32[32,256]{1,0:T(8,128)S(1)} %add.10.refs_0_), channel_id=1, source_target_pairs={{0,4},{1,5},{2,6},{3,7},{4,0},{5,1},{6,2},{7,3},{8,12},{9,13},{10,... | collective-permute-start | bytes 98312 | tf_op jit(solution)/shard_map/ppermute | solution.py:351
  27.7 1.8 %inverse.1.inverse_ref = f32[32,32]{1,0:T(8,128)S(1)} custom-call(bf16[4,32,512]{2,1,0:T(8,128)(2,1)S(1)} %pad_maximum_fusion.small_ref), custom_call_target="tpu_custom_call" | custom-call | bytes 135168 | tf_op jit(solution)/shard_map/inverse/pallas_call | solution.py:323
  29.5 1.1 %collective-permute-done.15.refs_3_ = f32[32,256]{1,0:T(8,128)S(1)} collective-permute-done((f32[32,256]{1,0:T(8,128)S(1)}, f32[32,256]{1,0:T(8,128)S(1)}, u32[]{:S(2)}, u32[]{:S(2)}) %collective-permute-start.15) | collective-permute-done | bytes 32800 | tf_op jit(solution)/shard_map/ppermute | solution.py:351
  30.5 1.2 %solve.1.refs_0_ = f32[64,256]{1,0:T(8,128)S(1)} custom-call(f32[32,32]{1,0:T(8,128)S(1)} %inverse.1.inverse_ref, bf16[32,2048]{1,0:T(8,128)(2,1)S(1)} %get-tuple-element.47.design_ref, bf16[2048,128]{1,0:T(8,128)(2,1)S(1)} %get-tuple-element.44.rows_ref, f32[1,512]{1,0:T(1,128)S(1)} %get-tuple-element.45.thresh_ref, ...), custom_call_target="tpu_custom_call" | custom-call | bytes 860160 | tf_op jit(solution)/shard_map/solve/pallas_call | solution.py:323
  33.0 0.9 %weight_side.1 = (bf16[128,512]{1,0:T(8,128)(2,1)S(1)}, bf16[512,512]{1,0:T(8,128)(2,1)S(1)}, bf16[128,512]{1,0:T(8,128)(2,1)S(1)}, bf16[128,512]{1,0:T(8,128)(2...) custom-call(bf16[512,512]{1,0:T(8,128)(2,1)S(1)} %get-tuple-element.35.refs_9_.member_ref, ...), custom_call_target="tpu_custom_call" | custom-call | bytes 3932160 | tf_op jit(solution)/shard_map/weight_side/pallas_call | solution.py:323
  34.6 1.1 %collective-permute-start.18 = (bf16[128,512]{1,0:T(8,128)(2,1)S(1)}, bf16[128,512]{1,0:T(8,128)(2,1)S(1)}, u32[]{:S(2)}, u32[]{:S(2)}) collective-permute-start(bf16[128,512]{1,0:T(8,128)(2,1)S(1)} %get-tuple-element.55), channel_id=1, source_target_pairs={{0,6},{1,7},{2,4},{3,5},{4,2},{5,3},{6,0},{7,1},{8,14},{9,15},{10,... | collective-permute-start | bytes 393224 | tf_op jit(solution)/shard_map/ppermute | solution.py:351
  35.7 1.0 %collective-permute-start.19 = (bf16[128,512]{1,0:T(8,128)(2,1)S(1)}, bf16[128,512]{1,0:T(8,128)(2,1)S(1)}, u32[]{:S(2)}, u32[]{:S(2)}) collective-permute-start(bf16[128,512]{1,0:T(8,128)(2,1)S(1)} %get-tuple-element.56), channel_id=1, source_target_pairs={{0,4},{1,5},{2,6},{3,7},{4,0},{5,1},{6,2},{7,3},{8,12},{9,13},{10,... | collective-permute-start | bytes 393224 | tf_op jit(solution)/shard_map/ppermute | solution.py:351
  36.7 1.8 %collective-permute-start.22 = (bf16[128,512]{1,0:T(8,128)(2,1)S(1)}, bf16[128,512]{1,0:T(8,128)(2,1)S(1)}, u32[]{:S(2)}, u32[]{:S(2)}) collective-permute-start(bf16[128,512]{1,0:T(8,128)(2,1)S(1)} %add_convert_fusion), channel_id=1, source_target_pairs={{0,8},{1,9},{2,10},{3,11},{4,12},{5,13},{6,14},{7,15},{8,0},{9,1},... | collective-permute-start | bytes 393224 | tf_op jit(solution)/shard_map/ppermute | solution.py:351
  38.8 1.6 %collective-permute-start.20 = (bf16[128,512]{1,0:T(8,128)(2,1)S(1)}, bf16[128,512]{1,0:T(8,128)(2,1)S(1)}, u32[]{:S(2)}, u32[]{:S(2)}) collective-permute-start(bf16[128,512]{1,0:T(8,128)(2,1)S(1)} %basis_side.5), channel_id=1, source_target_pairs={{0,2},{1,3},{2,0},{3,1},{4,6},{5,7},{6,4},{7,5},{8,10},{9,11},{10,... | collective-permute-start | bytes 393224 | tf_op jit(solution)/shard_map/ppermute | solution.py:351
  40.4 3.1 %loss.1 = (f32[8,128]{1,0:T(8,128)S(1)}, f32[128,128]{1,0:T(8,128)S(1)}) custom-call(bf16[2048,128]{1,0:T(8,128)(2,1)S(1)} %get-tuple-element.44.rows_ref, f32[1,512]{1,0:T(1,128)S(1)} %get-tuple-element.45.thresh_ref, f32[1,512]{1,0:T(1,128)S(1)} %get-tuple-element.46.rate_ref, f32[64,256]{1,0:T(8,128)S(1)} %solve.1.refs_0_, ...), custom_call_target="tpu_custom_call" | custom-call | bytes 729088 | tf_op jit(solution)/shard_map/loss/pallas_call | solution.py:323
  44.7 1.3 %collective-permute-done.19.refs_2_ = bf16[128,512]{1,0:T(8,128)(2,1)S(1)} collective-permute-done((bf16[128,512]{1,0:T(8,128)(2,1)S(1)}, bf16[128,512]{1,0:T(8,128)(2,1)S(1)}, u32[]{:S(2)}, u32[]{:S(2)}) %collective-permute-start.19) | collective-permute-done | bytes 131104 | tf_op jit(solution)/shard_map/ppermute | solution.py:351
  (55 shorter events, 8.5 us)
Async XLA Ops:
  0.6 7.7 %copy-start.2 = (s32[2048]{0:T(1024)S(1)}, s32[2048]{0:T(1024)}, u32[]{:S(2)}) copy-start(s32[2048]{0:T(1024)} %param.10) | copy-start | bytes 24580
  0.6 10.9 %collective-permute-start.3 = (bf16[128,512]{1,0:T(8,128)(2,1)}, bf16[128,512]{1,0:T(8,128)(2,1)S(1)}, u32[]{:S(2)}, u32[]{:S(2)}) collective-permute-start(bf16[128,512]{1,0:T(8,128)(2,1)} %w_ref.1), channel_id=1, source_target_pairs={{0,8},{1,9},{2,10},{3,11},{4,12},{5,13},{6,14},{7,15},{8,0},{9,1},... | collective-permute-start | bytes 393224 | tf_op jit(solution)/shard_map/ppermute | solution.py:351
  4.7 7.8 %collective-permute-start.1 = (bf16[128,512]{1,0:T(8,128)(2,1)}, bf16[128,512]{1,0:T(8,128)(2,1)S(1)}, u32[]{:S(2)}, u32[]{:S(2)}) collective-permute-start(bf16[128,512]{1,0:T(8,128)(2,1)} %x_ref.1), channel_id=1, source_target_pairs={{0,4},{1,5},{2,6},{3,7},{4,0},{5,1},{6,2},{7,3},{8,12},{9,13},{10,... | collective-permute-start | bytes 393224 | tf_op jit(solution)/shard_map/ppermute | solution.py:351
  6.3 9.1 %collective-permute-start = (bf16[128,512]{1,0:T(8,128)(2,1)}, bf16[128,512]{1,0:T(8,128)(2,1)S(1)}, u32[]{:S(2)}, u32[]{:S(2)}) collective-permute-start(bf16[128,512]{1,0:T(8,128)(2,1)} %x_ref.1), channel_id=1, source_target_pairs={{0,6},{1,7},{2,4},{3,5},{4,2},{5,3},{6,0},{7,1},{8,14},{9,15},{10,... | collective-permute-start | bytes 393224 | tf_op jit(solution)/shard_map/ppermute | solution.py:351
  7.7 7.7 %collective-permute-start.2 = (bf16[128,512]{1,0:T(8,128)(2,1)}, bf16[128,512]{1,0:T(8,128)(2,1)S(1)}, u32[]{:S(2)}, u32[]{:S(2)}) collective-permute-start(bf16[128,512]{1,0:T(8,128)(2,1)} %x_ref.1), channel_id=1, source_target_pairs={{0,2},{1,3},{2,0},{3,1},{4,6},{5,7},{6,4},{7,5},{8,10},{9,11},{10,... | collective-permute-start | bytes 393224 | tf_op jit(solution)/shard_map/ppermute | solution.py:351
  8.2 5.3 %collective-permute-start.6 = (bf16[128]{0:T(256)(128)(2,1)}, bf16[128]{0:T(256)(128)(2,1)S(1)}, u32[]{:S(2)}, u32[]{:S(2)}) collective-permute-start(bf16[128]{0:T(256)(128)(2,1)} %param.9), channel_id=1, source_target_pairs={{0,8},{1,9},{2,10},{3,11},{4,12},{5,13},{6,14},{7,15},{8,0},{9,1},... | collective-permute-start | bytes 776 | tf_op jit(solution)/shard_map/ppermute | solution.py:351
  11.5 3.1 %collective-permute-start.4 = (bf16[128,512]{1,0:T(8,128)(2,1)S(1)}, bf16[128,512]{1,0:T(8,128)(2,1)S(1)}, u32[]{:S(2)}, u32[]{:S(2)}) collective-permute-start(bf16[128,512]{1,0:T(8,128)(2,1)S(1)} %copy-done), channel_id=1, source_target_pairs={{0,1},{1,0},{2,3},{3,2},{4,5},{5,4},{6,7},{7,6},{8,9},{9,8},{10,11... | collective-permute-start | bytes 393224 | tf_op jit(solution)/shard_map/ppermute | solution.py:351
  12.6 2.8 %collective-permute-start.5 = (bf16[128,512]{1,0:T(8,128)(2,1)S(1)}, bf16[128,512]{1,0:T(8,128)(2,1)S(1)}, u32[]{:S(2)}, u32[]{:S(2)}) collective-permute-start(bf16[128,512]{1,0:T(8,128)(2,1)S(1)} %collective-permute-done.3.refs_5_.refs_1_), channel_id=1, source_target_pairs={{0,1},{1,0},{2,3},{3,2},{4,5},{5,4},{6,7},{7,6},{8,9},{9,8},{10,11... | collective-permute-start | bytes 393224 | tf_op jit(solution)/shard_map/ppermute | solution.py:351
  13.5 1.1 %collective-permute-start.7 = (bf16[2,128]{1,0:T(2,128)(2,1)S(1)}, bf16[2,128]{1,0:T(2,128)(2,1)S(1)}, u32[]{:S(2)}, u32[]{:S(2)}) collective-permute-start(bf16[2,128]{1,0:T(2,128)(2,1)S(1)} %pad_maximum_fusion.2), channel_id=1, source_target_pairs={{0,1},{1,0},{2,3},{3,2},{4,5},{5,4},{6,7},{7,6},{8,9},{9,8},{10,11... | collective-permute-start | bytes 1544 | tf_op jit(solution)/shard_map/ppermute | solution.py:351
  16.7 1.3 %collective-permute-start.8 = (f32[32,256]{1,0:T(8,128)S(1)}, f32[32,256]{1,0:T(8,128)S(1)}, u32[]{:S(2)}, u32[]{:S(2)}) collective-permute-start(f32[32,256]{1,0:T(8,128)S(1)} %get-tuple-element.42), channel_id=1, source_target_pairs={{0,1},{1,0},{2,3},{3,2},{4,5},{5,4},{6,7},{7,6},{8,9},{9,8},{10,11... | collective-permute-start | bytes 98312 | tf_op jit(solution)/shard_map/ppermute | solution.py:351
  17.9 5.6 %collective-permute-start.12 = (f32[32,256]{1,0:T(8,128)S(1)}, f32[32,256]{1,0:T(8,128)S(1)}, u32[]{:S(2)}, u32[]{:S(2)}) collective-permute-start(f32[32,256]{1,0:T(8,128)S(1)} %add.9), channel_id=1, source_target_pairs={{0,8},{1,9},{2,10},{3,11},{4,12},{5,13},{6,14},{7,15},{8,0},{9,1},... | collective-permute-start | bytes 98312 | tf_op jit(solution)/shard_map/ppermute | solution.py:351
  20.5 6.1 %collective-permute-start.9 = (bf16[32,512]{1,0:T(8,128)(2,1)S(1)}, bf16[32,512]{1,0:T(8,128)(2,1)S(1)}, u32[]{:S(2)}, u32[]{:S(2)}) collective-permute-start(bf16[32,512]{1,0:T(8,128)(2,1)S(1)} %get-tuple-element.43), channel_id=1, source_target_pairs={{0,8},{1,9},{2,10},{3,11},{4,12},{5,13},{6,14},{7,15},{8,0},{9,1},... | collective-permute-start | bytes 98312 | tf_op jit(solution)/shard_map/ppermute | solution.py:351
  20.9 6.3 %collective-permute-start.10 = (bf16[32,512]{1,0:T(8,128)(2,1)S(1)}, bf16[32,512]{1,0:T(8,128)(2,1)S(1)}, u32[]{:S(2)}, u32[]{:S(2)}) collective-permute-start(bf16[32,512]{1,0:T(8,128)(2,1)S(1)} %get-tuple-element.43), channel_id=1, source_target_pairs={{0,1},{1,0},{2,3},{3,2},{4,5},{5,4},{6,7},{7,6},{8,9},{9,8},{10,11... | collective-permute-start | bytes 98312 | tf_op jit(solution)/shard_map/ppermute | solution.py:351
  20.9 6.3 %collective-permute-start.11 = (bf16[32,512]{1,0:T(8,128)(2,1)S(1)}, bf16[32,512]{1,0:T(8,128)(2,1)S(1)}, u32[]{:S(2)}, u32[]{:S(2)}) collective-permute-start(bf16[32,512]{1,0:T(8,128)(2,1)S(1)} %get-tuple-element.43), channel_id=1, source_target_pairs={{0,9},{1,8},{2,11},{3,10},{4,13},{5,12},{6,15},{7,14},{8,1},{9,0},... | collective-permute-start | bytes 98312 | tf_op jit(solution)/shard_map/ppermute | solution.py:351
  23.6 5.9 %collective-permute-start.13 = (f32[32,256]{1,0:T(8,128)S(1)}, f32[32,256]{1,0:T(8,128)S(1)}, u32[]{:S(2)}, u32[]{:S(2)}) collective-permute-start(f32[32,256]{1,0:T(8,128)S(1)} %add.10.refs_0_), channel_id=1, source_target_pairs={{0,6},{1,7},{2,4},{3,5},{4,2},{5,3},{6,0},{7,1},{8,14},{9,15},{10,... | collective-permute-start | bytes 98312 | tf_op jit(solution)/shard_map/ppermute | solution.py:351
  25.4 4.0 %collective-permute-start.14 = (f32[32,256]{1,0:T(8,128)S(1)}, f32[32,256]{1,0:T(8,128)S(1)}, u32[]{:S(2)}, u32[]{:S(2)}) collective-permute-start(f32[32,256]{1,0:T(8,128)S(1)} %add.10.refs_0_), channel_id=1, source_target_pairs={{0,4},{1,5},{2,6},{3,7},{4,0},{5,1},{6,2},{7,3},{8,12},{9,13},{10,... | collective-permute-start | bytes 98312 | tf_op jit(solution)/shard_map/ppermute | solution.py:351
  26.6 3.9 %collective-permute-start.15 = (f32[32,256]{1,0:T(8,128)S(1)}, f32[32,256]{1,0:T(8,128)S(1)}, u32[]{:S(2)}, u32[]{:S(2)}) collective-permute-start(f32[32,256]{1,0:T(8,128)S(1)} %add.10.refs_0_), channel_id=1, source_target_pairs={{0,2},{1,3},{2,0},{3,1},{4,6},{5,7},{6,4},{7,5},{8,10},{9,11},{10,... | collective-permute-start | bytes 98312 | tf_op jit(solution)/shard_map/ppermute | solution.py:351
  31.8 1.3 %collective-permute-start.16 = (f32[64,256]{1,0:T(8,128)S(1)}, f32[64,256]{1,0:T(8,128)S(1)}, u32[]{:S(2)}, u32[]{:S(2)}) collective-permute-start(f32[64,256]{1,0:T(8,128)S(1)} %solve.1.refs_0_), channel_id=1, source_target_pairs={{0,1},{1,0},{2,3},{3,2},{4,5},{5,4},{6,7},{7,6},{8,9},{9,8},{10,11... | collective-permute-start | bytes 196616 | tf_op jit(solution)/shard_map/ppermute | solution.py:351
  33.9 2.7 %collective-permute-start.17 = (bf16[128,512]{1,0:T(8,128)(2,1)S(1)}, bf16[128,512]{1,0:T(8,128)(2,1)S(1)}, u32[]{:S(2)}, u32[]{:S(2)}) collective-permute-start(bf16[128,512]{1,0:T(8,128)(2,1)S(1)} %get-tuple-element.53), channel_id=1, source_target_pairs={{0,1},{1,0},{2,3},{3,2},{4,5},{5,4},{6,7},{7,6},{8,9},{9,8},{10,11... | collective-permute-start | bytes 393224 | tf_op jit(solution)/shard_map/ppermute | solution.py:351
  34.6 10.1 %collective-permute-start.18 = (bf16[128,512]{1,0:T(8,128)(2,1)S(1)}, bf16[128,512]{1,0:T(8,128)(2,1)S(1)}, u32[]{:S(2)}, u32[]{:S(2)}) collective-permute-start(bf16[128,512]{1,0:T(8,128)(2,1)S(1)} %get-tuple-element.55), channel_id=1, source_target_pairs={{0,6},{1,7},{2,4},{3,5},{4,2},{5,3},{6,0},{7,1},{8,14},{9,15},{10,... | collective-permute-start | bytes 393224 | tf_op jit(solution)/shard_map/ppermute | solution.py:351
  35.7 10.3 %collective-permute-start.19 = (bf16[128,512]{1,0:T(8,128)(2,1)S(1)}, bf16[128,512]{1,0:T(8,128)(2,1)S(1)}, u32[]{:S(2)}, u32[]{:S(2)}) collective-permute-start(bf16[128,512]{1,0:T(8,128)(2,1)S(1)} %get-tuple-element.56), channel_id=1, source_target_pairs={{0,4},{1,5},{2,6},{3,7},{4,0},{5,1},{6,2},{7,3},{8,12},{9,13},{10,... | collective-permute-start | bytes 393224 | tf_op jit(solution)/shard_map/ppermute | solution.py:351
  36.7 9.3 %collective-permute-start.22 = (bf16[128,512]{1,0:T(8,128)(2,1)S(1)}, bf16[128,512]{1,0:T(8,128)(2,1)S(1)}, u32[]{:S(2)}, u32[]{:S(2)}) collective-permute-start(bf16[128,512]{1,0:T(8,128)(2,1)S(1)} %add_convert_fusion), channel_id=1, source_target_pairs={{0,8},{1,9},{2,10},{3,11},{4,12},{5,13},{6,14},{7,15},{8,0},{9,1},... | collective-permute-start | bytes 393224 | tf_op jit(solution)/shard_map/ppermute | solution.py:351
  38.5 7.5 %collective-permute-start.21 = (bf16[128,512]{1,0:T(8,128)(2,1)S(1)}, bf16[128,512]{1,0:T(8,128)(2,1)S(1)}, u32[]{:S(2)}, u32[]{:S(2)}) collective-permute-start(bf16[128,512]{1,0:T(8,128)(2,1)S(1)} %get-tuple-element.59), channel_id=1, source_target_pairs={{0,1},{1,0},{2,3},{3,2},{4,5},{5,4},{6,7},{7,6},{8,9},{9,8},{10,11... | collective-permute-start | bytes 393224 | tf_op jit(solution)/shard_map/ppermute | solution.py:351
  38.8 7.2 %collective-permute-start.20 = (bf16[128,512]{1,0:T(8,128)(2,1)S(1)}, bf16[128,512]{1,0:T(8,128)(2,1)S(1)}, u32[]{:S(2)}, u32[]{:S(2)}) collective-permute-start(bf16[128,512]{1,0:T(8,128)(2,1)S(1)} %basis_side.5), channel_id=1, source_target_pairs={{0,2},{1,3},{2,0},{3,1},{4,6},{5,7},{6,4},{7,5},{8,10},{9,11},{10,... | collective-permute-start | bytes 393224 | tf_op jit(solution)/shard_map/ppermute | solution.py:351
  (6 other events, 4.6 us)
